TPU v7x, 32 devices: a whole 2x2x4 slice. The times are simulated.
32 devices in a mesh: grp: 2 (over x), blk: 8 (over z, y), proj: 2 (over core).
Axes of the slice: x: 2, y: 2, z: 4, core: 2. Of those that a mesh axis runs over, the one named last changes fastest.
Arguments:
- doc_inputs: bfloat16 [8192, 2, 64, 128], P(('grp', 'blk'), 'proj'), parts along dimension 0, may hold values from -6 to 6
- doc_outgrads: bfloat16 [8192, 2, 64, 128], P(('grp', 'blk'), 'proj'), parts along dimension 0, may hold values from -6 to 6
- token_mask: int32 [8192, 128], P(('grp', 'blk')), parts along dimension 0, may hold values 0 or 1
- query_grads: bfloat16 [4096, 8192], P(('grp', 'blk'), 'proj'), parts along dimension 0, may hold values from -0.0078125 to 0.0078125
Outputs:
- scores: float32 [8192, 2048], P(('grp', 'blk', 'proj')), parts along dimension 0
There are 2 independent parts, one for each index of `grp`. A program takes and returns all parts, laid end to end along the dimension named above; each array names one. Nothing has to cross between parts.
All inputs are finite; a program needn't handle non-finite values. No bound on the sum of `token_mask` on one device may be relied on, other than what follows from the above.
Results may differ from a plain program's by a relative error of at most 0.0029.
Values may be sent and summed in bfloat16 or wider, within the bound.
No kernel may reach another device: no remote copies, remote signals or barrier semaphores. Data moves between devices by JAX's collectives and lax.ppermute only.
A program may use at most 128 MiB of HBM per device.

v0:
```python
import jax
import jax.numpy as jnp
from jax import lax
from jax.sharding import PartitionSpec as P


def on_device(doc_inputs, doc_outgrads, token_mask, query_grads):
    masked = doc_outgrads * token_mask[:, None, None, :].astype(jnp.bfloat16)
    formed = jnp.einsum(
        "dlit,dljt->dlij", doc_inputs, masked, preferred_element_type=jnp.float32
    ).astype(jnp.bfloat16)
    doc_rows = formed.shape[0]
    doc_flat = formed.reshape(doc_rows, -1)
    contract = (((1,), (1,)), ((), ()))
    everyone = lax.all_gather(query_grads, "blk", axis=0, tiled=True)
    scores = lax.dot_general(doc_flat, everyone, contract, preferred_element_type=jnp.float32)
    summed = lax.psum(scores, "proj")
    portion = doc_rows // lax.axis_size("proj")
    return lax.dynamic_slice_in_dim(summed, lax.axis_index("proj") * portion, portion, 0)


def solution(mesh):
    placed = (
        P(("grp", "blk"), "proj", None, None),
        P(("grp", "blk"), "proj", None, None),
        P(("grp", "blk"), None),
        P(("grp", "blk"), "proj"),
    )
    return jax.shard_map(
        on_device,
        mesh=mesh,
        in_specs=placed,
        out_specs=P(("grp", "blk", "proj"), None),
        check_vma=False,
    )
```

profile of v0, /device:TPU:0, one launch (start us, length us, event | category | flops | bytes accessed | tf_op | source)
XLA Modules:
  0.0 291.7 jit_solution(6433464930710849669)
XLA Ops:
  6.5 0.0 all-gather.2.cloned.1.call-start
  6.5 0.7 all-gather.2.cloned.1.call-update
  7.3 0.0 all-reduce.2.cloned.1.call-start
  7.3 1.0 convert_element_type.11
  8.3 10.2 %convert_bitcast_fusion = bf16[512,64,64]{1,2,0:T(8,128)(2,1)} fusion(bf16[512,1,64,128]{3,2,1,0:T(8,128)(2,1)} %param.4, bf16[512,1,64,128]{3,2,1,0:T(8,128)(2,1)} %param.5, bf16[512,128]{1,0:T(8,128)(2,1)S(1)} %convert_element_type.11), kind=kOutput, calls=%fused_computation.3 | convolution fusion | flops 543162368 | bytes 21102592 | tf_op jit(solution)/shard_map/dlit,dljt->dlij/dot_general | solution.py:9
  18.4 12.4 %copy.5 = bf16[512,64,64]{0,2,1:T(8,128)(2,1)} copy(bf16[512,64,64]{1,2,0:T(8,128)(2,1)} %convert_bitcast_fusion) | data formatting | bytes 8388608 | tf_op jit(solution)/shard_map/convert_element_type | solution.py:11
  30.9 209.0 %all-gather.2.cloned.1.call-done = bf16[2048,4096]{1,0:T(8,128)(2,1)} async-done(((bf16[256,4096]{1,0:T(8,128)(2,1)}), bf16[2048,4096]{1,0:T(8,128)(2,1)}) %all-gather.2.cloned.1.call-update) | async-done | bytes 16777232 | tf_op jit(solution)/shard_map/all_gather | solution.py:15
  239.8 15.0 %fusion.9 = f32[512,2048]{1,0:T(8,128)} fusion(bf16[512,4096]{0,1:T(8,128)(2,1)} %bitcast.15, bf16[2048,4096]{1,0:T(8,128)(2,1)} %all-gather.2.cloned.1.call-done), kind=kOutput, calls=%fused_computation.7 | convolution fusion | flops 8589934592 | bytes 25165824 | tf_op jit(solution)/shard_map/dot_general | solution.py:16
  254.9 0.0 all-reduce.2.cloned.1.call-update
  254.9 26.8 %all-reduce.2.cloned.1.call-done = f32[512,2048]{1,0:T(8,128)} async-done(((f32[512,2048]{1,0:T(8,128)}), f32[512,2048]{1,0:T(8,128)}) %all-reduce.2.cloned.1.call-update) | async-done | bytes 4194320 | tf_op jit(solution)/shard_map/psum | solution.py:17
  281.7 3.1 %constant_dynamic-slice_fusion = f32[256,2048]{1,0:T(8,128)} fusion(f32[512,2048]{1,0:T(8,128)} %all-reduce.2.cloned.1.call-done, s32[]{:T(128)S(6)} %select_n.3), kind=kLoop, calls=%fused_computation.6 | loop fusion | bytes 4194308 | tf_op jit(solution)/shard_map/dynamic_slice | solution.py:19
Async XLA Ops:
  6.5 233.3 %all-gather.2.cloned.1.call-start = ((), (), s32[]{:S(2)}) async-start(), calls=%async_computation | async-start | bytes 18874368 | tf_op jit(solution)/shard_map/all_gather | solution.py:15
  7.3 274.4 %all-reduce.2.cloned.1.call-start = ((), (), s32[]{:S(2)}) async-start(), calls=%async_computation.1 | async-start | bytes 8388608 | tf_op jit(solution)/shard_map/psum | solution.py:17
Sparse Core Ops, SparseCore 0:
  9.5 230.3 all-gather.1
  255.0 26.6 all-reduce.1
where the time goes:
time: 292 us
  waiting for transfers between devices  236 us (81%)
  matrix products  25.2 us (9%)
  local copies, waits for them, and re-layouts  15.5 us (5%)
  between operations  13.4 us (5%)
    all_gather x1, waiting for transfers between devices, on_device(): everyone = lax.all_gather(query_grads, 'blk', axis=0, tiled=True)  209 us
    psum x1, waiting for transfers between devices, on_device(): summed = lax.psum(scores, 'proj')  26.8 us
    dot_general x1, matrix products, on_device(): lax.dot_general(doc_flat, everyone, contract, preferred_element_type=jnp....  15 us
    convert_element_type x1, local copies, waits for them, and re-layouts, on_device(): formed = jnp.einsum('dlit,dljt->dlij', doc_inputs, masked, preferred_elem...  12.4 us
    dot_general x1, matrix products, on_device(): jnp.einsum('dlit,dljt->dlij', doc_inputs, masked, preferred_element_type=...  10.2 us
  transfers between devices with their start and end apart: 2, of which 2 were waited for; matrix products, arithmetic and copies ran while one was open for 8% of the time, Pallas kernels for 0%

commit v1 on v0

v1 whole, which is shorter than its diff:
```python
import jax
import jax.numpy as jnp
from jax import lax
from jax.sharding import PartitionSpec as P


def on_device(doc_inputs, doc_outgrads, token_mask, query_grads):
    blk = lax.axis_size("blk")
    places = blk // 2
    me = lax.axis_index("blk")
    place, side = me // 2, me % 2
    core = lax.axis_index("proj")
    docs = doc_inputs.shape[0]
    rank = doc_inputs.shape[2]
    queries = query_grads.shape[0]
    half = query_grads.shape[1] // 2
    part = docs // 2

    across = [(b, b ^ 1) for b in range(blk)]
    onward = [(b, (b + 2) % blk) for b in range(blk)]
    cores = [(0, 1), (1, 0)]
    diagonal = [(2 * b + c, 2 * (b ^ 1) + (c ^ 1)) for b in range(blk) for c in range(2)]

    def columns(array, which):
        return lax.dynamic_slice_in_dim(array, which * half, half, 1)

    mine = columns(query_grads, side)
    other = lax.ppermute(columns(query_grads, 1 - side), "blk", across)

    masked = doc_outgrads * token_mask[:, None, None, :].astype(jnp.bfloat16)
    formed = jnp.einsum(
        "dlit,dljt->dlij", doc_inputs, masked, preferred_element_type=jnp.float32
    ).astype(jnp.bfloat16)
    flat = formed.reshape(docs, rank * rank)
    flat = jnp.where(core == 0, flat, jnp.roll(flat, part, 0))
    kept = columns(flat, side)
    received = lax.ppermute(columns(flat, 1 - side), "blk", across)
    rows = jnp.concatenate([kept, received], 0)

    out = jnp.zeros((part, blk * queries), jnp.float32)
    contract = (((1,), (1,)), ((), ()))
    flows = [mine, other]
    for step in range(places):
        origin = (place - step + places) % places
        following = []
        if step + 1 < places:
            following = [lax.ppermute(block, "blk", onward) for block in flows]
        partials = [
            lax.dot_general(rows, block, contract, preferred_element_type=jnp.float32)
            for block in flows
        ]
        for which in range(2):
            near, far = partials[which], partials[1 - which]
            total = near[:part]
            total += lax.ppermute(near[part:2 * part].astype(jnp.bfloat16), "proj", cores).astype(jnp.float32)
            total += lax.ppermute(far[2 * part:3 * part].astype(jnp.bfloat16), "blk", across).astype(jnp.float32)
            total += lax.ppermute(far[3 * part:].astype(jnp.bfloat16), ("blk", "proj"), diagonal).astype(jnp.float32)
            owner = origin * 2 + (side if which == 0 else 1 - side)
            out = lax.dynamic_update_slice_in_dim(out, total, owner * queries, 1)
        flows = following
    return out


def solution(mesh):
    placed = (
        P(("grp", "blk"), "proj", None, None),
        P(("grp", "blk"), "proj", None, None),
        P(("grp", "blk"), None),
        P(("grp", "blk"), "proj"),
    )
    return jax.shard_map(
        on_device,
        mesh=mesh,
        in_specs=placed,
        out_specs=P(("grp", "blk", "proj"), None),
        check_vma=False,
    )
```

time: 292 us -> 249 us (0.85)
  waiting for transfers between devices: 236 us -> 148 us
  starting transfers between devices: 0.04 us -> 24.2 us
  local copies, waits for them, and re-layouts: 15.5 us -> 37.8 us
  between operations: 13.4 us -> 0.34 us
  matrix products: 25.2 us -> 32.5 us
  other arithmetic: 0.97 us -> 5.54 us
    all_gather x1 -> x0, waiting for transfers between devices: 209 us -> none  [on_device(): everyone = lax.all_gather(query_grads, 'blk', axis=0, tiled=True)]
    ppermute x0 -> x32, waiting for transfers between devices: none -> 148 us  [the longest x6 88.6 us: on_device(): following = [lax.ppermute(block, 'blk', onward) for block in flows]]
    psum x1 -> x0, waiting for transfers between devices: 26.8 us -> none  [on_device(): summed = lax.psum(scores, 'proj')]
    ppermute x0 -> x32, starting transfers between devices: none -> 24.2 us  [the longest x8 6.59 us: on_device(): lax.ppermute(far[2 * part:3 * part].astype(jnp.bfloat16), 'blk', across)]
    slice x0 -> x11, local copies, waits for them, and re-layouts: none -> 19.2 us  [the longest x3 19 us: on_device(): flat = jnp.where(core == 0, flat, jnp.roll(flat, part, 0))]
    dot_general x1 -> x8, matrix products: 15 us -> 24.3 us  [on_device(): lax.dot_general(rows, block, contract, preferred_element_type=jnp.float32)]
    unnamed x0 -> x6, local copies, waits for them, and re-layouts: none -> 4.59 us
    select_n x0 -> x1, other arithmetic: none -> 3.42 us  [on_device(): flat = jnp.where(core == 0, flat, jnp.roll(flat, part, 0))]
  transfers between devices with their start and end apart: 2 -> 32, of which waited for: 2 -> 14; matrix products, arithmetic and copies ran while one was open for 8% -> 9% of each run, Pallas kernels for 0% -> 0%
where the time goes in v1:
time: 249 us
  waiting for transfers between devices  148 us (59%)
  local copies, waits for them, and re-layouts  37.8 us (15%)
  matrix products  32.5 us (13%)
  starting transfers between devices  24.2 us (10%)
  other arithmetic  5.54 us (2%)
    ppermute x6, waiting for transfers between devices, on_device(): following = [lax.ppermute(block, 'blk', onward) for block in flows]  88.6 us
    ppermute x1, waiting for transfers between devices, on_device(): other = lax.ppermute(columns(query_grads, 1 - side), 'blk', across)  41.6 us
    dot_general x8, matrix products, on_device(): lax.dot_general(rows, block, contract, preferred_element_type=jnp.float32)  24.3 us
    slice x3, local copies, waits for them, and re-layouts, on_device(): flat = jnp.where(core == 0, flat, jnp.roll(flat, part, 0))  19 us
    convert_element_type x1, local copies, waits for them, and re-layouts, on_device(): formed = jnp.einsum('dlit,dljt->dlij', doc_inputs, masked, preferred_elem...  12 us
    ppermute x8, waiting for transfers between devices, on_device(): lax.ppermute(far[2 * part:3 * part].astype(jnp.bfloat16), 'blk', across)  11.6 us
    dot_general x1, matrix products, on_device(): jnp.einsum('dlit,dljt->dlij', doc_inputs, masked, preferred_element_type=...  8.21 us
    ppermute x8, starting transfers between devices, on_device(): lax.ppermute(far[2 * part:3 * part].astype(jnp.bfloat16), 'blk', across)  6.59 us
  transfers between devices with their start and end apart: 32, of which 14 were waited for; matrix products, arithmetic and copies ran while one was open for 9% of the time, Pallas kernels for 0%

profile of v1, /device:TPU:0, one launch (start us, length us, event | category | flops | bytes accessed | tf_op | source)
XLA Modules:
  0.0 248.8 jit_solution(529194666457173168)
XLA Ops:
  0.0 1.0 convert_element_type.107
  1.0 8.2 %convert_bitcast_fusion = bf16[512,64,64]{1,2,0:T(8,128)(2,1)S(1)} fusion(bf16[512,1,64,128]{3,2,1,0:T(8,128)(2,1)} %param.4, bf16[512,1,64,128]{3,2,1,0:T(8,128)(2,1)} %param.5, bf16[512,128]{1,0:T(8,128)(2,1)S(1)} %convert_element_type.107), kind=kOutput, calls=%fused_computation.3 | convolution fusion | flops 543162368 | bytes 21102592 | tf_op jit(solution)/shard_map/dlit,dljt->dlij/dot_general | solution.py:31
  9.2 3.3 %copy-done = bf16[512,64,64]{1,2,0:T(8,128)(2,1)} copy-done((bf16[512,64,64]{1,2,0:T(8,128)(2,1)}, bf16[512,64,64]{1,2,0:T(8,128)(2,1)S(1)}, u32[]{:S(2)}) %copy-start) | copy-done | bytes 4194328
  12.5 4.2 %fusion.41 = (bf16[256,64,64]{1,2,0:T(8,128)(2,1)}, bf16[256,64,64]{1,2,0:T(8,128)(2,1)}) fusion(bf16[512,64,64]{1,2,0:T(8,128)(2,1)S(1)} %convert_bitcast_fusion), kind=kLoop, calls=%fused_computation.52 | loop fusion | bytes 8388608 | tf_op jit(solution)/shard_map/jit(_roll_static)/slice | solution.py:35
  16.7 12.0 %copy.5 = bf16[512,64,64]{0,2,1:T(8,128)(2,1)} copy(bf16[512,64,64]{1,2,0:T(8,128)(2,1)} %copy-done) | data formatting | bytes 8388608 | tf_op jit(solution)/shard_map/convert_element_type | solution.py:33
  28.7 7.0 %copy.6 = bf16[256,64,64]{0,2,1:T(8,128)(2,1)S(1)} copy(bf16[256,64,64]{1,2,0:T(8,128)(2,1)} %get-tuple-element.5) | data formatting | bytes 4194304 | tf_op jit(solution)/shard_map/jit(_roll_static)/slice | solution.py:35
  35.7 7.8 %copy.7 = bf16[256,64,64]{0,2,1:T(8,128)(2,1)} copy(bf16[256,64,64]{1,2,0:T(8,128)(2,1)} %get-tuple-element.6) | data formatting | bytes 4194304 | tf_op jit(solution)/shard_map/jit(_roll_static)/slice | solution.py:35
  43.5 3.4 %maximum_select_fusion = bf16[512,4096]{0,1:T(8,128)(2,1)S(1)} fusion(bf16[256,4096]{0,1:T(8,128)(2,1)} %bitcast.25, bf16[256,4096]{0,1:T(8,128)(2,1)S(1)} %bitcast.24, bf16[512,64,64]{0,2,1:T(8,128)(2,1)} %copy.5, pred[]{:T(512)S(6)} %eq.9), kind=kLoop, calls=%fused_computation.5 | loop fusion | flops 10485760 | bytes 12582913 | tf_op jit(solution)/shard_map/jit(_where)/select_n | solution.py:35
  47.0 1.6 constant_dynamic-slice_fusion.3
  48.6 3.0 %collective-permute-start = (bf16[512,2048]{0,1:T(8,128)(2,1)}, bf16[512,2048]{0,1:T(8,128)(2,1)}, u32[]{:S(2)}, u32[]{:S(2)}) collective-permute-start(bf16[512,2048]{0,1:T(8,128)(2,1)} %get-tuple-element.8), channel_id=1, source_target_pairs={{0,2},{2,0},{4,6},{6,4},{8,10},{10,8},{12,14},{14,12},{1,3},{3,1},... | collective-permute-start | bytes 6291464 | tf_op jit(solution)/shard_map/ppermute | solution.py:37
  51.5 0.2 constant_dynamic-slice_fusion
  51.7 1.6 collective-permute-start.8
  53.3 0.7 collective-permute-start.2
  54.1 24.3 %collective-permute-done.8 = bf16[256,2048]{1,0:T(8,128)(2,1)} collective-permute-done((bf16[256,2048]{1,0:T(8,128)(2,1)S(1)}, bf16[256,2048]{1,0:T(8,128)(2,1)}, u32[]{:S(2)}, u32[]{:S(2)}) %collective-permute-start.8) | collective-permute-done | bytes 1048608 | tf_op jit(solution)/shard_map/ppermute | solution.py:47
  78.3 41.6 %collective-permute-done.2 = bf16[256,2048]{1,0:T(8,128)(2,1)} collective-permute-done((bf16[256,2048]{1,0:T(8,128)(2,1)S(1)}, bf16[256,2048]{1,0:T(8,128)(2,1)}, u32[]{:S(2)}, u32[]{:S(2)}) %collective-permute-start.2) | collective-permute-done | bytes 1048608 | tf_op jit(solution)/shard_map/ppermute | solution.py:28
  119.9 1.8 collective-permute-start.10
  121.7 3.2 %fusion.54 = (bf16[1024,256]{1,0:T(8,128)(2,1)S(1)}, f32[1024,256]{1,0:T(8,128)S(1)}) fusion(bf16[256,2048]{1,0:T(8,128)(2,1)} %collective-permute-done.16, bf16[512,2048]{0,1:T(8,128)(2,1)} %collective-permute-done, bf16[512,2048]{0,1:T(8,128)(2,1)S(1)} %get-tuple-element.7), kind=kOutput, calls=%fused_computation.65 | convolution fusion | flops 1082392576 | bytes 6815744 | tf_op jit(solution)/shard_map/dot_general | solution.py:49
  124.9 21.4 %collective-permute-done.10 = bf16[256,2048]{1,0:T(8,128)(2,1)} collective-permute-done((bf16[256,2048]{1,0:T(8,128)(2,1)}, bf16[256,2048]{1,0:T(8,128)(2,1)}, u32[]{:S(2)}, u32[]{:S(2)}) %collective-permute-start.10) | collective-permute-done | bytes 1048608 | tf_op jit(solution)/shard_map/ppermute | solution.py:47
  146.4 3.2 %fusion.53 = (bf16[1024,256]{1,0:T(8,128)(2,1)S(1)}, f32[1024,256]{1,0:T(8,128)S(1)}) fusion(bf16[256,2048]{1,0:T(8,128)(2,1)} %collective-permute-done.10, bf16[512,2048]{0,1:T(8,128)(2,1)} %collective-permute-done, bf16[512,2048]{0,1:T(8,128)(2,1)S(1)} %get-tuple-element.7), kind=kOutput, calls=%fused_computation.64 | convolution fusion | flops 1082392576 | bytes 6815744 | tf_op jit(solution)/shard_map/dot_general | solution.py:49
  149.6 1.5 collective-permute-start.11
  151.1 3.2 %fusion.51 = (bf16[1024,256]{1,0:T(8,128)(2,1)S(1)}, f32[1024,256]{1,0:T(8,128)S(1)}) fusion(bf16[256,2048]{1,0:T(8,128)(2,1)} %collective-permute-done.2, bf16[512,2048]{0,1:T(8,128)(2,1)} %collective-permute-done, bf16[512,2048]{0,1:T(8,128)(2,1)S(1)} %get-tuple-element.7), kind=kOutput, calls=%fused_computation.62 | convolution fusion | flops 1082392576 | bytes 6815744 | tf_op jit(solution)/shard_map/dot_general | solution.py:49
  154.3 0.6 collective-permute-start.3
  155.0 2.9 %fusion.50 = (bf16[1024,256]{1,0:T(8,128)(2,1)S(1)}, f32[1024,256]{1,0:T(8,128)S(1)}) fusion(bf16[256,2048]{1,0:T(8,128)(2,1)S(1)} %get-tuple-element.10, bf16[512,2048]{0,1:T(8,128)(2,1)} %collective-permute-done, bf16[512,2048]{0,1:T(8,128)(2,1)S(1)} %get-tuple-element.7), kind=kOutput, calls=%fused_computation.61 | convolution fusion | flops 1082392576 | bytes 6815744 | tf_op jit(solution)/shard_map/dot_general | solution.py:49
  157.9 1.6 collective-permute-start.1
  159.5 3.2 %fusion.52 = (bf16[1024,256]{1,0:T(8,128)(2,1)S(1)}, f32[1024,256]{1,0:T(8,128)S(1)}) fusion(bf16[256,2048]{1,0:T(8,128)(2,1)} %collective-permute-done.8, bf16[512,2048]{0,1:T(8,128)(2,1)} %collective-permute-done, bf16[512,2048]{0,1:T(8,128)(2,1)S(1)} %get-tuple-element.7), kind=kOutput, calls=%fused_computation.63 | convolution fusion | flops 1082392576 | bytes 6815744 | tf_op jit(solution)/shard_map/dot_general | solution.py:49
  162.8 0.1 collective-permute-start.5
  162.9 0.6 collective-permute-start.6
  163.5 1.2 collective-permute-start.7
  164.7 0.2 broadcast_in_dim.4
  164.9 0.1 fusion.32
  165.0 0.6 collective-permute-start.12
  165.6 3.6 %collective-permute-done.6 = bf16[256,256]{1,0:T(8,128)(2,1)S(1)} collective-permute-done((bf16[256,256]{1,0:T(8,128)(2,1)S(1)}, bf16[256,256]{1,0:T(8,128)(2,1)S(1)}, u32[]{:S(2)}, u32[]{:S(2)}) %collective-permute-start.6) | collective-permute-done | bytes 131104 | tf_op jit(solution)/shard_map/ppermute | solution.py:56
  169.2 1.9 collective-permute-done.7
  171.1 1.0 collective-permute-start.13
  172.1 0.1 fusion.29
  172.2 0.6 collective-permute-start.14
  172.8 1.1 collective-permute-done.12
  173.9 0.7 collective-permute-start.15
  174.7 1.3 collective-permute-start.24
  175.9 0.1 fusion.26
  176.0 0.1 collective-permute-start.17
  176.1 2.4 collective-permute-done.14
  178.5 0.6 collective-permute-start.22
  179.0 0.7 collective-permute-done.15
  179.8 7.8 %collective-permute-done.18 = bf16[256,2048]{1,0:T(8,128)(2,1)S(1)} collective-permute-done((bf16[256,2048]{1,0:T(8,128)(2,1)}, bf16[256,2048]{1,0:T(8,128)(2,1)S(1)}, u32[]{:S(2)}, u32[]{:S(2)}) %collective-permute-start.18) | collective-permute-done | bytes 1048608 | tf_op jit(solution)/shard_map/ppermute | solution.py:47
  187.6 2.9 %fusion.55 = (bf16[1024,256]{1,0:T(8,128)(2,1)S(1)}, f32[1024,256]{1,0:T(8,128)S(1)}) fusion(bf16[256,2048]{1,0:T(8,128)(2,1)S(1)} %collective-permute-done.18, bf16[512,2048]{0,1:T(8,128)(2,1)} %collective-permute-done, bf16[512,2048]{0,1:T(8,128)(2,1)S(1)} %get-tuple-element.7), kind=kOutput, calls=%fused_computation.66 | convolution fusion | flops 1082392576 | bytes 6815744 | tf_op jit(solution)/shard_map/dot_general | solution.py:49
  190.5 0.6 collective-permute-start.19
  191.1 18.9 %collective-permute-done.24 = bf16[256,2048]{1,0:T(8,128)(2,1)S(1)} collective-permute-done((bf16[256,2048]{1,0:T(8,128)(2,1)}, bf16[256,2048]{1,0:T(8,128)(2,1)S(1)}, u32[]{:S(2)}, u32[]{:S(2)}) %collective-permute-start.24) | collective-permute-done | bytes 1048608 | tf_op jit(solution)/shard_map/ppermute | solution.py:47
  210.0 2.9 %fusion.56 = (bf16[1024,256]{1,0:T(8,128)(2,1)S(1)}, f32[1024,256]{1,0:T(8,128)S(1)}) fusion(bf16[256,2048]{1,0:T(8,128)(2,1)S(1)} %collective-permute-done.24, bf16[512,2048]{0,1:T(8,128)(2,1)} %collective-permute-done, bf16[512,2048]{0,1:T(8,128)(2,1)S(1)} %get-tuple-element.7), kind=kOutput, calls=%fused_computation.67 | convolution fusion | flops 1082392576 | bytes 6815744 | tf_op jit(solution)/shard_map/dot_general | solution.py:49
  213.0 1.8 collective-permute-start.23
  214.8 0.1 collective-permute-done.20
  214.9 0.4 collective-permute-start.21
  215.3 0.1 fusion.20
  215.4 16.2 %collective-permute-done.26 = bf16[256,2048]{1,0:T(8,128)(2,1)S(1)} collective-permute-done((bf16[256,2048]{1,0:T(8,128)(2,1)S(1)}, bf16[256,2048]{1,0:T(8,128)(2,1)S(1)}, u32[]{:S(2)}, u32[]{:S(2)}) %collective-permute-start.26) | collective-permute-done | bytes 1048608 | tf_op jit(solution)/shard_map/ppermute | solution.py:47
  231.6 0.6 collective-permute-start.30
  232.2 2.9 %fusion.57 = (bf16[1024,256]{1,0:T(8,128)(2,1)S(1)}, f32[1024,256]{1,0:T(8,128)S(1)}) fusion(bf16[256,2048]{1,0:T(8,128)(2,1)S(1)} %collective-permute-done.26, bf16[512,2048]{0,1:T(8,128)(2,1)} %collective-permute-done, bf16[512,2048]{0,1:T(8,128)(2,1)S(1)} %get-tuple-element.7), kind=kOutput, calls=%fused_computation.68 | convolution fusion | flops 1082392576 | bytes 6815744 | tf_op jit(solution)/shard_map/dot_general | solution.py:49
  235.2 0.1 collective-permute-start.31
  235.2 1.5 collective-permute-start.27
  236.8 1.4 collective-permute-start.28
  238.2 0.1 collective-permute-start.29
  238.3 5.5 %collective-permute-done.27 = bf16[256,256]{1,0:T(8,128)(2,1)S(1)} collective-permute-done((bf16[256,256]{1,0:T(8,128)(2,1)S(1)}, bf16[256,256]{1,0:T(8,128)(2,1)S(1)}, u32[]{:S(2)}, u32[]{:S(2)}) %collective-permute-start.27) | collective-permute-done | bytes 131104 | tf_op jit(solution)/shard_map/ppermute | solution.py:56
  243.8 2.8 %collective-permute-done.28 = bf16[256,256]{1,0:T(8,128)(2,1)S(1)} collective-permute-done((bf16[256,256]{1,0:T(8,128)(2,1)S(1)}, bf16[256,256]{1,0:T(8,128)(2,1)S(1)}, u32[]{:S(2)}, u32[]{:S(2)}) %collective-permute-start.28) | collective-permute-done | bytes 131104 | tf_op jit(solution)/shard_map/ppermute | solution.py:57
  246.7 1.3 copy-done.2
  248.0 0.8 fusion.11
  (40 shorter events, 0.5 us)
Async XLA Ops:
  9.2 3.3 %copy-start = (bf16[512,64,64]{1,2,0:T(8,128)(2,1)}, bf16[512,64,64]{1,2,0:T(8,128)(2,1)S(1)}, u32[]{:S(2)}) copy-start(bf16[512,64,64]{1,2,0:T(8,128)(2,1)S(1)} %convert_bitcast_fusion) | copy-start | bytes 12582916
  46.9 4.6 %copy-start.1 = (bf16[256,4096]{1,0:T(8,128)(2,1)S(1)}, bf16[256,4096]{1,0:T(8,128)(2,1)}, u32[]{:S(2)}) copy-start(bf16[256,4096]{1,0:T(8,128)(2,1)} %param.7) | copy-start | bytes 6291460
  48.6 73.2 %collective-permute-start = (bf16[512,2048]{0,1:T(8,128)(2,1)}, bf16[512,2048]{0,1:T(8,128)(2,1)}, u32[]{:S(2)}, u32[]{:S(2)}) collective-permute-start(bf16[512,2048]{0,1:T(8,128)(2,1)} %get-tuple-element.8), channel_id=1, source_target_pairs={{0,2},{2,0},{4,6},{6,4},{8,10},{10,8},{12,14},{14,12},{1,3},{3,1},... | collective-permute-start | bytes 6291464 | tf_op jit(solution)/shard_map/ppermute | solution.py:37
  51.7 26.6 %collective-permute-start.8 = (bf16[256,2048]{1,0:T(8,128)(2,1)S(1)}, bf16[256,2048]{1,0:T(8,128)(2,1)}, u32[]{:S(2)}, u32[]{:S(2)}) collective-permute-start(bf16[256,2048]{1,0:T(8,128)(2,1)S(1)} %get-tuple-element.10), channel_id=1, source_target_pairs={{0,4},{2,6},{4,8},{6,10},{8,12},{10,14},{12,0},{14,2},{1,5},{3,7},... | collective-permute-start | bytes 3145736 | tf_op jit(solution)/shard_map/ppermute | solution.py:47
  53.3 66.6 %collective-permute-start.2 = (bf16[256,2048]{1,0:T(8,128)(2,1)S(1)}, bf16[256,2048]{1,0:T(8,128)(2,1)}, u32[]{:S(2)}, u32[]{:S(2)}) collective-permute-start(bf16[256,2048]{1,0:T(8,128)(2,1)S(1)} %get-tuple-element.9), channel_id=1, source_target_pairs={{0,2},{2,0},{4,6},{6,4},{8,10},{10,8},{12,14},{14,12},{1,3},{3,1},... | collective-permute-start | bytes 3145736 | tf_op jit(solution)/shard_map/ppermute | solution.py:28
  78.3 43.4 %collective-permute-start.16 = (bf16[256,2048]{1,0:T(8,128)(2,1)}, bf16[256,2048]{1,0:T(8,128)(2,1)}, u32[]{:S(2)}, u32[]{:S(2)}) collective-permute-start(bf16[256,2048]{1,0:T(8,128)(2,1)} %collective-permute-done.8), channel_id=1, source_target_pairs={{0,4},{2,6},{4,8},{6,10},{8,12},{10,14},{12,0},{14,2},{1,5},{3,7},... | collective-permute-start | bytes 3145736 | tf_op jit(solution)/shard_map/ppermute | solution.py:47
  119.9 26.5 %collective-permute-start.10 = (bf16[256,2048]{1,0:T(8,128)(2,1)}, bf16[256,2048]{1,0:T(8,128)(2,1)}, u32[]{:S(2)}, u32[]{:S(2)}) collective-permute-start(bf16[256,2048]{1,0:T(8,128)(2,1)} %collective-permute-done.2), channel_id=1, source_target_pairs={{0,4},{2,6},{4,8},{6,10},{8,12},{10,14},{12,0},{14,2},{1,5},{3,7},... | collective-permute-start | bytes 3145736 | tf_op jit(solution)/shard_map/ppermute | solution.py:47
  149.6 22.6 %collective-permute-start.11 = (bf16[256,256]{1,0:T(8,128)(2,1)S(1)}, bf16[256,256]{1,0:T(8,128)(2,1)S(1)}, u32[]{:S(2)}, u32[]{:S(2)}) collective-permute-start(bf16[256,256]{1,0:T(8,128)(2,1)S(1)} %get-tuple-element.25), channel_id=1, source_target_pairs={{0,2},{2,0},{4,6},{6,4},{8,10},{10,8},{12,14},{14,12},{1,3},{3,1},... | collective-permute-start | bytes 393224 | tf_op jit(solution)/shard_map/ppermute | solution.py:56
  154.3 8.4 %collective-permute-start.3 = (bf16[256,256]{1,0:T(8,128)(2,1)S(1)}, bf16[256,256]{1,0:T(8,128)(2,1)S(1)}, u32[]{:S(2)}, u32[]{:S(2)}) collective-permute-start(bf16[256,256]{1,0:T(8,128)(2,1)S(1)} %get-tuple-element.31), channel_id=1, source_target_pairs={{0,2},{2,0},{4,6},{6,4},{8,10},{10,8},{12,14},{14,12},{1,3},{3,1},... | collective-permute-start | bytes 393224 | tf_op jit(solution)/shard_map/ppermute | solution.py:56
  155.0 8.0 %collective-permute-start.4 = (bf16[256,256]{1,0:T(8,128)(2,1)S(1)}, bf16[256,256]{1,0:T(8,128)(2,1)S(1)}, u32[]{:S(2)}, u32[]{:S(2)}) collective-permute-start(bf16[256,256]{1,0:T(8,128)(2,1)S(1)} %get-tuple-element.30), channel_id=1, source_target_pairs={{0,3},{1,2},{2,1},{3,0},{4,7},{5,6},{6,5},{7,4},{8,11},{9,10},{10,... | collective-permute-start | bytes 393224 | tf_op jit(solution)/shard_map/ppermute | solution.py:57
  157.9 5.6 %collective-permute-start.1 = (bf16[256,256]{1,0:T(8,128)(2,1)S(1)}, bf16[256,256]{1,0:T(8,128)(2,1)S(1)}, u32[]{:S(2)}, u32[]{:S(2)}) collective-permute-start(bf16[256,256]{1,0:T(8,128)(2,1)S(1)} %get-tuple-element.34), channel_id=1, source_target_pairs={{0,1},{1,0},{2,3},{3,2},{4,5},{5,4},{6,7},{7,6},{8,9},{9,8},{10,11... | collective-permute-start | bytes 393224 | tf_op jit(solution)/shard_map/ppermute | solution.py:55
  159.5 28.0 %collective-permute-start.18 = (bf16[256,2048]{1,0:T(8,128)(2,1)}, bf16[256,2048]{1,0:T(8,128)(2,1)S(1)}, u32[]{:S(2)}, u32[]{:S(2)}) collective-permute-start(bf16[256,2048]{1,0:T(8,128)(2,1)} %collective-permute-done.10), channel_id=1, source_target_pairs={{0,4},{2,6},{4,8},{6,10},{8,12},{10,14},{12,0},{14,2},{1,5},{3,7},... | collective-permute-start | bytes 3145736 | tf_op jit(solution)/shard_map/ppermute | solution.py:47
  162.8 2.3 collective-permute-start.5
  162.9 6.3 %collective-permute-start.6 = (bf16[256,256]{1,0:T(8,128)(2,1)S(1)}, bf16[256,256]{1,0:T(8,128)(2,1)S(1)}, u32[]{:S(2)}, u32[]{:S(2)}) collective-permute-start(bf16[256,256]{1,0:T(8,128)(2,1)S(1)} %get-tuple-element.32), channel_id=1, source_target_pairs={{0,2},{2,0},{4,6},{6,4},{8,10},{10,8},{12,14},{14,12},{1,3},{3,1},... | collective-permute-start | bytes 393224 | tf_op jit(solution)/shard_map/ppermute | solution.py:56
  163.5 7.6 %collective-permute-start.7 = (bf16[256,256]{1,0:T(8,128)(2,1)S(1)}, bf16[256,256]{1,0:T(8,128)(2,1)S(1)}, u32[]{:S(2)}, u32[]{:S(2)}) collective-permute-start(bf16[256,256]{1,0:T(8,128)(2,1)S(1)} %get-tuple-element.33), channel_id=1, source_target_pairs={{0,3},{1,2},{2,1},{3,0},{4,7},{5,6},{6,5},{7,4},{8,11},{9,10},{10,... | collective-permute-start | bytes 393224 | tf_op jit(solution)/shard_map/ppermute | solution.py:57
  165.0 8.9 %collective-permute-start.12 = (bf16[256,256]{1,0:T(8,128)(2,1)S(1)}, bf16[256,256]{1,0:T(8,128)(2,1)S(1)}, u32[]{:S(2)}, u32[]{:S(2)}) collective-permute-start(bf16[256,256]{1,0:T(8,128)(2,1)S(1)} %get-tuple-element.24), channel_id=1, source_target_pairs={{0,3},{1,2},{2,1},{3,0},{4,7},{5,6},{6,5},{7,4},{8,11},{9,10},{10,... | collective-permute-start | bytes 393224 | tf_op jit(solution)/shard_map/ppermute | solution.py:57
  169.2 5.4 %collective-permute-start.9 = (bf16[256,256]{1,0:T(8,128)(2,1)S(1)}, bf16[256,256]{1,0:T(8,128)(2,1)S(1)}, u32[]{:S(2)}, u32[]{:S(2)}) collective-permute-start(bf16[256,256]{1,0:T(8,128)(2,1)S(1)} %get-tuple-element.28), channel_id=1, source_target_pairs={{0,1},{1,0},{2,3},{3,2},{4,5},{5,4},{6,7},{7,6},{8,9},{9,8},{10,11... | collective-permute-start | bytes 393224 | tf_op jit(solution)/shard_map/ppermute | solution.py:55
  171.1 4.9 %collective-permute-start.13 = (bf16[256,256]{1,0:T(8,128)(2,1)S(1)}, bf16[256,256]{1,0:T(8,128)(2,1)S(1)}, u32[]{:S(2)}, u32[]{:S(2)}) collective-permute-start(bf16[256,256]{1,0:T(8,128)(2,1)S(1)} %get-tuple-element.23), channel_id=1, source_target_pairs={{0,1},{1,0},{2,3},{3,2},{4,5},{5,4},{6,7},{7,6},{8,9},{9,8},{10,11... | collective-permute-start | bytes 393224 | tf_op jit(solution)/shard_map/ppermute | solution.py:55
  172.2 6.3 %collective-permute-start.14 = (bf16[256,256]{1,0:T(8,128)(2,1)S(1)}, bf16[256,256]{1,0:T(8,128)(2,1)S(1)}, u32[]{:S(2)}, u32[]{:S(2)}) collective-permute-start(bf16[256,256]{1,0:T(8,128)(2,1)S(1)} %get-tuple-element.26), channel_id=1, source_target_pairs={{0,2},{2,0},{4,6},{6,4},{8,10},{10,8},{12,14},{14,12},{1,3},{3,1},... | collective-permute-start | bytes 393224 | tf_op jit(solution)/shard_map/ppermute | solution.py:56
  173.9 5.8 %collective-permute-start.15 = (bf16[256,256]{1,0:T(8,128)(2,1)S(1)}, bf16[256,256]{1,0:T(8,128)(2,1)S(1)}, u32[]{:S(2)}, u32[]{:S(2)}) collective-permute-start(bf16[256,256]{1,0:T(8,128)(2,1)S(1)} %get-tuple-element.27), channel_id=1, source_target_pairs={{0,3},{1,2},{2,1},{3,0},{4,7},{5,6},{6,5},{7,4},{8,11},{9,10},{10,... | collective-permute-start | bytes 393224 | tf_op jit(solution)/shard_map/ppermute | solution.py:57
  174.7 35.4 %collective-permute-start.24 = (bf16[256,2048]{1,0:T(8,128)(2,1)}, bf16[256,2048]{1,0:T(8,128)(2,1)S(1)}, u32[]{:S(2)}, u32[]{:S(2)}) collective-permute-start(bf16[256,2048]{1,0:T(8,128)(2,1)} %collective-permute-done.16), channel_id=1, source_target_pairs={{0,4},{2,6},{4,8},{6,10},{8,12},{10,14},{12,0},{14,2},{1,5},{3,7},... | collective-permute-start | bytes 3145736 | tf_op jit(solution)/shard_map/ppermute | solution.py:47
  176.0 37.0 %collective-permute-start.17 = (bf16[256,256]{1,0:T(8,128)(2,1)S(1)}, bf16[256,256]{1,0:T(8,128)(2,1)S(1)}, u32[]{:S(2)}, u32[]{:S(2)}) collective-permute-start(bf16[256,256]{1,0:T(8,128)(2,1)S(1)} %get-tuple-element.22), channel_id=1, source_target_pairs={{0,1},{1,0},{2,3},{3,2},{4,5},{5,4},{6,7},{7,6},{8,9},{9,8},{10,11... | collective-permute-start | bytes 393224 | tf_op jit(solution)/shard_map/ppermute | solution.py:55
  178.5 56.7 %collective-permute-start.22 = (bf16[256,256]{1,0:T(8,128)(2,1)S(1)}, bf16[256,256]{1,0:T(8,128)(2,1)S(1)}, u32[]{:S(2)}, u32[]{:S(2)}) collective-permute-start(bf16[256,256]{1,0:T(8,128)(2,1)S(1)} %get-tuple-element.20), channel_id=1, source_target_pairs={{0,2},{2,0},{4,6},{6,4},{8,10},{10,8},{12,14},{14,12},{1,3},{3,1},... | collective-permute-start | bytes 393224 | tf_op jit(solution)/shard_map/ppermute | solution.py:56
  187.6 44.1 %collective-permute-start.26 = (bf16[256,2048]{1,0:T(8,128)(2,1)S(1)}, bf16[256,2048]{1,0:T(8,128)(2,1)S(1)}, u32[]{:S(2)}, u32[]{:S(2)}) collective-permute-start(bf16[256,2048]{1,0:T(8,128)(2,1)S(1)} %collective-permute-done.18), channel_id=1, source_target_pairs={{0,4},{2,6},{4,8},{6,10},{8,12},{10,14},{12,0},{14,2},{1,5},{3,7},... | collective-permute-start | bytes 3145736 | tf_op jit(solution)/shard_map/ppermute | solution.py:47
  190.5 24.3 %collective-permute-start.19 = (bf16[256,256]{1,0:T(8,128)(2,1)S(1)}, bf16[256,256]{1,0:T(8,128)(2,1)S(1)}, u32[]{:S(2)}, u32[]{:S(2)}) collective-permute-start(bf16[256,256]{1,0:T(8,128)(2,1)S(1)} %get-tuple-element.19), channel_id=1, source_target_pairs={{0,2},{2,0},{4,6},{6,4},{8,10},{10,8},{12,14},{14,12},{1,3},{3,1},... | collective-permute-start | bytes 393224 | tf_op jit(solution)/shard_map/ppermute | solution.py:56
  210.0 4.9 %collective-permute-start.20 = (bf16[256,256]{1,0:T(8,128)(2,1)S(1)}, bf16[256,256]{1,0:T(8,128)(2,1)S(1)}, u32[]{:S(2)}, u32[]{:S(2)}) collective-permute-start(bf16[256,256]{1,0:T(8,128)(2,1)S(1)} %get-tuple-element.18), channel_id=1, source_target_pairs={{0,3},{1,2},{2,1},{3,0},{4,7},{5,6},{6,5},{7,4},{8,11},{9,10},{10,... | collective-permute-start | bytes 393224 | tf_op jit(solution)/shard_map/ppermute | solution.py:57
  213.0 22.2 %collective-permute-start.23 = (bf16[256,256]{1,0:T(8,128)(2,1)S(1)}, bf16[256,256]{1,0:T(8,128)(2,1)S(1)}, u32[]{:S(2)}, u32[]{:S(2)}) collective-permute-start(bf16[256,256]{1,0:T(8,128)(2,1)S(1)} %get-tuple-element.21), channel_id=1, source_target_pairs={{0,3},{1,2},{2,1},{3,0},{4,7},{5,6},{6,5},{7,4},{8,11},{9,10},{10,... | collective-permute-start | bytes 393224 | tf_op jit(solution)/shard_map/ppermute | solution.py:57
  214.8 23.4 %collective-permute-start.25 = (bf16[256,256]{1,0:T(8,128)(2,1)S(1)}, bf16[256,256]{1,0:T(8,128)(2,1)S(1)}, u32[]{:S(2)}, u32[]{:S(2)}) collective-permute-start(bf16[256,256]{1,0:T(8,128)(2,1)S(1)} %get-tuple-element.16), channel_id=1, source_target_pairs={{0,1},{1,0},{2,3},{3,2},{4,5},{5,4},{6,7},{7,6},{8,9},{9,8},{10,11... | collective-permute-start | bytes 393224 | tf_op jit(solution)/shard_map/ppermute | solution.py:55
  214.9 21.8 %collective-permute-start.21 = (bf16[256,256]{1,0:T(8,128)(2,1)S(1)}, bf16[256,256]{1,0:T(8,128)(2,1)S(1)}, u32[]{:S(2)}, u32[]{:S(2)}) collective-permute-start(bf16[256,256]{1,0:T(8,128)(2,1)S(1)} %get-tuple-element.17), channel_id=1, source_target_pairs={{0,1},{1,0},{2,3},{3,2},{4,5},{5,4},{6,7},{7,6},{8,9},{9,8},{10,11... | collective-permute-start | bytes 393224 | tf_op jit(solution)/shard_map/ppermute | solution.py:55
  231.6 15.1 %collective-permute-start.30 = (bf16[256,256]{1,0:T(8,128)(2,1)S(1)}, bf16[256,256]{1,0:T(8,128)(2,1)S(1)}, u32[]{:S(2)}, u32[]{:S(2)}) collective-permute-start(bf16[256,256]{1,0:T(8,128)(2,1)S(1)} %get-tuple-element.14), channel_id=1, source_target_pairs={{0,2},{2,0},{4,6},{6,4},{8,10},{10,8},{12,14},{14,12},{1,3},{3,1},... | collective-permute-start | bytes 393224 | tf_op jit(solution)/shard_map/ppermute | solution.py:56
  235.2 11.5 %collective-permute-start.31 = (bf16[256,256]{1,0:T(8,128)(2,1)S(1)}, bf16[256,256]{1,0:T(8,128)(2,1)S(1)}, u32[]{:S(2)}, u32[]{:S(2)}) collective-permute-start(bf16[256,256]{1,0:T(8,128)(2,1)S(1)} %get-tuple-element.15), channel_id=1, source_target_pairs={{0,3},{1,2},{2,1},{3,0},{4,7},{5,6},{6,5},{7,4},{8,11},{9,10},{10,... | collective-permute-start | bytes 393224 | tf_op jit(solution)/shard_map/ppermute | solution.py:57
  235.2 8.6 %collective-permute-start.27 = (bf16[256,256]{1,0:T(8,128)(2,1)S(1)}, bf16[256,256]{1,0:T(8,128)(2,1)S(1)}, u32[]{:S(2)}, u32[]{:S(2)}) collective-permute-start(bf16[256,256]{1,0:T(8,128)(2,1)S(1)} %get-tuple-element.13), channel_id=1, source_target_pairs={{0,2},{2,0},{4,6},{6,4},{8,10},{10,8},{12,14},{14,12},{1,3},{3,1},... | collective-permute-start | bytes 393224 | tf_op jit(solution)/shard_map/ppermute | solution.py:56
  236.8 9.8 %collective-permute-start.28 = (bf16[256,256]{1,0:T(8,128)(2,1)S(1)}, bf16[256,256]{1,0:T(8,128)(2,1)S(1)}, u32[]{:S(2)}, u32[]{:S(2)}) collective-permute-start(bf16[256,256]{1,0:T(8,128)(2,1)S(1)} %get-tuple-element.12), channel_id=1, source_target_pairs={{0,3},{1,2},{2,1},{3,0},{4,7},{5,6},{6,5},{7,4},{8,11},{9,10},{10,... | collective-permute-start | bytes 393224 | tf_op jit(solution)/shard_map/ppermute | solution.py:57
  238.2 8.5 %collective-permute-start.29 = (bf16[256,256]{1,0:T(8,128)(2,1)S(1)}, bf16[256,256]{1,0:T(8,128)(2,1)S(1)}, u32[]{:S(2)}, u32[]{:S(2)}) collective-permute-start(bf16[256,256]{1,0:T(8,128)(2,1)S(1)} %get-tuple-element.11), channel_id=1, source_target_pairs={{0,1},{1,0},{2,3},{3,2},{4,5},{5,4},{6,7},{7,6},{8,9},{9,8},{10,11... | collective-permute-start | bytes 393224 | tf_op jit(solution)/shard_map/ppermute | solution.py:55
  246.7 1.3 copy-start.2

commit v2 on v1

v2 whole, which is shorter than its diff:
```python
import functools

import jax
import jax.numpy as jnp
from jax import lax
from jax.experimental import pallas as pl
from jax.experimental.pallas import tpu as pltpu
from jax.sharding import PartitionSpec as P

LANES = 128
VMEM_LIMIT = 48 * 1024 * 1024
ANYWHERE = pl.BlockSpec(memory_space=pl.ANY)
NT = (((1,), (1,)), ((), ()))


def form_body(rows, rank, spot, inputs, outgrads, mask, _after, kept, sent, rounds):
    def one(d, carry):
        masked = outgrads[d] * mask[pl.ds(d, 1), :].astype(jnp.bfloat16)
        twice = jnp.concatenate([masked, masked], 0)
        product = lax.dot_general(inputs[d], twice, NT, preferred_element_type=jnp.float32)
        rounds[pl.ds(d, rank, stride=rows), :] = product
        return carry

    lax.fori_loop(0, rows, one, 0, unroll=8)
    first = lax.broadcasted_iota(jnp.int32, (rows, LANES), 1) < rank
    for out, side in ((kept, spot[0]), (sent, 1 - spot[0])):
        for k in range(rank // 4):
            at = pl.multiple_of((side * (rank // 2) + 2 * k) * rows, rows)
            even = rounds[pl.ds(at, rows), :]
            odd = rounds[pl.ds(at + rows, rows), :]
            out[:, k * LANES:(k + 1) * LANES] = jnp.where(first, even, odd).astype(jnp.bfloat16)


def form(doc_inputs, doc_outgrads, token_mask, side, core, after):
    docs, rank, length = doc_inputs.shape
    rows = 32
    steps = docs // rows
    half = rank * rank // 2

    def at(g, spot):
        return lax.rem(g + spot[1] * (steps // 2), steps)

    return pl.pallas_call(
        functools.partial(form_body, rows, rank),
        grid_spec=pltpu.PrefetchScalarGridSpec(
            num_scalar_prefetch=1,
            grid=(steps,),
            in_specs=[
                pl.BlockSpec((rows, rank, length), lambda g, spot: (at(g, spot), 0, 0)),
                pl.BlockSpec((rows, rank, length), lambda g, spot: (at(g, spot), 0, 0)),
                pl.BlockSpec((rows, length), lambda g, spot: (at(g, spot), 0)),
                ANYWHERE,
            ],
            out_specs=[pl.BlockSpec((rows, half), lambda g, spot: (g, 0))] * 2,
            scratch_shapes=[pltpu.VMEM((rank * rows, LANES), jnp.float32)],
        ),
        out_shape=[jax.ShapeDtypeStruct((docs, half), jnp.bfloat16)] * 2,
        compiler_params=pltpu.CompilerParams(vmem_limit_bytes=VMEM_LIMIT),
        cost_estimate=pl.CostEstimate(
            flops=2 * docs * rank * rank * length, bytes_accessed=4 * docs * rank * length + 2 * docs * rank * rank, transcendentals=0
        ),
    )(jnp.stack([side, core]).astype(jnp.int32), doc_inputs, doc_outgrads, token_mask, after)


def score_body(own, far, block, _after, near, mate, across, diagonal):
    part = near.shape[0]

    def dot(rows):
        return lax.dot_general(rows, block[...], NT, preferred_element_type=jnp.float32)

    near[...] = dot(own[:part, :])
    mate[...] = dot(own[part:, :]).astype(jnp.bfloat16)
    across[...] = dot(far[:part, :]).astype(jnp.bfloat16)
    diagonal[...] = dot(far[part:, :]).astype(jnp.bfloat16)


def score(own, far, block, after):
    docs, depth = own.shape
    queries = block.shape[0]
    shape = (docs // 2, queries)
    whole = pl.BlockSpec(memory_space=pltpu.VMEM)
    return pl.pallas_call(
        score_body,
        in_specs=[whole, whole, whole, ANYWHERE],
        out_specs=[whole] * 4,
        out_shape=[jax.ShapeDtypeStruct(shape, jnp.float32)] + [jax.ShapeDtypeStruct(shape, jnp.bfloat16)] * 3,
        compiler_params=pltpu.CompilerParams(vmem_limit_bytes=VMEM_LIMIT),
        cost_estimate=pl.CostEstimate(
            flops=4 * docs * queries * depth, bytes_accessed=4 * docs * depth + 2 * queries * depth, transcendentals=0
        ),
    )(own, far, block, after)


def on_device(doc_inputs, doc_outgrads, token_mask, query_grads):
    blk = lax.axis_size("blk")
    places = blk // 2
    me = lax.axis_index("blk")
    place, side = me // 2, me % 2
    core = lax.axis_index("proj")
    docs = doc_inputs.shape[0]
    queries = query_grads.shape[0]
    half = query_grads.shape[1] // 2
    part = docs // 2

    across = [(b, b ^ 1) for b in range(blk)]
    onward = [(b, (b + 2) % blk) for b in range(blk)]
    cores = [(0, 1), (1, 0)]
    diagonal = [(2 * b + c, 2 * (b ^ 1) + (c ^ 1)) for b in range(blk) for c in range(2)]

    def columns(array, which):
        return lax.dynamic_slice_in_dim(array, which * half, half, 1)

    flows = [[columns(query_grads, side)], [lax.ppermute(columns(query_grads, 1 - side), "blk", across)]]
    for step in range(1, places):
        for flow in flows:
            flow.append(lax.ppermute(flow[-1], "blk", onward))

    own, sent = form(
        doc_inputs.reshape(docs, *doc_inputs.shape[2:]), doc_outgrads.reshape(docs, *doc_outgrads.shape[2:]),
        token_mask, side, core, flows[0][min(1, places - 1)],
    )
    far = lax.ppermute(sent, "blk", across)

    out = jnp.zeros((part, blk * queries), jnp.float32)
    last = token_mask
    for step in range(places):
        origin = (place - step + places) % places
        pieces = []
        for flow in flows:
            pieces.append(score(own, far, flow[step], last))
            last = pieces[-1][0]
        for which in range(2):
            near, mate = pieces[which][:2]
            beside, opposite = pieces[1 - which][2:]
            total = near + lax.ppermute(mate, "proj", cores).astype(jnp.float32)
            total += lax.ppermute(beside, "blk", across).astype(jnp.float32)
            total += lax.ppermute(opposite, ("blk", "proj"), diagonal).astype(jnp.float32)
            owner = origin * 2 + (side if which == 0 else 1 - side)
            out = lax.dynamic_update_slice_in_dim(out, total, owner * queries, 1)
    return out


def solution(mesh):
    placed = (
        P(("grp", "blk"), "proj", None, None),
        P(("grp", "blk"), "proj", None, None),
        P(("grp", "blk"), None),
        P(("grp", "blk"), "proj"),
    )
    return jax.shard_map(
        on_device,
        mesh=mesh,
        in_specs=placed,
        out_specs=P(("grp", "blk", "proj"), None),
        check_vma=False,
    )
```

time: 249 us -> 208 us (0.84)
  Pallas kernels: 0 us -> 51.5 us
  matrix products: 32.5 us -> 0 us
  local copies, waits for them, and re-layouts: 37.8 us -> 6.5 us
  waiting for transfers between devices: 148 us -> 123 us
  other arithmetic: 5.54 us -> 1.22 us
    pallas_call x0 -> x9, Pallas kernels: none -> 51.5 us  [the longest x1 27.1 us: form(): pl.pallas_call(functools.partial(form_body, rows, rank), grid_spec=pltpu....]
    dot_general x9 -> x0, matrix products: 32.5 us -> none  [the longest x8 24.3 us: on_device(): lax.dot_general(rows, block, contract, preferred_element_type=jnp.float32)]
    ppermute x32, waiting for transfers between devices: 148 us -> 123 us  [the longest x6 94.9 us: on_device(): flow.append(lax.ppermute(flow[-1], 'blk', onward))]
    slice x11 -> x0, local copies, waits for them, and re-layouts: 19.2 us -> none  [the longest x3 19 us: on_device(): flat = jnp.where(core == 0, flat, jnp.roll(flat, part, 0))]
    convert_element_type x1 -> x0, local copies, waits for them, and re-layouts: 12 us -> none  [on_device(): formed = jnp.einsum('dlit,dljt->dlij', doc_inputs, masked, preferred_elem...]
    select_n x1 -> x0, other arithmetic: 3.42 us -> none  [on_device(): flat = jnp.where(core == 0, flat, jnp.roll(flat, part, 0))]
  transfers between devices with their start and end apart: 32 -> 32, of which waited for: 14 -> 16; matrix products, arithmetic and copies ran while one was open for 9% -> 0% of each run, Pallas kernels for 0% -> 25%
where the time goes in v2:
time: 208 us
  waiting for transfers between devices  123 us (59%)
  Pallas kernels  51.5 us (25%)
  starting transfers between devices  24.6 us (12%)
  local copies, waits for them, and re-layouts  6.5 us (3%)
    ppermute x6, waiting for transfers between devices, on_device(): flow.append(lax.ppermute(flow[-1], 'blk', onward))  94.9 us
    pallas_call x1, Pallas kernels, form(): pl.pallas_call(functools.partial(form_body, rows, rank), grid_spec=pltpu....  27.1 us
    pallas_call x8, Pallas kernels, score(): pl.pallas_call(score_body, in_specs=[whole, whole, whole, ANYWHERE], out_...  24.4 us
    ppermute x8, waiting for transfers between devices, on_device(): total += lax.ppermute(beside, 'blk', across).astype(jnp.float32)  20.2 us
    ppermute x8, waiting for transfers between devices, on_device(): lax.ppermute(opposite, ('blk', 'proj'), diagonal).astype(jnp.float32)  8.3 us
    ppermute x8, starting transfers between devices, on_device(): lax.ppermute(opposite, ('blk', 'proj'), diagonal).astype(jnp.float32)  6.78 us
    ppermute x8, starting transfers between devices, on_device(): total += lax.ppermute(beside, 'blk', across).astype(jnp.float32)  6.09 us
    ppermute x8, starting transfers between devices, on_device(): total = near + lax.ppermute(mate, 'proj', cores).astype(jnp.float32)  4.36 us
  transfers between devices with their start and end apart: 32, of which 16 were waited for; matrix products, arithmetic and copies ran while one was open for 0% of the time, Pallas kernels for 25%

profile of v2, /device:TPU:0, one launch (start us, length us, event | category | flops | bytes accessed | tf_op | source)
XLA Modules:
  0.0 207.5 jit_solution(5625777456524323706)
XLA Ops:
  0.0 2.8 %constant_dynamic-slice_fusion = (bf16[256,2048]{1,0:T(8,128)(2,1)}, bf16[256,2048]{1,0:T(8,128)(2,1)S(1)}) fusion(bf16[256,4096]{1,0:T(8,128)(2,1)} %param.7, s32[]{:T(128)S(6)} %select_n.59, s32[]{:T(128)S(6)} %select_n.58), kind=kLoop, calls=%fused_computation.8 | loop fusion | bytes 4194312 | tf_op jit(solution)/shard_map/dynamic_slice | solution.py:111
  2.8 3.0 %collective-permute-start = (bf16[256,2048]{1,0:T(8,128)(2,1)S(1)}, bf16[256,2048]{1,0:T(8,128)(2,1)S(1)}, u32[]{:S(2)}, u32[]{:S(2)}) collective-permute-start(bf16[256,2048]{1,0:T(8,128)(2,1)S(1)} %get-tuple-element.74.block), channel_id=1, source_target_pairs={{0,4},{2,6},{4,8},{6,10},{8,12},{10,14},{12,0},{14,2},{1,5},{3,7},... | collective-permute-start | bytes 3145736 | tf_op jit(solution)/shard_map/ppermute | solution.py:116
  5.8 1.5 collective-permute-start.3
  7.3 0.1 pad_add_fusion.spot
  7.4 23.6 %collective-permute-done._after.block = bf16[256,2048]{1,0:T(8,128)(2,1)S(1)} collective-permute-done((bf16[256,2048]{1,0:T(8,128)(2,1)S(1)}, bf16[256,2048]{1,0:T(8,128)(2,1)S(1)}, u32[]{:S(2)}, u32[]{:S(2)}) %collective-permute-start) | collective-permute-done | bytes 1048608 | tf_op jit(solution)/shard_map/ppermute | solution.py:116
  31.0 1.0 copy-done
  32.0 1.2 copy-done.1
  33.2 27.1 %shard_map.46 = (bf16[512,2048]{1,0:T(8,128)(2,1)S(1)}, bf16[512,2048]{1,0:T(8,128)(2,1)}) custom-call(s32[2]{0:T(128)S(1)} %pad_add_fusion.spot, bf16[512,64,128]{2,1,0:T(8,128)(2,1)} %bitcast.4, bf16[512,64,128]{2,1,0:T(8,128)(2,1)} %bitcast.5, s32[512,128]{1,0:T(8,128)S(1)} %copy-done.3, bf16[256,2048]{1,0:T(8,128)(2,1)S(1)} %copy-done.1), custom_call_target="tpu_custom_call" | custom-call | flops 536870912 | bytes 20971520 | tf_op jit(solution)/shard_map/pallas_call | solution.py:43
  60.3 1.5 collective-permute-start.1
  61.8 1.3 collective-permute-start.16
  63.1 26.9 %collective-permute-done.10.block = bf16[256,2048]{1,0:T(8,128)(2,1)} collective-permute-done((bf16[256,2048]{1,0:T(8,128)(2,1)}, bf16[256,2048]{1,0:T(8,128)(2,1)}, u32[]{:S(2)}, u32[]{:S(2)}) %collective-permute-start.10) | collective-permute-done | bytes 1048608 | tf_op jit(solution)/shard_map/ppermute | solution.py:116
  90.0 22.5 %collective-permute-done.16.block = bf16[256,2048]{1,0:T(8,128)(2,1)} collective-permute-done((bf16[256,2048]{1,0:T(8,128)(2,1)S(1)}, bf16[256,2048]{1,0:T(8,128)(2,1)}, u32[]{:S(2)}, u32[]{:S(2)}) %collective-permute-start.16) | collective-permute-done | bytes 1048608 | tf_op jit(solution)/shard_map/ppermute | solution.py:116
  112.5 2.9 %shard_map.47 = (f32[256,256]{1,0:T(8,128)S(1)}, bf16[256,256]{1,0:T(8,128)(2,1)S(1)}, bf16[256,256]{1,0:T(8,128)(2,1)S(1)}, bf16[256,256]{1,0:T(8,128)(2,1)S(1)}) custom-call(bf16[512,2048]{1,0:T(8,128)(2,1)S(1)} %get-tuple-element.39.own, bf16[512,2048]{1,0:T(8,128)(2,1)} %collective-permute-done.1.far, bf16[256,2048]{1,0:T(8,128)(2,1)S(1)} %get-tuple-element.74.block, ...), custom_call_target="tpu_custom_call" | custom-call | flops 1073741824 | bytes 5242880 | tf_op jit(solution)/shard_map/pallas_call | solution.py:82
  115.4 3.2 %shard_map.48 = (f32[256,256]{1,0:T(8,128)S(1)}, bf16[256,256]{1,0:T(8,128)(2,1)S(1)}, bf16[256,256]{1,0:T(8,128)(2,1)S(1)}, bf16[256,256]{1,0:T(8,128)(2,1)S(1)}) custom-call(bf16[512,2048]{1,0:T(8,128)(2,1)S(1)} %get-tuple-element.39.own, bf16[512,2048]{1,0:T(8,128)(2,1)} %collective-permute-done.1.far, bf16[256,2048]{1,0:T(8,128)(2,1)} %collective-permute-done.3.block, ...), custom_call_target="tpu_custom_call" | custom-call | flops 1073741824 | bytes 5242880 | tf_op jit(solution)/shard_map/pallas_call | solution.py:82
  118.6 0.6 collective-permute-start.4
  119.2 1.6 collective-permute-start.2
  120.9 2.9 %shard_map.49 = (f32[256,256]{1,0:T(8,128)S(1)}, bf16[256,256]{1,0:T(8,128)(2,1)S(1)}, bf16[256,256]{1,0:T(8,128)(2,1)S(1)}, bf16[256,256]{1,0:T(8,128)(2,1)S(1)}) custom-call(bf16[512,2048]{1,0:T(8,128)(2,1)S(1)} %get-tuple-element.39.own, bf16[512,2048]{1,0:T(8,128)(2,1)} %collective-permute-done.1.far, bf16[256,2048]{1,0:T(8,128)(2,1)S(1)} %copy-done.2, ...), custom_call_target="tpu_custom_call" | custom-call | flops 1073741824 | bytes 5242880 | tf_op jit(solution)/shard_map/pallas_call | solution.py:82
  123.7 3.1 %shard_map.50 = (f32[256,256]{1,0:T(8,128)S(1)}, bf16[256,256]{1,0:T(8,128)(2,1)S(1)}, bf16[256,256]{1,0:T(8,128)(2,1)S(1)}, bf16[256,256]{1,0:T(8,128)(2,1)S(1)}) custom-call(bf16[512,2048]{1,0:T(8,128)(2,1)S(1)} %get-tuple-element.39.own, bf16[512,2048]{1,0:T(8,128)(2,1)} %collective-permute-done.1.far, bf16[256,2048]{1,0:T(8,128)(2,1)} %collective-permute-done.10.block, ...), custom_call_target="tpu_custom_call" | custom-call | flops 1073741824 | bytes 5242880 | tf_op jit(solution)/shard_map/pallas_call | solution.py:82
  126.9 3.1 %shard_map.51 = (f32[256,256]{1,0:T(8,128)S(1)}, bf16[256,256]{1,0:T(8,128)(2,1)S(1)}, bf16[256,256]{1,0:T(8,128)(2,1)S(1)}, bf16[256,256]{1,0:T(8,128)(2,1)S(1)}) custom-call(bf16[512,2048]{1,0:T(8,128)(2,1)S(1)} %get-tuple-element.39.own, bf16[512,2048]{1,0:T(8,128)(2,1)} %collective-permute-done.1.far, bf16[256,2048]{1,0:T(8,128)(2,1)} %collective-permute-done.16.block, ...), custom_call_target="tpu_custom_call" | custom-call | flops 1073741824 | bytes 5242880 | tf_op jit(solution)/shard_map/pallas_call | solution.py:82
  130.0 4.9 %collective-permute-done.18.block = bf16[256,2048]{1,0:T(8,128)(2,1)} collective-permute-done((bf16[256,2048]{1,0:T(8,128)(2,1)}, bf16[256,2048]{1,0:T(8,128)(2,1)}, u32[]{:S(2)}, u32[]{:S(2)}) %collective-permute-start.18) | collective-permute-done | bytes 1048608 | tf_op jit(solution)/shard_map/ppermute | solution.py:116
  135.0 3.1 %shard_map.52 = (f32[256,256]{1,0:T(8,128)S(1)}, bf16[256,256]{1,0:T(8,128)(2,1)S(1)}, bf16[256,256]{1,0:T(8,128)(2,1)S(1)}, bf16[256,256]{1,0:T(8,128)(2,1)S(1)}) custom-call(bf16[512,2048]{1,0:T(8,128)(2,1)S(1)} %get-tuple-element.39.own, bf16[512,2048]{1,0:T(8,128)(2,1)} %collective-permute-done.1.far, bf16[256,2048]{1,0:T(8,128)(2,1)} %collective-permute-done.18.block, ...), custom_call_target="tpu_custom_call" | custom-call | flops 1073741824 | bytes 5242880 | tf_op jit(solution)/shard_map/pallas_call | solution.py:82
  138.1 17.0 %collective-permute-done.24.block = bf16[256,2048]{1,0:T(8,128)(2,1)} collective-permute-done((bf16[256,2048]{1,0:T(8,128)(2,1)}, bf16[256,2048]{1,0:T(8,128)(2,1)}, u32[]{:S(2)}, u32[]{:S(2)}) %collective-permute-start.24) | collective-permute-done | bytes 1048608 | tf_op jit(solution)/shard_map/ppermute | solution.py:116
  155.2 3.1 %shard_map.53 = (f32[256,256]{1,0:T(8,128)S(1)}, bf16[256,256]{1,0:T(8,128)(2,1)S(1)}, bf16[256,256]{1,0:T(8,128)(2,1)S(1)}, bf16[256,256]{1,0:T(8,128)(2,1)S(1)}) custom-call(bf16[512,2048]{1,0:T(8,128)(2,1)S(1)} %get-tuple-element.39.own, bf16[512,2048]{1,0:T(8,128)(2,1)} %collective-permute-done.1.far, bf16[256,2048]{1,0:T(8,128)(2,1)} %collective-permute-done.24.block, ...), custom_call_target="tpu_custom_call" | custom-call | flops 1073741824 | bytes 5242880 | tf_op jit(solution)/shard_map/pallas_call | solution.py:82
  158.3 0.1 collective-permute-start.25
  158.4 0.5 collective-permute-start.6
  158.9 0.8 collective-permute-start.7
  159.6 0.7 collective-permute-start.8
  160.3 0.2 broadcast_in_dim.3
  160.6 0.1 add_dynamic-update-slice_fusion.7
  160.6 0.9 collective-permute-start.11
  161.6 3.7 %collective-permute-done.7 = bf16[256,256]{1,0:T(8,128)(2,1)S(1)} collective-permute-done((bf16[256,256]{1,0:T(8,128)(2,1)S(1)}, bf16[256,256]{1,0:T(8,128)(2,1)S(1)}, u32[]{:S(2)}, u32[]{:S(2)}) %collective-permute-start.7) | collective-permute-done | bytes 131104 | tf_op jit(solution)/shard_map/ppermute | solution.py:136
  165.2 1.1 collective-permute-done.8
  166.3 1.8 collective-permute-start.9
  168.2 0.1 add_dynamic-update-slice_fusion.6
  168.2 2.6 %collective-permute-done.11 = bf16[256,256]{1,0:T(8,128)(2,1)S(1)} collective-permute-done((bf16[256,256]{1,0:T(8,128)(2,1)S(1)}, bf16[256,256]{1,0:T(8,128)(2,1)S(1)}, u32[]{:S(2)}, u32[]{:S(2)}) %collective-permute-start.11) | collective-permute-done | bytes 131104 | tf_op jit(solution)/shard_map/ppermute | solution.py:136
  170.9 1.1 collective-permute-done.12
  171.9 0.7 collective-permute-start.14
  172.7 1.6 collective-permute-start.15
  174.3 0.1 add_dynamic-update-slice_fusion.5
  174.3 0.8 collective-permute-start.19
  175.2 3.1 %collective-permute-done.14 = bf16[256,256]{1,0:T(8,128)(2,1)S(1)} collective-permute-done((bf16[256,256]{1,0:T(8,128)(2,1)S(1)}, bf16[256,256]{1,0:T(8,128)(2,1)S(1)}, u32[]{:S(2)}, u32[]{:S(2)}) %collective-permute-start.14) | collective-permute-done | bytes 131104 | tf_op jit(solution)/shard_map/ppermute | solution.py:136
  178.3 0.5 collective-permute-start.20
  178.8 2.3 %collective-permute-done.15 = bf16[256,256]{1,0:T(8,128)(2,1)S(1)} collective-permute-done((bf16[256,256]{1,0:T(8,128)(2,1)S(1)}, bf16[256,256]{1,0:T(8,128)(2,1)S(1)}, u32[]{:S(2)}, u32[]{:S(2)}) %collective-permute-start.15) | collective-permute-done | bytes 131104 | tf_op jit(solution)/shard_map/ppermute | solution.py:137
  181.1 0.1 collective-permute-start.17
  181.2 0.1 add_dynamic-update-slice_fusion.4
  181.2 2.6 %collective-permute-done.19 = bf16[256,256]{1,0:T(8,128)(2,1)S(1)} collective-permute-done((bf16[256,256]{1,0:T(8,128)(2,1)S(1)}, bf16[256,256]{1,0:T(8,128)(2,1)S(1)}, u32[]{:S(2)}, u32[]{:S(2)}) %collective-permute-start.19) | collective-permute-done | bytes 131104 | tf_op jit(solution)/shard_map/ppermute | solution.py:136
  183.9 0.2 collective-permute-start.21
  184.0 2.7 %collective-permute-done.20 = bf16[256,256]{1,0:T(8,128)(2,1)S(1)} collective-permute-done((bf16[256,256]{1,0:T(8,128)(2,1)S(1)}, bf16[256,256]{1,0:T(8,128)(2,1)S(1)}, u32[]{:S(2)}, u32[]{:S(2)}) %collective-permute-start.20) | collective-permute-done | bytes 131104 | tf_op jit(solution)/shard_map/ppermute | solution.py:137
  186.7 0.7 collective-permute-start.22
  187.5 0.7 collective-permute-start.23
  188.2 0.1 add_dynamic-update-slice_fusion.3
  188.2 0.8 collective-permute-start.30
  189.0 2.9 %shard_map.54 = (f32[256,256]{1,0:T(8,128)S(1)}, bf16[256,256]{1,0:T(8,128)(2,1)S(1)}, bf16[256,256]{1,0:T(8,128)(2,1)S(1)}, bf16[256,256]{1,0:T(8,128)(2,1)S(1)}) custom-call(bf16[512,2048]{1,0:T(8,128)(2,1)S(1)} %get-tuple-element.39.own, bf16[512,2048]{1,0:T(8,128)(2,1)} %collective-permute-done.1.far, ...), custom_call_target="tpu_custom_call" | custom-call | flops 1073741824 | bytes 5242880 | tf_op jit(solution)/shard_map/pallas_call | solution.py:82
  191.9 1.4 collective-permute-start.31
  193.3 0.7 collective-permute-start.27
  194.1 0.1 collective-permute-done.23
  194.2 1.9 collective-permute-start.28
  196.1 0.1 add_dynamic-update-slice_fusion.2
  196.1 0.1 collective-permute-start.29
  196.2 8.1 %collective-permute-done.27 = bf16[256,256]{1,0:T(8,128)(2,1)S(1)} collective-permute-done((bf16[256,256]{1,0:T(8,128)(2,1)S(1)}, bf16[256,256]{1,0:T(8,128)(2,1)S(1)}, u32[]{:S(2)}, u32[]{:S(2)}) %collective-permute-start.27) | collective-permute-done | bytes 131104 | tf_op jit(solution)/shard_map/ppermute | solution.py:136
  204.3 1.1 collective-permute-done.28
  205.4 0.1 add_dynamic-update-slice_fusion.1
  205.5 1.3 copy-done.4
  206.8 0.8 add_dynamic-update-slice_fusion
  (30 shorter events, 0.1 us)
Async XLA Ops:
  0.0 32.0 %copy-start.3 = (s32[512,128]{1,0:T(8,128)S(1)}, s32[512,128]{1,0:T(8,128)}, u32[]{:S(2)}) copy-start(s32[512,128]{1,0:T(8,128)} %_after.1) | copy-start | bytes 786436
  2.8 28.2 %collective-permute-start = (bf16[256,2048]{1,0:T(8,128)(2,1)S(1)}, bf16[256,2048]{1,0:T(8,128)(2,1)S(1)}, u32[]{:S(2)}, u32[]{:S(2)}) collective-permute-start(bf16[256,2048]{1,0:T(8,128)(2,1)S(1)} %get-tuple-element.74.block), channel_id=1, source_target_pairs={{0,4},{2,6},{4,8},{6,10},{8,12},{10,14},{12,0},{14,2},{1,5},{3,7},... | collective-permute-start | bytes 3145736 | tf_op jit(solution)/shard_map/ppermute | solution.py:116
  5.8 56.0 %collective-permute-start.3 = (bf16[256,2048]{1,0:T(8,128)(2,1)}, bf16[256,2048]{1,0:T(8,128)(2,1)}, u32[]{:S(2)}, u32[]{:S(2)}) collective-permute-start(bf16[256,2048]{1,0:T(8,128)(2,1)} %get-tuple-element.73), channel_id=1, source_target_pairs={{0,2},{2,0},{4,6},{6,4},{8,10},{10,8},{12,14},{14,12},{1,3},{3,1},... | collective-permute-start | bytes 3145736 | tf_op jit(solution)/shard_map/ppermute | solution.py:113
  31.0 1.0 copy-start
  32.0 1.2 copy-start.1
  60.3 52.2 %collective-permute-start.1 = (bf16[512,2048]{1,0:T(8,128)(2,1)}, bf16[512,2048]{1,0:T(8,128)(2,1)}, u32[]{:S(2)}, u32[]{:S(2)}) collective-permute-start(bf16[512,2048]{1,0:T(8,128)(2,1)} %get-tuple-element.40), channel_id=1, source_target_pairs={{0,2},{2,0},{4,6},{6,4},{8,10},{10,8},{12,14},{14,12},{1,3},{3,1},... | collective-permute-start | bytes 6291464 | tf_op jit(solution)/shard_map/ppermute | solution.py:122
  61.8 28.2 %collective-permute-start.10 = (bf16[256,2048]{1,0:T(8,128)(2,1)}, bf16[256,2048]{1,0:T(8,128)(2,1)}, u32[]{:S(2)}, u32[]{:S(2)}) collective-permute-start(bf16[256,2048]{1,0:T(8,128)(2,1)} %collective-permute-done.3.block), channel_id=1, source_target_pairs={{0,4},{2,6},{4,8},{6,10},{8,12},{10,14},{12,0},{14,2},{1,5},{3,7},... | collective-permute-start | bytes 3145736 | tf_op jit(solution)/shard_map/ppermute | solution.py:116
  61.8 50.7 %collective-permute-start.16 = (bf16[256,2048]{1,0:T(8,128)(2,1)S(1)}, bf16[256,2048]{1,0:T(8,128)(2,1)}, u32[]{:S(2)}, u32[]{:S(2)}) collective-permute-start(bf16[256,2048]{1,0:T(8,128)(2,1)S(1)} %copy-done.1), channel_id=1, source_target_pairs={{0,4},{2,6},{4,8},{6,10},{8,12},{10,14},{12,0},{14,2},{1,5},{3,7},... | collective-permute-start | bytes 3145736 | tf_op jit(solution)/shard_map/ppermute | solution.py:116
  90.0 44.9 %collective-permute-start.18 = (bf16[256,2048]{1,0:T(8,128)(2,1)}, bf16[256,2048]{1,0:T(8,128)(2,1)}, u32[]{:S(2)}, u32[]{:S(2)}) collective-permute-start(bf16[256,2048]{1,0:T(8,128)(2,1)} %collective-permute-done.10.block), channel_id=1, source_target_pairs={{0,4},{2,6},{4,8},{6,10},{8,12},{10,14},{12,0},{14,2},{1,5},{3,7},... | collective-permute-start | bytes 3145736 | tf_op jit(solution)/shard_map/ppermute | solution.py:116
  112.5 42.7 %collective-permute-start.24 = (bf16[256,2048]{1,0:T(8,128)(2,1)}, bf16[256,2048]{1,0:T(8,128)(2,1)}, u32[]{:S(2)}, u32[]{:S(2)}) collective-permute-start(bf16[256,2048]{1,0:T(8,128)(2,1)} %collective-permute-done.16.block), channel_id=1, source_target_pairs={{0,4},{2,6},{4,8},{6,10},{8,12},{10,14},{12,0},{14,2},{1,5},{3,7},... | collective-permute-start | bytes 3145736 | tf_op jit(solution)/shard_map/ppermute | solution.py:116
  115.4 5.5 %copy-start.2 = (bf16[256,2048]{1,0:T(8,128)(2,1)S(1)}, bf16[256,2048]{1,0:T(8,128)(2,1)}, u32[]{:S(2)}) copy-start(bf16[256,2048]{1,0:T(8,128)(2,1)} %copy-done) | copy-start | bytes 3145732
  118.6 40.2 %collective-permute-start.4 = (bf16[256,256]{1,0:T(8,128)(2,1)S(1)}, bf16[256,256]{1,0:T(8,128)(2,1)S(1)}, u32[]{:S(2)}, u32[]{:S(2)}) collective-permute-start(bf16[256,256]{1,0:T(8,128)(2,1)S(1)} %get-tuple-element.43), channel_id=1, source_target_pairs={{0,2},{2,0},{4,6},{6,4},{8,10},{10,8},{12,14},{14,12},{1,3},{3,1},... | collective-permute-start | bytes 393224 | tf_op jit(solution)/shard_map/ppermute | solution.py:136
  119.2 40.4 %collective-permute-start.5 = (bf16[256,256]{1,0:T(8,128)(2,1)S(1)}, bf16[256,256]{1,0:T(8,128)(2,1)S(1)}, u32[]{:S(2)}, u32[]{:S(2)}) collective-permute-start(bf16[256,256]{1,0:T(8,128)(2,1)S(1)} %get-tuple-element.44), channel_id=1, source_target_pairs={{0,3},{1,2},{2,1},{3,0},{4,7},{5,6},{6,5},{7,4},{8,11},{9,10},{10,... | collective-permute-start | bytes 393224 | tf_op jit(solution)/shard_map/ppermute | solution.py:137
  119.2 41.1 %collective-permute-start.2 = (bf16[256,256]{1,0:T(8,128)(2,1)S(1)}, bf16[256,256]{1,0:T(8,128)(2,1)S(1)}, u32[]{:S(2)}, u32[]{:S(2)}) collective-permute-start(bf16[256,256]{1,0:T(8,128)(2,1)S(1)} %get-tuple-element.42), channel_id=1, source_target_pairs={{0,1},{1,0},{2,3},{3,2},{4,5},{5,4},{6,7},{7,6},{8,9},{9,8},{10,11... | collective-permute-start | bytes 393224 | tf_op jit(solution)/shard_map/ppermute | solution.py:135
  158.3 37.8 %collective-permute-start.25 = (bf16[256,256]{1,0:T(8,128)(2,1)S(1)}, bf16[256,256]{1,0:T(8,128)(2,1)S(1)}, u32[]{:S(2)}, u32[]{:S(2)}) collective-permute-start(bf16[256,256]{1,0:T(8,128)(2,1)S(1)} %get-tuple-element.66), channel_id=1, source_target_pairs={{0,1},{1,0},{2,3},{3,2},{4,5},{5,4},{6,7},{7,6},{8,9},{9,8},{10,11... | collective-permute-start | bytes 393224 | tf_op jit(solution)/shard_map/ppermute | solution.py:135
  158.4 2.2 %collective-permute-start.6 = (bf16[256,256]{1,0:T(8,128)(2,1)S(1)}, bf16[256,256]{1,0:T(8,128)(2,1)S(1)}, u32[]{:S(2)}, u32[]{:S(2)}) collective-permute-start(bf16[256,256]{1,0:T(8,128)(2,1)S(1)} %get-tuple-element.46), channel_id=1, source_target_pairs={{0,1},{1,0},{2,3},{3,2},{4,5},{5,4},{6,7},{7,6},{8,9},{9,8},{10,11... | collective-permute-start | bytes 393224 | tf_op jit(solution)/shard_map/ppermute | solution.py:135
  158.9 6.4 %collective-permute-start.7 = (bf16[256,256]{1,0:T(8,128)(2,1)S(1)}, bf16[256,256]{1,0:T(8,128)(2,1)S(1)}, u32[]{:S(2)}, u32[]{:S(2)}) collective-permute-start(bf16[256,256]{1,0:T(8,128)(2,1)S(1)} %get-tuple-element.47), channel_id=1, source_target_pairs={{0,2},{2,0},{4,6},{6,4},{8,10},{10,8},{12,14},{14,12},{1,3},{3,1},... | collective-permute-start | bytes 393224 | tf_op jit(solution)/shard_map/ppermute | solution.py:136
  159.6 6.7 %collective-permute-start.8 = (bf16[256,256]{1,0:T(8,128)(2,1)S(1)}, bf16[256,256]{1,0:T(8,128)(2,1)S(1)}, u32[]{:S(2)}, u32[]{:S(2)}) collective-permute-start(bf16[256,256]{1,0:T(8,128)(2,1)S(1)} %get-tuple-element.48), channel_id=1, source_target_pairs={{0,3},{1,2},{2,1},{3,0},{4,7},{5,6},{6,5},{7,4},{8,11},{9,10},{10,... | collective-permute-start | bytes 393224 | tf_op jit(solution)/shard_map/ppermute | solution.py:137
  160.3 27.9 %collective-permute-start.26 = (bf16[256,2048]{1,0:T(8,128)(2,1)}, bf16[256,2048]{1,0:T(8,128)(2,1)S(1)}, u32[]{:S(2)}, u32[]{:S(2)}) collective-permute-start(bf16[256,2048]{1,0:T(8,128)(2,1)} %collective-permute-done.18.block), channel_id=1, source_target_pairs={{0,4},{2,6},{4,8},{6,10},{8,12},{10,14},{12,0},{14,2},{1,5},{3,7},... | collective-permute-start | bytes 3145736 | tf_op jit(solution)/shard_map/ppermute | solution.py:116
  160.6 10.2 %collective-permute-start.11 = (bf16[256,256]{1,0:T(8,128)(2,1)S(1)}, bf16[256,256]{1,0:T(8,128)(2,1)S(1)}, u32[]{:S(2)}, u32[]{:S(2)}) collective-permute-start(bf16[256,256]{1,0:T(8,128)(2,1)S(1)} %get-tuple-element.51), channel_id=1, source_target_pairs={{0,2},{2,0},{4,6},{6,4},{8,10},{10,8},{12,14},{14,12},{1,3},{3,1},... | collective-permute-start | bytes 393224 | tf_op jit(solution)/shard_map/ppermute | solution.py:136
  165.2 6.7 %collective-permute-start.12 = (bf16[256,256]{1,0:T(8,128)(2,1)S(1)}, bf16[256,256]{1,0:T(8,128)(2,1)S(1)}, u32[]{:S(2)}, u32[]{:S(2)}) collective-permute-start(bf16[256,256]{1,0:T(8,128)(2,1)S(1)} %get-tuple-element.52), channel_id=1, source_target_pairs={{0,3},{1,2},{2,1},{3,0},{4,7},{5,6},{6,5},{7,4},{8,11},{9,10},{10,... | collective-permute-start | bytes 393224 | tf_op jit(solution)/shard_map/ppermute | solution.py:137
  166.3 6.4 %collective-permute-start.9 = (bf16[256,256]{1,0:T(8,128)(2,1)S(1)}, bf16[256,256]{1,0:T(8,128)(2,1)S(1)}, u32[]{:S(2)}, u32[]{:S(2)}) collective-permute-start(bf16[256,256]{1,0:T(8,128)(2,1)S(1)} %get-tuple-element.50), channel_id=1, source_target_pairs={{0,1},{1,0},{2,3},{3,2},{4,5},{5,4},{6,7},{7,6},{8,9},{9,8},{10,11... | collective-permute-start | bytes 393224 | tf_op jit(solution)/shard_map/ppermute | solution.py:135
  170.9 3.5 %collective-permute-start.13 = (bf16[256,256]{1,0:T(8,128)(2,1)S(1)}, bf16[256,256]{1,0:T(8,128)(2,1)S(1)}, u32[]{:S(2)}, u32[]{:S(2)}) collective-permute-start(bf16[256,256]{1,0:T(8,128)(2,1)S(1)} %get-tuple-element.54), channel_id=1, source_target_pairs={{0,1},{1,0},{2,3},{3,2},{4,5},{5,4},{6,7},{7,6},{8,9},{9,8},{10,11... | collective-permute-start | bytes 393224 | tf_op jit(solution)/shard_map/ppermute | solution.py:135
  171.9 6.3 %collective-permute-start.14 = (bf16[256,256]{1,0:T(8,128)(2,1)S(1)}, bf16[256,256]{1,0:T(8,128)(2,1)S(1)}, u32[]{:S(2)}, u32[]{:S(2)}) collective-permute-start(bf16[256,256]{1,0:T(8,128)(2,1)S(1)} %get-tuple-element.55), channel_id=1, source_target_pairs={{0,2},{2,0},{4,6},{6,4},{8,10},{10,8},{12,14},{14,12},{1,3},{3,1},... | collective-permute-start | bytes 393224 | tf_op jit(solution)/shard_map/ppermute | solution.py:136
  172.7 8.4 %collective-permute-start.15 = (bf16[256,256]{1,0:T(8,128)(2,1)S(1)}, bf16[256,256]{1,0:T(8,128)(2,1)S(1)}, u32[]{:S(2)}, u32[]{:S(2)}) collective-permute-start(bf16[256,256]{1,0:T(8,128)(2,1)S(1)} %get-tuple-element.56), channel_id=1, source_target_pairs={{0,3},{1,2},{2,1},{3,0},{4,7},{5,6},{6,5},{7,4},{8,11},{9,10},{10,... | collective-permute-start | bytes 393224 | tf_op jit(solution)/shard_map/ppermute | solution.py:137
  174.3 9.5 %collective-permute-start.19 = (bf16[256,256]{1,0:T(8,128)(2,1)S(1)}, bf16[256,256]{1,0:T(8,128)(2,1)S(1)}, u32[]{:S(2)}, u32[]{:S(2)}) collective-permute-start(bf16[256,256]{1,0:T(8,128)(2,1)S(1)} %get-tuple-element.59), channel_id=1, source_target_pairs={{0,2},{2,0},{4,6},{6,4},{8,10},{10,8},{12,14},{14,12},{1,3},{3,1},... | collective-permute-start | bytes 393224 | tf_op jit(solution)/shard_map/ppermute | solution.py:136
  178.3 8.5 %collective-permute-start.20 = (bf16[256,256]{1,0:T(8,128)(2,1)S(1)}, bf16[256,256]{1,0:T(8,128)(2,1)S(1)}, u32[]{:S(2)}, u32[]{:S(2)}) collective-permute-start(bf16[256,256]{1,0:T(8,128)(2,1)S(1)} %get-tuple-element.60), channel_id=1, source_target_pairs={{0,3},{1,2},{2,1},{3,0},{4,7},{5,6},{6,5},{7,4},{8,11},{9,10},{10,... | collective-permute-start | bytes 393224 | tf_op jit(solution)/shard_map/ppermute | solution.py:137
  181.1 6.3 %collective-permute-start.17 = (bf16[256,256]{1,0:T(8,128)(2,1)S(1)}, bf16[256,256]{1,0:T(8,128)(2,1)S(1)}, u32[]{:S(2)}, u32[]{:S(2)}) collective-permute-start(bf16[256,256]{1,0:T(8,128)(2,1)S(1)} %get-tuple-element.58), channel_id=1, source_target_pairs={{0,1},{1,0},{2,3},{3,2},{4,5},{5,4},{6,7},{7,6},{8,9},{9,8},{10,11... | collective-permute-start | bytes 393224 | tf_op jit(solution)/shard_map/ppermute | solution.py:135
  183.9 8.0 %collective-permute-start.21 = (bf16[256,256]{1,0:T(8,128)(2,1)S(1)}, bf16[256,256]{1,0:T(8,128)(2,1)S(1)}, u32[]{:S(2)}, u32[]{:S(2)}) collective-permute-start(bf16[256,256]{1,0:T(8,128)(2,1)S(1)} %get-tuple-element.62), channel_id=1, source_target_pairs={{0,1},{1,0},{2,3},{3,2},{4,5},{5,4},{6,7},{7,6},{8,9},{9,8},{10,11... | collective-permute-start | bytes 393224 | tf_op jit(solution)/shard_map/ppermute | solution.py:135
  186.7 6.6 %collective-permute-start.22 = (bf16[256,256]{1,0:T(8,128)(2,1)S(1)}, bf16[256,256]{1,0:T(8,128)(2,1)S(1)}, u32[]{:S(2)}, u32[]{:S(2)}) collective-permute-start(bf16[256,256]{1,0:T(8,128)(2,1)S(1)} %get-tuple-element.63), channel_id=1, source_target_pairs={{0,2},{2,0},{4,6},{6,4},{8,10},{10,8},{12,14},{14,12},{1,3},{3,1},... | collective-permute-start | bytes 393224 | tf_op jit(solution)/shard_map/ppermute | solution.py:136
  187.5 6.7 %collective-permute-start.23 = (bf16[256,256]{1,0:T(8,128)(2,1)S(1)}, bf16[256,256]{1,0:T(8,128)(2,1)S(1)}, u32[]{:S(2)}, u32[]{:S(2)}) collective-permute-start(bf16[256,256]{1,0:T(8,128)(2,1)S(1)} %get-tuple-element.64), channel_id=1, source_target_pairs={{0,3},{1,2},{2,1},{3,0},{4,7},{5,6},{6,5},{7,4},{8,11},{9,10},{10,... | collective-permute-start | bytes 393224 | tf_op jit(solution)/shard_map/ppermute | solution.py:137
  188.2 17.2 %collective-permute-start.30 = (bf16[256,256]{1,0:T(8,128)(2,1)S(1)}, bf16[256,256]{1,0:T(8,128)(2,1)S(1)}, u32[]{:S(2)}, u32[]{:S(2)}) collective-permute-start(bf16[256,256]{1,0:T(8,128)(2,1)S(1)} %get-tuple-element.71), channel_id=1, source_target_pairs={{0,2},{2,0},{4,6},{6,4},{8,10},{10,8},{12,14},{14,12},{1,3},{3,1},... | collective-permute-start | bytes 393224 | tf_op jit(solution)/shard_map/ppermute | solution.py:136
  191.9 13.5 %collective-permute-start.31 = (bf16[256,256]{1,0:T(8,128)(2,1)S(1)}, bf16[256,256]{1,0:T(8,128)(2,1)S(1)}, u32[]{:S(2)}, u32[]{:S(2)}) collective-permute-start(bf16[256,256]{1,0:T(8,128)(2,1)S(1)} %get-tuple-element.72), channel_id=1, source_target_pairs={{0,3},{1,2},{2,1},{3,0},{4,7},{5,6},{6,5},{7,4},{8,11},{9,10},{10,... | collective-permute-start | bytes 393224 | tf_op jit(solution)/shard_map/ppermute | solution.py:137
  193.3 11.0 %collective-permute-start.27 = (bf16[256,256]{1,0:T(8,128)(2,1)S(1)}, bf16[256,256]{1,0:T(8,128)(2,1)S(1)}, u32[]{:S(2)}, u32[]{:S(2)}) collective-permute-start(bf16[256,256]{1,0:T(8,128)(2,1)S(1)} %get-tuple-element.67), channel_id=1, source_target_pairs={{0,2},{2,0},{4,6},{6,4},{8,10},{10,8},{12,14},{14,12},{1,3},{3,1},... | collective-permute-start | bytes 393224 | tf_op jit(solution)/shard_map/ppermute | solution.py:136
  194.2 11.2 %collective-permute-start.28 = (bf16[256,256]{1,0:T(8,128)(2,1)S(1)}, bf16[256,256]{1,0:T(8,128)(2,1)S(1)}, u32[]{:S(2)}, u32[]{:S(2)}) collective-permute-start(bf16[256,256]{1,0:T(8,128)(2,1)S(1)} %get-tuple-element.68), channel_id=1, source_target_pairs={{0,3},{1,2},{2,1},{3,0},{4,7},{5,6},{6,5},{7,4},{8,11},{9,10},{10,... | collective-permute-start | bytes 393224 | tf_op jit(solution)/shard_map/ppermute | solution.py:137
  196.1 9.4 %collective-permute-start.29 = (bf16[256,256]{1,0:T(8,128)(2,1)S(1)}, bf16[256,256]{1,0:T(8,128)(2,1)S(1)}, u32[]{:S(2)}, u32[]{:S(2)}) collective-permute-start(bf16[256,256]{1,0:T(8,128)(2,1)S(1)} %get-tuple-element.70), channel_id=1, source_target_pairs={{0,1},{1,0},{2,3},{3,2},{4,5},{5,4},{6,7},{7,6},{8,9},{9,8},{10,11... | collective-permute-start | bytes 393224 | tf_op jit(solution)/shard_map/ppermute | solution.py:135
  205.4 1.3 copy-start.4

commit v3 on v2

v3 whole, which is shorter than its diff:
```python
import functools

import jax
import jax.numpy as jnp
from jax import lax
from jax.experimental import pallas as pl
from jax.experimental.pallas import tpu as pltpu
from jax.sharding import PartitionSpec as P

LANES = 128
VMEM_LIMIT = 48 * 1024 * 1024
ANYWHERE = pl.BlockSpec(memory_space=pl.ANY)
SCALARS = pl.BlockSpec(memory_space=pltpu.SMEM)
WHOLE = pl.BlockSpec(memory_space=pltpu.VMEM)
NT = (((1,), (1,)), ((), ()))
bf16, f32 = jnp.bfloat16, jnp.float32


def prepare_body(spot, query_grads, mine, other):
    rank = LANES // 2
    width = query_grads.shape[1]
    for out, side in ((mine, spot[0]), (other, 1 - spot[0])):
        for m in range(width // 4 // LANES):
            at = pl.multiple_of(side * (width // 4) + m * LANES, LANES)
            low = query_grads[:, pl.ds(at, LANES)]
            high = query_grads[:, pl.ds(at + width // 2, LANES)]
            out[:, 2 * m * LANES:(2 * m + 1) * LANES] = jnp.concatenate([low[:, :rank], high[:, :rank]], 1)
            out[:, (2 * m + 1) * LANES:(2 * m + 2) * LANES] = jnp.concatenate([low[:, rank:], high[:, rank:]], 1)


def prepare(query_grads, spot):
    rows, width = query_grads.shape
    return pl.pallas_call(
        prepare_body,
        in_specs=[SCALARS, WHOLE],
        out_specs=[WHOLE] * 2,
        out_shape=[jax.ShapeDtypeStruct((rows, width // 2), bf16)] * 2,
        compiler_params=pltpu.CompilerParams(vmem_limit_bytes=VMEM_LIMIT),
    )(spot, query_grads)


def form_body(rows, rank, spot, inputs, outgrads, mask, _after, _later, kept, sent, rounds):
    def one(d, carry):
        masked = outgrads[d] * mask[pl.ds(d, 1), :].astype(bf16)
        product = lax.dot_general(inputs[d], masked, NT, preferred_element_type=f32)
        pairs = jnp.concatenate([product[:rank // 2], product[rank // 2:]], 1)
        rounds[pl.ds(d, rank // 2, stride=rows), :] = pairs
        return carry

    lax.fori_loop(0, rows, one, 0, unroll=8)
    for out, side in ((kept, spot[0]), (sent, 1 - spot[0])):
        for k in range(rank // 4):
            at = pl.multiple_of((side * (rank // 4) + k) * rows, rows)
            out[:, k * LANES:(k + 1) * LANES] = rounds[pl.ds(at, rows), :].astype(bf16)


def form(doc_inputs, doc_outgrads, token_mask, spot, after, later):
    docs, rank, length = doc_inputs.shape
    rows = 32
    steps = docs // rows
    half = rank * rank // 2

    def at(g, spot):
        return lax.rem(g + spot[1] * (steps // 2), steps)

    return pl.pallas_call(
        functools.partial(form_body, rows, rank),
        grid_spec=pltpu.PrefetchScalarGridSpec(
            num_scalar_prefetch=1,
            grid=(steps,),
            in_specs=[
                pl.BlockSpec((rows, rank, length), lambda g, spot: (at(g, spot), 0, 0)),
                pl.BlockSpec((rows, rank, length), lambda g, spot: (at(g, spot), 0, 0)),
                pl.BlockSpec((rows, length), lambda g, spot: (at(g, spot), 0)),
                ANYWHERE,
                ANYWHERE,
            ],
            out_specs=[pl.BlockSpec((rows, half), lambda g, spot: (g, 0))] * 2,
            scratch_shapes=[pltpu.VMEM((rank // 2 * rows, LANES), f32)],
        ),
        out_shape=[jax.ShapeDtypeStruct((docs, half), bf16)] * 2,
        compiler_params=pltpu.CompilerParams(vmem_limit_bytes=VMEM_LIMIT),
        cost_estimate=pl.CostEstimate(
            flops=40 * docs * rank * rank * length, bytes_accessed=4 * docs * rank * length + 2 * docs * rank * rank, transcendentals=0
        ),
    )(spot, doc_inputs, doc_outgrads, token_mask, after, later)


def tie_body(array, _after, out):
    pass


def tie(array, after):
    return pl.pallas_call(
        tie_body,
        in_specs=[ANYWHERE] * 2,
        out_specs=ANYWHERE,
        out_shape=jax.ShapeDtypeStruct(array.shape, array.dtype),
        input_output_aliases={0: 0},
        compiler_params=pltpu.CompilerParams(vmem_limit_bytes=VMEM_LIMIT),
    )(array, after)


def score_body(spot, own, far, first, second, _after, _later, keep, give):
    part = own.shape[0] // 2
    queries = first.shape[0]
    for block, slot in ((first, spot[0]), (second, 1 - spot[0])):
        at = pl.ds(pl.multiple_of(slot * queries, queries), queries)

        def dot(rows):
            return lax.dot_general(rows, block[...], NT, preferred_element_type=f32)

        keep[:part, at] = dot(own[:part, :])
        keep[part:, at] = dot(far[:part, :])
        give[:part, at] = dot(own[part:, :]).astype(bf16)
        give[part:, at] = dot(far[part:, :]).astype(bf16)


def score(spot, own, far, first, second, after, later):
    docs, depth = own.shape
    queries = first.shape[0]
    return pl.pallas_call(
        score_body,
        in_specs=[SCALARS, WHOLE, WHOLE, WHOLE, WHOLE, ANYWHERE, ANYWHERE],
        out_specs=[WHOLE] * 2,
        out_shape=[jax.ShapeDtypeStruct((docs, 2 * queries), f32), jax.ShapeDtypeStruct((docs, 2 * queries), bf16)],
        compiler_params=pltpu.CompilerParams(vmem_limit_bytes=VMEM_LIMIT),
        cost_estimate=pl.CostEstimate(
            flops=docs * queries, bytes_accessed=docs * queries, transcendentals=0
        ),
    )(spot, own, far, first, second, after, later)


def on_device(doc_inputs, doc_outgrads, token_mask, query_grads):
    blk = lax.axis_size("blk")
    places = blk // 2
    me = lax.axis_index("blk")
    place, side = me // 2, me % 2
    spot = jnp.stack([side, lax.axis_index("proj")]).astype(jnp.int32)
    docs = doc_inputs.shape[0]
    queries = query_grads.shape[0]
    part = docs // 2

    across = [(b, b ^ 1) for b in range(blk)]
    onward = [(b, (b + 2) % blk) for b in range(blk)]
    cores = [(0, 1), (1, 0)]

    mine, other = prepare(query_grads, spot)
    flows = [[mine], [lax.ppermute(other, "blk", across)]]
    for step in range(1, places):
        for flow in flows:
            flow.append(lax.ppermute(flow[-1], "blk", onward))

    own, sent = form(
        doc_inputs.reshape(docs, *doc_inputs.shape[2:]), doc_outgrads.reshape(docs, *doc_outgrads.shape[2:]),
        token_mask, spot, flows[0][min(1, places - 1)], flows[1][0],
    )
    far = lax.ppermute(tie(sent, flows[0][min(2, places - 1)]), "blk", across)

    out = jnp.zeros((part, blk * queries), f32)
    last = [flows[1][min(1, places - 1)], token_mask, token_mask]
    for step in range(places):
        origin = (place - step + places) % places
        keep, give = score(spot, own, far, flows[0][step], flows[1][step], last[0], last[1 + step])
        last[0] = give
        got = lax.ppermute(give, "proj", cores).astype(f32)
        beside = lax.ppermute((keep[part:] + got[part:]).astype(bf16), "blk", across)
        last.append(beside)
        out = lax.dynamic_update_slice_in_dim(out, keep[:part] + got[:part] + beside.astype(f32), origin * (2 * queries), 1)
    return out


def solution(mesh):
    placed = (
        P(("grp", "blk"), "proj", None, None),
        P(("grp", "blk"), "proj", None, None),
        P(("grp", "blk"), None),
        P(("grp", "blk"), "proj"),
    )
    return jax.shard_map(
        on_device,
        mesh=mesh,
        in_specs=placed,
        out_specs=P(("grp", "blk", "proj"), None),
        check_vma=False,
    )
```

time: 208 us -> 184 us (0.88)
  starting transfers between devices: 24.6 us -> 14.5 us
  waiting for transfers between devices: 123 us -> 113 us
  Pallas kernels: 51.5 us -> 44.2 us
  other arithmetic: 1.22 us -> 3.45 us
    ppermute x6, waiting for transfers between devices: 94.9 us -> 76.8 us  [on_device(): flow.append(lax.ppermute(flow[-1], 'blk', onward))]
    ppermute x26 -> x10, starting transfers between devices: 20.3 us -> 8.34 us  [the longest x4 5.33 us: on_device(): lax.ppermute((keep[part:] + got[part:]).astype(bf16), 'blk', across)]
    ppermute x26 -> x10, waiting for transfers between devices: 28.5 us -> 36.3 us  [the longest x1 19.7 us: on_device(): far = lax.ppermute(tie(sent, flows[0][min(2, places - 1)]), 'blk', across)]
    unnamed x10 -> x32, local copies, waits for them, and re-layouts: 3.49 us -> 8.05 us
    pallas_call x8 -> x6, Pallas kernels: 24.4 us -> 20.2 us  [the longest x4 18.9 us: score(): pl.pallas_call(score_body, in_specs=[SCALARS, WHOLE, WHOLE, WHOLE, WHOLE,...]
    pallas_call x1, Pallas kernels: 27.1 us -> 24 us  [form(): pl.pallas_call(functools.partial(form_body, rows, rank), grid_spec=pltpu....]
    dynamic_slice x1 -> x0, local copies, waits for them, and re-layouts: 2.79 us -> none  [columns(): return lax.dynamic_slice_in_dim(array, which * half, half, 1)]
  transfers between devices with their start and end apart: 32 -> 16, of which waited for: 16 -> 10; matrix products, arithmetic and copies ran while one was open for 0% -> 1% of each run, Pallas kernels for 25% -> 23%
where the time goes in v3:
time: 184 us
  waiting for transfers between devices  113 us (61%)
  Pallas kernels  44.2 us (24%)
  starting transfers between devices  14.5 us (8%)
  local copies, waits for them, and re-layouts  8.28 us (4%)
  other arithmetic  3.45 us (2%)
    ppermute x6, waiting for transfers between devices, on_device(): flow.append(lax.ppermute(flow[-1], 'blk', onward))  76.8 us
    pallas_call x1, Pallas kernels, form(): pl.pallas_call(functools.partial(form_body, rows, rank), grid_spec=pltpu....  24 us
    ppermute x1, waiting for transfers between devices, on_device(): far = lax.ppermute(tie(sent, flows[0][min(2, places - 1)]), 'blk', across)  19.7 us
    pallas_call x4, Pallas kernels, score(): pl.pallas_call(score_body, in_specs=[SCALARS, WHOLE, WHOLE, WHOLE, WHOLE,...  18.9 us
    ppermute x4, waiting for transfers between devices, on_device(): lax.ppermute((keep[part:] + got[part:]).astype(bf16), 'blk', across)  16.6 us
    unnamed x32, local copies, waits for them, and re-layouts  8.05 us
    ppermute x6, starting transfers between devices, on_device(): flow.append(lax.ppermute(flow[-1], 'blk', onward))  6.12 us
    ppermute x4, starting transfers between devices, on_device(): lax.ppermute((keep[part:] + got[part:]).astype(bf16), 'blk', across)  5.33 us
  transfers between devices with their start and end apart: 16, of which 10 were waited for; matrix products, arithmetic and copies ran while one was open for 1% of the time, Pallas kernels for 23%

profile of v3, /device:TPU:0, one launch (start us, length us, event | category | flops | bytes accessed | tf_op | source)
XLA Modules:
  0.0 183.7 jit_solution(10147589609627073914)
XLA Ops:
  0.0 0.1 pad_add_fusion.spot
  0.1 1.6 copy-done.1
  1.7 1.3 shard_map.46
  2.9 3.1 %collective-permute-start = (bf16[256,2048]{1,0:T(8,128)(2,1)S(1)}, bf16[256,2048]{1,0:T(8,128)(2,1)S(1)}, u32[]{:S(2)}, u32[]{:S(2)}) collective-permute-start(bf16[256,2048]{1,0:T(8,128)(2,1)S(1)} %get-tuple-element.17.first), channel_id=1, source_target_pairs={{0,4},{2,6},{4,8},{6,10},{8,12},{10,14},{12,0},{14,2},{1,5},{3,7},... | collective-permute-start | bytes 3145736 | tf_op jit(solution)/shard_map/ppermute | solution.py:152
  6.0 1.5 collective-permute-start.1
  7.5 23.7 %collective-permute-done._after.first = bf16[256,2048]{1,0:T(8,128)(2,1)S(1)} collective-permute-done((bf16[256,2048]{1,0:T(8,128)(2,1)S(1)}, bf16[256,2048]{1,0:T(8,128)(2,1)S(1)}, u32[]{:S(2)}, u32[]{:S(2)}) %collective-permute-start) | collective-permute-done | bytes 1048608 | tf_op jit(solution)/shard_map/ppermute | solution.py:152
  31.2 0.0 collective-permute-start.2
  31.2 0.0 collective-permute-done.1._later.second
  31.2 0.0 copy-done.3
  31.2 24.0 %shard_map.47 = (bf16[512,2048]{1,0:T(8,128)(2,1)S(1)}, bf16[512,2048]{1,0:T(8,128)(2,1)}) custom-call(s32[2]{0:T(128)S(1)} %pad_add_fusion.spot, bf16[512,64,128]{2,1,0:T(8,128)(2,1)} %bitcast.4, bf16[512,64,128]{2,1,0:T(8,128)(2,1)} %bitcast.5, s32[512,128]{1,0:T(8,128)S(1)} %copy-done.3, bf16[256,2048]{1,0:T(8,128)(2,1)S(1)} %collective-permute-done._after.first, ...), custom_call_target="tpu_custom_call" | custom-call | flops 10737418240 | bytes 20971520 | tf_op jit(solution)/shard_map/pallas_call | solution.py:66
  55.2 1.4 copy-done
  56.5 0.8 collective-permute-done.2._after.first
  57.3 1.6 copy-done.2
  58.9 1.3 collective-permute-start.3
  60.2 0.7 collective-permute-start.4
  60.9 24.3 %collective-permute-done.4._after.second = bf16[256,2048]{1,0:T(8,128)(2,1)S(1)} collective-permute-done((bf16[256,2048]{1,0:T(8,128)(2,1)S(1)}, bf16[256,2048]{1,0:T(8,128)(2,1)S(1)}, u32[]{:S(2)}, u32[]{:S(2)}) %collective-permute-start.4) | collective-permute-done | bytes 1048608 | tf_op jit(solution)/shard_map/ppermute | solution.py:152
  85.3 0.0 collective-permute-start.9
  85.3 19.7 %collective-permute-done.3.far = bf16[512,2048]{1,0:T(8,128)(2,1)S(1)} collective-permute-done((bf16[512,2048]{1,0:T(8,128)(2,1)S(1)}, bf16[512,2048]{1,0:T(8,128)(2,1)S(1)}, u32[]{:S(2)}, u32[]{:S(2)}) %collective-permute-start.3) | collective-permute-done | bytes 2097184 | tf_op jit(solution)/shard_map/ppermute | solution.py:158
  104.9 1.3 copy-done.10
  106.3 4.6 %shard_map.49 = (f32[512,512]{1,0:T(8,128)S(1)}, bf16[512,512]{1,0:T(8,128)(2,1)S(1)}) custom-call(s32[2]{0:T(128)S(1)} %pad_add_fusion.spot, bf16[512,2048]{1,0:T(8,128)(2,1)} %copy-done, bf16[512,2048]{1,0:T(8,128)(2,1)} %copy-done.10, bf16[256,2048]{1,0:T(8,128)(2,1)S(1)} %get-tuple-element.17.first, ...), custom_call_target="tpu_custom_call" | custom-call | flops 131072 | bytes 131072 | tf_op jit(solution)/shard_map/pallas_call | solution.py:122
  110.9 0.1 collective-permute-start.5
  110.9 0.8 collective-permute-start.12
  111.7 0.0 collective-permute-done.9.second
  111.7 1.6 collective-permute-start.13
  113.3 4.6 %shard_map.50 = (f32[512,512]{1,0:T(8,128)S(1)}, bf16[512,512]{1,0:T(8,128)(2,1)S(1)}) custom-call(s32[2]{0:T(128)S(1)} %pad_add_fusion.spot, bf16[512,2048]{1,0:T(8,128)(2,1)} %copy-done, bf16[512,2048]{1,0:T(8,128)(2,1)} %copy-done.10, bf16[256,2048]{1,0:T(8,128)(2,1)S(1)} %collective-permute-done._after.first, ...), custom_call_target="tpu_custom_call" | custom-call | flops 131072 | bytes 131072 | tf_op jit(solution)/shard_map/pallas_call | solution.py:122
  117.9 0.1 collective-permute-start.7
  118.0 0.0 collective-permute-done.5
  118.0 0.1 convert_element_type.36
  118.1 0.1 fusion.9
  118.2 1.6 collective-permute-start.6
  119.8 0.1 collective-permute-done.7
  119.9 0.1 convert_element_type.39
  120.0 0.0 copy-start.11
  120.0 0.0 copy-done.6
  120.0 0.1 fusion.6
  120.1 1.6 collective-permute-start.8
  121.7 5.7 %collective-permute-done.6._later = bf16[256,512]{1,0:T(8,128)(2,1)S(1)} collective-permute-done((bf16[256,512]{1,0:T(8,128)(2,1)S(1)}, bf16[256,512]{1,0:T(8,128)(2,1)S(1)}, u32[]{:S(2)}, u32[]{:S(2)}) %collective-permute-start.6) | collective-permute-done | bytes 262176 | tf_op jit(solution)/shard_map/ppermute | solution.py:167
  127.4 4.6 %shard_map.51 = (f32[512,512]{1,0:T(8,128)S(1)}, bf16[512,512]{1,0:T(8,128)(2,1)S(1)}) custom-call(s32[2]{0:T(128)S(1)} %pad_add_fusion.spot, bf16[512,2048]{1,0:T(8,128)(2,1)} %copy-done, bf16[512,2048]{1,0:T(8,128)(2,1)} %copy-done.10, bf16[256,2048]{1,0:T(8,128)(2,1)S(1)} %collective-permute-done.2._after.first, ...), custom_call_target="tpu_custom_call" | custom-call | flops 131072 | bytes 131072 | tf_op jit(solution)/shard_map/pallas_call | solution.py:122
  132.0 0.9 copy-done.8
  132.9 0.0 collective-permute-start.10
  133.0 5.9 %collective-permute-done.12.first = bf16[256,2048]{1,0:T(8,128)(2,1)} collective-permute-done((bf16[256,2048]{1,0:T(8,128)(2,1)S(1)}, bf16[256,2048]{1,0:T(8,128)(2,1)}, u32[]{:S(2)}, u32[]{:S(2)}) %collective-permute-start.12) | collective-permute-done | bytes 1048608 | tf_op jit(solution)/shard_map/ppermute | solution.py:152
  138.9 22.0 %collective-permute-done.13.second = bf16[256,2048]{1,0:T(8,128)(2,1)} collective-permute-done((bf16[256,2048]{1,0:T(8,128)(2,1)S(1)}, bf16[256,2048]{1,0:T(8,128)(2,1)}, u32[]{:S(2)}, u32[]{:S(2)}) %collective-permute-start.13) | collective-permute-done | bytes 1048608 | tf_op jit(solution)/shard_map/ppermute | solution.py:152
  160.9 0.0 collective-permute-done.8._later
  160.9 5.2 %shard_map.52 = (f32[512,512]{1,0:T(8,128)S(1)}, bf16[512,512]{1,0:T(8,128)(2,1)S(1)}) custom-call(s32[2]{0:T(128)S(1)} %pad_add_fusion.spot, bf16[512,2048]{1,0:T(8,128)(2,1)} %copy-done, bf16[512,2048]{1,0:T(8,128)(2,1)} %copy-done.10, bf16[256,2048]{1,0:T(8,128)(2,1)} %collective-permute-done.12.first, bf16[256,2048]{1,0:T(8,128)(2,1)} %collective-permute-done.13.second, ...), custom_call_target="tpu_custom_call" | custom-call | flops 131072 | bytes 131072 | tf_op jit(solution)/shard_map/pallas_call | solution.py:122
  166.1 0.1 collective-permute-start.14
  166.2 0.2 broadcast_in_dim.3
  166.4 0.9 copy-done.5
  167.3 0.3 copy-done.14
  167.6 0.1 fusion.11
  167.7 0.0 collective-permute-done.10
  167.8 1.3 convert_element_type.42
  169.1 0.0 copy-done.9
  169.1 0.1 fusion.3
  169.2 1.3 collective-permute-start.11
  170.5 0.1 fusion.8
  170.7 0.0 collective-permute-done.14
  170.7 0.1 convert_element_type.45
  170.8 0.1 fusion
  170.9 0.8 collective-permute-start.15
  171.7 6.7 %collective-permute-done.11 = bf16[256,512]{1,0:T(8,128)(2,1)S(1)} collective-permute-done((bf16[256,512]{1,0:T(8,128)(2,1)S(1)}, bf16[256,512]{1,0:T(8,128)(2,1)S(1)}, u32[]{:S(2)}, u32[]{:S(2)}) %collective-permute-start.11) | collective-permute-done | bytes 262176 | tf_op jit(solution)/shard_map/ppermute | solution.py:167
  178.5 0.1 fusion.5
  178.6 0.0 copy-start.15
  178.6 4.2 %collective-permute-done.15 = bf16[256,512]{1,0:T(8,128)(2,1)S(1)} collective-permute-done((bf16[256,512]{1,0:T(8,128)(2,1)S(1)}, bf16[256,512]{1,0:T(8,128)(2,1)S(1)}, u32[]{:S(2)}, u32[]{:S(2)}) %collective-permute-start.15) | collective-permute-done | bytes 262176 | tf_op jit(solution)/shard_map/ppermute | solution.py:167
  182.8 0.9 fusion.2
  (21 shorter events, 0.0 us)
Async XLA Ops:
  0.1 1.6 copy-start.1
  1.7 29.5 %copy-start.3 = (s32[512,128]{1,0:T(8,128)S(1)}, s32[512,128]{1,0:T(8,128)}, u32[]{:S(2)}) copy-start(s32[512,128]{1,0:T(8,128)} %_later.3) | copy-start | bytes 786436
  2.9 28.3 %collective-permute-start = (bf16[256,2048]{1,0:T(8,128)(2,1)S(1)}, bf16[256,2048]{1,0:T(8,128)(2,1)S(1)}, u32[]{:S(2)}, u32[]{:S(2)}) collective-permute-start(bf16[256,2048]{1,0:T(8,128)(2,1)S(1)} %get-tuple-element.17.first), channel_id=1, source_target_pairs={{0,4},{2,6},{4,8},{6,10},{8,12},{10,14},{12,0},{14,2},{1,5},{3,7},... | collective-permute-start | bytes 3145736 | tf_op jit(solution)/shard_map/ppermute | solution.py:152
  6.0 25.2 %collective-permute-start.1 = (bf16[256,2048]{1,0:T(8,128)(2,1)S(1)}, bf16[256,2048]{1,0:T(8,128)(2,1)S(1)}, u32[]{:S(2)}, u32[]{:S(2)}) collective-permute-start(bf16[256,2048]{1,0:T(8,128)(2,1)S(1)} %get-tuple-element.18), channel_id=1, source_target_pairs={{0,2},{2,0},{4,6},{6,4},{8,10},{10,8},{12,14},{14,12},{1,3},{3,1},... | collective-permute-start | bytes 3145736 | tf_op jit(solution)/shard_map/ppermute | solution.py:149
  31.2 26.1 %collective-permute-start.2 = (bf16[256,2048]{1,0:T(8,128)(2,1)S(1)}, bf16[256,2048]{1,0:T(8,128)(2,1)S(1)}, u32[]{:S(2)}, u32[]{:S(2)}) collective-permute-start(bf16[256,2048]{1,0:T(8,128)(2,1)S(1)} %collective-permute-done._after.first), channel_id=1, source_target_pairs={{0,4},{2,6},{4,8},{6,10},{8,12},{10,14},{12,0},{14,2},{1,5},{3,7},... | collective-permute-start | bytes 3145736 | tf_op jit(solution)/shard_map/ppermute | solution.py:152
  55.2 1.4 copy-start
  57.3 1.6 copy-start.2
  58.9 46.0 %collective-permute-start.3 = (bf16[512,2048]{1,0:T(8,128)(2,1)S(1)}, bf16[512,2048]{1,0:T(8,128)(2,1)S(1)}, u32[]{:S(2)}, u32[]{:S(2)}) collective-permute-start(bf16[512,2048]{1,0:T(8,128)(2,1)S(1)} %shard_map.48), channel_id=1, source_target_pairs={{0,2},{2,0},{4,6},{6,4},{8,10},{10,8},{12,14},{14,12},{1,3},{3,1},... | collective-permute-start | bytes 6291464 | tf_op jit(solution)/shard_map/ppermute | solution.py:158
  60.2 25.0 %collective-permute-start.4 = (bf16[256,2048]{1,0:T(8,128)(2,1)S(1)}, bf16[256,2048]{1,0:T(8,128)(2,1)S(1)}, u32[]{:S(2)}, u32[]{:S(2)}) collective-permute-start(bf16[256,2048]{1,0:T(8,128)(2,1)S(1)} %collective-permute-done.1._later.second), channel_id=1, source_target_pairs={{0,4},{2,6},{4,8},{6,10},{8,12},{10,14},{12,0},{14,2},{1,5},{3,7},... | collective-permute-start | bytes 3145736 | tf_op jit(solution)/shard_map/ppermute | solution.py:152
  85.3 26.4 %collective-permute-start.9 = (bf16[256,2048]{1,0:T(8,128)(2,1)S(1)}, bf16[256,2048]{1,0:T(8,128)(2,1)S(1)}, u32[]{:S(2)}, u32[]{:S(2)}) collective-permute-start(bf16[256,2048]{1,0:T(8,128)(2,1)S(1)} %collective-permute-done.4._after.second), channel_id=1, source_target_pairs={{0,4},{2,6},{4,8},{6,10},{8,12},{10,14},{12,0},{14,2},{1,5},{3,7},... | collective-permute-start | bytes 3145736 | tf_op jit(solution)/shard_map/ppermute | solution.py:152
  104.9 1.3 copy-start.10
  110.9 7.3 %copy-start.4 = (f32[512,512]{1,0:T(8,128)}, f32[512,512]{1,0:T(8,128)S(1)}, u32[]{:S(2)}) copy-start(f32[512,512]{1,0:T(8,128)S(1)} %get-tuple-element.21) | copy-start | bytes 3145732
  110.9 7.1 %collective-permute-start.5 = (bf16[512,512]{1,0:T(8,128)(2,1)S(1)}, bf16[512,512]{1,0:T(8,128)(2,1)S(1)}, u32[]{:S(2)}, u32[]{:S(2)}) collective-permute-start(bf16[512,512]{1,0:T(8,128)(2,1)S(1)} %get-tuple-element.22._after), channel_id=1, source_target_pairs={{0,1},{1,0},{2,3},{3,2},{4,5},{5,4},{6,7},{7,6},{8,9},{9,8},{10,11... | collective-permute-start | bytes 1572872 | tf_op jit(solution)/shard_map/ppermute | solution.py:166
  110.9 27.9 %collective-permute-start.12 = (bf16[256,2048]{1,0:T(8,128)(2,1)S(1)}, bf16[256,2048]{1,0:T(8,128)(2,1)}, u32[]{:S(2)}, u32[]{:S(2)}) collective-permute-start(bf16[256,2048]{1,0:T(8,128)(2,1)S(1)} %collective-permute-done.2._after.first), channel_id=1, source_target_pairs={{0,4},{2,6},{4,8},{6,10},{8,12},{10,14},{12,0},{14,2},{1,5},{3,7},... | collective-permute-start | bytes 3145736 | tf_op jit(solution)/shard_map/ppermute | solution.py:152
  111.7 49.2 %collective-permute-start.13 = (bf16[256,2048]{1,0:T(8,128)(2,1)S(1)}, bf16[256,2048]{1,0:T(8,128)(2,1)}, u32[]{:S(2)}, u32[]{:S(2)}) collective-permute-start(bf16[256,2048]{1,0:T(8,128)(2,1)S(1)} %collective-permute-done.9.second), channel_id=1, source_target_pairs={{0,4},{2,6},{4,8},{6,10},{8,12},{10,14},{12,0},{14,2},{1,5},{3,7},... | collective-permute-start | bytes 3145736 | tf_op jit(solution)/shard_map/ppermute | solution.py:152
  117.9 2.1 %copy-start.6 = (f32[512,512]{1,0:T(8,128)}, f32[512,512]{1,0:T(8,128)S(1)}, u32[]{:S(2)}) copy-start(f32[512,512]{1,0:T(8,128)S(1)} %get-tuple-element.23) | copy-start | bytes 3145732
  117.9 2.0 %collective-permute-start.7 = (bf16[512,512]{1,0:T(8,128)(2,1)S(1)}, bf16[512,512]{1,0:T(8,128)(2,1)S(1)}, u32[]{:S(2)}, u32[]{:S(2)}) collective-permute-start(bf16[512,512]{1,0:T(8,128)(2,1)S(1)} %get-tuple-element.24._after), channel_id=1, source_target_pairs={{0,1},{1,0},{2,3},{3,2},{4,5},{5,4},{6,7},{7,6},{8,9},{9,8},{10,11... | collective-permute-start | bytes 1572872 | tf_op jit(solution)/shard_map/ppermute | solution.py:166
  118.1 1.7 copy-start.13
  118.2 9.2 %collective-permute-start.6 = (bf16[256,512]{1,0:T(8,128)(2,1)S(1)}, bf16[256,512]{1,0:T(8,128)(2,1)S(1)}, u32[]{:S(2)}, u32[]{:S(2)}) collective-permute-start(bf16[256,512]{1,0:T(8,128)(2,1)S(1)} %fusion.9), channel_id=1, source_target_pairs={{0,2},{2,0},{4,6},{6,4},{8,10},{10,8},{12,14},{14,12},{1,3},{3,1},... | collective-permute-start | bytes 786440 | tf_op jit(solution)/shard_map/ppermute | solution.py:167
  120.0 12.0 %copy-start.11 = (f32[512,512]{1,0:T(8,128)}, f32[512,512]{1,0:T(8,128)S(1)}, u32[]{:S(2)}) copy-start(f32[512,512]{1,0:T(8,128)S(1)} %convert_element_type.39) | copy-start | bytes 3145732
  120.1 40.8 %collective-permute-start.8 = (bf16[256,512]{1,0:T(8,128)(2,1)S(1)}, bf16[256,512]{1,0:T(8,128)(2,1)S(1)}, u32[]{:S(2)}, u32[]{:S(2)}) collective-permute-start(bf16[256,512]{1,0:T(8,128)(2,1)S(1)} %fusion.6), channel_id=1, source_target_pairs={{0,2},{2,0},{4,6},{6,4},{8,10},{10,8},{12,14},{14,12},{1,3},{3,1},... | collective-permute-start | bytes 786440 | tf_op jit(solution)/shard_map/ppermute | solution.py:167
  132.0 1.0 copy-start.8
  132.9 34.8 %collective-permute-start.10 = (bf16[512,512]{1,0:T(8,128)(2,1)S(1)}, bf16[512,512]{1,0:T(8,128)(2,1)}, u32[]{:S(2)}, u32[]{:S(2)}) collective-permute-start(bf16[512,512]{1,0:T(8,128)(2,1)S(1)} %get-tuple-element.26._after), channel_id=1, source_target_pairs={{0,1},{1,0},{2,3},{3,2},{4,5},{5,4},{6,7},{7,6},{8,9},{9,8},{10,11... | collective-permute-start | bytes 1572872 | tf_op jit(solution)/shard_map/ppermute | solution.py:166
  166.1 1.2 copy-start.5
  166.1 1.5 copy-start.14
  166.1 4.6 %collective-permute-start.14 = (bf16[512,512]{1,0:T(8,128)(2,1)S(1)}, bf16[512,512]{1,0:T(8,128)(2,1)S(1)}, u32[]{:S(2)}, u32[]{:S(2)}) collective-permute-start(bf16[512,512]{1,0:T(8,128)(2,1)S(1)} %get-tuple-element.28), channel_id=1, source_target_pairs={{0,1},{1,0},{2,3},{3,2},{4,5},{5,4},{6,7},{7,6},{8,9},{9,8},{10,11... | collective-permute-start | bytes 1572872 | tf_op jit(solution)/shard_map/ppermute | solution.py:166
  167.6 1.5 copy-start.9
  167.6 2.9 %copy-start.7 = (f32[512,512]{1,0:T(8,128)S(1)}, f32[512,512]{1,0:T(8,128)}, u32[]{:S(2)}) copy-start(f32[512,512]{1,0:T(8,128)} %copy-done.6) | copy-start | bytes 3145732
  167.6 2.9 %copy-start.12 = (f32[512,512]{1,0:T(8,128)S(1)}, f32[512,512]{1,0:T(8,128)}, u32[]{:S(2)}) copy-start(f32[512,512]{1,0:T(8,128)} %copy-done.11) | copy-start | bytes 3145732
  169.2 9.3 %collective-permute-start.11 = (bf16[256,512]{1,0:T(8,128)(2,1)S(1)}, bf16[256,512]{1,0:T(8,128)(2,1)S(1)}, u32[]{:S(2)}, u32[]{:S(2)}) collective-permute-start(bf16[256,512]{1,0:T(8,128)(2,1)S(1)} %fusion.3), channel_id=1, source_target_pairs={{0,2},{2,0},{4,6},{6,4},{8,10},{10,8},{12,14},{14,12},{1,3},{3,1},... | collective-permute-start | bytes 786440 | tf_op jit(solution)/shard_map/ppermute | solution.py:167
  170.9 11.8 %collective-permute-start.15 = (bf16[256,512]{1,0:T(8,128)(2,1)S(1)}, bf16[256,512]{1,0:T(8,128)(2,1)S(1)}, u32[]{:S(2)}, u32[]{:S(2)}) collective-permute-start(bf16[256,512]{1,0:T(8,128)(2,1)S(1)} %fusion), channel_id=1, source_target_pairs={{0,2},{2,0},{4,6},{6,4},{8,10},{10,8},{12,14},{14,12},{1,3},{3,1},... | collective-permute-start | bytes 786440 | tf_op jit(solution)/shard_map/ppermute | solution.py:167
  178.6 4.2 %copy-start.15 = (f32[256,2048]{1,0:T(8,128)}, f32[256,2048]{1,0:T(8,128)S(1)}, u32[]{:S(2)}) copy-start(f32[256,2048]{1,0:T(8,128)S(1)} %fusion.5) | copy-start | bytes 6291460

commit v4 on v0

v4 whole, which is shorter than its diff:
```python
import functools

import jax
import jax.numpy as jnp
from jax import lax
from jax.experimental import pallas as pl
from jax.experimental.pallas import tpu as pltpu
from jax.sharding import PartitionSpec as P

LANES = 128
VMEM_LIMIT = 48 * 1024 * 1024
ANYWHERE = pl.BlockSpec(memory_space=pl.ANY)
SCALARS = pl.BlockSpec(memory_space=pltpu.SMEM)
WHOLE = pl.BlockSpec(memory_space=pltpu.VMEM)
NT = (((1,), (1,)), ((), ()))
bf16, f32 = jnp.bfloat16, jnp.float32
LIMIT = pltpu.CompilerParams(vmem_limit_bytes=VMEM_LIMIT)


def shaped(kind, *shape):
    return jax.ShapeDtypeStruct(shape, kind)


def prepare_body(spot, query_grads, mine, start, other):
    rank = LANES // 2
    width = query_grads.shape[1]
    for outs, side in (((mine, start), spot[0]), ((other,), 1 - spot[0])):
        for m in range(width // 4 // LANES):
            at = pl.multiple_of(side * (width // 4) + m * LANES, LANES)
            low = query_grads[:, pl.ds(at, LANES)]
            high = query_grads[:, pl.ds(at + width // 2, LANES)]
            for odd, block in enumerate((
                jnp.concatenate([low[:, :rank], high[:, :rank]], 1),
                jnp.concatenate([low[:, rank:], high[:, rank:]], 1),
            )):
                k = 2 * m + odd
                for out in outs:
                    if k * LANES < out.shape[1]:
                        out[:, k * LANES:(k + 1) * LANES] = block


def prepare(query_grads, spot, stay):
    rows, width = query_grads.shape
    return pl.pallas_call(
        prepare_body,
        in_specs=[SCALARS, WHOLE],
        out_specs=[WHOLE] * 3,
        out_shape=[shaped(bf16, rows, width // 2), shaped(bf16, rows, stay), shaped(bf16, rows, width // 2)],
        compiler_params=LIMIT,
    )(spot, query_grads)


def form_body(rows, rank, spot, inputs, outgrads, mask, *refs):
    kept, lent, sent, sent_lent, rounds = refs[-5:]
    for d in range(rows):
        masked = outgrads[d] * mask[d:d + 1, :].astype(bf16)
        product = lax.dot_general(inputs[d], masked, NT, preferred_element_type=f32)
        pairs = jnp.concatenate([product[:rank // 2], product[rank // 2:]], 1)
        rounds[pl.ds(d, rank // 2, stride=rows), :] = pairs
    stay = sent.shape[1] // LANES
    for which in range(2):
        side = spot[0] if which == 0 else 1 - spot[0]
        for k in range(rank // 4):
            at = pl.multiple_of((side * (rank // 4) + k) * rows, rows)
            block = rounds[pl.ds(at, rows), :].astype(bf16)
            if which == 0:
                kept[:, k * LANES:(k + 1) * LANES] = block
                if k >= stay:
                    lent[:, (k - stay) * LANES:(k - stay + 1) * LANES] = block
            elif k < stay:
                sent[:, k * LANES:(k + 1) * LANES] = block
            else:
                sent_lent[:, (k - stay) * LANES:(k - stay + 1) * LANES] = block


def form(doc_inputs, doc_outgrads, token_mask, spot, stay, *after):
    docs, rank, length = doc_inputs.shape
    rows = 64
    steps = docs // rows
    half = rank * rank // 2
    widths = (half, half - stay, stay, half - stay)

    def at(g, spot):
        return lax.rem(g + spot[1] * (steps // 2), steps)

    return pl.pallas_call(
        functools.partial(form_body, rows, rank),
        grid_spec=pltpu.PrefetchScalarGridSpec(
            num_scalar_prefetch=1,
            grid=(steps,),
            in_specs=[
                pl.BlockSpec((rows, rank, length), lambda g, spot: (at(g, spot), 0, 0)),
                pl.BlockSpec((rows, rank, length), lambda g, spot: (at(g, spot), 0, 0)),
                pl.BlockSpec((rows, length), lambda g, spot: (at(g, spot), 0)),
            ] + [ANYWHERE] * len(after),
            out_specs=[pl.BlockSpec((rows, width), lambda g, spot: (g, 0)) for width in widths],
            scratch_shapes=[pltpu.VMEM((rank // 2 * rows, LANES), f32)],
        ),
        out_shape=[shaped(bf16, docs, width) for width in widths],
        compiler_params=LIMIT,
        cost_estimate=pl.CostEstimate(
            flops=40 * docs * rank * rank * length, bytes_accessed=4 * docs * rank * length + 2 * docs * rank * rank, transcendentals=0
        ),
    )(spot, doc_inputs, doc_outgrads, token_mask, *after)


def tie(arrays, *after):
    count = len(arrays)
    return pl.pallas_call(
        lambda *refs: None,
        in_specs=[ANYWHERE] * (count + len(after)),
        out_specs=[ANYWHERE] * count,
        out_shape=[shaped(a.dtype, *a.shape) for a in arrays],
        input_output_aliases={i: i for i in range(count)},
        compiler_params=LIMIT,
    )(*arrays, *after)


def store_products(spot, blocks, rows_of, keep, give):
    part = keep.shape[0] // 2
    queries = blocks[0].shape[0]
    for block, slot in zip(blocks, (spot[0], 1 - spot[0])):
        at = pl.ds(pl.multiple_of(slot * queries, queries), queries)
        products = rows_of(block)
        keep[:part, at] = products[0]
        give[:part, at] = products[1].astype(bf16)
        keep[part:, at] = products[2]
        give[part:, at] = products[3].astype(bf16)


def dot(rows, block):
    return lax.dot_general(rows, block, NT, preferred_element_type=f32)


def own_body(stay, spot, own, far, far_lent, first, second, first_stay, second_stay, *refs):
    keep, give = refs[-2:]
    part = own.shape[0] // 2

    def all_features(block):
        out = []
        for h in range(2):
            out.append(dot(own[h * part:(h + 1) * part, :], block[...]))
        for h in range(2):
            rows = slice(h * part, (h + 1) * part)
            out.append(dot(far[rows, :], block[:, :stay]) + dot(far_lent[rows, :], block[:, stay:]))
        return out

    def staying(block):
        out = []
        for h in range(2):
            out.append(dot(own[h * part:(h + 1) * part, :stay], block[:, :stay]))
        for h in range(2):
            out.append(dot(far[h * part:(h + 1) * part, :], block[:, :stay]))
        return out

    @pl.when(spot[2] == 1)
    def _():
        store_products(spot, (first, second), all_features, keep, give)

    @pl.when(spot[2] == 0)
    def _():
        store_products(spot, (first_stay, second_stay), staying, keep, give)


def lent_body(stay, spot, near, far, first, second, *refs):
    keep, give = refs[-2:]
    part = near.shape[0] // 2

    def products(block):
        return [
            dot(rows[h * part:(h + 1) * part, :], block[:, stay:]) for rows in (near, far) for h in range(2)
        ]

    @pl.when(spot[2] == 1)
    def _():
        store_products(spot, (first, second), products, keep, give)


def score(body, stay, spot, operands, docs, queries, after):
    return pl.pallas_call(
        functools.partial(body, stay),
        in_specs=[SCALARS] + [WHOLE] * len(operands) + [ANYWHERE] * len(after),
        out_specs=[WHOLE] * 2,
        out_shape=[shaped(f32, docs, 2 * queries), shaped(bf16, docs, 2 * queries)],
        compiler_params=LIMIT,
        cost_estimate=pl.CostEstimate(flops=docs * queries, bytes_accessed=docs * queries, transcendentals=0),
    )(spot, *operands, *after)


def on_device(doc_inputs, doc_outgrads, token_mask, query_grads):
    blk = lax.axis_size("blk")
    places = blk // 2
    me = lax.axis_index("blk")
    place, side = me // 2, me % 2
    docs, rank = doc_inputs.shape[0], doc_inputs.shape[2]
    queries = query_grads.shape[0]
    part = docs // 2
    half = rank * rank // 2
    doc_inputs = doc_inputs.reshape(docs, *doc_inputs.shape[2:])
    doc_outgrads = doc_outgrads.reshape(docs, *doc_outgrads.shape[2:])
    lending = places == 4
    stay = half * 10 // 16
    inner = jnp.where((place == 1) | (place == 2), 1, 0) if lending else 1
    spot = jnp.stack([side, lax.axis_index("proj"), inner]).astype(jnp.int32)

    across = [(b, b ^ 1) for b in range(blk)]
    onward = [(b, (b + 2) % blk) for b in range(blk)]
    cores = [(0, 1), (1, 0)]

    mine, mine_stay, sending = prepare(query_grads, spot, stay)
    other = lax.ppermute(sending, "blk", across)

    def take(keep, give, far_across, far_cores):
        got = far_cores(give)
        beside = far_across((keep[part:] + got[part:].astype(f32)).astype(bf16))
        return keep[:part] + got[:part].astype(f32) + beside.astype(f32), beside

    def swap_across(x):
        return lax.ppermute(x, "blk", across)

    def swap_cores(x):
        return lax.ppermute(x, "proj", cores)

    out = jnp.zeros((part, blk * queries), f32)
    if not lending:
        flows = [[mine], [other]]
        for step in range(1, places):
            for flow in flows:
                flow.append(lax.ppermute(flow[-1], "blk", onward))
        own, _, sent, sent_lent = form(doc_inputs, doc_outgrads, token_mask, spot, stay)
        far, far_lent = swap_across(sent), swap_across(sent_lent)
        for step in range(places):
            first, second = flows[0][step], flows[1][step]
            keep, give = score(
                own_body, stay, spot, (own, far, far_lent, first, second, first, second), docs, queries, ()
            )
            total, _ = take(keep, give, swap_across, swap_cores)
            origin = (place - step + places) % places
            out = lax.dynamic_update_slice_in_dim(out, total, origin * (2 * queries), 1)
        return out

    def at(place):
        return [2 * place, 2 * place + 1]

    inward = list(zip(at(0) + at(3), at(1) + at(2)))
    outward = [(b, a) for a, b in inward]
    centre = list(zip(at(1) + at(2), at(2) + at(1)))
    inner_across = [(b, b ^ 1) for b in at(1) + at(2)]
    inner_cores = [(2 * b + c, 2 * b + 1 - c) for b in at(1) + at(2) for c in range(2)]

    def move(x, pairs):
        return lax.ppermute(x, "blk", pairs)

    def staying(x):
        return x[:, :stay]

    mate_a = move(mine, inward)
    near_a = move(mine, centre)
    outer_mate_a = move(mine_stay, outward)
    own, lent, sent, sent_lent = form(doc_inputs, doc_outgrads, token_mask, spot, stay, outer_mate_a)
    sent, sent_lent = tie((sent, sent_lent), mate_a, near_a, other)

    far_lent = swap_across(sent_lent)
    far = swap_across(sent)
    mate_b = move(other, inward)
    near_b = move(other, centre)
    outer_near_a = move(staying(near_a), outward)
    outer_mate_b = move(staying(other), outward)
    lent, far_lent = tie((lent, far_lent), mate_b, near_b, outer_near_a)

    lent_near = move(lent, inward)
    lent_far = move(far_lent, inward)
    away_a = move(mate_a, centre)
    outer_near_b = move(staying(near_b), outward)
    outer_away_a = move(staying(away_a), outward)
    away_b = move(mate_b, centre)
    outer_away_b = move(staying(away_b), outward)

    groups = {
        "self": (mine, other, mine, other),
        "mate": (mate_a, mate_b, outer_mate_a, outer_mate_b),
        "near": (near_a, near_b, outer_near_a, outer_near_b),
        "away": (away_a, away_b, outer_away_a, outer_away_b),
    }
    opposite = place < 2
    origins = {
        "self": place,
        "mate": place ^ 1,
        "near": jnp.where(opposite, 2, 1),
        "away": jnp.where(opposite, 3, 0),
    }

    def own_part(name, *after):
        return score(own_body, stay, spot, (own, far, far_lent) + groups[name], docs, queries, after)

    def lent_part(name, *after):
        return score(lent_body, stay, spot, (lent_near, lent_far) + groups[name][:2], docs, queries, after)

    def back(keep, give):
        total, beside = take(
            keep, give, lambda x: move(x, inner_across), lambda x: lax.ppermute(x, ("blk", "proj"), inner_cores)
        )
        return move(total.astype(bf16), outward), beside

    totals, besides, returned = {}, {}, {}

    last = (away_a, outer_mate_b, outer_near_b)
    for name in ("self", "near", "mate"):
        k, g = own_part(name, *last)
        totals[name], besides[name] = take(k, g, swap_across, swap_cores)
        last = (g,)
    forced = {"self": outer_away_a, "near": besides["self"], "mate": besides["near"], "away": besides["mate"]}
    for name in ("self", "near", "mate", "away"):
        k, g = lent_part(name, *last, forced[name])
        returned[name], _ = back(k, g)
        last = (g,)
    k, g = own_part("away", *last)
    totals["away"], _ = take(k, g, swap_across, swap_cores)
    backs = {"self": "mate", "mate": "self", "near": "near", "away": "away"}
    for name in ("self", "near", "mate", "away"):
        total = totals[name] + returned[backs[name]].astype(f32)
        out = lax.dynamic_update_slice_in_dim(out, total, origins[name] * (2 * queries), 1)
    return out


def solution(mesh):
    placed = (
        P(("grp", "blk"), "proj", None, None),
        P(("grp", "blk"), "proj", None, None),
        P(("grp", "blk"), None),
        P(("grp", "blk"), "proj"),
    )
    return jax.shard_map(
        on_device,
        mesh=mesh,
        in_specs=placed,
        out_specs=P(("grp", "blk", "proj"), None),
        check_vma=False,
    )
```

time: 292 us -> 211 us (0.72)
  waiting for transfers between devices: 236 us -> 94.1 us
  starting transfers between devices: 0.04 us -> 57.8 us
  Pallas kernels: 0 us -> 35.8 us
  matrix products: 25.2 us -> 0 us
  between operations: 13.4 us -> 0.79 us
  other arithmetic: 0.97 us -> 11 us
  local copies, waits for them, and re-layouts: 15.5 us -> 10.7 us
    all_gather x1 -> x0, waiting for transfers between devices: 209 us -> none  [on_device(): everyone = lax.all_gather(query_grads, 'blk', axis=0, tiled=True)]
    ppermute x0 -> x37, waiting for transfers between devices: none -> 94.1 us  [the longest x22 60.9 us: move(): return lax.ppermute(x, 'blk', pairs)]
    ppermute x0 -> x37, starting transfers between devices: none -> 57.8 us  [the longest x22 42.4 us: move(): return lax.ppermute(x, 'blk', pairs)]
    pallas_call x0 -> x12, Pallas kernels: none -> 35.8 us  [the longest x8 21 us: score(): pl.pallas_call(functools.partial(body, stay), in_specs=[SCALARS] + [WHOLE...]
    psum x1 -> x0, waiting for transfers between devices: 26.8 us -> none  [on_device(): summed = lax.psum(scores, 'proj')]
    dot_general x2 -> x0, matrix products: 25.2 us -> none  [the longest x1 15 us: on_device(): lax.dot_general(doc_flat, everyone, contract, preferred_element_type=jnp....]
    convert_element_type x1 -> x0, local copies, waits for them, and re-layouts: 12.4 us -> none  [on_device(): formed = jnp.einsum('dlit,dljt->dlij', doc_inputs, masked, preferred_elem...]
    unnamed x0 -> x76, local copies, waits for them, and re-layouts: none -> 8.44 us
  transfers between devices with their start and end apart: 2 -> 37, of which waited for: 2 -> 10; matrix products, arithmetic and copies ran while one was open for 8% -> 6% of each run, Pallas kernels for 0% -> 16%
where the time goes in v4:
time: 211 us; the launch traced here: 210 us
  waiting for transfers between devices  94.1 us (45%)
  starting transfers between devices  57.8 us (27%)
  Pallas kernels  35.8 us (17%)
  other arithmetic  11 us (5%)
  local copies, waits for them, and re-layouts  10.7 us (5%)
    ppermute x22, waiting for transfers between devices, move(): return lax.ppermute(x, 'blk', pairs)  60.9 us
    ppermute x22, starting transfers between devices, move(): return lax.ppermute(x, 'blk', pairs)  42.4 us
    pallas_call x8, Pallas kernels, score(): pl.pallas_call(functools.partial(body, stay), in_specs=[SCALARS] + [WHOLE...  21 us
    ppermute x6, waiting for transfers between devices, swap_across(): return lax.ppermute(x, 'blk', across)  19 us
    ppermute x1, waiting for transfers between devices, on_device(): other = lax.ppermute(sending, 'blk', across)  14.1 us
    pallas_call x1, Pallas kernels, form(): pl.pallas_call(functools.partial(form_body, rows, rank), grid_spec=pltpu....  13.5 us
    unnamed x76, local copies, waits for them, and re-layouts  8.44 us
    ppermute x6, starting transfers between devices, swap_across(): return lax.ppermute(x, 'blk', across)  6.63 us
  transfers between devices with their start and end apart: 37, of which 10 were waited for; matrix products, arithmetic and copies ran while one was open for 6% of the time, Pallas kernels for 16%

profile of v4, /device:TPU:0, one launch (start us, length us, event | category | flops | bytes accessed | tf_op | source)
XLA Modules:
  0.0 210.2 jit_solution(17387218363623337306)
XLA Ops:
  0.1 1.6 copy-done.9
  1.7 1.3 shard_map.46
  3.0 0.7 collective-permute-start.2
  3.7 3.0 %collective-permute-start.3 = (bf16[256,2048]{1,0:T(8,128)(2,1)S(1)}, bf16[256,2048]{1,0:T(8,128)(2,1)S(1)}, u32[]{:S(2)}, u32[]{:S(2)}) collective-permute-start(bf16[256,2048]{1,0:T(8,128)(2,1)S(1)} %get-tuple-element.37), channel_id=1, source_target_pairs={{0,2},{2,0},{4,6},{6,4},{8,10},{10,8},{12,14},{14,12},{1,3},{3,1},... | collective-permute-start | bytes 3145736 | tf_op jit(solution)/shard_map/ppermute | solution.py:211
  6.7 1.3 collective-permute-start
  8.0 6.3 %collective-permute-start.1 = (bf16[256,2048]{1,0:T(8,128)(2,1)S(1)}, bf16[256,2048]{1,0:T(8,128)(2,1)S(1)}, u32[]{:S(2)}, u32[]{:S(2)}) collective-permute-start(bf16[256,2048]{1,0:T(8,128)(2,1)S(1)} %get-tuple-element.36.first.first_stay), channel_id=1, source_target_pairs={{0,4},{2,6},{12,8},{14,10},{1,5},{3,7},{13,9},{15,11},{16,20},{18,... | collective-permute-start | bytes 3145736 | tf_op jit(solution)/shard_map/ppermute | solution.py:252
  14.5 1.3 collective-permute-start.8
  15.8 14.1 %collective-permute-done.3.refs_4_.second.second_stay = bf16[256,2048]{1,0:T(8,128)(2,1)S(1)} collective-permute-done((bf16[256,2048]{1,0:T(8,128)(2,1)S(1)}, bf16[256,2048]{1,0:T(8,128)(2,1)S(1)}, u32[]{:S(2)}, u32[]{:S(2)}) %collective-permute-start.3) | collective-permute-done | bytes 1048608 | tf_op jit(solution)/shard_map/ppermute | solution.py:211
  29.9 0.7 collective-permute-start.7
  30.7 13.5 %shard_map.47 = (bf16[512,2048]{1,0:T(8,128)(2,1)S(1)}, bf16[512,768]{1,0:T(8,128)(2,1)S(1)}, bf16[512,1280]{1,0:T(8,128)(2,1)S(1)}, bf16[512,768]{1,0:T(8,128)(2,1)S(1)}) custom-call(s32[3]{0:T(128)S(1)} %pad_add_fusion.spot, bf16[512,64,128]{2,1,0:T(8,128)(2,1)} %bitcast.5, bf16[512,64,128]{2,1,0:T(8,128)(2,1)} %bitcast.6, s32[512,128]{1,0:T(8,128)S(1)} %copy-done.31, ...), custom_call_target="tpu_custom_call" | custom-call | flops 10737418240 | bytes 20971520 | tf_op jit(solution)/shard_map/pallas_call | solution.py:86
  44.2 1.3 copy-done
  45.5 1.7 collective-permute-start.5
  47.2 8.8 %collective-permute-start.6 = (bf16[256,2048]{1,0:T(8,128)(2,1)S(1)}, bf16[256,2048]{1,0:T(8,128)(2,1)S(1)}, u32[]{:S(2)}, u32[]{:S(2)}) collective-permute-start(bf16[256,2048]{1,0:T(8,128)(2,1)S(1)} %collective-permute-done.3.refs_4_.second.second_stay), channel_id=1, source_target_pairs={{0,4},{2,6},{12,8},{14,10},{1,5},{3,7},{13,9},{15,11},{16,20},{18,... | collective-permute-start | bytes 3145736 | tf_op jit(solution)/shard_map/ppermute | solution.py:252
  56.6 0.7 collective-permute-start.9
  57.4 1.3 collective-permute-start.10
  58.8 7.2 %collective-permute-done.5.refs_1_ = bf16[512,768]{1,0:T(8,128)(2,1)S(1)} collective-permute-done((bf16[512,768]{1,0:T(8,128)(2,1)S(1)}, bf16[512,768]{1,0:T(8,128)(2,1)S(1)}, u32[]{:S(2)}, u32[]{:S(2)}) %collective-permute-start.5) | collective-permute-done | bytes 786464 | tf_op jit(solution)/shard_map/ppermute | solution.py:219
  65.9 1.3 collective-permute-start.11
  67.2 9.7 %collective-permute-done.6.refs_2_.second = bf16[256,2048]{1,0:T(8,128)(2,1)S(1)} collective-permute-done((bf16[256,2048]{1,0:T(8,128)(2,1)S(1)}, bf16[256,2048]{1,0:T(8,128)(2,1)S(1)}, u32[]{:S(2)}, u32[]{:S(2)}) %collective-permute-start.6) | collective-permute-done | bytes 1048608 | tf_op jit(solution)/shard_map/ppermute | solution.py:252
  76.9 4.4 %collective-permute-start.14 = (bf16[512,768]{1,0:T(8,128)(2,1)S(1)}, bf16[512,768]{1,0:T(8,128)(2,1)S(1)}, u32[]{:S(2)}, u32[]{:S(2)}) collective-permute-start(bf16[512,768]{1,0:T(8,128)(2,1)S(1)} %get-tuple-element.44), channel_id=1, source_target_pairs={{0,4},{2,6},{12,8},{14,10},{1,5},{3,7},{13,9},{15,11},{16,20},{18,... | collective-permute-start | bytes 2359304 | tf_op jit(solution)/shard_map/ppermute | solution.py:252
  81.4 3.2 %collective-permute-start.15 = (bf16[512,768]{1,0:T(8,128)(2,1)S(1)}, bf16[512,768]{1,0:T(8,128)(2,1)S(1)}, u32[]{:S(2)}, u32[]{:S(2)}) collective-permute-start(bf16[512,768]{1,0:T(8,128)(2,1)S(1)} %get-tuple-element.41.far_lent), channel_id=1, source_target_pairs={{0,4},{2,6},{12,8},{14,10},{1,5},{3,7},{13,9},{15,11},{16,20},{18,... | collective-permute-start | bytes 2359304 | tf_op jit(solution)/shard_map/ppermute | solution.py:252
  84.6 0.9 slice.153
  85.5 1.3 collective-permute-start.16
  86.7 5.5 %collective-permute-done.4.far = bf16[512,1280]{1,0:T(8,128)(2,1)S(1)} collective-permute-done((bf16[512,1280]{1,0:T(8,128)(2,1)S(1)}, bf16[512,1280]{1,0:T(8,128)(2,1)S(1)}, u32[]{:S(2)}, u32[]{:S(2)}) %collective-permute-start.4) | collective-permute-done | bytes 1310752 | tf_op jit(solution)/shard_map/ppermute | solution.py:219
  92.3 1.1 copy-done.32
  93.4 3.5 %shard_map.50 = (f32[512,512]{1,0:T(8,128)S(1)}, bf16[512,512]{1,0:T(8,128)(2,1)S(1)}) custom-call(s32[3]{0:T(128)S(1)} %pad_add_fusion.spot, bf16[512,2048]{1,0:T(8,128)(2,1)} %copy-done, bf16[512,1280]{1,0:T(8,128)(2,1)} %copy-done.32, bf16[512,768]{1,0:T(8,128)(2,1)S(1)} %get-tuple-element.41.far_lent, ...), custom_call_target="tpu_custom_call" | custom-call | flops 131072 | bytes 131072 | tf_op jit(solution)/shard_map/pallas_call | solution.py:180
  96.9 4.2 %shard_map.51 = (f32[512,512]{1,0:T(8,128)S(1)}, bf16[512,512]{1,0:T(8,128)(2,1)S(1)}) custom-call(s32[3]{0:T(128)S(1)} %pad_add_fusion.spot, bf16[512,2048]{1,0:T(8,128)(2,1)} %copy-done, bf16[512,1280]{1,0:T(8,128)(2,1)} %copy-done.32, bf16[512,768]{1,0:T(8,128)(2,1)S(1)} %get-tuple-element.41.far_lent, ...), custom_call_target="tpu_custom_call" | custom-call | flops 131072 | bytes 131072 | tf_op jit(solution)/shard_map/pallas_call | solution.py:180
  101.7 0.8 collective-permute-done.16.refs_1_.first_stay
  102.5 0.7 collective-permute-start.30
  103.2 4.0 %shard_map.52 = (f32[512,512]{1,0:T(8,128)S(1)}, bf16[512,512]{1,0:T(8,128)(2,1)S(1)}) custom-call(s32[3]{0:T(128)S(1)} %pad_add_fusion.spot, bf16[512,2048]{1,0:T(8,128)(2,1)} %copy-done, bf16[512,1280]{1,0:T(8,128)(2,1)} %copy-done.32, bf16[512,768]{1,0:T(8,128)(2,1)S(1)} %get-tuple-element.41.far_lent, ...), custom_call_target="tpu_custom_call" | custom-call | flops 131072 | bytes 131072 | tf_op jit(solution)/shard_map/pallas_call | solution.py:180
  107.3 5.3 %collective-permute-done.15.far = bf16[512,768]{1,0:T(8,128)(2,1)S(1)} collective-permute-done((bf16[512,768]{1,0:T(8,128)(2,1)S(1)}, bf16[512,768]{1,0:T(8,128)(2,1)S(1)}, u32[]{:S(2)}, u32[]{:S(2)}) %collective-permute-start.15) | collective-permute-done | bytes 786464 | tf_op jit(solution)/shard_map/ppermute | solution.py:252
  112.6 2.0 shard_map.53
  114.6 1.5 collective-permute-start.27
  116.8 1.0 add_convert_fusion.11
  117.8 1.6 collective-permute-start.13
  119.4 0.8 copy-done.36
  120.8 1.0 slice.164
  121.8 1.4 collective-permute-start.31
  123.2 6.2 %collective-permute-done.13.refs_1_ = bf16[256,512]{1,0:T(8,128)(2,1)S(1)} collective-permute-done((bf16[256,512]{1,0:T(8,128)(2,1)S(1)}, bf16[256,512]{1,0:T(8,128)(2,1)S(1)}, u32[]{:S(2)}, u32[]{:S(2)}) %collective-permute-start.13) | collective-permute-done | bytes 262176 | tf_op jit(solution)/shard_map/ppermute | solution.py:219
  130.2 1.0 copy-done.10
  131.2 1.4 shard_map.55
  132.7 1.4 shard_map.56
  134.1 1.0 copy-done.12
  135.1 1.5 collective-permute-start.34
  136.5 1.7 add_convert_fusion.4
  138.2 1.4 collective-permute-start.28
  139.6 1.5 collective-permute-start.19
  141.1 0.7 collective-permute-start.22
  141.8 1.1 add_convert_fusion.3
  142.9 1.4 collective-permute-start.29
  144.4 9.3 %collective-permute-done.31.second_stay = bf16[256,1280]{1,0:T(8,128)(2,1)} collective-permute-done((bf16[256,1280]{1,0:T(8,128)(2,1)}, bf16[256,1280]{1,0:T(8,128)(2,1)}, u32[]{:S(2)}, u32[]{:S(2)}) %collective-permute-start.31) | collective-permute-done | bytes 655392 | tf_op jit(solution)/shard_map/ppermute | solution.py:252
  153.7 4.0 %shard_map.57 = (f32[512,512]{1,0:T(8,128)S(1)}, bf16[512,512]{1,0:T(8,128)(2,1)S(1)}) custom-call(s32[3]{0:T(128)S(1)} %pad_add_fusion.spot, bf16[512,2048]{1,0:T(8,128)(2,1)} %copy-done, bf16[512,1280]{1,0:T(8,128)(2,1)} %copy-done.32, bf16[512,768]{1,0:T(8,128)(2,1)S(1)} %get-tuple-element.41.far_lent, bf16[256,2048]{1,0:T(8,128)(2,1)S(1)} %copy-done.5, ...), custom_call_target="tpu_custom_call" | custom-call | flops 131072 | bytes 131072 | tf_op jit(solution)/shard_map/pallas_call | solution.py:180
  157.8 1.1 add_convert_fusion.1
  159.6 1.0 add_convert_fusion.9
  162.2 1.6 collective-permute-start.33
  163.8 1.1 add_convert_fusion.8
  164.8 1.4 collective-permute-start.21
  166.3 1.1 add_convert_fusion
  167.3 1.3 collective-permute-start.36
  168.8 1.4 collective-permute-start.24
  170.2 27.7 %collective-permute-done.21 = bf16[256,512]{1,0:T(8,128)(2,1)S(1)} collective-permute-done((bf16[256,512]{1,0:T(8,128)(2,1)S(1)}, bf16[256,512]{1,0:T(8,128)(2,1)S(1)}, u32[]{:S(2)}, u32[]{:S(2)}) %collective-permute-start.21) | collective-permute-done | bytes 262176 | tf_op jit(solution)/shard_map/ppermute | solution.py:252
  198.2 1.2 add_dynamic-update-slice_fusion.3
  199.5 8.1 %collective-permute-done.24 = bf16[256,512]{1,0:T(8,128)(2,1)S(1)} collective-permute-done((bf16[256,512]{1,0:T(8,128)(2,1)S(1)}, bf16[256,512]{1,0:T(8,128)(2,1)S(1)}, u32[]{:S(2)}, u32[]{:S(2)}) %collective-permute-start.24) | collective-permute-done | bytes 262176 | tf_op jit(solution)/shard_map/ppermute | solution.py:252
  208.0 1.3 copy-done.33
  209.3 0.9 add_dynamic-update-slice_fusion
  (121 shorter events, 6.6 us)
Async XLA Ops:
  0.1 1.6 copy-start.9
  1.7 29.0 %copy-start.31 = (s32[512,128]{1,0:T(8,128)S(1)}, s32[512,128]{1,0:T(8,128)}, u32[]{:S(2)}) copy-start(s32[512,128]{1,0:T(8,128)} %mask.1) | copy-start | bytes 786436
  3.0 11.4 %collective-permute-start.2 = (bf16[256,2048]{1,0:T(8,128)(2,1)S(1)}, bf16[256,2048]{1,0:T(8,128)(2,1)S(1)}, u32[]{:S(2)}, u32[]{:S(2)}) collective-permute-start(bf16[256,2048]{1,0:T(8,128)(2,1)S(1)} %get-tuple-element.36.first.first_stay), channel_id=1, source_target_pairs={{4,8},{6,10},{8,4},{10,6},{5,9},{7,11},{9,5},{11,7},{20,24},{22,26... | collective-permute-start | bytes 3145736 | tf_op jit(solution)/shard_map/ppermute | solution.py:252
  3.7 26.2 %collective-permute-start.3 = (bf16[256,2048]{1,0:T(8,128)(2,1)S(1)}, bf16[256,2048]{1,0:T(8,128)(2,1)S(1)}, u32[]{:S(2)}, u32[]{:S(2)}) collective-permute-start(bf16[256,2048]{1,0:T(8,128)(2,1)S(1)} %get-tuple-element.37), channel_id=1, source_target_pairs={{0,2},{2,0},{4,6},{6,4},{8,10},{10,8},{12,14},{14,12},{1,3},{3,1},... | collective-permute-start | bytes 3145736 | tf_op jit(solution)/shard_map/ppermute | solution.py:211
  6.7 23.9 %collective-permute-start = (bf16[256,1280]{1,0:T(8,128)(2,1)S(1)}, bf16[256,1280]{1,0:T(8,128)(2,1)S(1)}, u32[]{:S(2)}, u32[]{:S(2)}) collective-permute-start(bf16[256,1280]{1,0:T(8,128)(2,1)S(1)} %get-tuple-element.32), channel_id=1, source_target_pairs={{4,0},{6,2},{8,12},{10,14},{5,1},{7,3},{9,13},{11,15},{20,16},{22,... | collective-permute-start | bytes 1966088 | tf_op jit(solution)/shard_map/ppermute | solution.py:252
  8.0 37.4 %collective-permute-start.1 = (bf16[256,2048]{1,0:T(8,128)(2,1)S(1)}, bf16[256,2048]{1,0:T(8,128)(2,1)S(1)}, u32[]{:S(2)}, u32[]{:S(2)}) collective-permute-start(bf16[256,2048]{1,0:T(8,128)(2,1)S(1)} %get-tuple-element.36.first.first_stay), channel_id=1, source_target_pairs={{0,4},{2,6},{12,8},{14,10},{1,5},{3,7},{13,9},{15,11},{16,20},{18,... | collective-permute-start | bytes 3145736 | tf_op jit(solution)/shard_map/ppermute | solution.py:252
  14.5 42.2 %collective-permute-start.8 = (bf16[256,1280]{1,0:T(8,128)(2,1)S(1)}, bf16[256,1280]{1,0:T(8,128)(2,1)S(1)}, u32[]{:S(2)}, u32[]{:S(2)}) collective-permute-start(bf16[256,1280]{1,0:T(8,128)(2,1)S(1)} %slice.148), channel_id=1, source_target_pairs={{4,0},{6,2},{8,12},{10,14},{5,1},{7,3},{9,13},{11,15},{20,16},{22,... | collective-permute-start | bytes 1966088 | tf_op jit(solution)/shard_map/ppermute | solution.py:252
  29.9 63.5 %copy-start.1 = (bf16[256,2048]{1,0:T(8,128)(2,1)}, bf16[256,2048]{1,0:T(8,128)(2,1)S(1)}, u32[]{:S(2)}) copy-start(bf16[256,2048]{1,0:T(8,128)(2,1)S(1)} %collective-permute-done.3.refs_4_.second.second_stay) | copy-start | bytes 3145732
  29.9 27.5 %collective-permute-start.7 = (bf16[256,2048]{1,0:T(8,128)(2,1)S(1)}, bf16[256,2048]{1,0:T(8,128)(2,1)S(1)}, u32[]{:S(2)}, u32[]{:S(2)}) collective-permute-start(bf16[256,2048]{1,0:T(8,128)(2,1)S(1)} %collective-permute-done.3.refs_4_.second.second_stay), channel_id=1, source_target_pairs={{4,8},{6,10},{8,4},{10,6},{5,9},{7,11},{9,5},{11,7},{20,24},{22,26... | collective-permute-start | bytes 3145736 | tf_op jit(solution)/shard_map/ppermute | solution.py:252
  30.6 13.5 %copy-start.28 = (bf16[256,1280]{1,0:T(8,128)(2,1)}, bf16[256,1280]{1,0:T(8,128)(2,1)S(1)}, u32[]{:S(2)}) copy-start(bf16[256,1280]{1,0:T(8,128)(2,1)S(1)} %collective-permute-done.refs_0_.first_stay) | copy-start | bytes 1966084
  45.5 20.5 %collective-permute-start.5 = (bf16[512,768]{1,0:T(8,128)(2,1)S(1)}, bf16[512,768]{1,0:T(8,128)(2,1)S(1)}, u32[]{:S(2)}, u32[]{:S(2)}) collective-permute-start(bf16[512,768]{1,0:T(8,128)(2,1)S(1)} %get-tuple-element.40), channel_id=1, source_target_pairs={{0,2},{2,0},{4,6},{6,4},{8,10},{10,8},{12,14},{14,12},{1,3},{3,1},... | collective-permute-start | bytes 2359304 | tf_op jit(solution)/shard_map/ppermute | solution.py:219
  47.2 29.7 %collective-permute-start.6 = (bf16[256,2048]{1,0:T(8,128)(2,1)S(1)}, bf16[256,2048]{1,0:T(8,128)(2,1)S(1)}, u32[]{:S(2)}, u32[]{:S(2)}) collective-permute-start(bf16[256,2048]{1,0:T(8,128)(2,1)S(1)} %collective-permute-done.3.refs_4_.second.second_stay), channel_id=1, source_target_pairs={{0,4},{2,6},{12,8},{14,10},{1,5},{3,7},{13,9},{15,11},{16,20},{18,... | collective-permute-start | bytes 3145736 | tf_op jit(solution)/shard_map/ppermute | solution.py:252
  56.0 36.3 %collective-permute-start.4 = (bf16[512,1280]{1,0:T(8,128)(2,1)S(1)}, bf16[512,1280]{1,0:T(8,128)(2,1)S(1)}, u32[]{:S(2)}, u32[]{:S(2)}) collective-permute-start(bf16[512,1280]{1,0:T(8,128)(2,1)S(1)} %get-tuple-element.38), channel_id=1, source_target_pairs={{0,2},{2,0},{4,6},{6,4},{8,10},{10,8},{12,14},{14,12},{1,3},{3,1},... | collective-permute-start | bytes 3932168 | tf_op jit(solution)/shard_map/ppermute | solution.py:219
  56.6 24.8 %collective-permute-start.9 = (bf16[256,2048]{1,0:T(8,128)(2,1)S(1)}, bf16[256,2048]{1,0:T(8,128)(2,1)S(1)}, u32[]{:S(2)}, u32[]{:S(2)}) collective-permute-start(bf16[256,2048]{1,0:T(8,128)(2,1)S(1)} %collective-permute-done.1.refs_2_.first), channel_id=1, source_target_pairs={{4,8},{6,10},{8,4},{10,6},{5,9},{7,11},{9,5},{11,7},{20,24},{22,26... | collective-permute-start | bytes 3145736 | tf_op jit(solution)/shard_map/ppermute | solution.py:252
  57.4 19.5 %copy-start.2 = (bf16[256,2048]{1,0:T(8,128)(2,1)}, bf16[256,2048]{1,0:T(8,128)(2,1)S(1)}, u32[]{:S(2)}) copy-start(bf16[256,2048]{1,0:T(8,128)(2,1)S(1)} %collective-permute-done.7.refs_3_.second) | copy-start | bytes 3145732
  57.4 28.0 %collective-permute-start.10 = (bf16[256,1280]{1,0:T(8,128)(2,1)S(1)}, bf16[256,1280]{1,0:T(8,128)(2,1)S(1)}, u32[]{:S(2)}, u32[]{:S(2)}) collective-permute-start(bf16[256,1280]{1,0:T(8,128)(2,1)S(1)} %slice.149), channel_id=1, source_target_pairs={{4,0},{6,2},{8,12},{10,14},{5,1},{7,3},{9,13},{11,15},{20,16},{22,... | collective-permute-start | bytes 1966088 | tf_op jit(solution)/shard_map/ppermute | solution.py:252
  65.9 26.3 %collective-permute-start.11 = (bf16[256,1280]{1,0:T(8,128)(2,1)S(1)}, bf16[256,1280]{1,0:T(8,128)(2,1)S(1)}, u32[]{:S(2)}, u32[]{:S(2)}) collective-permute-start(bf16[256,1280]{1,0:T(8,128)(2,1)S(1)} %slice.150), channel_id=1, source_target_pairs={{4,0},{6,2},{8,12},{10,14},{5,1},{7,3},{9,13},{11,15},{20,16},{22,... | collective-permute-start | bytes 1966088 | tf_op jit(solution)/shard_map/ppermute | solution.py:252
  76.9 25.5 %copy-start.6 = (bf16[256,2048]{1,0:T(8,128)(2,1)}, bf16[256,2048]{1,0:T(8,128)(2,1)S(1)}, u32[]{:S(2)}) copy-start(bf16[256,2048]{1,0:T(8,128)(2,1)S(1)} %collective-permute-done.6.refs_2_.second) | copy-start | bytes 3145732
  76.9 30.3 %collective-permute-start.14 = (bf16[512,768]{1,0:T(8,128)(2,1)S(1)}, bf16[512,768]{1,0:T(8,128)(2,1)S(1)}, u32[]{:S(2)}, u32[]{:S(2)}) collective-permute-start(bf16[512,768]{1,0:T(8,128)(2,1)S(1)} %get-tuple-element.44), channel_id=1, source_target_pairs={{0,4},{2,6},{12,8},{14,10},{1,5},{3,7},{13,9},{15,11},{16,20},{18,... | collective-permute-start | bytes 2359304 | tf_op jit(solution)/shard_map/ppermute | solution.py:252
  81.4 12.0 %copy-start.4 = (bf16[256,2048]{1,0:T(8,128)(2,1)}, bf16[256,2048]{1,0:T(8,128)(2,1)S(1)}, u32[]{:S(2)}) copy-start(bf16[256,2048]{1,0:T(8,128)(2,1)S(1)} %collective-permute-done.9.refs_0_.first) | copy-start | bytes 3145732
  81.4 31.2 %collective-permute-start.15 = (bf16[512,768]{1,0:T(8,128)(2,1)S(1)}, bf16[512,768]{1,0:T(8,128)(2,1)S(1)}, u32[]{:S(2)}, u32[]{:S(2)}) collective-permute-start(bf16[512,768]{1,0:T(8,128)(2,1)S(1)} %get-tuple-element.41.far_lent), channel_id=1, source_target_pairs={{0,4},{2,6},{12,8},{14,10},{1,5},{3,7},{13,9},{15,11},{16,20},{18,... | collective-permute-start | bytes 2359304 | tf_op jit(solution)/shard_map/ppermute | solution.py:252
  85.5 17.0 %collective-permute-start.16 = (bf16[256,1280]{1,0:T(8,128)(2,1)}, bf16[256,1280]{1,0:T(8,128)(2,1)S(1)}, u32[]{:S(2)}, u32[]{:S(2)}) collective-permute-start(bf16[256,1280]{1,0:T(8,128)(2,1)} %slice.153), channel_id=1, source_target_pairs={{4,0},{6,2},{8,12},{10,14},{5,1},{7,3},{9,13},{11,15},{20,16},{22,... | collective-permute-start | bytes 1966088 | tf_op jit(solution)/shard_map/ppermute | solution.py:252
  96.9 19.9 %copy-start.24 = (f32[512,512]{1,0:T(8,128)}, f32[512,512]{1,0:T(8,128)S(1)}, u32[]{:S(2)}) copy-start(f32[512,512]{1,0:T(8,128)S(1)} %get-tuple-element.42) | copy-start | bytes 3145732
  96.9 6.3 %copy-start.29 = (bf16[256,1280]{1,0:T(8,128)(2,1)S(1)}, bf16[256,1280]{1,0:T(8,128)(2,1)}, u32[]{:S(2)}) copy-start(bf16[256,1280]{1,0:T(8,128)(2,1)} %copy-done.28) | copy-start | bytes 1966084
  101.1 15.0 %copy-start.22 = (f32[512,512]{1,0:T(8,128)}, f32[512,512]{1,0:T(8,128)S(1)}, u32[]{:S(2)}) copy-start(f32[512,512]{1,0:T(8,128)S(1)} %get-tuple-element.49) | copy-start | bytes 3145732
  101.1 15.0 %collective-permute-start.17 = (bf16[512,512]{1,0:T(8,128)(2,1)S(1)}, bf16[512,512]{1,0:T(8,128)(2,1)S(1)}, u32[]{:S(2)}, u32[]{:S(2)}) collective-permute-start(bf16[512,512]{1,0:T(8,128)(2,1)S(1)} %get-tuple-element.45.refs_0_), channel_id=1, source_target_pairs={{0,1},{1,0},{2,3},{3,2},{4,5},{5,4},{6,7},{7,6},{8,9},{9,8},{10,11... | collective-permute-start | bytes 1572872 | tf_op jit(solution)/shard_map/ppermute | solution.py:222
  101.2 15.5 %collective-permute-start.12 = (bf16[512,512]{1,0:T(8,128)(2,1)S(1)}, bf16[512,512]{1,0:T(8,128)(2,1)}, u32[]{:S(2)}, u32[]{:S(2)}) collective-permute-start(bf16[512,512]{1,0:T(8,128)(2,1)S(1)} %get-tuple-element.43.refs_0_), channel_id=1, source_target_pairs={{0,1},{1,0},{2,3},{3,2},{4,5},{5,4},{6,7},{7,6},{8,9},{9,8},{10,11... | collective-permute-start | bytes 1572872 | tf_op jit(solution)/shard_map/ppermute | solution.py:222
  102.5 18.3 %collective-permute-start.30 = (bf16[256,2048]{1,0:T(8,128)(2,1)S(1)}, bf16[256,2048]{1,0:T(8,128)(2,1)S(1)}, u32[]{:S(2)}, u32[]{:S(2)}) collective-permute-start(bf16[256,2048]{1,0:T(8,128)(2,1)S(1)} %collective-permute-done.6.refs_2_.second), channel_id=1, source_target_pairs={{4,8},{6,10},{8,4},{10,6},{5,9},{7,11},{9,5},{11,7},{20,24},{22,26... | collective-permute-start | bytes 3145736 | tf_op jit(solution)/shard_map/ppermute | solution.py:252
  107.2 12.2 %copy-start.26 = (f32[512,512]{1,0:T(8,128)}, f32[512,512]{1,0:T(8,128)S(1)}, u32[]{:S(2)}) copy-start(f32[512,512]{1,0:T(8,128)S(1)} %get-tuple-element.53) | copy-start | bytes 3145732
  107.2 12.1 %collective-permute-start.25 = (bf16[512,512]{1,0:T(8,128)(2,1)S(1)}, bf16[512,512]{1,0:T(8,128)(2,1)S(1)}, u32[]{:S(2)}, u32[]{:S(2)}) collective-permute-start(bf16[512,512]{1,0:T(8,128)(2,1)S(1)} %get-tuple-element.46.refs_0_), channel_id=1, source_target_pairs={{0,1},{1,0},{2,3},{3,2},{4,5},{5,4},{6,7},{7,6},{8,9},{9,8},{10,11... | collective-permute-start | bytes 1572872 | tf_op jit(solution)/shard_map/ppermute | solution.py:222
  114.6 21.9 %collective-permute-start.27 = (bf16[512,512]{1,0:T(8,128)(2,1)}, bf16[512,512]{1,0:T(8,128)(2,1)}, u32[]{:S(2)}, u32[]{:S(2)}) collective-permute-start(bf16[512,512]{1,0:T(8,128)(2,1)} %get-tuple-element.47.refs_0_), channel_id=1, source_target_pairs={{4,5},{5,4},{6,7},{7,6},{8,9},{9,8},{10,11},{11,10},{20,21},{21,20... | collective-permute-start | bytes 1572872 | tf_op jit(solution)/shard_map/ppermute | solution.py:301
  116.1 5.7 %copy-start.34 = (bf16[512,512]{1,0:T(8,128)(2,1)}, bf16[512,512]{1,0:T(8,128)(2,1)S(1)}, u32[]{:S(2)}) copy-start(bf16[512,512]{1,0:T(8,128)(2,1)S(1)} %collective-permute-done.17) | copy-start | bytes 1572868
  116.1 13.4 %copy-start.3 = (bf16[256,2048]{1,0:T(8,128)(2,1)S(1)}, bf16[256,2048]{1,0:T(8,128)(2,1)}, u32[]{:S(2)}) copy-start(bf16[256,2048]{1,0:T(8,128)(2,1)} %copy-done.2) | copy-start | bytes 3145732
  116.2 15.0 %collective-permute-start.18 = (bf16[256,512]{1,0:T(8,128)(2,1)S(1)}, bf16[256,512]{1,0:T(8,128)(2,1)S(1)}, u32[]{:S(2)}, u32[]{:S(2)}) collective-permute-start(bf16[256,512]{1,0:T(8,128)(2,1)S(1)} %add_convert_fusion.10), channel_id=1, source_target_pairs={{0,2},{2,0},{4,6},{6,4},{8,10},{10,8},{12,14},{14,12},{1,3},{3,1},... | collective-permute-start | bytes 786440 | tf_op jit(solution)/shard_map/ppermute | solution.py:219
  117.8 11.7 %collective-permute-start.13 = (bf16[256,512]{1,0:T(8,128)(2,1)S(1)}, bf16[256,512]{1,0:T(8,128)(2,1)S(1)}, u32[]{:S(2)}, u32[]{:S(2)}) collective-permute-start(bf16[256,512]{1,0:T(8,128)(2,1)S(1)} %add_convert_fusion.11), channel_id=1, source_target_pairs={{0,2},{2,0},{4,6},{6,4},{8,10},{10,8},{12,14},{14,12},{1,3},{3,1},... | collective-permute-start | bytes 786440 | tf_op jit(solution)/shard_map/ppermute | solution.py:219
  120.3 12.3 %collective-permute-start.26 = (bf16[256,512]{1,0:T(8,128)(2,1)S(1)}, bf16[256,512]{1,0:T(8,128)(2,1)S(1)}, u32[]{:S(2)}, u32[]{:S(2)}) collective-permute-start(bf16[256,512]{1,0:T(8,128)(2,1)S(1)} %add_convert_fusion.5), channel_id=1, source_target_pairs={{0,2},{2,0},{4,6},{6,4},{8,10},{10,8},{12,14},{14,12},{1,3},{3,1},... | collective-permute-start | bytes 786440 | tf_op jit(solution)/shard_map/ppermute | solution.py:219
  120.8 11.7 %copy-start.8 = (bf16[256,2048]{1,0:T(8,128)(2,1)}, bf16[256,2048]{1,0:T(8,128)(2,1)S(1)}, u32[]{:S(2)}) copy-start(bf16[256,2048]{1,0:T(8,128)(2,1)S(1)} %collective-permute-done.30.second) | copy-start | bytes 3145732
  121.8 9.4 %copy-start.7 = (bf16[256,2048]{1,0:T(8,128)(2,1)S(1)}, bf16[256,2048]{1,0:T(8,128)(2,1)}, u32[]{:S(2)}) copy-start(bf16[256,2048]{1,0:T(8,128)(2,1)} %copy-done.6) | copy-start | bytes 3145732
  121.8 31.9 %collective-permute-start.31 = (bf16[256,1280]{1,0:T(8,128)(2,1)}, bf16[256,1280]{1,0:T(8,128)(2,1)}, u32[]{:S(2)}, u32[]{:S(2)}) collective-permute-start(bf16[256,1280]{1,0:T(8,128)(2,1)} %slice.164), channel_id=1, source_target_pairs={{4,0},{6,2},{8,12},{10,14},{5,1},{7,3},{9,13},{11,15},{20,16},{22,... | collective-permute-start | bytes 1966088 | tf_op jit(solution)/shard_map/ppermute | solution.py:252
  131.2 1.6 copy-start.5
  135.1 22.7 %collective-permute-start.34 = (bf16[512,512]{1,0:T(8,128)(2,1)}, bf16[512,512]{1,0:T(8,128)(2,1)}, u32[]{:S(2)}, u32[]{:S(2)}) collective-permute-start(bf16[512,512]{1,0:T(8,128)(2,1)} %get-tuple-element.55.refs_0_), channel_id=1, source_target_pairs={{4,5},{5,4},{6,7},{7,6},{8,9},{9,8},{10,11},{11,10},{20,21},{21,20... | collective-permute-start | bytes 1572872 | tf_op jit(solution)/shard_map/ppermute | solution.py:301
  138.2 3.5 %collective-permute-start.28 = (bf16[256,512]{1,0:T(8,128)(2,1)}, bf16[256,512]{1,0:T(8,128)(2,1)}, u32[]{:S(2)}, u32[]{:S(2)}) collective-permute-start(bf16[256,512]{1,0:T(8,128)(2,1)} %add_convert_fusion.4), channel_id=1, source_target_pairs={{4,6},{6,4},{8,10},{10,8},{5,7},{7,5},{9,11},{11,9},{20,22},{22,20... | collective-permute-start | bytes 786440 | tf_op jit(solution)/shard_map/ppermute | solution.py:252
  139.6 20.0 %collective-permute-start.19 = (bf16[512,512]{1,0:T(8,128)(2,1)}, bf16[512,512]{1,0:T(8,128)(2,1)}, u32[]{:S(2)}, u32[]{:S(2)}) collective-permute-start(bf16[512,512]{1,0:T(8,128)(2,1)} %get-tuple-element.51.refs_0_), channel_id=1, source_target_pairs={{4,5},{5,4},{6,7},{7,6},{8,9},{9,8},{10,11},{11,10},{20,21},{21,20... | collective-permute-start | bytes 1572872 | tf_op jit(solution)/shard_map/ppermute | solution.py:301
  141.1 20.2 %collective-permute-start.22 = (bf16[512,512]{1,0:T(8,128)(2,1)}, bf16[512,512]{1,0:T(8,128)(2,1)S(1)}, u32[]{:S(2)}, u32[]{:S(2)}) collective-permute-start(bf16[512,512]{1,0:T(8,128)(2,1)} %copy-done.30), channel_id=1, source_target_pairs={{4,5},{5,4},{6,7},{7,6},{8,9},{9,8},{10,11},{11,10},{20,21},{21,20... | collective-permute-start | bytes 1572872 | tf_op jit(solution)/shard_map/ppermute | solution.py:301
  142.9 14.9 %copy-start.13 = (f32[512,512]{1,0:T(8,128)S(1)}, f32[512,512]{1,0:T(8,128)}, u32[]{:S(2)}) copy-start(f32[512,512]{1,0:T(8,128)} %copy-done.12) | copy-start | bytes 3145732
  142.9 16.7 %copy-start.15 = (f32[512,512]{1,0:T(8,128)S(1)}, f32[512,512]{1,0:T(8,128)}, u32[]{:S(2)}) copy-start(f32[512,512]{1,0:T(8,128)} %copy-done.14) | copy-start | bytes 3145732
  142.9 64.8 %collective-permute-start.29 = (bf16[256,512]{1,0:T(8,128)(2,1)S(1)}, bf16[256,512]{1,0:T(8,128)(2,1)S(1)}, u32[]{:S(2)}, u32[]{:S(2)}) collective-permute-start(bf16[256,512]{1,0:T(8,128)(2,1)S(1)} %add_convert_fusion.3), channel_id=1, source_target_pairs={{4,0},{6,2},{8,12},{10,14},{5,1},{7,3},{9,13},{11,15},{20,16},{22,... | collective-permute-start | bytes 786440 | tf_op jit(solution)/shard_map/ppermute | solution.py:252
  157.7 3.6 %copy-start.11 = (f32[512,512]{1,0:T(8,128)S(1)}, f32[512,512]{1,0:T(8,128)}, u32[]{:S(2)}) copy-start(f32[512,512]{1,0:T(8,128)} %copy-done.10) | copy-start | bytes 3145732
  157.7 4.4 %collective-permute-start.32 = (bf16[512,512]{1,0:T(8,128)(2,1)S(1)}, bf16[512,512]{1,0:T(8,128)(2,1)S(1)}, u32[]{:S(2)}, u32[]{:S(2)}) collective-permute-start(bf16[512,512]{1,0:T(8,128)(2,1)S(1)} %get-tuple-element.57), channel_id=1, source_target_pairs={{0,1},{1,0},{2,3},{3,2},{4,5},{5,4},{6,7},{7,6},{8,9},{9,8},{10,11... | collective-permute-start | bytes 1572872 | tf_op jit(solution)/shard_map/ppermute | solution.py:222
  158.9 7.4 %collective-permute-start.35 = (bf16[256,512]{1,0:T(8,128)(2,1)S(1)}, bf16[256,512]{1,0:T(8,128)(2,1)S(1)}, u32[]{:S(2)}, u32[]{:S(2)}) collective-permute-start(bf16[256,512]{1,0:T(8,128)(2,1)S(1)} %add_convert_fusion.1), channel_id=1, source_target_pairs={{4,6},{6,4},{8,10},{10,8},{5,7},{7,5},{9,11},{11,9},{20,22},{22,20... | collective-permute-start | bytes 786440 | tf_op jit(solution)/shard_map/ppermute | solution.py:252
  160.6 3.2 %collective-permute-start.20 = (bf16[256,512]{1,0:T(8,128)(2,1)S(1)}, bf16[256,512]{1,0:T(8,128)(2,1)S(1)}, u32[]{:S(2)}, u32[]{:S(2)}) collective-permute-start(bf16[256,512]{1,0:T(8,128)(2,1)S(1)} %add_convert_fusion.9), channel_id=1, source_target_pairs={{4,6},{6,4},{8,10},{10,8},{5,7},{7,5},{9,11},{11,9},{20,22},{22,20... | collective-permute-start | bytes 786440 | tf_op jit(solution)/shard_map/ppermute | solution.py:252
  161.4 7.3 %collective-permute-start.23 = (bf16[256,512]{1,0:T(8,128)(2,1)S(1)}, bf16[256,512]{1,0:T(8,128)(2,1)S(1)}, u32[]{:S(2)}, u32[]{:S(2)}) collective-permute-start(bf16[256,512]{1,0:T(8,128)(2,1)S(1)} %add_convert_fusion.7), channel_id=1, source_target_pairs={{4,6},{6,4},{8,10},{10,8},{5,7},{7,5},{9,11},{11,9},{20,22},{22,20... | collective-permute-start | bytes 786440 | tf_op jit(solution)/shard_map/ppermute | solution.py:252
  162.2 45.8 %collective-permute-start.33 = (bf16[256,512]{1,0:T(8,128)(2,1)S(1)}, bf16[256,512]{1,0:T(8,128)(2,1)S(1)}, u32[]{:S(2)}, u32[]{:S(2)}) collective-permute-start(bf16[256,512]{1,0:T(8,128)(2,1)S(1)} %add_convert_fusion.2), channel_id=1, source_target_pairs={{0,2},{2,0},{4,6},{6,4},{8,10},{10,8},{12,14},{14,12},{1,3},{3,1},... | collective-permute-start | bytes 786440 | tf_op jit(solution)/shard_map/ppermute | solution.py:219
  164.8 33.4 %copy-start.21 = (bf16[256,512]{1,0:T(8,128)(2,1)S(1)}, bf16[256,512]{1,0:T(8,128)(2,1)}, u32[]{:S(2)}) copy-start(bf16[256,512]{1,0:T(8,128)(2,1)} %copy-done.20) | copy-start | bytes 786436
  164.8 33.4 %copy-start.25 = (f32[512,512]{1,0:T(8,128)S(1)}, f32[512,512]{1,0:T(8,128)}, u32[]{:S(2)}) copy-start(f32[512,512]{1,0:T(8,128)} %copy-done.24) | copy-start | bytes 3145732
  164.8 33.1 %collective-permute-start.21 = (bf16[256,512]{1,0:T(8,128)(2,1)S(1)}, bf16[256,512]{1,0:T(8,128)(2,1)S(1)}, u32[]{:S(2)}, u32[]{:S(2)}) collective-permute-start(bf16[256,512]{1,0:T(8,128)(2,1)S(1)} %add_convert_fusion.8), channel_id=1, source_target_pairs={{4,0},{6,2},{8,12},{10,14},{5,1},{7,3},{9,13},{11,15},{20,16},{22,... | collective-permute-start | bytes 786440 | tf_op jit(solution)/shard_map/ppermute | solution.py:252
  167.3 40.6 %collective-permute-start.36 = (bf16[256,512]{1,0:T(8,128)(2,1)S(1)}, bf16[256,512]{1,0:T(8,128)(2,1)S(1)}, u32[]{:S(2)}, u32[]{:S(2)}) collective-permute-start(bf16[256,512]{1,0:T(8,128)(2,1)S(1)} %add_convert_fusion), channel_id=1, source_target_pairs={{4,0},{6,2},{8,12},{10,14},{5,1},{7,3},{9,13},{11,15},{20,16},{22,... | collective-permute-start | bytes 786440 | tf_op jit(solution)/shard_map/ppermute | solution.py:252
  168.8 38.8 %copy-start.17 = (bf16[256,512]{1,0:T(8,128)(2,1)S(1)}, bf16[256,512]{1,0:T(8,128)(2,1)}, u32[]{:S(2)}) copy-start(bf16[256,512]{1,0:T(8,128)(2,1)} %copy-done.16) | copy-start | bytes 786436
  168.8 38.8 %copy-start.23 = (f32[512,512]{1,0:T(8,128)S(1)}, f32[512,512]{1,0:T(8,128)}, u32[]{:S(2)}) copy-start(f32[512,512]{1,0:T(8,128)} %copy-done.22) | copy-start | bytes 3145732
  168.8 38.8 %copy-start.35 = (bf16[512,512]{1,0:T(8,128)(2,1)S(1)}, bf16[512,512]{1,0:T(8,128)(2,1)}, u32[]{:S(2)}) copy-start(bf16[512,512]{1,0:T(8,128)(2,1)} %copy-done.34) | copy-start | bytes 1572868
  168.8 38.8 %collective-permute-start.24 = (bf16[256,512]{1,0:T(8,128)(2,1)S(1)}, bf16[256,512]{1,0:T(8,128)(2,1)S(1)}, u32[]{:S(2)}, u32[]{:S(2)}) collective-permute-start(bf16[256,512]{1,0:T(8,128)(2,1)S(1)} %add_convert_fusion.6), channel_id=1, source_target_pairs={{4,0},{6,2},{8,12},{10,14},{5,1},{7,3},{9,13},{11,15},{20,16},{22,... | collective-permute-start | bytes 786440 | tf_op jit(solution)/shard_map/ppermute | solution.py:252
  198.2 9.6 %copy-start.19 = (bf16[256,512]{1,0:T(8,128)(2,1)S(1)}, bf16[256,512]{1,0:T(8,128)(2,1)}, u32[]{:S(2)}) copy-start(bf16[256,512]{1,0:T(8,128)(2,1)} %copy-done.18) | copy-start | bytes 786436
  198.2 9.6 %copy-start.27 = (f32[512,512]{1,0:T(8,128)S(1)}, f32[512,512]{1,0:T(8,128)}, u32[]{:S(2)}) copy-start(f32[512,512]{1,0:T(8,128)} %copy-done.26) | copy-start | bytes 3145732
  198.2 9.6 %copy-start.37 = (bf16[512,512]{1,0:T(8,128)(2,1)S(1)}, bf16[512,512]{1,0:T(8,128)(2,1)}, u32[]{:S(2)}) copy-start(bf16[512,512]{1,0:T(8,128)(2,1)} %copy-done.36) | copy-start | bytes 1572868
  (11 other events, 13.0 us)

commit v5 on v4

--- a/solution.py
+++ b/solution.py
@@ -257,8 +257,8 @@
     mate_a = move(mine, inward)
     near_a = move(mine, centre)
     outer_mate_a = move(mine_stay, outward)
-    own, lent, sent, sent_lent = form(doc_inputs, doc_outgrads, token_mask, spot, stay, outer_mate_a)
-    sent, sent_lent = tie((sent, sent_lent), mate_a, near_a, other)
+    own, lent, sent, sent_lent = form(doc_inputs, doc_outgrads, token_mask, spot, stay)
+    sent, sent_lent, mate_a, near_a, other = tie((sent, sent_lent, mate_a, near_a, other), outer_mate_a)
 
     far_lent = swap_across(sent_lent)
     far = swap_across(sent)

time: 211 us -> 205 us (0.972)
  waiting for transfers between devices: 94.1 us -> 78.2 us
  starting transfers between devices: 57.8 us -> 69.3 us
  local copies, waits for them, and re-layouts: 10.7 us -> 7.68 us
    ppermute x22, starting transfers between devices: 42.4 us -> 54.4 us  [move(): return lax.ppermute(x, 'blk', pairs)]
    ppermute x1, waiting for transfers between devices: 14.1 us -> 3.08 us  [on_device(): other = lax.ppermute(sending, 'blk', across)]
    ppermute x6, waiting for transfers between devices: 19 us -> 13.6 us  [swap_across(): return lax.ppermute(x, 'blk', across)]
    unnamed x76 -> x72, local copies, waits for them, and re-layouts: 8.44 us -> 5.41 us
  transfers between devices with their start and end apart: 37 -> 37, of which waited for: 10 -> 13; matrix products, arithmetic and copies ran while one was open for 6% -> 7% of each run, Pallas kernels for 16% -> 17%
where the time goes in v5:
time: 205 us; the launch traced here: 204 us
  waiting for transfers between devices  78.2 us (38%)
  starting transfers between devices  69.3 us (34%)
  Pallas kernels  35.3 us (17%)
  other arithmetic  13 us (6%)
  local copies, waits for them, and re-layouts  7.68 us (4%)
    ppermute x22, waiting for transfers between devices, move(): return lax.ppermute(x, 'blk', pairs)  61.5 us
    ppermute x22, starting transfers between devices, move(): return lax.ppermute(x, 'blk', pairs)  54.4 us
    pallas_call x8, Pallas kernels, score(): pl.pallas_call(functools.partial(body, stay), in_specs=[SCALARS] + [WHOLE...  20.5 us
    ppermute x6, waiting for transfers between devices, swap_across(): return lax.ppermute(x, 'blk', across)  13.6 us
    pallas_call x1, Pallas kernels, form(): pl.pallas_call(functools.partial(form_body, rows, rank), grid_spec=pltpu....  13.5 us
    ppermute x6, starting transfers between devices, swap_across(): return lax.ppermute(x, 'blk', across)  7.48 us
    convert_element_type x8, other arithmetic, take(): beside = far_across((keep[part:] + got[part:].astype(f32)).astype(bf16))  6.17 us
    unnamed x72, local copies, waits for them, and re-layouts  5.41 us
  transfers between devices with their start and end apart: 37, of which 13 were waited for; matrix products, arithmetic and copies ran while one was open for 7% of the time, Pallas kernels for 17%

profile of v5, /device:TPU:0, one launch (start us, length us, event | category | flops | bytes accessed | tf_op | source)
XLA Modules:
  0.0 204.2 jit_solution(6826313662611324162)
XLA Ops:
  0.1 1.6 copy-done.11
  1.7 1.3 shard_map.47
  3.0 5.0 %collective-permute-start = (bf16[256,2048]{1,0:T(8,128)(2,1)S(1)}, bf16[256,2048]{1,0:T(8,128)(2,1)S(1)}, u32[]{:S(2)}, u32[]{:S(2)}) collective-permute-start(bf16[256,2048]{1,0:T(8,128)(2,1)S(1)} %get-tuple-element.38.first.first_stay), channel_id=1, source_target_pairs={{0,4},{2,6},{12,8},{14,10},{1,5},{3,7},{13,9},{15,11},{16,20},{18,... | collective-permute-start | bytes 3145736 | tf_op jit(solution)/shard_map/ppermute | solution.py:252
  8.0 0.7 collective-permute-start.1
  8.7 1.6 collective-permute-start.2
  10.3 1.3 collective-permute-start.3
  11.6 13.5 %shard_map.46 = (bf16[512,2048]{1,0:T(8,128)(2,1)S(1)}, bf16[512,768]{1,0:T(8,128)(2,1)S(1)}, bf16[512,1280]{1,0:T(8,128)(2,1)S(1)}, bf16[512,768]{1,0:T(8,128)(2,1)S(1)}) custom-call(s32[3]{0:T(128)S(1)} %pad_add_fusion.spot, bf16[512,64,128]{2,1,0:T(8,128)(2,1)} %bitcast.5, bf16[512,64,128]{2,1,0:T(8,128)(2,1)} %bitcast.6, s32[512,128]{1,0:T(8,128)S(1)} %copy-done.31), custom_call_target="tpu_custom_call" | custom-call | flops 10737418240 | bytes 20971520 | tf_op jit(solution)/shard_map/pallas_call | solution.py:86
  25.1 1.3 copy-done
  26.4 1.7 collective-permute-done.3.refs_5_.first_stay
  28.1 2.2 %collective-permute-done.refs_2_ = bf16[256,2048]{1,0:T(8,128)(2,1)S(1)} collective-permute-done((bf16[256,2048]{1,0:T(8,128)(2,1)S(1)}, bf16[256,2048]{1,0:T(8,128)(2,1)S(1)}, u32[]{:S(2)}, u32[]{:S(2)}) %collective-permute-start) | collective-permute-done | bytes 1048608 | tf_op jit(solution)/shard_map/ppermute | solution.py:252
  30.3 3.1 %collective-permute-done.2.refs_4_ = bf16[256,2048]{1,0:T(8,128)(2,1)S(1)} collective-permute-done((bf16[256,2048]{1,0:T(8,128)(2,1)S(1)}, bf16[256,2048]{1,0:T(8,128)(2,1)S(1)}, u32[]{:S(2)}, u32[]{:S(2)}) %collective-permute-start.2) | collective-permute-done | bytes 1048608 | tf_op jit(solution)/shard_map/ppermute | solution.py:211
  33.5 1.3 collective-permute-start.8
  34.8 0.7 collective-permute-start.7
  35.5 1.6 collective-permute-start.5
  37.1 7.4 %collective-permute-start.6 = (bf16[256,2048]{1,0:T(8,128)(2,1)S(1)}, bf16[256,2048]{1,0:T(8,128)(2,1)S(1)}, u32[]{:S(2)}, u32[]{:S(2)}) collective-permute-start(bf16[256,2048]{1,0:T(8,128)(2,1)S(1)} %get-tuple-element.44.second.second_stay), channel_id=1, source_target_pairs={{0,4},{2,6},{12,8},{14,10},{1,5},{3,7},{13,9},{15,11},{16,20},{18,... | collective-permute-start | bytes 3145736 | tf_op jit(solution)/shard_map/ppermute | solution.py:252
  45.1 5.6 %collective-permute-done.8.refs_4_.first_stay = bf16[256,1280]{1,0:T(8,128)(2,1)S(1)} collective-permute-done((bf16[256,1280]{1,0:T(8,128)(2,1)S(1)}, bf16[256,1280]{1,0:T(8,128)(2,1)S(1)}, u32[]{:S(2)}, u32[]{:S(2)}) %collective-permute-start.8) | collective-permute-done | bytes 655392 | tf_op jit(solution)/shard_map/ppermute | solution.py:252
  51.4 1.3 collective-permute-start.10
  52.8 3.2 %collective-permute-done.5.refs_1_ = bf16[512,768]{1,0:T(8,128)(2,1)S(1)} collective-permute-done((bf16[512,768]{1,0:T(8,128)(2,1)S(1)}, bf16[512,768]{1,0:T(8,128)(2,1)S(1)}, u32[]{:S(2)}, u32[]{:S(2)}) %collective-permute-start.5) | collective-permute-done | bytes 786464 | tf_op jit(solution)/shard_map/ppermute | solution.py:219
  56.0 1.3 collective-permute-start.11
  57.3 7.5 %collective-permute-done.6.refs_2_.second = bf16[256,2048]{1,0:T(8,128)(2,1)S(1)} collective-permute-done((bf16[256,2048]{1,0:T(8,128)(2,1)S(1)}, bf16[256,2048]{1,0:T(8,128)(2,1)S(1)}, u32[]{:S(2)}, u32[]{:S(2)}) %collective-permute-start.6) | collective-permute-done | bytes 1048608 | tf_op jit(solution)/shard_map/ppermute | solution.py:252
  64.8 5.4 %collective-permute-start.14 = (bf16[512,768]{1,0:T(8,128)(2,1)S(1)}, bf16[512,768]{1,0:T(8,128)(2,1)S(1)}, u32[]{:S(2)}, u32[]{:S(2)}) collective-permute-start(bf16[512,768]{1,0:T(8,128)(2,1)S(1)} %get-tuple-element.50), channel_id=1, source_target_pairs={{0,4},{2,6},{12,8},{14,10},{1,5},{3,7},{13,9},{15,11},{16,20},{18,... | collective-permute-start | bytes 2359304 | tf_op jit(solution)/shard_map/ppermute | solution.py:252
  70.2 17.0 %collective-permute-start.15 = (bf16[512,768]{1,0:T(8,128)(2,1)S(1)}, bf16[512,768]{1,0:T(8,128)(2,1)S(1)}, u32[]{:S(2)}, u32[]{:S(2)}) collective-permute-start(bf16[512,768]{1,0:T(8,128)(2,1)S(1)} %get-tuple-element.46.far_lent), channel_id=1, source_target_pairs={{0,4},{2,6},{12,8},{14,10},{1,5},{3,7},{13,9},{15,11},{16,20},{18,... | collective-permute-start | bytes 2359304 | tf_op jit(solution)/shard_map/ppermute | solution.py:252
  87.2 0.9 slice.151
  88.1 1.3 collective-permute-start.16
  89.4 1.4 collective-permute-done.11.refs_2_.second_stay
  90.8 3.5 %shard_map.50 = (f32[512,512]{1,0:T(8,128)S(1)}, bf16[512,512]{1,0:T(8,128)(2,1)S(1)}) custom-call(s32[3]{0:T(128)S(1)} %pad_add_fusion.spot, bf16[512,2048]{1,0:T(8,128)(2,1)} %copy-done, bf16[512,1280]{1,0:T(8,128)(2,1)} %copy-done.32, bf16[512,768]{1,0:T(8,128)(2,1)S(1)} %get-tuple-element.46.far_lent, ...), custom_call_target="tpu_custom_call" | custom-call | flops 131072 | bytes 131072 | tf_op jit(solution)/shard_map/pallas_call | solution.py:180
  94.4 4.2 %shard_map.51 = (f32[512,512]{1,0:T(8,128)S(1)}, bf16[512,512]{1,0:T(8,128)(2,1)S(1)}) custom-call(s32[3]{0:T(128)S(1)} %pad_add_fusion.spot, bf16[512,2048]{1,0:T(8,128)(2,1)} %copy-done, bf16[512,1280]{1,0:T(8,128)(2,1)} %copy-done.32, bf16[512,768]{1,0:T(8,128)(2,1)S(1)} %get-tuple-element.46.far_lent, bf16[256,2048]{1,0:T(8,128)(2,1)S(1)} %get-tuple-element.45.first, ...), custom_call_target="tpu_custom_call" | custom-call | flops 131072 | bytes 131072 | tf_op jit(solution)/shard_map/pallas_call | solution.py:180
  99.2 5.3 %collective-permute-done.16.refs_1_.first_stay = bf16[256,1280]{1,0:T(8,128)(2,1)S(1)} collective-permute-done((bf16[256,1280]{1,0:T(8,128)(2,1)}, bf16[256,1280]{1,0:T(8,128)(2,1)S(1)}, u32[]{:S(2)}, u32[]{:S(2)}) %collective-permute-start.16) | collective-permute-done | bytes 655392 | tf_op jit(solution)/shard_map/ppermute | solution.py:252
  105.2 4.0 %shard_map.52 = (f32[512,512]{1,0:T(8,128)S(1)}, bf16[512,512]{1,0:T(8,128)(2,1)S(1)}) custom-call(s32[3]{0:T(128)S(1)} %pad_add_fusion.spot, bf16[512,2048]{1,0:T(8,128)(2,1)} %copy-done, bf16[512,1280]{1,0:T(8,128)(2,1)} %copy-done.32, bf16[512,768]{1,0:T(8,128)(2,1)S(1)} %get-tuple-element.46.far_lent, bf16[256,2048]{1,0:T(8,128)(2,1)S(1)} %get-tuple-element.47.first, ...), custom_call_target="tpu_custom_call" | custom-call | flops 131072 | bytes 131072 | tf_op jit(solution)/shard_map/pallas_call | solution.py:180
  109.3 1.5 shard_map.53
  110.8 1.5 collective-permute-start.27
  112.3 1.1 add_convert_fusion.10
  113.5 1.6 collective-permute-start.18
  115.0 1.0 add_convert_fusion.11
  116.7 1.6 collective-permute-start.26
  118.3 1.0 slice.162
  119.3 1.4 collective-permute-start.31
  120.7 7.6 %collective-permute-done.13.refs_1_ = bf16[256,512]{1,0:T(8,128)(2,1)S(1)} collective-permute-done((bf16[256,512]{1,0:T(8,128)(2,1)S(1)}, bf16[256,512]{1,0:T(8,128)(2,1)S(1)}, u32[]{:S(2)}, u32[]{:S(2)}) %collective-permute-start.13) | collective-permute-done | bytes 262176 | tf_op jit(solution)/shard_map/ppermute | solution.py:219
  129.0 1.4 shard_map.55
  130.4 2.8 %collective-permute-done.26.refs_1_ = bf16[256,512]{1,0:T(8,128)(2,1)S(1)} collective-permute-done((bf16[256,512]{1,0:T(8,128)(2,1)S(1)}, bf16[256,512]{1,0:T(8,128)(2,1)S(1)}, u32[]{:S(2)}, u32[]{:S(2)}) %collective-permute-start.26) | collective-permute-done | bytes 262176 | tf_op jit(solution)/shard_map/ppermute | solution.py:219
  133.2 1.4 shard_map.56
  134.6 1.0 copy-done.14
  135.5 1.5 collective-permute-start.34
  137.0 1.7 add_convert_fusion.4
  138.7 1.4 collective-permute-start.28
  140.1 1.5 collective-permute-start.19
  142.2 1.1 add_convert_fusion.3
  143.4 1.4 collective-permute-start.29
  144.8 1.1 collective-permute-done.31.second_stay
  145.9 4.0 %shard_map.57 = (f32[512,512]{1,0:T(8,128)S(1)}, bf16[512,512]{1,0:T(8,128)(2,1)S(1)}) custom-call(s32[3]{0:T(128)S(1)} %pad_add_fusion.spot, bf16[512,2048]{1,0:T(8,128)(2,1)} %copy-done, bf16[512,1280]{1,0:T(8,128)(2,1)} %copy-done.32, bf16[512,768]{1,0:T(8,128)(2,1)S(1)} %get-tuple-element.46.far_lent, bf16[256,2048]{1,0:T(8,128)(2,1)S(1)} %copy-done.5, ...), custom_call_target="tpu_custom_call" | custom-call | flops 131072 | bytes 131072 | tf_op jit(solution)/shard_map/pallas_call | solution.py:180
  150.0 1.1 add_convert_fusion.1
  151.8 1.0 add_convert_fusion.9
  154.4 1.6 collective-permute-start.33
  156.0 1.1 add_convert_fusion.8
  157.1 1.4 collective-permute-start.21
  158.5 1.1 add_convert_fusion
  159.6 1.3 collective-permute-start.36
  161.0 1.4 collective-permute-start.24
  162.5 28.5 %collective-permute-done.21 = bf16[256,512]{1,0:T(8,128)(2,1)S(1)} collective-permute-done((bf16[256,512]{1,0:T(8,128)(2,1)S(1)}, bf16[256,512]{1,0:T(8,128)(2,1)S(1)}, u32[]{:S(2)}, u32[]{:S(2)}) %collective-permute-start.21) | collective-permute-done | bytes 262176 | tf_op jit(solution)/shard_map/ppermute | solution.py:252
  191.3 1.2 add_dynamic-update-slice_fusion.3
  192.5 8.1 %collective-permute-done.24 = bf16[256,512]{1,0:T(8,128)(2,1)S(1)} collective-permute-done((bf16[256,512]{1,0:T(8,128)(2,1)S(1)}, bf16[256,512]{1,0:T(8,128)(2,1)S(1)}, u32[]{:S(2)}, u32[]{:S(2)}) %collective-permute-start.24) | collective-permute-done | bytes 262176 | tf_op jit(solution)/shard_map/ppermute | solution.py:252
  200.7 1.1 add_dynamic-update-slice_fusion.2
  202.0 1.3 copy-done.33
  203.2 0.9 add_dynamic-update-slice_fusion
  (117 shorter events, 7.8 us)
Async XLA Ops:
  0.1 1.6 copy-start.11
  1.7 9.9 %copy-start.31 = (s32[512,128]{1,0:T(8,128)S(1)}, s32[512,128]{1,0:T(8,128)}, u32[]{:S(2)}) copy-start(s32[512,128]{1,0:T(8,128)} %mask.1) | copy-start | bytes 786436
  3.0 27.3 %collective-permute-start = (bf16[256,2048]{1,0:T(8,128)(2,1)S(1)}, bf16[256,2048]{1,0:T(8,128)(2,1)S(1)}, u32[]{:S(2)}, u32[]{:S(2)}) collective-permute-start(bf16[256,2048]{1,0:T(8,128)(2,1)S(1)} %get-tuple-element.38.first.first_stay), channel_id=1, source_target_pairs={{0,4},{2,6},{12,8},{14,10},{1,5},{3,7},{13,9},{15,11},{16,20},{18,... | collective-permute-start | bytes 3145736 | tf_op jit(solution)/shard_map/ppermute | solution.py:252
  8.0 22.3 %collective-permute-start.1 = (bf16[256,2048]{1,0:T(8,128)(2,1)S(1)}, bf16[256,2048]{1,0:T(8,128)(2,1)S(1)}, u32[]{:S(2)}, u32[]{:S(2)}) collective-permute-start(bf16[256,2048]{1,0:T(8,128)(2,1)S(1)} %get-tuple-element.38.first.first_stay), channel_id=1, source_target_pairs={{4,8},{6,10},{8,4},{10,6},{5,9},{7,11},{9,5},{11,7},{20,24},{22,26... | collective-permute-start | bytes 3145736 | tf_op jit(solution)/shard_map/ppermute | solution.py:252
  8.7 24.7 %collective-permute-start.2 = (bf16[256,2048]{1,0:T(8,128)(2,1)S(1)}, bf16[256,2048]{1,0:T(8,128)(2,1)S(1)}, u32[]{:S(2)}, u32[]{:S(2)}) collective-permute-start(bf16[256,2048]{1,0:T(8,128)(2,1)S(1)} %get-tuple-element.39), channel_id=1, source_target_pairs={{0,2},{2,0},{4,6},{6,4},{8,10},{10,8},{12,14},{14,12},{1,3},{3,1},... | collective-permute-start | bytes 3145736 | tf_op jit(solution)/shard_map/ppermute | solution.py:211
  10.3 17.8 %collective-permute-start.3 = (bf16[256,1280]{1,0:T(8,128)(2,1)S(1)}, bf16[256,1280]{1,0:T(8,128)(2,1)S(1)}, u32[]{:S(2)}, u32[]{:S(2)}) collective-permute-start(bf16[256,1280]{1,0:T(8,128)(2,1)S(1)} %get-tuple-element.40), channel_id=1, source_target_pairs={{4,0},{6,2},{8,12},{10,14},{5,1},{7,3},{9,13},{11,15},{20,16},{22,... | collective-permute-start | bytes 1966088 | tf_op jit(solution)/shard_map/ppermute | solution.py:252
  28.1 5.3 %copy-start.9 = (bf16[256,1280]{1,0:T(8,128)(2,1)}, bf16[256,1280]{1,0:T(8,128)(2,1)S(1)}, u32[]{:S(2)}) copy-start(bf16[256,1280]{1,0:T(8,128)(2,1)S(1)} %collective-permute-done.3.refs_5_.first_stay) | copy-start | bytes 1966084
  33.4 57.4 %copy-start.1 = (bf16[256,2048]{1,0:T(8,128)(2,1)}, bf16[256,2048]{1,0:T(8,128)(2,1)S(1)}, u32[]{:S(2)}) copy-start(bf16[256,2048]{1,0:T(8,128)(2,1)S(1)} %get-tuple-element.44.second.second_stay) | copy-start | bytes 3145732
  33.5 17.2 %collective-permute-start.8 = (bf16[256,1280]{1,0:T(8,128)(2,1)S(1)}, bf16[256,1280]{1,0:T(8,128)(2,1)S(1)}, u32[]{:S(2)}, u32[]{:S(2)}) collective-permute-start(bf16[256,1280]{1,0:T(8,128)(2,1)S(1)} %slice.111), channel_id=1, source_target_pairs={{4,0},{6,2},{8,12},{10,14},{5,1},{7,3},{9,13},{11,15},{20,16},{22,... | collective-permute-start | bytes 1966088 | tf_op jit(solution)/shard_map/ppermute | solution.py:252
  34.8 16.7 %collective-permute-start.7 = (bf16[256,2048]{1,0:T(8,128)(2,1)S(1)}, bf16[256,2048]{1,0:T(8,128)(2,1)S(1)}, u32[]{:S(2)}, u32[]{:S(2)}) collective-permute-start(bf16[256,2048]{1,0:T(8,128)(2,1)S(1)} %get-tuple-element.44.second.second_stay), channel_id=1, source_target_pairs={{4,8},{6,10},{8,4},{10,6},{5,9},{7,11},{9,5},{11,7},{20,24},{22,26... | collective-permute-start | bytes 3145736 | tf_op jit(solution)/shard_map/ppermute | solution.py:252
  35.5 20.5 %collective-permute-start.5 = (bf16[512,768]{1,0:T(8,128)(2,1)S(1)}, bf16[512,768]{1,0:T(8,128)(2,1)S(1)}, u32[]{:S(2)}, u32[]{:S(2)}) collective-permute-start(bf16[512,768]{1,0:T(8,128)(2,1)S(1)} %get-tuple-element.43), channel_id=1, source_target_pairs={{0,2},{2,0},{4,6},{6,4},{8,10},{10,8},{12,14},{14,12},{1,3},{3,1},... | collective-permute-start | bytes 2359304 | tf_op jit(solution)/shard_map/ppermute | solution.py:219
  37.1 27.7 %collective-permute-start.6 = (bf16[256,2048]{1,0:T(8,128)(2,1)S(1)}, bf16[256,2048]{1,0:T(8,128)(2,1)S(1)}, u32[]{:S(2)}, u32[]{:S(2)}) collective-permute-start(bf16[256,2048]{1,0:T(8,128)(2,1)S(1)} %get-tuple-element.44.second.second_stay), channel_id=1, source_target_pairs={{0,4},{2,6},{12,8},{14,10},{1,5},{3,7},{13,9},{15,11},{16,20},{18,... | collective-permute-start | bytes 3145736 | tf_op jit(solution)/shard_map/ppermute | solution.py:252
  44.5 44.9 %collective-permute-start.4 = (bf16[512,1280]{1,0:T(8,128)(2,1)S(1)}, bf16[512,1280]{1,0:T(8,128)(2,1)S(1)}, u32[]{:S(2)}, u32[]{:S(2)}) collective-permute-start(bf16[512,1280]{1,0:T(8,128)(2,1)S(1)} %get-tuple-element.41), channel_id=1, source_target_pairs={{0,2},{2,0},{4,6},{6,4},{8,10},{10,8},{12,14},{14,12},{1,3},{3,1},... | collective-permute-start | bytes 3932168 | tf_op jit(solution)/shard_map/ppermute | solution.py:219
  50.6 19.5 %collective-permute-start.9 = (bf16[256,2048]{1,0:T(8,128)(2,1)S(1)}, bf16[256,2048]{1,0:T(8,128)(2,1)S(1)}, u32[]{:S(2)}, u32[]{:S(2)}) collective-permute-start(bf16[256,2048]{1,0:T(8,128)(2,1)S(1)} %get-tuple-element.47.first), channel_id=1, source_target_pairs={{4,8},{6,10},{8,4},{10,6},{5,9},{7,11},{9,5},{11,7},{20,24},{22,26... | collective-permute-start | bytes 3145736 | tf_op jit(solution)/shard_map/ppermute | solution.py:252
  51.4 13.4 %copy-start.2 = (bf16[256,2048]{1,0:T(8,128)(2,1)}, bf16[256,2048]{1,0:T(8,128)(2,1)S(1)}, u32[]{:S(2)}) copy-start(bf16[256,2048]{1,0:T(8,128)(2,1)S(1)} %collective-permute-done.7.refs_3_.second) | copy-start | bytes 3145732
  51.4 36.6 %collective-permute-start.10 = (bf16[256,1280]{1,0:T(8,128)(2,1)S(1)}, bf16[256,1280]{1,0:T(8,128)(2,1)S(1)}, u32[]{:S(2)}, u32[]{:S(2)}) collective-permute-start(bf16[256,1280]{1,0:T(8,128)(2,1)S(1)} %slice.112), channel_id=1, source_target_pairs={{4,0},{6,2},{8,12},{10,14},{5,1},{7,3},{9,13},{11,15},{20,16},{22,... | collective-permute-start | bytes 1966088 | tf_op jit(solution)/shard_map/ppermute | solution.py:252
  56.0 34.8 %collective-permute-start.11 = (bf16[256,1280]{1,0:T(8,128)(2,1)S(1)}, bf16[256,1280]{1,0:T(8,128)(2,1)S(1)}, u32[]{:S(2)}, u32[]{:S(2)}) collective-permute-start(bf16[256,1280]{1,0:T(8,128)(2,1)S(1)} %slice.148), channel_id=1, source_target_pairs={{4,0},{6,2},{8,12},{10,14},{5,1},{7,3},{9,13},{11,15},{20,16},{22,... | collective-permute-start | bytes 1966088 | tf_op jit(solution)/shard_map/ppermute | solution.py:252
  64.8 39.7 %copy-start.6 = (bf16[256,2048]{1,0:T(8,128)(2,1)}, bf16[256,2048]{1,0:T(8,128)(2,1)S(1)}, u32[]{:S(2)}) copy-start(bf16[256,2048]{1,0:T(8,128)(2,1)S(1)} %collective-permute-done.6.refs_2_.second) | copy-start | bytes 3145732
  64.8 44.4 %collective-permute-start.14 = (bf16[512,768]{1,0:T(8,128)(2,1)S(1)}, bf16[512,768]{1,0:T(8,128)(2,1)S(1)}, u32[]{:S(2)}, u32[]{:S(2)}) collective-permute-start(bf16[512,768]{1,0:T(8,128)(2,1)S(1)} %get-tuple-element.50), channel_id=1, source_target_pairs={{0,4},{2,6},{12,8},{14,10},{1,5},{3,7},{13,9},{15,11},{16,20},{18,... | collective-permute-start | bytes 2359304 | tf_op jit(solution)/shard_map/ppermute | solution.py:252
  70.2 20.6 %copy-start.4 = (bf16[256,2048]{1,0:T(8,128)(2,1)}, bf16[256,2048]{1,0:T(8,128)(2,1)S(1)}, u32[]{:S(2)}) copy-start(bf16[256,2048]{1,0:T(8,128)(2,1)S(1)} %collective-permute-done.9.refs_0_.first) | copy-start | bytes 3145732
  70.2 39.1 %collective-permute-start.15 = (bf16[512,768]{1,0:T(8,128)(2,1)S(1)}, bf16[512,768]{1,0:T(8,128)(2,1)S(1)}, u32[]{:S(2)}, u32[]{:S(2)}) collective-permute-start(bf16[512,768]{1,0:T(8,128)(2,1)S(1)} %get-tuple-element.46.far_lent), channel_id=1, source_target_pairs={{0,4},{2,6},{12,8},{14,10},{1,5},{3,7},{13,9},{15,11},{16,20},{18,... | collective-permute-start | bytes 2359304 | tf_op jit(solution)/shard_map/ppermute | solution.py:252
  88.1 16.4 %collective-permute-start.16 = (bf16[256,1280]{1,0:T(8,128)(2,1)}, bf16[256,1280]{1,0:T(8,128)(2,1)S(1)}, u32[]{:S(2)}, u32[]{:S(2)}) collective-permute-start(bf16[256,1280]{1,0:T(8,128)(2,1)} %slice.151), channel_id=1, source_target_pairs={{4,0},{6,2},{8,12},{10,14},{5,1},{7,3},{9,13},{11,15},{20,16},{22,... | collective-permute-start | bytes 1966088 | tf_op jit(solution)/shard_map/ppermute | solution.py:252
  94.4 20.7 %copy-start.26 = (f32[512,512]{1,0:T(8,128)}, f32[512,512]{1,0:T(8,128)S(1)}, u32[]{:S(2)}) copy-start(f32[512,512]{1,0:T(8,128)S(1)} %get-tuple-element.48) | copy-start | bytes 3145732
  94.4 10.8 %copy-start.10 = (bf16[256,1280]{1,0:T(8,128)(2,1)S(1)}, bf16[256,1280]{1,0:T(8,128)(2,1)}, u32[]{:S(2)}) copy-start(bf16[256,1280]{1,0:T(8,128)(2,1)} %copy-done.9) | copy-start | bytes 1966084
  98.6 13.7 %copy-start.24 = (f32[512,512]{1,0:T(8,128)}, f32[512,512]{1,0:T(8,128)S(1)}, u32[]{:S(2)}) copy-start(f32[512,512]{1,0:T(8,128)S(1)} %get-tuple-element.55) | copy-start | bytes 3145732
  98.6 13.7 %collective-permute-start.17 = (bf16[512,512]{1,0:T(8,128)(2,1)S(1)}, bf16[512,512]{1,0:T(8,128)(2,1)}, u32[]{:S(2)}, u32[]{:S(2)}) collective-permute-start(bf16[512,512]{1,0:T(8,128)(2,1)S(1)} %get-tuple-element.51.refs_0_), channel_id=1, source_target_pairs={{0,1},{1,0},{2,3},{3,2},{4,5},{5,4},{6,7},{7,6},{8,9},{9,8},{10,11... | collective-permute-start | bytes 1572872 | tf_op jit(solution)/shard_map/ppermute | solution.py:222
  98.7 16.4 %collective-permute-start.12 = (bf16[512,512]{1,0:T(8,128)(2,1)S(1)}, bf16[512,512]{1,0:T(8,128)(2,1)}, u32[]{:S(2)}, u32[]{:S(2)}) collective-permute-start(bf16[512,512]{1,0:T(8,128)(2,1)S(1)} %get-tuple-element.49.refs_0_), channel_id=1, source_target_pairs={{0,1},{1,0},{2,3},{3,2},{4,5},{5,4},{6,7},{7,6},{8,9},{9,8},{10,11... | collective-permute-start | bytes 1572872 | tf_op jit(solution)/shard_map/ppermute | solution.py:222
  104.5 13.8 %collective-permute-start.30 = (bf16[256,2048]{1,0:T(8,128)(2,1)S(1)}, bf16[256,2048]{1,0:T(8,128)(2,1)S(1)}, u32[]{:S(2)}, u32[]{:S(2)}) collective-permute-start(bf16[256,2048]{1,0:T(8,128)(2,1)S(1)} %collective-permute-done.6.refs_2_.second), channel_id=1, source_target_pairs={{4,8},{6,10},{8,4},{10,6},{5,9},{7,11},{9,5},{11,7},{20,24},{22,26... | collective-permute-start | bytes 3145736 | tf_op jit(solution)/shard_map/ppermute | solution.py:252
  109.2 7.4 %copy-start.28 = (f32[512,512]{1,0:T(8,128)}, f32[512,512]{1,0:T(8,128)S(1)}, u32[]{:S(2)}) copy-start(f32[512,512]{1,0:T(8,128)S(1)} %get-tuple-element.59) | copy-start | bytes 3145732
  109.2 7.4 %collective-permute-start.25 = (bf16[512,512]{1,0:T(8,128)(2,1)S(1)}, bf16[512,512]{1,0:T(8,128)(2,1)S(1)}, u32[]{:S(2)}, u32[]{:S(2)}) collective-permute-start(bf16[512,512]{1,0:T(8,128)(2,1)S(1)} %get-tuple-element.52.refs_0_), channel_id=1, source_target_pairs={{0,1},{1,0},{2,3},{3,2},{4,5},{5,4},{6,7},{7,6},{8,9},{9,8},{10,11... | collective-permute-start | bytes 1572872 | tf_op jit(solution)/shard_map/ppermute | solution.py:222
  110.8 26.1 %collective-permute-start.27 = (bf16[512,512]{1,0:T(8,128)(2,1)S(1)}, bf16[512,512]{1,0:T(8,128)(2,1)}, u32[]{:S(2)}, u32[]{:S(2)}) collective-permute-start(bf16[512,512]{1,0:T(8,128)(2,1)S(1)} %get-tuple-element.53.refs_0_), channel_id=1, source_target_pairs={{4,5},{5,4},{6,7},{7,6},{8,9},{9,8},{10,11},{11,10},{20,21},{21,20... | collective-permute-start | bytes 1572872 | tf_op jit(solution)/shard_map/ppermute | solution.py:301
  112.3 15.9 %copy-start.3 = (bf16[256,2048]{1,0:T(8,128)(2,1)S(1)}, bf16[256,2048]{1,0:T(8,128)(2,1)}, u32[]{:S(2)}) copy-start(bf16[256,2048]{1,0:T(8,128)(2,1)} %copy-done.2) | copy-start | bytes 3145732
  113.5 15.5 %collective-permute-start.18 = (bf16[256,512]{1,0:T(8,128)(2,1)S(1)}, bf16[256,512]{1,0:T(8,128)(2,1)S(1)}, u32[]{:S(2)}, u32[]{:S(2)}) collective-permute-start(bf16[256,512]{1,0:T(8,128)(2,1)S(1)} %add_convert_fusion.10), channel_id=1, source_target_pairs={{0,2},{2,0},{4,6},{6,4},{8,10},{10,8},{12,14},{14,12},{1,3},{3,1},... | collective-permute-start | bytes 786440 | tf_op jit(solution)/shard_map/ppermute | solution.py:219
  116.1 12.2 %collective-permute-start.13 = (bf16[256,512]{1,0:T(8,128)(2,1)S(1)}, bf16[256,512]{1,0:T(8,128)(2,1)S(1)}, u32[]{:S(2)}, u32[]{:S(2)}) collective-permute-start(bf16[256,512]{1,0:T(8,128)(2,1)S(1)} %add_convert_fusion.11), channel_id=1, source_target_pairs={{0,2},{2,0},{4,6},{6,4},{8,10},{10,8},{12,14},{14,12},{1,3},{3,1},... | collective-permute-start | bytes 786440 | tf_op jit(solution)/shard_map/ppermute | solution.py:219
  116.6 4.1 %copy-start.34 = (bf16[512,512]{1,0:T(8,128)(2,1)}, bf16[512,512]{1,0:T(8,128)(2,1)S(1)}, u32[]{:S(2)}) copy-start(bf16[512,512]{1,0:T(8,128)(2,1)S(1)} %collective-permute-done.25) | copy-start | bytes 1572868
  116.7 16.5 %collective-permute-start.26 = (bf16[256,512]{1,0:T(8,128)(2,1)S(1)}, bf16[256,512]{1,0:T(8,128)(2,1)S(1)}, u32[]{:S(2)}, u32[]{:S(2)}) collective-permute-start(bf16[256,512]{1,0:T(8,128)(2,1)S(1)} %add_convert_fusion.5), channel_id=1, source_target_pairs={{0,2},{2,0},{4,6},{6,4},{8,10},{10,8},{12,14},{14,12},{1,3},{3,1},... | collective-permute-start | bytes 786440 | tf_op jit(solution)/shard_map/ppermute | solution.py:219
  118.3 14.9 %copy-start.8 = (bf16[256,2048]{1,0:T(8,128)(2,1)}, bf16[256,2048]{1,0:T(8,128)(2,1)S(1)}, u32[]{:S(2)}) copy-start(bf16[256,2048]{1,0:T(8,128)(2,1)S(1)} %collective-permute-done.30.second) | copy-start | bytes 3145732
  119.3 9.7 %copy-start.7 = (bf16[256,2048]{1,0:T(8,128)(2,1)S(1)}, bf16[256,2048]{1,0:T(8,128)(2,1)}, u32[]{:S(2)}) copy-start(bf16[256,2048]{1,0:T(8,128)(2,1)} %copy-done.6) | copy-start | bytes 3145732
  119.3 26.6 %collective-permute-start.31 = (bf16[256,1280]{1,0:T(8,128)(2,1)}, bf16[256,1280]{1,0:T(8,128)(2,1)}, u32[]{:S(2)}, u32[]{:S(2)}) collective-permute-start(bf16[256,1280]{1,0:T(8,128)(2,1)} %slice.162), channel_id=1, source_target_pairs={{4,0},{6,2},{8,12},{10,14},{5,1},{7,3},{9,13},{11,15},{20,16},{22,... | collective-permute-start | bytes 1966088 | tf_op jit(solution)/shard_map/ppermute | solution.py:252
  129.0 4.2 %copy-start.5 = (bf16[256,2048]{1,0:T(8,128)(2,1)S(1)}, bf16[256,2048]{1,0:T(8,128)(2,1)}, u32[]{:S(2)}) copy-start(bf16[256,2048]{1,0:T(8,128)(2,1)} %copy-done.4) | copy-start | bytes 3145732
  130.4 4.2 %copy-start.16 = (f32[512,512]{1,0:T(8,128)}, f32[512,512]{1,0:T(8,128)S(1)}, u32[]{:S(2)}) copy-start(f32[512,512]{1,0:T(8,128)S(1)} %get-tuple-element.56) | copy-start | bytes 3145732
  135.5 14.5 %collective-permute-start.34 = (bf16[512,512]{1,0:T(8,128)(2,1)}, bf16[512,512]{1,0:T(8,128)(2,1)}, u32[]{:S(2)}, u32[]{:S(2)}) collective-permute-start(bf16[512,512]{1,0:T(8,128)(2,1)} %get-tuple-element.61.refs_0_), channel_id=1, source_target_pairs={{4,5},{5,4},{6,7},{7,6},{8,9},{9,8},{10,11},{11,10},{20,21},{21,20... | collective-permute-start | bytes 1572872 | tf_op jit(solution)/shard_map/ppermute | solution.py:301
  138.7 3.5 %collective-permute-start.28 = (bf16[256,512]{1,0:T(8,128)(2,1)}, bf16[256,512]{1,0:T(8,128)(2,1)}, u32[]{:S(2)}, u32[]{:S(2)}) collective-permute-start(bf16[256,512]{1,0:T(8,128)(2,1)} %add_convert_fusion.4), channel_id=1, source_target_pairs={{4,6},{6,4},{8,10},{10,8},{5,7},{7,5},{9,11},{11,9},{20,22},{22,20... | collective-permute-start | bytes 786440 | tf_op jit(solution)/shard_map/ppermute | solution.py:252
  140.1 11.8 %collective-permute-start.19 = (bf16[512,512]{1,0:T(8,128)(2,1)}, bf16[512,512]{1,0:T(8,128)(2,1)}, u32[]{:S(2)}, u32[]{:S(2)}) collective-permute-start(bf16[512,512]{1,0:T(8,128)(2,1)} %get-tuple-element.57.refs_0_), channel_id=1, source_target_pairs={{4,5},{5,4},{6,7},{7,6},{8,9},{9,8},{10,11},{11,10},{20,21},{21,20... | collective-permute-start | bytes 1572872 | tf_op jit(solution)/shard_map/ppermute | solution.py:301
  141.5 12.0 %collective-permute-start.22 = (bf16[512,512]{1,0:T(8,128)(2,1)}, bf16[512,512]{1,0:T(8,128)(2,1)S(1)}, u32[]{:S(2)}, u32[]{:S(2)}) collective-permute-start(bf16[512,512]{1,0:T(8,128)(2,1)} %copy-done.30), channel_id=1, source_target_pairs={{4,5},{5,4},{6,7},{7,6},{8,9},{9,8},{10,11},{11,10},{20,21},{21,20... | collective-permute-start | bytes 1572872 | tf_op jit(solution)/shard_map/ppermute | solution.py:301
  143.4 6.7 %copy-start.15 = (f32[512,512]{1,0:T(8,128)S(1)}, f32[512,512]{1,0:T(8,128)}, u32[]{:S(2)}) copy-start(f32[512,512]{1,0:T(8,128)} %copy-done.14) | copy-start | bytes 3145732
  143.4 8.5 %copy-start.17 = (f32[512,512]{1,0:T(8,128)S(1)}, f32[512,512]{1,0:T(8,128)}, u32[]{:S(2)}) copy-start(f32[512,512]{1,0:T(8,128)} %copy-done.16) | copy-start | bytes 3145732
  143.4 58.4 %collective-permute-start.29 = (bf16[256,512]{1,0:T(8,128)(2,1)S(1)}, bf16[256,512]{1,0:T(8,128)(2,1)S(1)}, u32[]{:S(2)}, u32[]{:S(2)}) collective-permute-start(bf16[256,512]{1,0:T(8,128)(2,1)S(1)} %add_convert_fusion.3), channel_id=1, source_target_pairs={{4,0},{6,2},{8,12},{10,14},{5,1},{7,3},{9,13},{11,15},{20,16},{22,... | collective-permute-start | bytes 786440 | tf_op jit(solution)/shard_map/ppermute | solution.py:252
  149.9 3.6 %copy-start.13 = (f32[512,512]{1,0:T(8,128)S(1)}, f32[512,512]{1,0:T(8,128)}, u32[]{:S(2)}) copy-start(f32[512,512]{1,0:T(8,128)} %copy-done.12) | copy-start | bytes 3145732
  149.9 4.4 %collective-permute-start.32 = (bf16[512,512]{1,0:T(8,128)(2,1)S(1)}, bf16[512,512]{1,0:T(8,128)(2,1)S(1)}, u32[]{:S(2)}, u32[]{:S(2)}) collective-permute-start(bf16[512,512]{1,0:T(8,128)(2,1)S(1)} %get-tuple-element.63), channel_id=1, source_target_pairs={{0,1},{1,0},{2,3},{3,2},{4,5},{5,4},{6,7},{7,6},{8,9},{9,8},{10,11... | collective-permute-start | bytes 1572872 | tf_op jit(solution)/shard_map/ppermute | solution.py:222
  151.1 7.4 %collective-permute-start.35 = (bf16[256,512]{1,0:T(8,128)(2,1)S(1)}, bf16[256,512]{1,0:T(8,128)(2,1)S(1)}, u32[]{:S(2)}, u32[]{:S(2)}) collective-permute-start(bf16[256,512]{1,0:T(8,128)(2,1)S(1)} %add_convert_fusion.1), channel_id=1, source_target_pairs={{4,6},{6,4},{8,10},{10,8},{5,7},{7,5},{9,11},{11,9},{20,22},{22,20... | collective-permute-start | bytes 786440 | tf_op jit(solution)/shard_map/ppermute | solution.py:252
  152.9 3.1 %collective-permute-start.20 = (bf16[256,512]{1,0:T(8,128)(2,1)S(1)}, bf16[256,512]{1,0:T(8,128)(2,1)S(1)}, u32[]{:S(2)}, u32[]{:S(2)}) collective-permute-start(bf16[256,512]{1,0:T(8,128)(2,1)S(1)} %add_convert_fusion.9), channel_id=1, source_target_pairs={{4,6},{6,4},{8,10},{10,8},{5,7},{7,5},{9,11},{11,9},{20,22},{22,20... | collective-permute-start | bytes 786440 | tf_op jit(solution)/shard_map/ppermute | solution.py:252
  153.6 7.2 %collective-permute-start.23 = (bf16[256,512]{1,0:T(8,128)(2,1)S(1)}, bf16[256,512]{1,0:T(8,128)(2,1)S(1)}, u32[]{:S(2)}, u32[]{:S(2)}) collective-permute-start(bf16[256,512]{1,0:T(8,128)(2,1)S(1)} %add_convert_fusion.7), channel_id=1, source_target_pairs={{4,6},{6,4},{8,10},{10,8},{5,7},{7,5},{9,11},{11,9},{20,22},{22,20... | collective-permute-start | bytes 786440 | tf_op jit(solution)/shard_map/ppermute | solution.py:252
  154.4 47.5 %collective-permute-start.33 = (bf16[256,512]{1,0:T(8,128)(2,1)S(1)}, bf16[256,512]{1,0:T(8,128)(2,1)S(1)}, u32[]{:S(2)}, u32[]{:S(2)}) collective-permute-start(bf16[256,512]{1,0:T(8,128)(2,1)S(1)} %add_convert_fusion.2), channel_id=1, source_target_pairs={{0,2},{2,0},{4,6},{6,4},{8,10},{10,8},{12,14},{14,12},{1,3},{3,1},... | collective-permute-start | bytes 786440 | tf_op jit(solution)/shard_map/ppermute | solution.py:219
  157.1 34.2 %copy-start.23 = (bf16[256,512]{1,0:T(8,128)(2,1)S(1)}, bf16[256,512]{1,0:T(8,128)(2,1)}, u32[]{:S(2)}) copy-start(bf16[256,512]{1,0:T(8,128)(2,1)} %copy-done.22) | copy-start | bytes 786436
  157.1 34.2 %copy-start.27 = (f32[512,512]{1,0:T(8,128)S(1)}, f32[512,512]{1,0:T(8,128)}, u32[]{:S(2)}) copy-start(f32[512,512]{1,0:T(8,128)} %copy-done.26) | copy-start | bytes 3145732
  157.1 33.9 %collective-permute-start.21 = (bf16[256,512]{1,0:T(8,128)(2,1)S(1)}, bf16[256,512]{1,0:T(8,128)(2,1)S(1)}, u32[]{:S(2)}, u32[]{:S(2)}) collective-permute-start(bf16[256,512]{1,0:T(8,128)(2,1)S(1)} %add_convert_fusion.8), channel_id=1, source_target_pairs={{4,0},{6,2},{8,12},{10,14},{5,1},{7,3},{9,13},{11,15},{20,16},{22,... | collective-permute-start | bytes 786440 | tf_op jit(solution)/shard_map/ppermute | solution.py:252
  159.6 42.4 %collective-permute-start.36 = (bf16[256,512]{1,0:T(8,128)(2,1)S(1)}, bf16[256,512]{1,0:T(8,128)(2,1)S(1)}, u32[]{:S(2)}, u32[]{:S(2)}) collective-permute-start(bf16[256,512]{1,0:T(8,128)(2,1)S(1)} %add_convert_fusion), channel_id=1, source_target_pairs={{4,0},{6,2},{8,12},{10,14},{5,1},{7,3},{9,13},{11,15},{20,16},{22,... | collective-permute-start | bytes 786440 | tf_op jit(solution)/shard_map/ppermute | solution.py:252
  161.0 39.6 %copy-start.19 = (bf16[256,512]{1,0:T(8,128)(2,1)S(1)}, bf16[256,512]{1,0:T(8,128)(2,1)}, u32[]{:S(2)}) copy-start(bf16[256,512]{1,0:T(8,128)(2,1)} %copy-done.18) | copy-start | bytes 786436
  161.0 39.6 %copy-start.25 = (f32[512,512]{1,0:T(8,128)S(1)}, f32[512,512]{1,0:T(8,128)}, u32[]{:S(2)}) copy-start(f32[512,512]{1,0:T(8,128)} %copy-done.24) | copy-start | bytes 3145732
  161.0 39.6 %collective-permute-start.24 = (bf16[256,512]{1,0:T(8,128)(2,1)S(1)}, bf16[256,512]{1,0:T(8,128)(2,1)S(1)}, u32[]{:S(2)}, u32[]{:S(2)}) collective-permute-start(bf16[256,512]{1,0:T(8,128)(2,1)S(1)} %add_convert_fusion.6), channel_id=1, source_target_pairs={{4,0},{6,2},{8,12},{10,14},{5,1},{7,3},{9,13},{11,15},{20,16},{22,... | collective-permute-start | bytes 786440 | tf_op jit(solution)/shard_map/ppermute | solution.py:252
  191.3 10.5 %copy-start.21 = (bf16[256,512]{1,0:T(8,128)(2,1)S(1)}, bf16[256,512]{1,0:T(8,128)(2,1)}, u32[]{:S(2)}) copy-start(bf16[256,512]{1,0:T(8,128)(2,1)} %copy-done.20) | copy-start | bytes 786436
  191.3 10.5 %copy-start.29 = (f32[512,512]{1,0:T(8,128)S(1)}, f32[512,512]{1,0:T(8,128)}, u32[]{:S(2)}) copy-start(f32[512,512]{1,0:T(8,128)} %copy-done.28) | copy-start | bytes 3145732
  191.3 10.5 %copy-start.35 = (bf16[512,512]{1,0:T(8,128)(2,1)S(1)}, bf16[512,512]{1,0:T(8,128)(2,1)}, u32[]{:S(2)}) copy-start(bf16[512,512]{1,0:T(8,128)(2,1)} %copy-done.34) | copy-start | bytes 1572868
  (9 other events, 11.3 us)

commit v6 on v3

v6 whole, which is shorter than its diff:
```python
import functools

import jax
import jax.numpy as jnp
from jax import lax
from jax.experimental import pallas as pl
from jax.experimental.pallas import tpu as pltpu
from jax.sharding import PartitionSpec as P

LANES = 128
VMEM_LIMIT = 48 * 1024 * 1024
ANYWHERE = pl.BlockSpec(memory_space=pl.ANY)
SCALARS = pl.BlockSpec(memory_space=pltpu.SMEM)
WHOLE = pl.BlockSpec(memory_space=pltpu.VMEM)
NT = (((1,), (1,)), ((), ()))
bf16, f32 = jnp.bfloat16, jnp.float32
LIMIT = pltpu.CompilerParams(vmem_limit_bytes=VMEM_LIMIT)


def shaped(kind, *shape):
    return jax.ShapeDtypeStruct(shape, kind)


def prepare_body(spot, query_grads, mine, other):
    rank = LANES // 2
    width = query_grads.shape[1]
    for out, side in ((mine, spot[0]), (other, 1 - spot[0])):
        for m in range(width // 4 // LANES):
            at = pl.multiple_of(side * (width // 4) + m * LANES, LANES)
            low = query_grads[:, pl.ds(at, LANES)]
            high = query_grads[:, pl.ds(at + width // 2, LANES)]
            out[:, 2 * m * LANES:(2 * m + 1) * LANES] = jnp.concatenate([low[:, :rank], high[:, :rank]], 1)
            out[:, (2 * m + 1) * LANES:(2 * m + 2) * LANES] = jnp.concatenate([low[:, rank:], high[:, rank:]], 1)


def prepare(query_grads, spot):
    rows, width = query_grads.shape
    return pl.pallas_call(
        prepare_body,
        in_specs=[SCALARS, WHOLE],
        out_specs=[WHOLE] * 2,
        out_shape=[shaped(bf16, rows, width // 2)] * 2,
        compiler_params=LIMIT,
    )(spot, query_grads)


def form_body(rows, rank, spot, inputs, outgrads, mask, kept, sent, rounds):
    for d in range(rows):
        masked = outgrads[d] * mask[d:d + 1, :].astype(bf16)
        product = lax.dot_general(inputs[d], masked, NT, preferred_element_type=f32)
        pairs = jnp.concatenate([product[:rank // 2], product[rank // 2:]], 1)
        rounds[pl.ds(d, rank // 2, stride=rows), :] = pairs
    for out, side in ((kept, spot[0]), (sent, 1 - spot[0])):
        for k in range(rank // 4):
            at = pl.multiple_of((side * (rank // 4) + k) * rows, rows)
            out[:, k * LANES:(k + 1) * LANES] = rounds[pl.ds(at, rows), :].astype(bf16)


def form(doc_inputs, doc_outgrads, token_mask, spot):
    docs, rank, length = doc_inputs.shape
    rows = 64
    steps = docs // rows
    half = rank * rank // 2

    def at(g, spot):
        return lax.rem(g + spot[1] * (steps // 2), steps)

    return pl.pallas_call(
        functools.partial(form_body, rows, rank),
        grid_spec=pltpu.PrefetchScalarGridSpec(
            num_scalar_prefetch=1,
            grid=(steps,),
            in_specs=[
                pl.BlockSpec((rows, rank, length), lambda g, spot: (at(g, spot), 0, 0)),
                pl.BlockSpec((rows, rank, length), lambda g, spot: (at(g, spot), 0, 0)),
                pl.BlockSpec((rows, length), lambda g, spot: (at(g, spot), 0)),
            ],
            out_specs=[pl.BlockSpec((rows, half), lambda g, spot: (g, 0))] * 2,
            scratch_shapes=[pltpu.VMEM((rank // 2 * rows, LANES), f32)],
        ),
        out_shape=[shaped(bf16, docs, half)] * 2,
        compiler_params=LIMIT,
        cost_estimate=pl.CostEstimate(
            flops=40 * docs * rank * rank * length, bytes_accessed=4 * docs * rank * length + 2 * docs * rank * rank, transcendentals=0
        ),
    )(spot, doc_inputs, doc_outgrads, token_mask)


def tie(arrays, *after):
    count = len(arrays)
    return pl.pallas_call(
        lambda *refs: None,
        in_specs=[ANYWHERE] * (count + len(after)),
        out_specs=[ANYWHERE] * count,
        out_shape=[shaped(a.dtype, *a.shape) for a in arrays],
        input_output_aliases={i: i for i in range(count)},
        compiler_params=LIMIT,
    )(*arrays, *after)


def dot(rows, block):
    return lax.dot_general(rows, block, NT, preferred_element_type=f32)


FREE = pl.CostEstimate(flops=1024, bytes_accessed=1024, transcendentals=0)


def score_body(count, spot, own, far, *refs):
    keep, give = refs[-2:]
    part = own.shape[0] // 2
    blocks = refs[:count]
    queries = blocks[0].shape[0]
    slots = (spot[0], 1 - spot[0]) if count == 2 else (0,)
    for block, slot in zip(blocks, slots):
        at = pl.ds(pl.multiple_of(slot * queries, queries), queries) if count == 2 else slice(None)
        keep[:part, at] = dot(own[:part, :], block[...])
        keep[part:, at] = dot(far[:part, :], block[...])
        give[:part, at] = dot(own[part:, :], block[...]).astype(bf16)
        give[part:, at] = dot(far[part:, :], block[...]).astype(bf16)


def score(spot, own, far, blocks, *after):
    docs = own.shape[0]
    count = len(blocks)
    queries = count * blocks[0].shape[0]
    return pl.pallas_call(
        functools.partial(score_body, count),
        in_specs=[SCALARS] + [WHOLE] * (2 + count) + [ANYWHERE] * len(after),
        out_specs=[WHOLE] * 2,
        out_shape=[shaped(f32, docs, queries), shaped(bf16, docs, queries)],
        compiler_params=LIMIT,
        cost_estimate=FREE,
    )(spot, own, far, *blocks, *after)


def last_body(own, far, block, *refs):
    near, mate, across, diagonal = refs[-4:]
    part = near.shape[0]
    mate[...] = dot(own[part:, :], block[...]).astype(bf16)
    across[...] = dot(far[:part, :], block[...]).astype(bf16)
    diagonal[...] = dot(far[part:, :], block[...]).astype(bf16)
    near[...] = dot(own[:part, :], block[...])


def last_score(own, far, block, *after):
    shape = (own.shape[0] // 2, block.shape[0])
    return pl.pallas_call(
        last_body,
        in_specs=[WHOLE] * 3 + [ANYWHERE] * len(after),
        out_specs=[WHOLE] * 4,
        out_shape=[shaped(f32, *shape)] + [shaped(bf16, *shape)] * 3,
        compiler_params=LIMIT,
        cost_estimate=FREE,
    )(own, far, block, *after)


def on_device(doc_inputs, doc_outgrads, token_mask, query_grads):
    blk = lax.axis_size("blk")
    places = blk // 2
    me = lax.axis_index("blk")
    place, side = me // 2, me % 2
    spot = jnp.stack([side, lax.axis_index("proj")]).astype(jnp.int32)
    docs = doc_inputs.shape[0]
    queries = query_grads.shape[0]
    part = docs // 2

    across = [(b, b ^ 1) for b in range(blk)]
    onward = [(b, (b + 2) % blk) for b in range(blk)]
    diagonal = [(2 * b + c, 2 * (b ^ 1) + (c ^ 1)) for b in range(blk) for c in range(2)]

    def swap_across(x):
        return lax.ppermute(x, "blk", across)

    def swap_cores(x):
        return lax.ppermute(x, "proj", [(0, 1), (1, 0)])

    def pass_on(x):
        return lax.ppermute(x, "blk", onward)

    def swap_diagonal(x):
        return lax.ppermute(x, ("blk", "proj"), diagonal)

    mine, sending = prepare(query_grads, spot)
    other = swap_across(sending)
    first = [mine, pass_on(mine)]
    own, sent = form(
        doc_inputs.reshape(docs, *doc_inputs.shape[2:]), doc_outgrads.reshape(docs, *doc_outgrads.shape[2:]), token_mask, spot
    )
    sent, first[1], other = tie((sent, first[1], other))
    second = [other]
    far = swap_across(sent)
    for step in range(2, places):
        first.append(pass_on(first[-1]))
    for step in range(1, places - 1):
        second.append(pass_on(second[-1]))
    pieces = [pass_on(piece) for piece in jnp.split(second[-1], 2, 0)]

    out = jnp.zeros((part, blk * queries), f32)

    def put(out, total, step, at):
        origin = (place - step + places) % places
        return lax.dynamic_update_slice_in_dim(out, total, origin * (2 * queries) + at, 1)

    def over_cores(keep, give):
        got = swap_cores(give).astype(f32)
        return keep[:part] + got[:part], (keep[part:] + got[part:]).astype(bf16)

    besides = []
    last = ()
    for step in range(places - 1):
        if step == places - 2:
            keep, give = score(spot, own, far, (first[-1],), *last)
            final_own, final_far = over_cores(keep, give)
            final_beside = swap_across(final_far)
            last = (give,) + tuple(besides)
        keep, give = score(spot, own, far, (first[step], second[step]), *last)
        total, reach = over_cores(keep, give)
        besides.append(swap_across(reach))
        out = put(out, total + besides[-1].astype(f32), step, 0)
        last = (give,)
    last = (give, final_beside)

    size = queries // 2
    for i, piece in enumerate(pieces):
        near, mate, reach, opposite = last_score(own, far, piece, *last)
        cut = slice(i * size, (i + 1) * size)
        mine_total = final_own[:, cut] + swap_across(reach).astype(f32) + swap_diagonal(opposite).astype(f32)
        other_total = near + swap_cores(mate).astype(f32) + final_beside[:, cut].astype(f32)
        out = put(out, mine_total, places - 1, side * queries + i * size)
        out = put(out, other_total, places - 1, (1 - side) * queries + i * size)
        last = (near, besides[-1])
    return out


def solution(mesh):
    placed = (
        P(("grp", "blk"), "proj", None, None),
        P(("grp", "blk"), "proj", None, None),
        P(("grp", "blk"), None),
        P(("grp", "blk"), "proj"),
    )
    return jax.shard_map(
        on_device,
        mesh=mesh,
        in_specs=placed,
        out_specs=P(("grp", "blk", "proj"), None),
        check_vma=False,
    )
```

time: 184 us -> 167 us (0.908)
  waiting for transfers between devices: 113 us -> 100 us
  Pallas kernels: 44.2 us -> 35 us
  starting transfers between devices: 14.5 us -> 17.6 us
    ppermute x16 -> x23, waiting for transfers between devices: 113 us -> 100 us  [the longest x7 86.2 us: pass_on(): return lax.ppermute(x, 'blk', onward)]
    pallas_call x1, Pallas kernels: 24 us -> 13.4 us  [form(): pl.pallas_call(functools.partial(form_body, rows, rank), grid_spec=pltpu....]
    ppermute x16 -> x23, starting transfers between devices: 14.5 us -> 17.6 us  [the longest x8 8.26 us: swap_across(): return lax.ppermute(x, 'blk', across)]
    pallas_call x5 -> x7, Pallas kernels: 18.9 us -> 20.4 us  [the longest x4 16.9 us: score(): pl.pallas_call(functools.partial(score_body, count), in_specs=[SCALARS] +...]
    unnamed x32 -> x40, local copies, waits for them, and re-layouts: 8.05 us -> 7.81 us
  transfers between devices with their start and end apart: 16 -> 23, of which waited for: 10 -> 11; matrix products, arithmetic and copies ran while one was open for 1% -> 3% of each run, Pallas kernels for 23% -> 20%
where the time goes in v6:
time: 167 us
  waiting for transfers between devices  100 us (60%)
  Pallas kernels  35 us (21%)
  starting transfers between devices  17.6 us (11%)
  local copies, waits for them, and re-layouts  9.14 us (5%)
  other arithmetic  3.78 us (2%)
    ppermute x7, waiting for transfers between devices, pass_on(): return lax.ppermute(x, 'blk', onward)  86.2 us
    pallas_call x4, Pallas kernels, score(): pl.pallas_call(functools.partial(score_body, count), in_specs=[SCALARS] +...  16.9 us
    ppermute x8, waiting for transfers between devices, swap_across(): return lax.ppermute(x, 'blk', across)  14 us
    pallas_call x1, Pallas kernels, form(): pl.pallas_call(functools.partial(form_body, rows, rank), grid_spec=pltpu....  13.4 us
    ppermute x8, starting transfers between devices, swap_across(): return lax.ppermute(x, 'blk', across)  8.26 us
    unnamed x40, local copies, waits for them, and re-layouts  7.81 us
    ppermute x7, starting transfers between devices, pass_on(): return lax.ppermute(x, 'blk', onward)  5.81 us
    ppermute x6, starting transfers between devices, swap_cores(): return lax.ppermute(x, 'proj', [(0, 1), (1, 0)])  3.57 us
  transfers between devices with their start and end apart: 23, of which 11 were waited for; matrix products, arithmetic and copies ran while one was open for 3% of the time, Pallas kernels for 20%

profile of v6, /device:TPU:0, one launch (start us, length us, event | category | flops | bytes accessed | tf_op | source)
XLA Modules:
  0.0 166.5 jit_solution(10974427448729178903)
XLA Ops:
  0.0 0.1 pad_add_fusion.spot
  0.1 1.6 copy-done.5
  1.7 1.3 shard_map.47
  2.9 3.1 %collective-permute-start = (bf16[256,2048]{1,0:T(8,128)(2,1)S(1)}, bf16[256,2048]{1,0:T(8,128)(2,1)S(1)}, u32[]{:S(2)}, u32[]{:S(2)}) collective-permute-start(bf16[256,2048]{1,0:T(8,128)(2,1)S(1)} %get-tuple-element.30.refs_0_), channel_id=1, source_target_pairs={{0,4},{2,6},{4,8},{6,10},{8,12},{10,14},{12,0},{14,2},{1,5},{3,7},... | collective-permute-start | bytes 3145736 | tf_op jit(solution)/shard_map/ppermute | solution.py:178
  6.0 1.5 collective-permute-start.1
  7.5 13.4 %shard_map.46 = (bf16[512,2048]{1,0:T(8,128)(2,1)S(1)}, bf16[512,2048]{1,0:T(8,128)(2,1)S(1)}) custom-call(s32[2]{0:T(128)S(1)} %pad_add_fusion.spot, bf16[512,64,128]{2,1,0:T(8,128)(2,1)} %bitcast.4, bf16[512,64,128]{2,1,0:T(8,128)(2,1)} %bitcast.5, s32[512,128]{1,0:T(8,128)S(1)} %copy-done.14), custom_call_target="tpu_custom_call" | custom-call | flops 10737418240 | bytes 20971520 | tf_op jit(solution)/shard_map/pallas_call | solution.py:68
  21.0 10.2 %collective-permute-done.refs_1_ = bf16[256,2048]{1,0:T(8,128)(2,1)S(1)} collective-permute-done((bf16[256,2048]{1,0:T(8,128)(2,1)S(1)}, bf16[256,2048]{1,0:T(8,128)(2,1)S(1)}, u32[]{:S(2)}, u32[]{:S(2)}) %collective-permute-start) | collective-permute-done | bytes 1048608 | tf_op jit(solution)/shard_map/ppermute | solution.py:178
  31.2 1.5 collective-permute-start.2
  32.7 1.0 collective-permute-start.8
  33.7 1.6 collective-permute-start.5
  35.3 25.3 %collective-permute-done.8.refs_0_ = bf16[256,2048]{1,0:T(8,128)(2,1)S(1)} collective-permute-done((bf16[256,2048]{1,0:T(8,128)(2,1)S(1)}, bf16[256,2048]{1,0:T(8,128)(2,1)S(1)}, u32[]{:S(2)}, u32[]{:S(2)}) %collective-permute-start.8) | collective-permute-done | bytes 1048608 | tf_op jit(solution)/shard_map/ppermute | solution.py:178
  60.6 0.0 collective-permute-start.10
  60.6 1.0 copy-done.6
  61.6 21.6 %collective-permute-done.5.refs_1_ = bf16[256,2048]{1,0:T(8,128)(2,1)} collective-permute-done((bf16[256,2048]{1,0:T(8,128)(2,1)S(1)}, bf16[256,2048]{1,0:T(8,128)(2,1)}, u32[]{:S(2)}, u32[]{:S(2)}) %collective-permute-start.5) | collective-permute-done | bytes 1048608 | tf_op jit(solution)/shard_map/ppermute | solution.py:178
  83.2 1.3 copy-done.3
  84.5 4.0 %shard_map.49 = (f32[512,512]{1,0:T(8,128)S(1)}, bf16[512,512]{1,0:T(8,128)(2,1)S(1)}) custom-call(s32[2]{0:T(128)S(1)} %pad_add_fusion.spot, bf16[512,2048]{1,0:T(8,128)(2,1)S(1)} %get-tuple-element.28.own, bf16[512,2048]{1,0:T(8,128)(2,1)} %copy-done.3, bf16[256,2048]{1,0:T(8,128)(2,1)S(1)} %get-tuple-element.30.refs_0_, ...), custom_call_target="tpu_custom_call" | custom-call | flops 1024 | bytes 1024 | tf_op jit(solution)/shard_map/pallas_call | solution.py:126
  88.5 5.3 %shard_map.50 = (f32[512,512]{1,0:T(8,128)S(1)}, bf16[512,512]{1,0:T(8,128)(2,1)S(1)}) custom-call(s32[2]{0:T(128)S(1)} %pad_add_fusion.spot, bf16[512,2048]{1,0:T(8,128)(2,1)} %copy-done, bf16[512,2048]{1,0:T(8,128)(2,1)} %copy-done.3, bf16[256,2048]{1,0:T(8,128)(2,1)S(1)} %get-tuple-element.36.refs_0_, bf16[256,2048]{1,0:T(8,128)(2,1)} %collective-permute-done.5.refs_1_, ...), custom_call_target="tpu_custom_call" | custom-call | flops 1024 | bytes 1024 | tf_op jit(solution)/shard_map/pallas_call | solution.py:126
  93.8 0.1 collective-permute-start.6
  93.9 0.5 collective-permute-start.3
  94.4 11.2 %collective-permute-done.10.refs_0_ = bf16[256,2048]{1,0:T(8,128)(2,1)S(1)} collective-permute-done((bf16[256,2048]{1,0:T(8,128)(2,1)S(1)}, bf16[256,2048]{1,0:T(8,128)(2,1)S(1)}, u32[]{:S(2)}, u32[]{:S(2)}) %collective-permute-start.10) | collective-permute-done | bytes 1048608 | tf_op jit(solution)/shard_map/ppermute | solution.py:178
  105.6 2.9 %shard_map.51 = (f32[512,256]{1,0:T(8,128)S(1)}, bf16[512,256]{1,0:T(8,128)(2,1)S(1)}) custom-call(s32[2]{0:T(128)S(1)} %pad_add_fusion.spot, bf16[512,2048]{1,0:T(8,128)(2,1)S(1)} %copy-done.1, bf16[512,2048]{1,0:T(8,128)(2,1)} %copy-done.3, bf16[256,2048]{1,0:T(8,128)(2,1)S(1)} %collective-permute-done.10.refs_0_, ...), custom_call_target="tpu_custom_call" | custom-call | flops 1024 | bytes 1024 | tf_op jit(solution)/shard_map/pallas_call | solution.py:126
  108.5 0.1 collective-permute-start.13
  108.5 0.1 convert_element_type.60
  108.7 0.1 fusion.3
  108.8 0.6 collective-permute-start.7
  109.4 0.0 collective-permute-done.3
  109.4 0.1 convert_element_type.57
  109.5 0.1 fusion.6
  109.6 0.0 copy-done.15
  109.6 1.6 collective-permute-start.4
  111.2 14.5 %collective-permute-done.9.refs_1_ = bf16[256,2048]{1,0:T(8,128)(2,1)S(1)} collective-permute-done((bf16[256,2048]{1,0:T(8,128)(2,1)}, bf16[256,2048]{1,0:T(8,128)(2,1)S(1)}, u32[]{:S(2)}, u32[]{:S(2)}) %collective-permute-start.9) | collective-permute-done | bytes 1048608 | tf_op jit(solution)/shard_map/ppermute | solution.py:178
  125.8 1.1 fusion.14
  126.9 0.0 collective-permute-start.14
  126.9 0.0 collective-permute-done.13
  126.9 0.0 collective-permute-done.7.refs_4_
  127.0 4.7 %shard_map.52 = (f32[512,512]{1,0:T(8,128)S(1)}, bf16[512,512]{1,0:T(8,128)(2,1)S(1)}) custom-call(s32[2]{0:T(128)S(1)} %pad_add_fusion.spot, bf16[512,2048]{1,0:T(8,128)(2,1)} %copy-done, bf16[512,2048]{1,0:T(8,128)(2,1)} %copy-done.3, bf16[256,2048]{1,0:T(8,128)(2,1)S(1)} %copy-done.7, bf16[256,2048]{1,0:T(8,128)(2,1)S(1)} %collective-permute-done.9.refs_1_, ...), custom_call_target="tpu_custom_call" | custom-call | flops 1024 | bytes 1024 | tf_op jit(solution)/shard_map/pallas_call | solution.py:126
  131.7 1.0 copy-done.12
  132.7 0.0 collective-permute-start.11
  132.7 0.7 fusion.9
  133.4 0.7 collective-permute-start.15
  134.1 0.1 collective-permute-start.19
  134.3 5.2 %collective-permute-done.15.refs_1_ = bf16[256,256]{1,0:T(8,128)(2,1)S(1)} collective-permute-done((bf16[256,256]{1,0:T(8,128)(2,1)}, bf16[256,256]{1,0:T(8,128)(2,1)S(1)}, u32[]{:S(2)}, u32[]{:S(2)}) %collective-permute-start.15) | collective-permute-done | bytes 131104 | tf_op jit(solution)/shard_map/ppermute | solution.py:172
  139.5 2.3 %collective-permute-done.14.block = bf16[128,2048]{1,0:T(8,128)(2,1)} collective-permute-done((bf16[128,2048]{1,0:T(8,128)(2,1)}, bf16[128,2048]{1,0:T(8,128)(2,1)}, u32[]{:S(2)}, u32[]{:S(2)}) %collective-permute-start.14) | collective-permute-done | bytes 524320 | tf_op jit(solution)/shard_map/ppermute | solution.py:178
  141.9 1.6 copy-done.4
  143.4 2.3 %shard_map.53 = (f32[256,128]{1,0:T(8,128)S(1)}, bf16[256,128]{1,0:T(8,128)(2,1)S(1)}, bf16[256,128]{1,0:T(8,128)(2,1)S(1)}, bf16[256,128]{1,0:T(8,128)(2,1)S(1)}) custom-call(bf16[512,2048]{1,0:T(8,128)(2,1)S(1)} %copy-done.2, bf16[512,2048]{1,0:T(8,128)(2,1)S(1)} %copy-done.4, bf16[128,2048]{1,0:T(8,128)(2,1)} %collective-permute-done.14.block, ...), custom_call_target="tpu_custom_call" | custom-call | flops 1024 | bytes 1024 | tf_op jit(solution)/shard_map/pallas_call | solution.py:147
  145.7 0.8 collective-permute-start.16
  146.5 1.4 collective-permute-start.18
  148.0 0.2 broadcast_in_dim.3
  148.2 0.1 fusion.8
  148.4 1.3 convert_element_type.63
  149.7 0.1 fusion
  149.8 0.8 collective-permute-start.12
  150.6 0.1 fusion.5
  150.7 1.0 collective-permute-done.19.block
  151.8 6.3 %collective-permute-done.12.refs_1_ = bf16[256,512]{1,0:T(8,128)(2,1)S(1)} collective-permute-done((bf16[256,512]{1,0:T(8,128)(2,1)S(1)}, bf16[256,512]{1,0:T(8,128)(2,1)S(1)}, u32[]{:S(2)}, u32[]{:S(2)}) %collective-permute-start.12) | collective-permute-done | bytes 262176 | tf_op jit(solution)/shard_map/ppermute | solution.py:172
  158.1 1.2 shard_map.54
  159.3 0.8 collective-permute-start.20
  160.1 0.1 fusion.2
  160.3 1.5 collective-permute-start.22
  161.8 2.4 %collective-permute-done.20 = bf16[256,128]{1,0:T(8,128)(2,1)S(1)} collective-permute-done((bf16[256,128]{1,0:T(8,128)(2,1)S(1)}, bf16[256,128]{1,0:T(8,128)(2,1)S(1)}, u32[]{:S(2)}, u32[]{:S(2)}) %collective-permute-start.20) | collective-permute-done | bytes 65568 | tf_op jit(solution)/shard_map/ppermute | solution.py:172
  164.2 0.3 collective-permute-done.21
  164.5 0.0 copy-start.19
  164.6 1.3 copy-done.19
  165.9 0.7 add_dynamic-update-slice_fusion
  (49 shorter events, 0.2 us)
Async XLA Ops:
  0.1 1.6 copy-start.5
  1.7 5.9 %copy-start.14 = (s32[512,128]{1,0:T(8,128)S(1)}, s32[512,128]{1,0:T(8,128)}, u32[]{:S(2)}) copy-start(s32[512,128]{1,0:T(8,128)} %mask.1) | copy-start | bytes 786436
  2.9 28.3 %collective-permute-start = (bf16[256,2048]{1,0:T(8,128)(2,1)S(1)}, bf16[256,2048]{1,0:T(8,128)(2,1)S(1)}, u32[]{:S(2)}, u32[]{:S(2)}) collective-permute-start(bf16[256,2048]{1,0:T(8,128)(2,1)S(1)} %get-tuple-element.30.refs_0_), channel_id=1, source_target_pairs={{0,4},{2,6},{4,8},{6,10},{8,12},{10,14},{12,0},{14,2},{1,5},{3,7},... | collective-permute-start | bytes 3145736 | tf_op jit(solution)/shard_map/ppermute | solution.py:178
  6.0 25.2 %collective-permute-start.1 = (bf16[256,2048]{1,0:T(8,128)(2,1)S(1)}, bf16[256,2048]{1,0:T(8,128)(2,1)S(1)}, u32[]{:S(2)}, u32[]{:S(2)}) collective-permute-start(bf16[256,2048]{1,0:T(8,128)(2,1)S(1)} %get-tuple-element.31), channel_id=1, source_target_pairs={{0,2},{2,0},{4,6},{6,4},{8,10},{10,8},{12,14},{14,12},{1,3},{3,1},... | collective-permute-start | bytes 3145736 | tf_op jit(solution)/shard_map/ppermute | solution.py:172
  20.9 62.3 %copy-start = (bf16[512,2048]{1,0:T(8,128)(2,1)}, bf16[512,2048]{1,0:T(8,128)(2,1)S(1)}, u32[]{:S(2)}) copy-start(bf16[512,2048]{1,0:T(8,128)(2,1)S(1)} %get-tuple-element.28.own) | copy-start | bytes 6291460
  31.2 52.0 %collective-permute-start.2 = (bf16[512,2048]{1,0:T(8,128)(2,1)S(1)}, bf16[512,2048]{1,0:T(8,128)(2,1)S(1)}, u32[]{:S(2)}, u32[]{:S(2)}) collective-permute-start(bf16[512,2048]{1,0:T(8,128)(2,1)S(1)} %get-tuple-element.32), channel_id=1, source_target_pairs={{0,2},{2,0},{4,6},{6,4},{8,10},{10,8},{12,14},{14,12},{1,3},{3,1},... | collective-permute-start | bytes 6291464 | tf_op jit(solution)/shard_map/ppermute | solution.py:172
  32.7 27.9 %collective-permute-start.8 = (bf16[256,2048]{1,0:T(8,128)(2,1)S(1)}, bf16[256,2048]{1,0:T(8,128)(2,1)S(1)}, u32[]{:S(2)}, u32[]{:S(2)}) collective-permute-start(bf16[256,2048]{1,0:T(8,128)(2,1)S(1)} %get-tuple-element.36.refs_0_), channel_id=1, source_target_pairs={{0,4},{2,6},{4,8},{6,10},{8,12},{10,14},{12,0},{14,2},{1,5},{3,7},... | collective-permute-start | bytes 3145736 | tf_op jit(solution)/shard_map/ppermute | solution.py:178
  33.7 49.5 %collective-permute-start.5 = (bf16[256,2048]{1,0:T(8,128)(2,1)S(1)}, bf16[256,2048]{1,0:T(8,128)(2,1)}, u32[]{:S(2)}, u32[]{:S(2)}) collective-permute-start(bf16[256,2048]{1,0:T(8,128)(2,1)S(1)} %get-tuple-element.33.refs_1_), channel_id=1, source_target_pairs={{0,4},{2,6},{4,8},{6,10},{8,12},{10,14},{12,0},{14,2},{1,5},{3,7},... | collective-permute-start | bytes 3145736 | tf_op jit(solution)/shard_map/ppermute | solution.py:178
  60.6 44.9 %collective-permute-start.10 = (bf16[256,2048]{1,0:T(8,128)(2,1)S(1)}, bf16[256,2048]{1,0:T(8,128)(2,1)S(1)}, u32[]{:S(2)}, u32[]{:S(2)}) collective-permute-start(bf16[256,2048]{1,0:T(8,128)(2,1)S(1)} %collective-permute-done.8.refs_0_), channel_id=1, source_target_pairs={{0,4},{2,6},{4,8},{6,10},{8,12},{10,14},{12,0},{14,2},{1,5},{3,7},... | collective-permute-start | bytes 3145736 | tf_op jit(solution)/shard_map/ppermute | solution.py:178
  60.6 1.0 copy-start.6
  83.2 42.6 %collective-permute-start.9 = (bf16[256,2048]{1,0:T(8,128)(2,1)}, bf16[256,2048]{1,0:T(8,128)(2,1)S(1)}, u32[]{:S(2)}, u32[]{:S(2)}) collective-permute-start(bf16[256,2048]{1,0:T(8,128)(2,1)} %collective-permute-done.5.refs_1_), channel_id=1, source_target_pairs={{0,4},{2,6},{4,8},{6,10},{8,12},{10,14},{12,0},{14,2},{1,5},{3,7},... | collective-permute-start | bytes 3145736 | tf_op jit(solution)/shard_map/ppermute | solution.py:178
  83.2 1.3 copy-start.3
  88.5 21.0 %copy-start.10 = (f32[512,512]{1,0:T(8,128)}, f32[512,512]{1,0:T(8,128)S(1)}, u32[]{:S(2)}) copy-start(f32[512,512]{1,0:T(8,128)S(1)} %get-tuple-element.34) | copy-start | bytes 3145732
  88.5 17.1 %copy-start.1 = (bf16[512,2048]{1,0:T(8,128)(2,1)S(1)}, bf16[512,2048]{1,0:T(8,128)(2,1)}, u32[]{:S(2)}) copy-start(bf16[512,2048]{1,0:T(8,128)(2,1)} %copy-done) | copy-start | bytes 6291460
  93.8 14.9 %copy-start.8 = (f32[512,512]{1,0:T(8,128)}, f32[512,512]{1,0:T(8,128)S(1)}, u32[]{:S(2)}) copy-start(f32[512,512]{1,0:T(8,128)S(1)} %get-tuple-element.37) | copy-start | bytes 3145732
  93.8 14.7 %collective-permute-start.6 = (bf16[512,512]{1,0:T(8,128)(2,1)S(1)}, bf16[512,512]{1,0:T(8,128)(2,1)S(1)}, u32[]{:S(2)}, u32[]{:S(2)}) collective-permute-start(bf16[512,512]{1,0:T(8,128)(2,1)S(1)} %get-tuple-element.38.refs_1_), channel_id=1, source_target_pairs={{0,1},{1,0},{2,3},{3,2},{4,5},{5,4},{6,7},{7,6},{8,9},{9,8},{10,11... | collective-permute-start | bytes 1572872 | tf_op jit(solution)/shard_map/ppermute | solution.py:175
  93.9 15.5 %collective-permute-start.3 = (bf16[512,512]{1,0:T(8,128)(2,1)S(1)}, bf16[512,512]{1,0:T(8,128)(2,1)S(1)}, u32[]{:S(2)}, u32[]{:S(2)}) collective-permute-start(bf16[512,512]{1,0:T(8,128)(2,1)S(1)} %get-tuple-element.35.refs_2_), channel_id=1, source_target_pairs={{0,1},{1,0},{2,3},{3,2},{4,5},{5,4},{6,7},{7,6},{8,9},{9,8},{10,11... | collective-permute-start | bytes 1572872 | tf_op jit(solution)/shard_map/ppermute | solution.py:175
  108.5 18.4 %collective-permute-start.13 = (bf16[512,256]{1,0:T(8,128)(2,1)S(1)}, bf16[512,256]{1,0:T(8,128)(2,1)S(1)}, u32[]{:S(2)}, u32[]{:S(2)}) collective-permute-start(bf16[512,256]{1,0:T(8,128)(2,1)S(1)} %get-tuple-element.39.refs_2_), channel_id=1, source_target_pairs={{0,1},{1,0},{2,3},{3,2},{4,5},{5,4},{6,7},{7,6},{8,9},{9,8},{10,11... | collective-permute-start | bytes 786440 | tf_op jit(solution)/shard_map/ppermute | solution.py:175
  108.7 1.0 copy-start.15
  108.8 18.1 %collective-permute-start.7 = (bf16[256,512]{1,0:T(8,128)(2,1)S(1)}, bf16[256,512]{1,0:T(8,128)(2,1)S(1)}, u32[]{:S(2)}, u32[]{:S(2)}) collective-permute-start(bf16[256,512]{1,0:T(8,128)(2,1)S(1)} %fusion.3), channel_id=1, source_target_pairs={{0,2},{2,0},{4,6},{6,4},{8,10},{10,8},{12,14},{14,12},{1,3},{3,1},... | collective-permute-start | bytes 786440 | tf_op jit(solution)/shard_map/ppermute | solution.py:172
  109.5 17.4 %copy-start.17 = (f32[512,512]{1,0:T(8,128)}, f32[512,512]{1,0:T(8,128)S(1)}, u32[]{:S(2)}) copy-start(f32[512,512]{1,0:T(8,128)S(1)} %convert_element_type.57) | copy-start | bytes 3145732
  109.5 17.4 %copy-start.7 = (bf16[256,2048]{1,0:T(8,128)(2,1)S(1)}, bf16[256,2048]{1,0:T(8,128)(2,1)}, u32[]{:S(2)}) copy-start(bf16[256,2048]{1,0:T(8,128)(2,1)} %copy-done.6) | copy-start | bytes 3145732
  109.6 17.3 %collective-permute-start.4 = (bf16[256,512]{1,0:T(8,128)(2,1)S(1)}, bf16[256,512]{1,0:T(8,128)(2,1)S(1)}, u32[]{:S(2)}, u32[]{:S(2)}) collective-permute-start(bf16[256,512]{1,0:T(8,128)(2,1)S(1)} %fusion.6), channel_id=1, source_target_pairs={{0,2},{2,0},{4,6},{6,4},{8,10},{10,8},{12,14},{14,12},{1,3},{3,1},... | collective-permute-start | bytes 786440 | tf_op jit(solution)/shard_map/ppermute | solution.py:172
  126.9 15.0 %collective-permute-start.14 = (bf16[128,2048]{1,0:T(8,128)(2,1)}, bf16[128,2048]{1,0:T(8,128)(2,1)}, u32[]{:S(2)}, u32[]{:S(2)}) collective-permute-start(bf16[128,2048]{1,0:T(8,128)(2,1)} %get-tuple-element.52), channel_id=1, source_target_pairs={{0,4},{2,6},{4,8},{6,10},{8,12},{10,14},{12,0},{14,2},{1,5},{3,7},... | collective-permute-start | bytes 1572872 | tf_op jit(solution)/shard_map/ppermute | solution.py:178
  126.9 14.9 %copy-start.2 = (bf16[512,2048]{1,0:T(8,128)(2,1)S(1)}, bf16[512,2048]{1,0:T(8,128)(2,1)}, u32[]{:S(2)}) copy-start(bf16[512,2048]{1,0:T(8,128)(2,1)} %copy-done) | copy-start | bytes 6291460
  131.7 1.0 copy-start.12
  132.7 15.7 %collective-permute-start.11 = (bf16[512,512]{1,0:T(8,128)(2,1)S(1)}, bf16[512,512]{1,0:T(8,128)(2,1)}, u32[]{:S(2)}, u32[]{:S(2)}) collective-permute-start(bf16[512,512]{1,0:T(8,128)(2,1)S(1)} %get-tuple-element.41.refs_0_), channel_id=1, source_target_pairs={{0,1},{1,0},{2,3},{3,2},{4,5},{5,4},{6,7},{7,6},{8,9},{9,8},{10,11... | collective-permute-start | bytes 1572872 | tf_op jit(solution)/shard_map/ppermute | solution.py:175
  133.4 6.1 %collective-permute-start.15 = (bf16[256,256]{1,0:T(8,128)(2,1)}, bf16[256,256]{1,0:T(8,128)(2,1)S(1)}, u32[]{:S(2)}, u32[]{:S(2)}) collective-permute-start(bf16[256,256]{1,0:T(8,128)(2,1)} %get-tuple-element.53), channel_id=1, source_target_pairs={{0,2},{2,0},{4,6},{6,4},{8,10},{10,8},{12,14},{14,12},{1,3},{3,1},... | collective-permute-start | bytes 393224 | tf_op jit(solution)/shard_map/ppermute | solution.py:172
  134.1 17.6 %collective-permute-start.19 = (bf16[128,2048]{1,0:T(8,128)(2,1)}, bf16[128,2048]{1,0:T(8,128)(2,1)S(1)}, u32[]{:S(2)}, u32[]{:S(2)}) collective-permute-start(bf16[128,2048]{1,0:T(8,128)(2,1)} %get-tuple-element.51), channel_id=1, source_target_pairs={{0,4},{2,6},{4,8},{6,10},{8,12},{10,14},{12,0},{14,2},{1,5},{3,7},... | collective-permute-start | bytes 1572872 | tf_op jit(solution)/shard_map/ppermute | solution.py:178
  141.8 1.6 copy-start.4
  145.7 2.5 %copy-start.11 = (f32[512,512]{1,0:T(8,128)S(1)}, f32[512,512]{1,0:T(8,128)}, u32[]{:S(2)}) copy-start(f32[512,512]{1,0:T(8,128)} %copy-done.10) | copy-start | bytes 3145732
  145.7 2.5 %copy-start.18 = (f32[512,512]{1,0:T(8,128)S(1)}, f32[512,512]{1,0:T(8,128)}, u32[]{:S(2)}) copy-start(f32[512,512]{1,0:T(8,128)} %copy-done.17) | copy-start | bytes 3145732
  145.7 14.5 %collective-permute-start.16 = (bf16[256,128]{1,0:T(8,128)(2,1)S(1)}, bf16[256,128]{1,0:T(8,128)(2,1)S(1)}, u32[]{:S(2)}, u32[]{:S(2)}) collective-permute-start(bf16[256,128]{1,0:T(8,128)(2,1)S(1)} %get-tuple-element.43), channel_id=1, source_target_pairs={{0,2},{2,0},{4,6},{6,4},{8,10},{10,8},{12,14},{14,12},{1,3},{3,1},... | collective-permute-start | bytes 196616 | tf_op jit(solution)/shard_map/ppermute | solution.py:172
  146.5 15.2 %collective-permute-start.17 = (bf16[256,128]{1,0:T(8,128)(2,1)S(1)}, bf16[256,128]{1,0:T(8,128)(2,1)S(1)}, u32[]{:S(2)}, u32[]{:S(2)}) collective-permute-start(bf16[256,128]{1,0:T(8,128)(2,1)S(1)} %get-tuple-element.44), channel_id=1, source_target_pairs={{0,3},{1,2},{2,1},{3,0},{4,7},{5,6},{6,5},{7,4},{8,11},{9,10},{10,... | collective-permute-start | bytes 196616 | tf_op jit(solution)/shard_map/ppermute | solution.py:181
  146.5 15.3 %collective-permute-start.18 = (bf16[256,128]{1,0:T(8,128)(2,1)S(1)}, bf16[256,128]{1,0:T(8,128)(2,1)S(1)}, u32[]{:S(2)}, u32[]{:S(2)}) collective-permute-start(bf16[256,128]{1,0:T(8,128)(2,1)S(1)} %get-tuple-element.46), channel_id=1, source_target_pairs={{0,1},{1,0},{2,3},{3,2},{4,5},{5,4},{6,7},{7,6},{8,9},{9,8},{10,11... | collective-permute-start | bytes 196616 | tf_op jit(solution)/shard_map/ppermute | solution.py:175
  148.2 1.5 copy-start.13
  148.2 2.4 %copy-start.9 = (f32[512,512]{1,0:T(8,128)S(1)}, f32[512,512]{1,0:T(8,128)}, u32[]{:S(2)}) copy-start(f32[512,512]{1,0:T(8,128)} %copy-done.8) | copy-start | bytes 3145732
  148.2 2.4 %copy-start.16 = (f32[512,512]{1,0:T(8,128)S(1)}, f32[512,512]{1,0:T(8,128)}, u32[]{:S(2)}) copy-start(f32[512,512]{1,0:T(8,128)} %copy-done.15) | copy-start | bytes 3145732
  149.8 8.3 %collective-permute-start.12 = (bf16[256,512]{1,0:T(8,128)(2,1)S(1)}, bf16[256,512]{1,0:T(8,128)(2,1)S(1)}, u32[]{:S(2)}, u32[]{:S(2)}) collective-permute-start(bf16[256,512]{1,0:T(8,128)(2,1)S(1)} %fusion), channel_id=1, source_target_pairs={{0,2},{2,0},{4,6},{6,4},{8,10},{10,8},{12,14},{14,12},{1,3},{3,1},... | collective-permute-start | bytes 786440 | tf_op jit(solution)/shard_map/ppermute | solution.py:172
  159.3 4.9 %collective-permute-start.20 = (bf16[256,128]{1,0:T(8,128)(2,1)S(1)}, bf16[256,128]{1,0:T(8,128)(2,1)S(1)}, u32[]{:S(2)}, u32[]{:S(2)}) collective-permute-start(bf16[256,128]{1,0:T(8,128)(2,1)S(1)} %get-tuple-element.47), channel_id=1, source_target_pairs={{0,2},{2,0},{4,6},{6,4},{8,10},{10,8},{12,14},{14,12},{1,3},{3,1},... | collective-permute-start | bytes 196616 | tf_op jit(solution)/shard_map/ppermute | solution.py:172
  160.1 4.4 %collective-permute-start.21 = (bf16[256,128]{1,0:T(8,128)(2,1)S(1)}, bf16[256,128]{1,0:T(8,128)(2,1)S(1)}, u32[]{:S(2)}, u32[]{:S(2)}) collective-permute-start(bf16[256,128]{1,0:T(8,128)(2,1)S(1)} %get-tuple-element.48), channel_id=1, source_target_pairs={{0,3},{1,2},{2,1},{3,0},{4,7},{5,6},{6,5},{7,4},{8,11},{9,10},{10,... | collective-permute-start | bytes 196616 | tf_op jit(solution)/shard_map/ppermute | solution.py:181
  160.3 4.3 %collective-permute-start.22 = (bf16[256,128]{1,0:T(8,128)(2,1)S(1)}, bf16[256,128]{1,0:T(8,128)(2,1)S(1)}, u32[]{:S(2)}, u32[]{:S(2)}) collective-permute-start(bf16[256,128]{1,0:T(8,128)(2,1)S(1)} %get-tuple-element.50), channel_id=1, source_target_pairs={{0,1},{1,0},{2,3},{3,2},{4,5},{5,4},{6,7},{7,6},{8,9},{9,8},{10,11... | collective-permute-start | bytes 196616 | tf_op jit(solution)/shard_map/ppermute | solution.py:175
  164.5 1.3 copy-start.19

commit v7 on v6

--- a/solution.py
+++ b/solution.py
@@ -21,16 +21,20 @@
     return jax.ShapeDtypeStruct(shape, kind)
 
 
-def prepare_body(spot, query_grads, mine, other):
+def prepare_body(spot, query_grads, mine, *sending):
     rank = LANES // 2
-    width = query_grads.shape[1]
-    for out, side in ((mine, spot[0]), (other, 1 - spot[0])):
+    rows, width = query_grads.shape
+    for outs, side in (((mine,), spot[0]), (sending, 1 - spot[0])):
         for m in range(width // 4 // LANES):
             at = pl.multiple_of(side * (width // 4) + m * LANES, LANES)
             low = query_grads[:, pl.ds(at, LANES)]
             high = query_grads[:, pl.ds(at + width // 2, LANES)]
-            out[:, 2 * m * LANES:(2 * m + 1) * LANES] = jnp.concatenate([low[:, :rank], high[:, :rank]], 1)
-            out[:, (2 * m + 1) * LANES:(2 * m + 2) * LANES] = jnp.concatenate([low[:, rank:], high[:, rank:]], 1)
+            even = jnp.concatenate([low[:, :rank], high[:, :rank]], 1)
+            odd = jnp.concatenate([low[:, rank:], high[:, rank:]], 1)
+            for i, out in enumerate(outs):
+                cut = slice(i * out.shape[0], (i + 1) * out.shape[0])
+                out[:, 2 * m * LANES:(2 * m + 1) * LANES] = even[cut, :]
+                out[:, (2 * m + 1) * LANES:(2 * m + 2) * LANES] = odd[cut, :]
 
 
 def prepare(query_grads, spot):
@@ -38,8 +42,8 @@
     return pl.pallas_call(
         prepare_body,
         in_specs=[SCALARS, WHOLE],
-        out_specs=[WHOLE] * 2,
-        out_shape=[shaped(bf16, rows, width // 2)] * 2,
+        out_specs=[WHOLE] * 3,
+        out_shape=[shaped(bf16, size, width // 2) for size in (rows, rows // 2, rows // 2)],
         compiler_params=LIMIT,
     )(spot, query_grads)
 
@@ -108,11 +112,15 @@
 def score_body(count, spot, own, far, *refs):
     keep, give = refs[-2:]
     part = own.shape[0] // 2
-    blocks = refs[:count]
-    queries = blocks[0].shape[0]
-    slots = (spot[0], 1 - spot[0]) if count == 2 else (0,)
-    for block, slot in zip(blocks, slots):
-        at = pl.ds(pl.multiple_of(slot * queries, queries), queries) if count == 2 else slice(None)
+    rows = refs[0].shape[0]
+    for i, block in enumerate(refs[:count]):
+        size = block.shape[0]
+        if count == 1:
+            at = slice(None)
+        elif i == 0:
+            at = pl.ds(pl.multiple_of(spot[0] * rows, rows), size)
+        else:
+            at = pl.ds(pl.multiple_of((1 - spot[0]) * rows + (i - 1) * size, size), size)
         keep[:part, at] = dot(own[:part, :], block[...])
         keep[part:, at] = dot(far[:part, :], block[...])
         give[:part, at] = dot(own[part:, :], block[...]).astype(bf16)
@@ -122,7 +130,7 @@
 def score(spot, own, far, blocks, *after):
     docs = own.shape[0]
     count = len(blocks)
-    queries = count * blocks[0].shape[0]
+    queries = sum(block.shape[0] for block in blocks)
     return pl.pallas_call(
         functools.partial(score_body, count),
         in_specs=[SCALARS] + [WHOLE] * (2 + count) + [ANYWHERE] * len(after),
@@ -180,20 +188,20 @@
     def swap_diagonal(x):
         return lax.ppermute(x, ("blk", "proj"), diagonal)
 
-    mine, sending = prepare(query_grads, spot)
-    other = swap_across(sending)
-    first = [mine, pass_on(mine)]
+    mine, *sending = prepare(query_grads, spot)
+    ahead = pass_on(mine)
+    other = [swap_across(x) for x in sending]
     own, sent = form(
         doc_inputs.reshape(docs, *doc_inputs.shape[2:]), doc_outgrads.reshape(docs, *doc_outgrads.shape[2:]), token_mask, spot
     )
-    sent, first[1], other = tie((sent, first[1], other))
-    second = [other]
+    sent, ahead, *other = tie((sent, ahead, *other))
     far = swap_across(sent)
+    first, second = [mine, ahead], [other]
     for step in range(2, places):
         first.append(pass_on(first[-1]))
-    for step in range(1, places - 1):
-        second.append(pass_on(second[-1]))
-    pieces = [pass_on(piece) for piece in jnp.split(second[-1], 2, 0)]
+    for step in range(1, places):
+        second.append([pass_on(x) for x in second[-1]])
+    pieces = second[-1]
 
     out = jnp.zeros((part, blk * queries), f32)
 
@@ -209,26 +217,26 @@
     last = ()
     for step in range(places - 1):
         if step == places - 2:
-            keep, give = score(spot, own, far, (first[-1],), *last)
+            keep, give = score(spot, own, far, [first[-1]], *last)
             final_own, final_far = over_cores(keep, give)
             final_beside = swap_across(final_far)
             last = (give,) + tuple(besides)
-        keep, give = score(spot, own, far, (first[step], second[step]), *last)
+        keep, give = score(spot, own, far, [first[step]] + second[step], *last)
         total, reach = over_cores(keep, give)
         besides.append(swap_across(reach))
         out = put(out, total + besides[-1].astype(f32), step, 0)
         last = (give,)
-    last = (give, final_beside)
+    last = (give,)
 
     size = queries // 2
     for i, piece in enumerate(pieces):
-        near, mate, reach, opposite = last_score(own, far, piece, *last)
+        near, give, facing, opposite = last_score(own, far, piece, *last)
         cut = slice(i * size, (i + 1) * size)
-        mine_total = final_own[:, cut] + swap_across(reach).astype(f32) + swap_diagonal(opposite).astype(f32)
-        other_total = near + swap_cores(mate).astype(f32) + final_beside[:, cut].astype(f32)
+        mine_total = final_own[:, cut] + swap_across(facing).astype(f32) + swap_diagonal(opposite).astype(f32)
+        other_total = near + swap_cores(give).astype(f32) + final_beside[:, cut].astype(f32)
         out = put(out, mine_total, places - 1, side * queries + i * size)
         out = put(out, other_total, places - 1, (1 - side) * queries + i * size)
-        last = (near, besides[-1])
+        last = (near, final_beside, reach)
     return out
 
 

time: 167 us -> 161 us (0.964)
  waiting for transfers between devices: 100 us -> 90.1 us
  Pallas kernels: 35 us -> 38.7 us
    ppermute x7 -> x9, waiting for transfers between devices: 86.2 us -> 71.3 us  [pass_on(): return lax.ppermute(x, 'blk', onward)]
    pallas_call x4, Pallas kernels: 16.9 us -> 20.6 us  [score(): pl.pallas_call(functools.partial(score_body, count), in_specs=[SCALARS] +...]
    ppermute x8 -> x9, waiting for transfers between devices: 14 us -> 17.4 us  [swap_across(): return lax.ppermute(x, 'blk', across)]
    ppermute x6, starting transfers between devices: 3.57 us -> 1.29 us  [swap_cores(): return lax.ppermute(x, 'proj', [(0, 1), (1, 0)])]
    ppermute x8 -> x9, starting transfers between devices: 8.26 us -> 9.9 us  [swap_across(): return lax.ppermute(x, 'blk', across)]
    ppermute x7 -> x9, starting transfers between devices: 5.81 us -> 6.42 us  [pass_on(): return lax.ppermute(x, 'blk', onward)]
    unnamed x40 -> x38, local copies, waits for them, and re-layouts: 7.81 us -> 7.67 us
  transfers between devices with their start and end apart: 23 -> 26, of which waited for: 11 -> 11; matrix products, arithmetic and copies ran while one was open for 3% -> 3% of each run, Pallas kernels for 20% -> 23%
where the time goes in v7:
time: 161 us
  waiting for transfers between devices  90.1 us (56%)
  Pallas kernels  38.7 us (24%)
  starting transfers between devices  18.6 us (12%)
  local copies, waits for them, and re-layouts  7.89 us (5%)
  other arithmetic  5.26 us (3%)
    ppermute x9, waiting for transfers between devices, pass_on(): return lax.ppermute(x, 'blk', onward)  71.3 us
    pallas_call x4, Pallas kernels, score(): pl.pallas_call(functools.partial(score_body, count), in_specs=[SCALARS] +...  20.6 us
    ppermute x9, waiting for transfers between devices, swap_across(): return lax.ppermute(x, 'blk', across)  17.4 us
    pallas_call x1, Pallas kernels, form(): pl.pallas_call(functools.partial(form_body, rows, rank), grid_spec=pltpu....  13.4 us
    ppermute x9, starting transfers between devices, swap_across(): return lax.ppermute(x, 'blk', across)  9.9 us
    unnamed x38, local copies, waits for them, and re-layouts  7.67 us
    ppermute x9, starting transfers between devices, pass_on(): return lax.ppermute(x, 'blk', onward)  6.42 us
    pallas_call x2, Pallas kernels, last_score(): pl.pallas_call(last_body, in_specs=[WHOLE] * 3 + [ANYWHERE] * len(after),...  3.51 us
  transfers between devices with their start and end apart: 26, of which 11 were waited for; matrix products, arithmetic and copies ran while one was open for 3% of the time, Pallas kernels for 23%

profile of v7, /device:TPU:0, one launch (start us, length us, event | category | flops | bytes accessed | tf_op | source)
XLA Modules:
  0.0 161.0 jit_solution(2857531488790908331)
XLA Ops:
  0.0 0.1 pad_add_fusion.spot
  0.1 1.6 copy-done.5
  1.7 1.3 shard_map.47
  2.9 3.1 %collective-permute-start = (bf16[256,2048]{1,0:T(8,128)(2,1)S(1)}, bf16[256,2048]{1,0:T(8,128)(2,1)S(1)}, u32[]{:S(2)}, u32[]{:S(2)}) collective-permute-start(bf16[256,2048]{1,0:T(8,128)(2,1)S(1)} %get-tuple-element.32.refs_0_), channel_id=1, source_target_pairs={{0,4},{2,6},{4,8},{6,10},{8,12},{10,14},{12,0},{14,2},{1,5},{3,7},... | collective-permute-start | bytes 3145736 | tf_op jit(solution)/shard_map/ppermute | solution.py:186
  6.0 1.5 collective-permute-start.1
  7.5 0.5 collective-permute-start.2
  8.0 13.4 %shard_map.46 = (bf16[512,2048]{1,0:T(8,128)(2,1)S(1)}, bf16[512,2048]{1,0:T(8,128)(2,1)S(1)}) custom-call(s32[2]{0:T(128)S(1)} %pad_add_fusion.spot, bf16[512,64,128]{2,1,0:T(8,128)(2,1)} %bitcast.4, bf16[512,64,128]{2,1,0:T(8,128)(2,1)} %bitcast.5, s32[512,128]{1,0:T(8,128)S(1)} %copy-done.13), custom_call_target="tpu_custom_call" | custom-call | flops 10737418240 | bytes 20971520 | tf_op jit(solution)/shard_map/pallas_call | solution.py:72
  21.5 9.2 %collective-permute-done.2.refs_3_ = bf16[128,2048]{1,0:T(8,128)(2,1)S(1)} collective-permute-done((bf16[128,2048]{1,0:T(8,128)(2,1)S(1)}, bf16[128,2048]{1,0:T(8,128)(2,1)S(1)}, u32[]{:S(2)}, u32[]{:S(2)}) %collective-permute-start.2) | collective-permute-done | bytes 524320 | tf_op jit(solution)/shard_map/ppermute | solution.py:180
  30.6 0.6 collective-permute-done.refs_1_
  31.2 1.5 collective-permute-start.3
  32.7 1.0 collective-permute-start.10
  33.7 1.6 collective-permute-start.6
  35.3 0.4 collective-permute-start.7
  35.7 24.9 %collective-permute-done.10.refs_0_ = bf16[256,2048]{1,0:T(8,128)(2,1)S(1)} collective-permute-done((bf16[256,2048]{1,0:T(8,128)(2,1)S(1)}, bf16[256,2048]{1,0:T(8,128)(2,1)S(1)}, u32[]{:S(2)}, u32[]{:S(2)}) %collective-permute-start.10) | collective-permute-done | bytes 1048608 | tf_op jit(solution)/shard_map/ppermute | solution.py:186
  60.6 11.2 %collective-permute-done.6.refs_1_ = bf16[128,2048]{1,0:T(8,128)(2,1)S(1)} collective-permute-done((bf16[128,2048]{1,0:T(8,128)(2,1)S(1)}, bf16[128,2048]{1,0:T(8,128)(2,1)S(1)}, u32[]{:S(2)}, u32[]{:S(2)}) %collective-permute-start.6) | collective-permute-done | bytes 524320 | tf_op jit(solution)/shard_map/ppermute | solution.py:186
  71.8 6.2 %collective-permute-done.3.far = bf16[512,2048]{1,0:T(8,128)(2,1)S(1)} collective-permute-done((bf16[512,2048]{1,0:T(8,128)(2,1)S(1)}, bf16[512,2048]{1,0:T(8,128)(2,1)S(1)}, u32[]{:S(2)}, u32[]{:S(2)}) %collective-permute-start.3) | collective-permute-done | bytes 2097184 | tf_op jit(solution)/shard_map/ppermute | solution.py:180
  78.0 1.3 copy-done.3
  79.3 5.0 %shard_map.49 = (f32[512,512]{1,0:T(8,128)S(1)}, bf16[512,512]{1,0:T(8,128)(2,1)S(1)}) custom-call(s32[2]{0:T(128)S(1)} %pad_add_fusion.spot, bf16[512,2048]{1,0:T(8,128)(2,1)S(1)} %get-tuple-element.30.own, bf16[512,2048]{1,0:T(8,128)(2,1)} %copy-done.3, bf16[256,2048]{1,0:T(8,128)(2,1)S(1)} %get-tuple-element.32.refs_0_, ...), custom_call_target="tpu_custom_call" | custom-call | flops 1024 | bytes 1024 | tf_op jit(solution)/shard_map/pallas_call | solution.py:134
  84.4 0.0 collective-permute-done.7.refs_2_
  84.4 6.1 %shard_map.50 = (f32[512,512]{1,0:T(8,128)S(1)}, bf16[512,512]{1,0:T(8,128)(2,1)S(1)}) custom-call(s32[2]{0:T(128)S(1)} %pad_add_fusion.spot, bf16[512,2048]{1,0:T(8,128)(2,1)} %copy-done, bf16[512,2048]{1,0:T(8,128)(2,1)} %copy-done.3, bf16[256,2048]{1,0:T(8,128)(2,1)S(1)} %get-tuple-element.40.refs_0_, ...), custom_call_target="tpu_custom_call" | custom-call | flops 1024 | bytes 1024 | tf_op jit(solution)/shard_map/pallas_call | solution.py:134
  90.5 0.1 collective-permute-start.8
  90.5 0.5 collective-permute-start.4
  91.0 0.4 collective-permute-start.12
  91.4 25.5 %collective-permute-done.11.refs_1_ = bf16[128,2048]{1,0:T(8,128)(2,1)} collective-permute-done((bf16[128,2048]{1,0:T(8,128)(2,1)S(1)}, bf16[128,2048]{1,0:T(8,128)(2,1)}, u32[]{:S(2)}, u32[]{:S(2)}) %collective-permute-start.11) | collective-permute-done | bytes 524320 | tf_op jit(solution)/shard_map/ppermute | solution.py:186
  116.9 0.0 collective-permute-start.17
  116.9 0.0 collective-permute-done.8
  116.9 0.1 convert_element_type.60
  117.0 0.1 fusion.3
  117.1 0.6 collective-permute-start.9
  117.7 0.0 collective-permute-done.4
  117.7 0.1 convert_element_type.57
  117.9 0.1 fusion.6
  118.0 0.0 copy-done.14
  118.0 1.6 collective-permute-start.5
  119.6 0.0 collective-permute-done.13.refs_0_
  119.6 2.9 %shard_map.51 = (f32[512,256]{1,0:T(8,128)S(1)}, bf16[512,256]{1,0:T(8,128)(2,1)S(1)}) custom-call(s32[2]{0:T(128)S(1)} %pad_add_fusion.spot, bf16[512,2048]{1,0:T(8,128)(2,1)S(1)} %copy-done.1, bf16[512,2048]{1,0:T(8,128)(2,1)} %copy-done.3, bf16[256,2048]{1,0:T(8,128)(2,1)S(1)} %collective-permute-done.13.refs_0_, ...), custom_call_target="tpu_custom_call" | custom-call | flops 1024 | bytes 1024 | tf_op jit(solution)/shard_map/pallas_call | solution.py:134
  122.5 0.8 copy-done.12
  123.3 4.7 %collective-permute-done.12.refs_2_ = bf16[128,2048]{1,0:T(8,128)(2,1)S(1)} collective-permute-done((bf16[128,2048]{1,0:T(8,128)(2,1)S(1)}, bf16[128,2048]{1,0:T(8,128)(2,1)S(1)}, u32[]{:S(2)}, u32[]{:S(2)}) %collective-permute-start.12) | collective-permute-done | bytes 524320 | tf_op jit(solution)/shard_map/ppermute | solution.py:186
  128.0 6.6 %shard_map.52 = (f32[512,512]{1,0:T(8,128)S(1)}, bf16[512,512]{1,0:T(8,128)(2,1)}) custom-call(s32[2]{0:T(128)S(1)} %pad_add_fusion.spot, bf16[512,2048]{1,0:T(8,128)(2,1)} %copy-done, bf16[512,2048]{1,0:T(8,128)(2,1)} %copy-done.3, bf16[256,2048]{1,0:T(8,128)(2,1)S(1)} %collective-permute-done.10.refs_0_, ...), custom_call_target="tpu_custom_call" | custom-call | flops 1024 | bytes 1024 | tf_op jit(solution)/shard_map/pallas_call | solution.py:134
  134.6 1.0 copy-done.10
  135.6 1.1 convert_element_type.66
  136.7 1.1 fusion.9
  137.8 0.6 collective-permute-start.21
  138.4 1.6 copy-done.4
  140.0 2.3 %shard_map.53 = (f32[256,128]{1,0:T(8,128)S(1)}, bf16[256,128]{1,0:T(8,128)(2,1)S(1)}, bf16[256,128]{1,0:T(8,128)(2,1)S(1)}, bf16[256,128]{1,0:T(8,128)(2,1)S(1)}) custom-call(bf16[512,2048]{1,0:T(8,128)(2,1)S(1)} %copy-done.2, bf16[512,2048]{1,0:T(8,128)(2,1)S(1)} %copy-done.4, bf16[128,2048]{1,0:T(8,128)(2,1)} %collective-permute-done.17.block, ...), custom_call_target="tpu_custom_call" | custom-call | flops 1024 | bytes 1024 | tf_op jit(solution)/shard_map/pallas_call | solution.py:155
  142.3 1.6 collective-permute-start.18
  143.9 0.2 broadcast_in_dim.3
  144.2 0.1 fusion.8
  144.3 1.3 convert_element_type.63
  145.6 0.1 fusion.refs_2_
  145.7 1.5 collective-permute-start.15
  147.2 0.1 fusion.5
  147.4 4.3 %collective-permute-done.22.block = bf16[128,2048]{1,0:T(8,128)(2,1)S(1)} collective-permute-done((bf16[128,2048]{1,0:T(8,128)(2,1)S(1)}, bf16[128,2048]{1,0:T(8,128)(2,1)S(1)}, u32[]{:S(2)}, u32[]{:S(2)}) %collective-permute-start.22) | collective-permute-done | bytes 524320 | tf_op jit(solution)/shard_map/ppermute | solution.py:186
  151.7 1.2 shard_map.54
  153.0 0.6 collective-permute-start.23
  153.5 1.1 collective-permute-done.15
  154.6 1.0 collective-permute-start.24
  155.6 0.1 fusion.2
  155.8 0.7 collective-permute-start.25
  156.5 1.0 collective-permute-done.23
  157.5 1.4 collective-permute-done.24
  159.0 0.0 copy-start.18
  159.0 1.3 copy-done.18
  160.3 0.7 add_dynamic-update-slice_fusion
  (52 shorter events, 0.2 us)
Async XLA Ops:
  0.1 1.6 copy-start.5
  1.7 6.4 %copy-start.13 = (s32[512,128]{1,0:T(8,128)S(1)}, s32[512,128]{1,0:T(8,128)}, u32[]{:S(2)}) copy-start(s32[512,128]{1,0:T(8,128)} %mask.1) | copy-start | bytes 786436
  2.9 28.3 %collective-permute-start = (bf16[256,2048]{1,0:T(8,128)(2,1)S(1)}, bf16[256,2048]{1,0:T(8,128)(2,1)S(1)}, u32[]{:S(2)}, u32[]{:S(2)}) collective-permute-start(bf16[256,2048]{1,0:T(8,128)(2,1)S(1)} %get-tuple-element.32.refs_0_), channel_id=1, source_target_pairs={{0,4},{2,6},{4,8},{6,10},{8,12},{10,14},{12,0},{14,2},{1,5},{3,7},... | collective-permute-start | bytes 3145736 | tf_op jit(solution)/shard_map/ppermute | solution.py:186
  6.0 15.4 %collective-permute-start.1 = (bf16[128,2048]{1,0:T(8,128)(2,1)S(1)}, bf16[128,2048]{1,0:T(8,128)(2,1)S(1)}, u32[]{:S(2)}, u32[]{:S(2)}) collective-permute-start(bf16[128,2048]{1,0:T(8,128)(2,1)S(1)} %get-tuple-element.33), channel_id=1, source_target_pairs={{0,2},{2,0},{4,6},{6,4},{8,10},{10,8},{12,14},{14,12},{1,3},{3,1},... | collective-permute-start | bytes 1572872 | tf_op jit(solution)/shard_map/ppermute | solution.py:180
  7.5 23.1 %collective-permute-start.2 = (bf16[128,2048]{1,0:T(8,128)(2,1)S(1)}, bf16[128,2048]{1,0:T(8,128)(2,1)S(1)}, u32[]{:S(2)}, u32[]{:S(2)}) collective-permute-start(bf16[128,2048]{1,0:T(8,128)(2,1)S(1)} %get-tuple-element.34), channel_id=1, source_target_pairs={{0,2},{2,0},{4,6},{6,4},{8,10},{10,8},{12,14},{14,12},{1,3},{3,1},... | collective-permute-start | bytes 1572872 | tf_op jit(solution)/shard_map/ppermute | solution.py:180
  21.4 56.6 %copy-start = (bf16[512,2048]{1,0:T(8,128)(2,1)}, bf16[512,2048]{1,0:T(8,128)(2,1)S(1)}, u32[]{:S(2)}) copy-start(bf16[512,2048]{1,0:T(8,128)(2,1)S(1)} %get-tuple-element.30.own) | copy-start | bytes 6291460
  31.2 46.8 %collective-permute-start.3 = (bf16[512,2048]{1,0:T(8,128)(2,1)S(1)}, bf16[512,2048]{1,0:T(8,128)(2,1)S(1)}, u32[]{:S(2)}, u32[]{:S(2)}) collective-permute-start(bf16[512,2048]{1,0:T(8,128)(2,1)S(1)} %get-tuple-element.35), channel_id=1, source_target_pairs={{0,2},{2,0},{4,6},{6,4},{8,10},{10,8},{12,14},{14,12},{1,3},{3,1},... | collective-permute-start | bytes 6291464 | tf_op jit(solution)/shard_map/ppermute | solution.py:180
  32.7 27.9 %collective-permute-start.10 = (bf16[256,2048]{1,0:T(8,128)(2,1)S(1)}, bf16[256,2048]{1,0:T(8,128)(2,1)S(1)}, u32[]{:S(2)}, u32[]{:S(2)}) collective-permute-start(bf16[256,2048]{1,0:T(8,128)(2,1)S(1)} %get-tuple-element.40.refs_0_), channel_id=1, source_target_pairs={{0,4},{2,6},{4,8},{6,10},{8,12},{10,14},{12,0},{14,2},{1,5},{3,7},... | collective-permute-start | bytes 3145736 | tf_op jit(solution)/shard_map/ppermute | solution.py:186
  33.7 38.1 %collective-permute-start.6 = (bf16[128,2048]{1,0:T(8,128)(2,1)S(1)}, bf16[128,2048]{1,0:T(8,128)(2,1)S(1)}, u32[]{:S(2)}, u32[]{:S(2)}) collective-permute-start(bf16[128,2048]{1,0:T(8,128)(2,1)S(1)} %get-tuple-element.36.refs_1_), channel_id=1, source_target_pairs={{0,4},{2,6},{4,8},{6,10},{8,12},{10,14},{12,0},{14,2},{1,5},{3,7},... | collective-permute-start | bytes 1572872 | tf_op jit(solution)/shard_map/ppermute | solution.py:186
  35.3 49.1 %collective-permute-start.7 = (bf16[128,2048]{1,0:T(8,128)(2,1)S(1)}, bf16[128,2048]{1,0:T(8,128)(2,1)S(1)}, u32[]{:S(2)}, u32[]{:S(2)}) collective-permute-start(bf16[128,2048]{1,0:T(8,128)(2,1)S(1)} %get-tuple-element.37.refs_2_), channel_id=1, source_target_pairs={{0,4},{2,6},{4,8},{6,10},{8,12},{10,14},{12,0},{14,2},{1,5},{3,7},... | collective-permute-start | bytes 1572872 | tf_op jit(solution)/shard_map/ppermute | solution.py:186
  60.6 59.0 %collective-permute-start.13 = (bf16[256,2048]{1,0:T(8,128)(2,1)S(1)}, bf16[256,2048]{1,0:T(8,128)(2,1)S(1)}, u32[]{:S(2)}, u32[]{:S(2)}) collective-permute-start(bf16[256,2048]{1,0:T(8,128)(2,1)S(1)} %collective-permute-done.10.refs_0_), channel_id=1, source_target_pairs={{0,4},{2,6},{4,8},{6,10},{8,12},{10,14},{12,0},{14,2},{1,5},{3,7},... | collective-permute-start | bytes 3145736 | tf_op jit(solution)/shard_map/ppermute | solution.py:186
  71.8 45.0 %collective-permute-start.11 = (bf16[128,2048]{1,0:T(8,128)(2,1)S(1)}, bf16[128,2048]{1,0:T(8,128)(2,1)}, u32[]{:S(2)}, u32[]{:S(2)}) collective-permute-start(bf16[128,2048]{1,0:T(8,128)(2,1)S(1)} %collective-permute-done.6.refs_1_), channel_id=1, source_target_pairs={{0,4},{2,6},{4,8},{6,10},{8,12},{10,14},{12,0},{14,2},{1,5},{3,7},... | collective-permute-start | bytes 1572872 | tf_op jit(solution)/shard_map/ppermute | solution.py:186
  78.0 1.3 copy-start.3
  84.4 33.5 %copy-start.8 = (f32[512,512]{1,0:T(8,128)}, f32[512,512]{1,0:T(8,128)S(1)}, u32[]{:S(2)}) copy-start(f32[512,512]{1,0:T(8,128)S(1)} %get-tuple-element.38) | copy-start | bytes 3145732
  90.5 27.4 %copy-start.6 = (f32[512,512]{1,0:T(8,128)}, f32[512,512]{1,0:T(8,128)S(1)}, u32[]{:S(2)}) copy-start(f32[512,512]{1,0:T(8,128)S(1)} %get-tuple-element.41) | copy-start | bytes 3145732
  90.5 26.4 %collective-permute-start.8 = (bf16[512,512]{1,0:T(8,128)(2,1)S(1)}, bf16[512,512]{1,0:T(8,128)(2,1)S(1)}, u32[]{:S(2)}, u32[]{:S(2)}) collective-permute-start(bf16[512,512]{1,0:T(8,128)(2,1)S(1)} %get-tuple-element.42.refs_1_), channel_id=1, source_target_pairs={{0,1},{1,0},{2,3},{3,2},{4,5},{5,4},{6,7},{7,6},{8,9},{9,8},{10,11... | collective-permute-start | bytes 1572872 | tf_op jit(solution)/shard_map/ppermute | solution.py:183
  90.5 27.2 %collective-permute-start.4 = (bf16[512,512]{1,0:T(8,128)(2,1)S(1)}, bf16[512,512]{1,0:T(8,128)(2,1)S(1)}, u32[]{:S(2)}, u32[]{:S(2)}) collective-permute-start(bf16[512,512]{1,0:T(8,128)(2,1)S(1)} %get-tuple-element.39.refs_3_), channel_id=1, source_target_pairs={{0,1},{1,0},{2,3},{3,2},{4,5},{5,4},{6,7},{7,6},{8,9},{9,8},{10,11... | collective-permute-start | bytes 1572872 | tf_op jit(solution)/shard_map/ppermute | solution.py:183
  91.0 37.0 %collective-permute-start.12 = (bf16[128,2048]{1,0:T(8,128)(2,1)S(1)}, bf16[128,2048]{1,0:T(8,128)(2,1)S(1)}, u32[]{:S(2)}, u32[]{:S(2)}) collective-permute-start(bf16[128,2048]{1,0:T(8,128)(2,1)S(1)} %collective-permute-done.7.refs_2_), channel_id=1, source_target_pairs={{0,4},{2,6},{4,8},{6,10},{8,12},{10,14},{12,0},{14,2},{1,5},{3,7},... | collective-permute-start | bytes 1572872 | tf_op jit(solution)/shard_map/ppermute | solution.py:186
  116.9 21.5 %collective-permute-start.17 = (bf16[128,2048]{1,0:T(8,128)(2,1)}, bf16[128,2048]{1,0:T(8,128)(2,1)}, u32[]{:S(2)}, u32[]{:S(2)}) collective-permute-start(bf16[128,2048]{1,0:T(8,128)(2,1)} %collective-permute-done.11.refs_1_), channel_id=1, source_target_pairs={{0,4},{2,6},{4,8},{6,10},{8,12},{10,14},{12,0},{14,2},{1,5},{3,7},... | collective-permute-start | bytes 1572872 | tf_op jit(solution)/shard_map/ppermute | solution.py:186
  117.0 1.0 copy-start.14
  117.0 2.5 %copy-start.1 = (bf16[512,2048]{1,0:T(8,128)(2,1)S(1)}, bf16[512,2048]{1,0:T(8,128)(2,1)}, u32[]{:S(2)}) copy-start(bf16[512,2048]{1,0:T(8,128)(2,1)} %copy-done) | copy-start | bytes 6291460
  117.1 10.9 %collective-permute-start.9 = (bf16[256,512]{1,0:T(8,128)(2,1)S(1)}, bf16[256,512]{1,0:T(8,128)(2,1)S(1)}, u32[]{:S(2)}, u32[]{:S(2)}) collective-permute-start(bf16[256,512]{1,0:T(8,128)(2,1)S(1)} %fusion.3), channel_id=1, source_target_pairs={{0,2},{2,0},{4,6},{6,4},{8,10},{10,8},{12,14},{14,12},{1,3},{3,1},... | collective-permute-start | bytes 786440 | tf_op jit(solution)/shard_map/ppermute | solution.py:180
  117.9 4.6 %copy-start.16 = (f32[512,512]{1,0:T(8,128)}, f32[512,512]{1,0:T(8,128)S(1)}, u32[]{:S(2)}) copy-start(f32[512,512]{1,0:T(8,128)S(1)} %convert_element_type.57) | copy-start | bytes 3145732
  118.0 10.0 %collective-permute-start.5 = (bf16[256,512]{1,0:T(8,128)(2,1)S(1)}, bf16[256,512]{1,0:T(8,128)(2,1)S(1)}, u32[]{:S(2)}, u32[]{:S(2)}) collective-permute-start(bf16[256,512]{1,0:T(8,128)(2,1)S(1)} %fusion.6), channel_id=1, source_target_pairs={{0,2},{2,0},{4,6},{6,4},{8,10},{10,8},{12,14},{14,12},{1,3},{3,1},... | collective-permute-start | bytes 786440 | tf_op jit(solution)/shard_map/ppermute | solution.py:180
  122.5 0.8 copy-start.12
  123.3 12.3 %collective-permute-start.16 = (bf16[512,256]{1,0:T(8,128)(2,1)S(1)}, bf16[512,256]{1,0:T(8,128)(2,1)}, u32[]{:S(2)}, u32[]{:S(2)}) collective-permute-start(bf16[512,256]{1,0:T(8,128)(2,1)S(1)} %get-tuple-element.43.refs_3_), channel_id=1, source_target_pairs={{0,1},{1,0},{2,3},{3,2},{4,5},{5,4},{6,7},{7,6},{8,9},{9,8},{10,11... | collective-permute-start | bytes 786440 | tf_op jit(solution)/shard_map/ppermute | solution.py:183
  134.6 1.0 copy-start.10
  135.6 2.8 %copy-start.2 = (bf16[512,2048]{1,0:T(8,128)(2,1)S(1)}, bf16[512,2048]{1,0:T(8,128)(2,1)}, u32[]{:S(2)}) copy-start(bf16[512,2048]{1,0:T(8,128)(2,1)} %copy-done) | copy-start | bytes 6291460
  135.6 8.7 %collective-permute-start.14 = (bf16[512,512]{1,0:T(8,128)(2,1)}, bf16[512,512]{1,0:T(8,128)(2,1)}, u32[]{:S(2)}, u32[]{:S(2)}) collective-permute-start(bf16[512,512]{1,0:T(8,128)(2,1)} %get-tuple-element.45.refs_0_), channel_id=1, source_target_pairs={{0,1},{1,0},{2,3},{3,2},{4,5},{5,4},{6,7},{7,6},{8,9},{9,8},{10,11... | collective-permute-start | bytes 1572872 | tf_op jit(solution)/shard_map/ppermute | solution.py:183
  135.6 16.1 %collective-permute-start.22 = (bf16[128,2048]{1,0:T(8,128)(2,1)S(1)}, bf16[128,2048]{1,0:T(8,128)(2,1)S(1)}, u32[]{:S(2)}, u32[]{:S(2)}) collective-permute-start(bf16[128,2048]{1,0:T(8,128)(2,1)S(1)} %collective-permute-done.12.refs_2_), channel_id=1, source_target_pairs={{0,4},{2,6},{4,8},{6,10},{8,12},{10,14},{12,0},{14,2},{1,5},{3,7},... | collective-permute-start | bytes 1572872 | tf_op jit(solution)/shard_map/ppermute | solution.py:186
  137.8 13.9 %collective-permute-start.21 = (bf16[256,256]{1,0:T(8,128)(2,1)S(1)}, bf16[256,256]{1,0:T(8,128)(2,1)S(1)}, u32[]{:S(2)}, u32[]{:S(2)}) collective-permute-start(bf16[256,256]{1,0:T(8,128)(2,1)S(1)} %get-tuple-element.55), channel_id=1, source_target_pairs={{0,2},{2,0},{4,6},{6,4},{8,10},{10,8},{12,14},{14,12},{1,3},{3,1},... | collective-permute-start | bytes 393224 | tf_op jit(solution)/shard_map/ppermute | solution.py:180
  138.4 1.6 copy-start.4
  142.3 1.8 %copy-start.9 = (f32[512,512]{1,0:T(8,128)S(1)}, f32[512,512]{1,0:T(8,128)}, u32[]{:S(2)}) copy-start(f32[512,512]{1,0:T(8,128)} %copy-done.8) | copy-start | bytes 3145732
  142.3 1.8 %copy-start.17 = (f32[512,512]{1,0:T(8,128)S(1)}, f32[512,512]{1,0:T(8,128)}, u32[]{:S(2)}) copy-start(f32[512,512]{1,0:T(8,128)} %copy-done.16) | copy-start | bytes 3145732
  142.3 13.5 %collective-permute-start.18 = (bf16[256,128]{1,0:T(8,128)(2,1)S(1)}, bf16[256,128]{1,0:T(8,128)(2,1)S(1)}, u32[]{:S(2)}, u32[]{:S(2)}) collective-permute-start(bf16[256,128]{1,0:T(8,128)(2,1)S(1)} %get-tuple-element.47), channel_id=1, source_target_pairs={{0,2},{2,0},{4,6},{6,4},{8,10},{10,8},{12,14},{14,12},{1,3},{3,1},... | collective-permute-start | bytes 196616 | tf_op jit(solution)/shard_map/ppermute | solution.py:180
  143.9 12.6 %collective-permute-start.19 = (bf16[256,128]{1,0:T(8,128)(2,1)S(1)}, bf16[256,128]{1,0:T(8,128)(2,1)S(1)}, u32[]{:S(2)}, u32[]{:S(2)}) collective-permute-start(bf16[256,128]{1,0:T(8,128)(2,1)S(1)} %get-tuple-element.48), channel_id=1, source_target_pairs={{0,3},{1,2},{2,1},{3,0},{4,7},{5,6},{6,5},{7,4},{8,11},{9,10},{10,... | collective-permute-start | bytes 196616 | tf_op jit(solution)/shard_map/ppermute | solution.py:189
  144.1 1.5 copy-start.11
  144.1 3.1 %copy-start.7 = (f32[512,512]{1,0:T(8,128)S(1)}, f32[512,512]{1,0:T(8,128)}, u32[]{:S(2)}) copy-start(f32[512,512]{1,0:T(8,128)} %copy-done.6) | copy-start | bytes 3145732
  144.1 3.1 %copy-start.15 = (f32[512,512]{1,0:T(8,128)S(1)}, f32[512,512]{1,0:T(8,128)}, u32[]{:S(2)}) copy-start(f32[512,512]{1,0:T(8,128)} %copy-done.14) | copy-start | bytes 3145732
  145.7 8.9 %collective-permute-start.15 = (bf16[256,512]{1,0:T(8,128)(2,1)S(1)}, bf16[256,512]{1,0:T(8,128)(2,1)S(1)}, u32[]{:S(2)}, u32[]{:S(2)}) collective-permute-start(bf16[256,512]{1,0:T(8,128)(2,1)S(1)} %fusion.refs_2_), channel_id=1, source_target_pairs={{0,2},{2,0},{4,6},{6,4},{8,10},{10,8},{12,14},{14,12},{1,3},{3,1},... | collective-permute-start | bytes 786440 | tf_op jit(solution)/shard_map/ppermute | solution.py:180
  151.7 4.8 %collective-permute-start.20 = (bf16[256,128]{1,0:T(8,128)(2,1)S(1)}, bf16[256,128]{1,0:T(8,128)(2,1)S(1)}, u32[]{:S(2)}, u32[]{:S(2)}) collective-permute-start(bf16[256,128]{1,0:T(8,128)(2,1)S(1)} %get-tuple-element.50), channel_id=1, source_target_pairs={{0,1},{1,0},{2,3},{3,2},{4,5},{5,4},{6,7},{7,6},{8,9},{9,8},{10,11... | collective-permute-start | bytes 196616 | tf_op jit(solution)/shard_map/ppermute | solution.py:183
  153.0 4.6 %collective-permute-start.23 = (bf16[256,128]{1,0:T(8,128)(2,1)S(1)}, bf16[256,128]{1,0:T(8,128)(2,1)S(1)}, u32[]{:S(2)}, u32[]{:S(2)}) collective-permute-start(bf16[256,128]{1,0:T(8,128)(2,1)S(1)} %get-tuple-element.51), channel_id=1, source_target_pairs={{0,2},{2,0},{4,6},{6,4},{8,10},{10,8},{12,14},{14,12},{1,3},{3,1},... | collective-permute-start | bytes 196616 | tf_op jit(solution)/shard_map/ppermute | solution.py:180
  154.6 4.3 %collective-permute-start.24 = (bf16[256,128]{1,0:T(8,128)(2,1)S(1)}, bf16[256,128]{1,0:T(8,128)(2,1)S(1)}, u32[]{:S(2)}, u32[]{:S(2)}) collective-permute-start(bf16[256,128]{1,0:T(8,128)(2,1)S(1)} %get-tuple-element.52), channel_id=1, source_target_pairs={{0,3},{1,2},{2,1},{3,0},{4,7},{5,6},{6,5},{7,4},{8,11},{9,10},{10,... | collective-permute-start | bytes 196616 | tf_op jit(solution)/shard_map/ppermute | solution.py:189
  155.8 3.2 %collective-permute-start.25 = (bf16[256,128]{1,0:T(8,128)(2,1)S(1)}, bf16[256,128]{1,0:T(8,128)(2,1)S(1)}, u32[]{:S(2)}, u32[]{:S(2)}) collective-permute-start(bf16[256,128]{1,0:T(8,128)(2,1)S(1)} %get-tuple-element.54), channel_id=1, source_target_pairs={{0,1},{1,0},{2,3},{3,2},{4,5},{5,4},{6,7},{7,6},{8,9},{9,8},{10,11... | collective-permute-start | bytes 196616 | tf_op jit(solution)/shard_map/ppermute | solution.py:183
  159.0 1.3 copy-start.18

commit v8 on v7

v8 whole, which is shorter than its diff:
```python
import functools

import jax
import jax.numpy as jnp
from jax import lax
from jax.experimental import pallas as pl
from jax.experimental.pallas import tpu as pltpu
from jax.sharding import PartitionSpec as P

LANES = 128
LENT = 6
VMEM_LIMIT = 48 * 1024 * 1024
ANYWHERE = pl.BlockSpec(memory_space=pl.ANY)
SCALARS = pl.BlockSpec(memory_space=pltpu.SMEM)
WHOLE = pl.BlockSpec(memory_space=pltpu.VMEM)
NT = (((1,), (1,)), ((), ()))
bf16, f32 = jnp.bfloat16, jnp.float32
LIMIT = pltpu.CompilerParams(vmem_limit_bytes=VMEM_LIMIT)
FREE = pl.CostEstimate(flops=1024, bytes_accessed=1024, transcendentals=0)


def work(flops):
    return pl.CostEstimate(flops=int(flops), bytes_accessed=1024, transcendentals=0)


def shaped(kind, *shape):
    return jax.ShapeDtypeStruct(shape, kind)


def prepare_body(spot, query_grads, mine, mine_stay, sending):
    rank = LANES // 2
    rows, width = query_grads.shape
    for outs, side in (((mine, mine_stay), spot[0]), ((sending,), 1 - spot[0])):
        for m in range(width // 4 // LANES):
            at = pl.multiple_of(side * (width // 4) + m * LANES, LANES)
            low = query_grads[:, pl.ds(at, LANES)]
            high = query_grads[:, pl.ds(at + width // 2, LANES)]
            even = jnp.concatenate([low[:, :rank], high[:, :rank]], 1)
            odd = jnp.concatenate([low[:, rank:], high[:, rank:]], 1)
            for out in outs:
                for k, block in ((2 * m, even), (2 * m + 1, odd)):
                    if k * LANES < out.shape[1]:
                        out[:, k * LANES:(k + 1) * LANES] = block


def prepare(query_grads, spot, stay):
    rows, width = query_grads.shape
    half = width // 2
    return pl.pallas_call(
        prepare_body,
        in_specs=[SCALARS, WHOLE],
        out_specs=[WHOLE] * 3,
        out_shape=[shaped(bf16, *size) for size in ((rows, half), (rows, stay), (rows, half))],
        compiler_params=LIMIT,
    )(spot, query_grads)


def form_body(rows, rank, spot, inputs, outgrads, mask, *refs):
    kept, lent, sent, sent_lent, rounds = refs[-5:]
    for d in range(rows):
        masked = outgrads[d] * mask[d:d + 1, :].astype(bf16)
        product = lax.dot_general(inputs[d], masked, NT, preferred_element_type=f32)
        pairs = jnp.concatenate([product[:rank // 2], product[rank // 2:]], 1)
        rounds[pl.ds(d, rank // 2, stride=rows), :] = pairs
    stay = sent.shape[1] // LANES
    for which in range(2):
        side = spot[0] if which == 0 else 1 - spot[0]
        for k in range(rank // 4):
            at = pl.multiple_of((side * (rank // 4) + k) * rows, rows)
            block = rounds[pl.ds(at, rows), :].astype(bf16)
            if which == 0:
                kept[:, k * LANES:(k + 1) * LANES] = block
                if k >= stay:
                    lent[:, (k - stay) * LANES:(k - stay + 1) * LANES] = block
            elif k < stay:
                sent[:, k * LANES:(k + 1) * LANES] = block
            else:
                sent_lent[:, (k - stay) * LANES:(k - stay + 1) * LANES] = block


def form(doc_inputs, doc_outgrads, token_mask, spot, stay, *after):
    docs, rank, length = doc_inputs.shape
    rows = 64
    steps = docs // rows
    half = rank * rank // 2
    widths = (half, half - stay, stay, half - stay)

    def at(g, spot):
        return lax.rem(g + spot[1] * (steps // 2), steps)

    return pl.pallas_call(
        functools.partial(form_body, rows, rank),
        grid_spec=pltpu.PrefetchScalarGridSpec(
            num_scalar_prefetch=1,
            grid=(steps,),
            in_specs=[
                pl.BlockSpec((rows, rank, length), lambda g, spot: (at(g, spot), 0, 0)),
                pl.BlockSpec((rows, rank, length), lambda g, spot: (at(g, spot), 0, 0)),
                pl.BlockSpec((rows, length), lambda g, spot: (at(g, spot), 0)),
            ] + [ANYWHERE] * len(after),
            out_specs=[pl.BlockSpec((rows, width), lambda g, spot: (g, 0)) for width in widths],
            scratch_shapes=[pltpu.VMEM((rank // 2 * rows, LANES), f32)],
        ),
        out_shape=[shaped(bf16, docs, width) for width in widths],
        compiler_params=LIMIT,
        cost_estimate=pl.CostEstimate(
            flops=40 * docs * rank * rank * length, bytes_accessed=4 * docs * rank * length + 2 * docs * rank * rank, transcendentals=0
        ),
    )(spot, doc_inputs, doc_outgrads, token_mask, *after)


def tie(arrays, *after):
    count = len(arrays)
    return pl.pallas_call(
        lambda *refs: None,
        in_specs=[ANYWHERE] * (count + len(after)),
        out_specs=[ANYWHERE] * count,
        out_shape=[shaped(a.dtype, *a.shape) for a in arrays],
        input_output_aliases={i: i for i in range(count)},
        compiler_params=LIMIT,
        cost_estimate=FREE,
    )(*arrays, *after)


def dot(rows, block):
    return lax.dot_general(rows, block, NT, preferred_element_type=f32)


def score_body(stay, counts, spot, own, far, far_lent, *refs):
    keep, give = refs[-2:]
    part = own.shape[0] // 2

    def put(block, at):
        width = block.shape[1]
        lent = block.shape[1] > stay

        def products(h):
            rows = slice(h * part, (h + 1) * part)
            reach = dot(far[rows, :], block[:, :stay])
            if lent:
                reach += dot(far_lent[rows, :], block[:, stay:])
            return dot(own[rows, :width], block[...]), reach

        keep[:part, at], keep[part:, at] = products(0)
        mate, opposite = products(1)
        give[:part, at] = mate.astype(bf16)
        give[part:, at] = opposite.astype(bf16)

    def group(blocks):
        for i, block in enumerate(blocks):
            size = block.shape[0]
            if len(blocks) == 1:
                at = slice(None)
            else:
                at = pl.ds(pl.multiple_of((spot[0] if i == 0 else 1 - spot[0]) * size, size), size)
            put(block, at)

    if counts[1]:
        pl.when(spot[2] == 1)(lambda: group(refs[:counts[0]]))
        pl.when(spot[2] == 0)(lambda: group(refs[counts[0]:sum(counts)]))
    else:
        group(refs[:counts[0]])


def score(spot, stay, docs, blocks, outer, *after):
    rows = docs[0].shape[0]
    queries = sum(block.shape[0] for block in blocks)
    return pl.pallas_call(
        functools.partial(score_body, stay, (len(blocks), len(outer))),
        in_specs=[SCALARS] + [WHOLE] * (3 + len(blocks) + len(outer)) + [ANYWHERE] * len(after),
        out_specs=[WHOLE] * 2,
        out_shape=[shaped(f32, rows, queries), shaped(bf16, rows, queries)],
        compiler_params=LIMIT,
        cost_estimate=work(5 * rows * 2 * queries * docs[0].shape[1]) if outer else FREE,
    )(spot, *docs, *blocks, *outer, *after)


def lent_body(stay, count, spot, near, far, *refs):
    keep, give = refs[-2:]
    part = near.shape[0] // 2

    @pl.when(spot[2] == 1)
    def _():
        for g in range(count // 2):
            blocks = refs[2 * g:2 * g + 2]
            rows = blocks[0].shape[0]
            for i, block in enumerate(blocks):
                size = block.shape[0]
                slot = 2 * g * rows + (spot[0] if i == 0 else 1 - spot[0]) * rows
                at = pl.ds(pl.multiple_of(slot, size), size)
                for r, docs in enumerate((near, far)):
                    rows_at = slice(r * part, (r + 1) * part)
                    keep[rows_at, at] = dot(docs[:part, :], block[:, stay:])
                    give[rows_at, at] = dot(docs[part:, :], block[:, stay:]).astype(bf16)


def lent_score(spot, stay, near, far, blocks, *after):
    docs = near.shape[0]
    queries = sum(block.shape[0] for block in blocks)
    return pl.pallas_call(
        functools.partial(lent_body, stay, len(blocks)),
        in_specs=[SCALARS] + [WHOLE] * (2 + len(blocks)) + [ANYWHERE] * len(after),
        out_specs=[WHOLE] * 2,
        out_shape=[shaped(f32, docs, queries), shaped(bf16, docs, queries)],
        compiler_params=LIMIT,
        cost_estimate=work(2.5 * 2 * docs * 2 * queries * near.shape[1]),
    )(spot, near, far, *blocks, *after)


def last_body(stay, spot, own, far, far_lent, inner, outer, *refs):
    near, mate, across, diagonal = refs[-4:]
    part = near.shape[0]

    def products(block):
        def reach(rows):
            return dot(far[rows, :], block[:, :stay]) + dot(far_lent[rows, :], block[:, stay:])

        mate[...] = dot(own[part:, :], block[...]).astype(bf16)
        across[...] = reach(slice(part)).astype(bf16)
        diagonal[...] = reach(slice(part, None)).astype(bf16)
        near[...] = dot(own[:part, :], block[...])

    pl.when(spot[2] == 1)(lambda: products(inner))
    pl.when(spot[2] == 0)(lambda: products(outer))


def last_score(spot, stay, docs, inner, outer, *after):
    shape = (docs[0].shape[0] // 2, inner.shape[0])
    return pl.pallas_call(
        functools.partial(last_body, stay),
        in_specs=[SCALARS] + [WHOLE] * 5 + [ANYWHERE] * len(after),
        out_specs=[WHOLE] * 4,
        out_shape=[shaped(f32, *shape)] + [shaped(bf16, *shape)] * 3,
        compiler_params=LIMIT,
        cost_estimate=work(2 * 2 * docs[0].shape[0] * 2 * inner.shape[0] * inner.shape[1]),
    )(spot, *docs, inner, outer, *after)


def on_device(doc_inputs, doc_outgrads, token_mask, query_grads):
    blk = lax.axis_size("blk")
    places = blk // 2
    me = lax.axis_index("blk")
    place, side = me // 2, me % 2
    docs, rank = doc_inputs.shape[0], doc_inputs.shape[2]
    queries = query_grads.shape[0]
    part = docs // 2
    half = rank * rank // 2
    doc_inputs = doc_inputs.reshape(docs, *doc_inputs.shape[2:])
    doc_outgrads = doc_outgrads.reshape(docs, *doc_outgrads.shape[2:])
    lending = places == 4
    stay = half // 16 * (16 - LENT)
    inner = jnp.where((place == 1) | (place == 2), 1, 0) if lending else 1
    spot = jnp.stack([side, lax.axis_index("proj"), inner]).astype(jnp.int32)

    def at(place):
        return [2 * place, 2 * place + 1]

    across = [(b, b ^ 1) for b in range(blk)]
    onward = [(b, (b + 2) % blk) for b in range(blk)]
    inward = list(zip(at(0) + at(3), at(1) + at(2)))
    outward = [(b, a) for a, b in inward]
    centre = list(zip(at(1) + at(2), at(2) + at(1)))
    inner_across = [(b, b ^ 1) for b in at(1) + at(2)]
    inner_cores = [(2 * b + c, 2 * b + 1 - c) for b in at(1) + at(2) for c in range(2)]
    diagonal = [(2 * b + c, 2 * (b ^ 1) + (c ^ 1)) for b in range(blk) for c in range(2)]

    def move(x, pairs):
        return lax.ppermute(x, "blk", pairs)

    def swap_across(x):
        return move(x, across)

    def swap_cores(x):
        return lax.ppermute(x, "proj", [(0, 1), (1, 0)])

    def swap_diagonal(x):
        return lax.ppermute(x, ("blk", "proj"), diagonal)

    def over_cores(keep, give, swap=swap_cores):
        got = swap(give).astype(f32)
        return keep[:part] + got[:part], (keep[part:] + got[part:]).astype(bf16)

    out = jnp.zeros((part, blk * queries), f32)

    def put(out, total, origin, at):
        return lax.dynamic_update_slice_in_dim(out, total, origin * (2 * queries) + at, 1)

    mine, mine_stay, sending = prepare(query_grads, spot, stay)

    if not lending:
        flow = [mine, swap_across(sending)]
        own, _, sent, sent_lent = form(doc_inputs, doc_outgrads, token_mask, spot, stay)
        rows = own, swap_across(sent), swap_across(sent_lent)
        for step in range(places):
            keep, give = score(spot, stay, rows, flow, [])
            total, reach = over_cores(keep, give)
            out = put(out, total + swap_across(reach).astype(f32), (place - step + places) % places, 0)
            if step + 1 < places:
                flow = [move(x, onward) for x in flow]
        return out

    def staying(*blocks):
        return jnp.concatenate([x[:, :stay] for x in blocks], 0)

    mate_a = move(mine, inward)
    near_a = move(mine, centre)
    outer_mate_a = move(mine_stay, outward)
    other = swap_across(sending)
    own, lent, sent, sent_lent = form(doc_inputs, doc_outgrads, token_mask, spot, stay)
    sent, sent_lent, mate_a, near_a, other = tie((sent, sent_lent, mate_a, near_a, other), outer_mate_a)

    outer_mate_b = move(other[:, :stay], outward)
    outer_near_a = move(near_a[:, :stay], outward)
    away_a = move(mate_a, centre)
    mate_b = move(other, inward)
    far = swap_across(sent)
    lent, sent_lent, away_a, other, mate_b = tie(
        (lent, sent_lent, away_a, other, mate_b), outer_mate_b, outer_near_a, far
    )

    outer_away_a = move(away_a, outward)
    near_b = move(other, centre)
    lent_near = move(lent, inward)
    far_lent = swap_across(sent_lent)
    lent_far = move(far_lent, inward)
    outer_near_b = move(near_b[:, :stay], outward)
    away_b = [move(x, centre) for x in jnp.split(mate_b, 2, 0)]
    outer_away_b = [move(x, outward) for x in away_b]

    rows = own, far, far_lent
    origins = {"self": place, "mate": place ^ 1, "near": jnp.where(place < 2, 2, 1), "away": jnp.where(place < 2, 3, 0)}

    keep, give = score(spot, stay, rows, [mine, other], [], near_b, outer_away_a, lent_near)
    self_total, self_reach = over_cores(keep, give)
    self_beside = swap_across(self_reach)
    keep, give = score(spot, stay, rows, [mate_a, mate_b], [outer_mate_a, outer_mate_b], give, outer_near_b, lent_far, away_b[0])
    mate_total, mate_reach = over_cores(keep, give)
    mate_beside = swap_across(mate_reach)
    keep, give = lent_score(spot, stay, lent_near, lent_far, [mine, other, near_a, near_b], give, self_reach)
    lent_total, lent_reach = over_cores(keep, give, lambda x: lax.ppermute(x, ("blk", "proj"), inner_cores))
    lent_beside = move(lent_reach, inner_across)
    returned = move((lent_total + lent_beside.astype(f32)).astype(bf16), outward).astype(f32)
    keep, give = score(
        spot, stay, rows, [near_a, near_b], [outer_near_a, outer_near_b], give, mate_reach, lent_reach, outer_away_b[0], away_b[1]
    )
    near_total, near_reach = over_cores(keep, give)
    near_beside = swap_across(near_reach)
    keep, give = score(spot, stay, rows, [away_a], [outer_away_a], give)
    away_total, reach = over_cores(keep, give)
    away_beside = swap_across(reach)
    out = put(out, self_total + self_beside.astype(f32), origins["self"], 0)

    size = queries // 2
    last = (give, lent_beside, self_beside)
    for i in range(2):
        near, give, facing, opposite = last_score(spot, stay, rows, away_b[i], outer_away_b[i], *last)
        cut = slice(i * size, (i + 1) * size)
        mine_total = away_total[:, cut] + swap_across(facing).astype(f32) + swap_diagonal(opposite).astype(f32)
        other_total = near + swap_cores(give).astype(f32) + away_beside[:, cut].astype(f32)
        out = put(out, mine_total, origins["away"], side * queries + i * size)
        out = put(out, other_total, origins["away"], (1 - side) * queries + i * size)
        last = (near,)

    out = put(out, mate_total + mate_beside.astype(f32) + returned[:, :2 * queries], origins["mate"], 0)
    out = put(out, near_total + near_beside.astype(f32) + returned[:, 2 * queries:], origins["near"], 0)
    return out


def solution(mesh):
    placed = (
        P(("grp", "blk"), "proj", None, None),
        P(("grp", "blk"), "proj", None, None),
        P(("grp", "blk"), None),
        P(("grp", "blk"), "proj"),
    )
    return jax.shard_map(
        on_device,
        mesh=mesh,
        in_specs=placed,
        out_specs=P(("grp", "blk", "proj"), None),
        check_vma=False,
    )
```

time: 161 us -> 207 us (1.29)
  starting transfers between devices: 18.6 us -> 48.8 us
  waiting for transfers between devices: 90.1 us -> 97.9 us
  other arithmetic: 5.26 us -> 9.96 us
    ppermute x18 -> x28, starting transfers between devices: 16.3 us -> 46.7 us  [the longest x27 45 us: move(): return lax.ppermute(x, 'blk', pairs)]
    ppermute x18 -> x28, waiting for transfers between devices: 88.7 us -> 97.2 us  [the longest x27 97.2 us: move(): return lax.ppermute(x, 'blk', pairs)]
    dynamic_update_slice x7, other arithmetic: 1.13 us -> 4.82 us  [put(): lax.dynamic_update_slice_in_dim(out, total, origin * (2 * queries) + at, 1)]
    convert_element_type x4 -> x7, other arithmetic: 2.69 us -> 4.53 us  [the longest x5 2.93 us: over_cores(): got = swap(give).astype(f32)]
    pallas_call x6 -> x7, Pallas kernels: 24.1 us -> 25.2 us  [the longest x4 16.7 us: score(): pl.pallas_call(functools.partial(score_body, stay, (len(blocks), len(oute...]
    unnamed x38 -> x48, local copies, waits for them, and re-layouts: 7.67 us -> 7.46 us
  transfers between devices with their start and end apart: 26 -> 36, of which waited for: 11 -> 14; matrix products, arithmetic and copies ran while one was open for 3% -> 5% of each run, Pallas kernels for 23% -> 15%
where the time goes in v8:
time: 207 us; the launch traced here: 206 us
  waiting for transfers between devices  97.9 us (47%)
  starting transfers between devices  48.8 us (24%)
  Pallas kernels  40 us (19%)
  other arithmetic  9.96 us (5%)
  local copies, waits for them, and re-layouts  8.89 us (4%)
    ppermute x27, waiting for transfers between devices, move(): return lax.ppermute(x, 'blk', pairs)  97.2 us
    ppermute x27, starting transfers between devices, move(): return lax.ppermute(x, 'blk', pairs)  45 us
    pallas_call x4, Pallas kernels, score(): pl.pallas_call(functools.partial(score_body, stay, (len(blocks), len(oute...  16.7 us
    pallas_call x1, Pallas kernels, form(): pl.pallas_call(functools.partial(form_body, rows, rank), grid_spec=pltpu....  13.5 us
    unnamed x48, local copies, waits for them, and re-layouts  7.46 us
    pallas_call x2, Pallas kernels, last_score(): pl.pallas_call(functools.partial(last_body, stay), in_specs=[SCALARS] + [...  5.24 us
    dynamic_update_slice x7, other arithmetic, put(): lax.dynamic_update_slice_in_dim(out, total, origin * (2 * queries) + at, 1)  4.82 us
  transfers between devices with their start and end apart: 36, of which 14 were waited for; matrix products, arithmetic and copies ran while one was open for 5% of the time, Pallas kernels for 15%

profile of v8, /device:TPU:0, one launch (start us, length us, event | category | flops | bytes accessed | tf_op | source)
XLA Modules:
  0.0 206.1 jit_solution(4945221687243548719)
XLA Ops:
  0.1 1.6 copy-done.6
  1.7 1.3 shard_map.47
  3.0 5.0 %collective-permute-start = (bf16[256,2048]{1,0:T(8,128)(2,1)S(1)}, bf16[256,2048]{1,0:T(8,128)(2,1)S(1)}, u32[]{:S(2)}, u32[]{:S(2)}) collective-permute-start(bf16[256,2048]{1,0:T(8,128)(2,1)S(1)} %get-tuple-element.43.refs_0_), channel_id=1, source_target_pairs={{0,4},{2,6},{12,8},{14,10},{1,5},{3,7},{13,9},{15,11},{16,20},{18,... | collective-permute-start | bytes 3145736 | tf_op jit(solution)/shard_map/ppermute | solution.py:268
  8.0 0.7 collective-permute-start.1
  8.7 1.6 collective-permute-start.2
  10.3 1.3 collective-permute-start.3
  11.6 13.5 %shard_map.46 = (bf16[512,2048]{1,0:T(8,128)(2,1)S(1)}, bf16[512,768]{1,0:T(8,128)(2,1)S(1)}, bf16[512,1280]{1,0:T(8,128)(2,1)S(1)}, bf16[512,768]{1,0:T(8,128)(2,1)S(1)}) custom-call(s32[3]{0:T(128)S(1)} %pad_add_fusion.spot, bf16[512,64,128]{2,1,0:T(8,128)(2,1)} %bitcast.5, bf16[512,64,128]{2,1,0:T(8,128)(2,1)} %bitcast.6, s32[512,128]{1,0:T(8,128)S(1)} %copy-done.16), custom_call_target="tpu_custom_call" | custom-call | flops 10737418240 | bytes 20971520 | tf_op jit(solution)/shard_map/pallas_call | solution.py:91
  25.1 1.3 copy-done.2
  26.4 1.7 collective-permute-done.3.refs_5_.refs_2_
  28.1 2.2 %collective-permute-done.refs_2_ = bf16[256,2048]{1,0:T(8,128)(2,1)S(1)} collective-permute-done((bf16[256,2048]{1,0:T(8,128)(2,1)S(1)}, bf16[256,2048]{1,0:T(8,128)(2,1)S(1)}, u32[]{:S(2)}, u32[]{:S(2)}) %collective-permute-start) | collective-permute-done | bytes 1048608 | tf_op jit(solution)/shard_map/ppermute | solution.py:268
  30.3 3.1 %collective-permute-done.2.refs_4_ = bf16[256,2048]{1,0:T(8,128)(2,1)S(1)} collective-permute-done((bf16[256,2048]{1,0:T(8,128)(2,1)S(1)}, bf16[256,2048]{1,0:T(8,128)(2,1)S(1)}, u32[]{:S(2)}, u32[]{:S(2)}) %collective-permute-start.2) | collective-permute-done | bytes 1048608 | tf_op jit(solution)/shard_map/ppermute | solution.py:268
  33.4 1.5 collective-permute-start.4
  34.9 0.7 collective-permute-start.5
  35.6 5.7 %collective-permute-start.6 = (bf16[256,2048]{1,0:T(8,128)(2,1)S(1)}, bf16[256,2048]{1,0:T(8,128)(2,1)S(1)}, u32[]{:S(2)}, u32[]{:S(2)}) collective-permute-start(bf16[256,2048]{1,0:T(8,128)(2,1)S(1)} %get-tuple-element.50.refs_3_), channel_id=1, source_target_pairs={{0,4},{2,6},{12,8},{14,10},{1,5},{3,7},{13,9},{15,11},{16,20},{18,... | collective-permute-start | bytes 3145736 | tf_op jit(solution)/shard_map/ppermute | solution.py:268
  41.4 1.3 collective-permute-start.7
  42.8 1.3 collective-permute-start.8
  44.1 16.9 %collective-permute-done.7.refs_5_.refs_3_ = bf16[256,1280]{1,0:T(8,128)(2,1)S(1)} collective-permute-done((bf16[256,1280]{1,0:T(8,128)(2,1)S(1)}, bf16[256,1280]{1,0:T(8,128)(2,1)S(1)}, u32[]{:S(2)}, u32[]{:S(2)}) %collective-permute-start.7) | collective-permute-done | bytes 655392 | tf_op jit(solution)/shard_map/ppermute | solution.py:268
  61.0 10.9 %collective-permute-done.8.refs_6_.refs_2_ = bf16[256,1280]{1,0:T(8,128)(2,1)S(1)} collective-permute-done((bf16[256,1280]{1,0:T(8,128)(2,1)S(1)}, bf16[256,1280]{1,0:T(8,128)(2,1)S(1)}, u32[]{:S(2)}, u32[]{:S(2)}) %collective-permute-start.8) | collective-permute-done | bytes 655392 | tf_op jit(solution)/shard_map/ppermute | solution.py:268
  71.9 1.0 copy-done
  73.0 0.8 copy-done.12
  73.8 0.7 collective-permute-start.10
  74.6 1.3 collective-permute-start.11
  76.4 4.6 %collective-permute-start.12 = (bf16[512,768]{1,0:T(8,128)(2,1)S(1)}, bf16[512,768]{1,0:T(8,128)(2,1)S(1)}, u32[]{:S(2)}, u32[]{:S(2)}) collective-permute-start(bf16[512,768]{1,0:T(8,128)(2,1)S(1)} %get-tuple-element.55), channel_id=1, source_target_pairs={{0,4},{2,6},{12,8},{14,10},{1,5},{3,7},{13,9},{15,11},{16,20},{18,... | collective-permute-start | bytes 2359304 | tf_op jit(solution)/shard_map/ppermute | solution.py:268
  81.1 11.3 %collective-permute-done.9.far_lent = bf16[512,768]{1,0:T(8,128)(2,1)S(1)} collective-permute-done((bf16[512,768]{1,0:T(8,128)(2,1)S(1)}, bf16[512,768]{1,0:T(8,128)(2,1)S(1)}, u32[]{:S(2)}, u32[]{:S(2)}) %collective-permute-start.9) | collective-permute-done | bytes 786464 | tf_op jit(solution)/shard_map/ppermute | solution.py:268
  92.4 4.4 %collective-permute-start.16 = (bf16[512,768]{1,0:T(8,128)(2,1)S(1)}, bf16[512,768]{1,0:T(8,128)(2,1)S(1)}, u32[]{:S(2)}, u32[]{:S(2)}) collective-permute-start(bf16[512,768]{1,0:T(8,128)(2,1)S(1)} %collective-permute-done.9.far_lent), channel_id=1, source_target_pairs={{0,4},{2,6},{12,8},{14,10},{1,5},{3,7},{13,9},{15,11},{16,20},{18,... | collective-permute-start | bytes 2359304 | tf_op jit(solution)/shard_map/ppermute | solution.py:268
  96.8 1.3 collective-permute-start.15
  98.1 2.0 collective-permute-done.11.refs_3_.refs_1_
  100.1 1.0 copy-done.7
  101.1 4.3 %shard_map.50 = (f32[512,512]{1,0:T(8,128)S(1)}, bf16[512,512]{1,0:T(8,128)(2,1)S(1)}) custom-call(s32[3]{0:T(128)S(1)} %pad_add_fusion.spot, bf16[512,2048]{1,0:T(8,128)(2,1)} %copy-done.2, bf16[512,1280]{1,0:T(8,128)(2,1)} %copy-done, bf16[512,768]{1,0:T(8,128)(2,1)S(1)} %collective-permute-done.9.far_lent, ...), custom_call_target="tpu_custom_call" | custom-call | flops 1024 | bytes 1024 | tf_op jit(solution)/shard_map/pallas_call | solution.py:168
  105.6 1.0 fusion.17
  106.6 1.4 collective-permute-start.17
  108.3 3.0 %collective-permute-done.16.refs_6_.far = bf16[512,768]{1,0:T(8,128)(2,1)S(1)} collective-permute-done((bf16[512,768]{1,0:T(8,128)(2,1)S(1)}, bf16[512,768]{1,0:T(8,128)(2,1)S(1)}, u32[]{:S(2)}, u32[]{:S(2)}) %collective-permute-start.16) | collective-permute-done | bytes 786464 | tf_op jit(solution)/shard_map/ppermute | solution.py:268
  111.3 1.3 collective-permute-done.15.refs_5_.refs_3_
  112.6 5.2 %shard_map.51 = (f32[512,512]{1,0:T(8,128)S(1)}, bf16[512,512]{1,0:T(8,128)(2,1)}) custom-call(s32[3]{0:T(128)S(1)} %pad_add_fusion.spot, bf16[512,2048]{1,0:T(8,128)(2,1)} %copy-done.2, bf16[512,1280]{1,0:T(8,128)(2,1)} %copy-done, bf16[512,768]{1,0:T(8,128)(2,1)S(1)} %collective-permute-done.9.far_lent, bf16[256,2048]{1,0:T(8,128)(2,1)} %copy-done.11, ...), custom_call_target="tpu_custom_call" | custom-call | flops 5368709120 | bytes 1024 | tf_op jit(solution)/shard_map/pallas_call | solution.py:168
  117.8 3.2 %shard_map.52 = (f32[512,1024]{1,0:T(8,128)}, bf16[512,1024]{1,0:T(8,128)(2,1)}) custom-call(s32[3]{0:T(128)S(1)} %pad_add_fusion.spot, bf16[512,768]{1,0:T(8,128)(2,1)S(1)} %collective-permute-done.12.refs_4_.near, bf16[512,768]{1,0:T(8,128)(2,1)S(1)} %collective-permute-done.16.refs_6_.far, bf16[256,2048]{1,0:T(8,128)(2,1)S(1)} %get-tuple-element.43.refs_0_, ...), custom_call_target="tpu_custom_call" | custom-call | flops 4026531840 | bytes 1024 | tf_op jit(solution)/shard_map/pallas_call | solution.py:200
  121.0 1.7 collective-permute-start.19
  122.7 1.5 collective-permute-start.21
  124.2 1.3 collective-permute-start.20
  125.5 1.3 collective-permute-start.28
  126.8 0.6 collective-permute-start.14
  127.3 1.2 convert_element_type.75
  128.6 0.9 copy-done.17
  129.5 1.5 convert_element_type.77
  131.2 0.8 collective-permute-start.23
  132.1 21.8 %collective-permute-done.20.refs_7_.outer = bf16[128,2048]{1,0:T(8,128)(2,1)S(1)} collective-permute-done((bf16[128,2048]{1,0:T(8,128)(2,1)}, bf16[128,2048]{1,0:T(8,128)(2,1)S(1)}, u32[]{:S(2)}, u32[]{:S(2)}) %collective-permute-start.20) | collective-permute-done | bytes 524320 | tf_op jit(solution)/shard_map/ppermute | solution.py:268
  153.9 4.3 %shard_map.53 = (f32[512,512]{1,0:T(8,128)S(1)}, bf16[512,512]{1,0:T(8,128)(2,1)S(1)}) custom-call(s32[3]{0:T(128)S(1)} %pad_add_fusion.spot, bf16[512,2048]{1,0:T(8,128)(2,1)} %copy-done.2, bf16[512,1280]{1,0:T(8,128)(2,1)} %copy-done, bf16[512,768]{1,0:T(8,128)(2,1)S(1)} %collective-permute-done.9.far_lent, bf16[256,2048]{1,0:T(8,128)(2,1)} %copy-done.5, ...), custom_call_target="tpu_custom_call" | custom-call | flops 5368709120 | bytes 1024 | tf_op jit(solution)/shard_map/pallas_call | solution.py:168
  158.3 2.9 %shard_map.54 = (f32[512,256]{1,0:T(8,128)S(1)}, bf16[512,256]{1,0:T(8,128)(2,1)S(1)}) custom-call(s32[3]{0:T(128)S(1)} %pad_add_fusion.spot, bf16[512,2048]{1,0:T(8,128)(2,1)} %copy-done.2, bf16[512,1280]{1,0:T(8,128)(2,1)S(1)} %copy-done.1, bf16[512,768]{1,0:T(8,128)(2,1)S(1)} %collective-permute-done.9.far_lent, ...), custom_call_target="tpu_custom_call" | custom-call | flops 2684354560 | bytes 1024 | tf_op jit(solution)/shard_map/pallas_call | solution.py:168
  163.6 1.6 collective-permute-start.27
  166.0 2.9 %shard_map.55 = (f32[256,128]{1,0:T(8,128)S(1)}, bf16[256,128]{1,0:T(8,128)(2,1)S(1)}, bf16[256,128]{1,0:T(8,128)(2,1)S(1)}, bf16[256,128]{1,0:T(8,128)(2,1)S(1)}) custom-call(s32[3]{0:T(128)S(1)} %pad_add_fusion.spot, bf16[512,2048]{1,0:T(8,128)(2,1)} %copy-done.2, bf16[512,1280]{1,0:T(8,128)(2,1)S(1)} %copy-done.1, ...), custom_call_target="tpu_custom_call" | custom-call | flops 1073741824 | bytes 1024 | tf_op jit(solution)/shard_map/pallas_call | solution.py:229
  168.9 1.6 collective-permute-start.24
  170.5 1.5 fusion.1
  172.1 2.3 %shard_map.56 = (f32[256,128]{1,0:T(8,128)S(1)}, bf16[256,128]{1,0:T(8,128)(2,1)S(1)}, bf16[256,128]{1,0:T(8,128)(2,1)S(1)}, bf16[256,128]{1,0:T(8,128)(2,1)S(1)}) custom-call(s32[3]{0:T(128)S(1)} %pad_add_fusion.spot, bf16[512,2048]{1,0:T(8,128)(2,1)S(1)} %copy-done.3, bf16[512,1280]{1,0:T(8,128)(2,1)S(1)} %copy-done.1, ...), custom_call_target="tpu_custom_call" | custom-call | flops 1073741824 | bytes 1024 | tf_op jit(solution)/shard_map/pallas_call | solution.py:229
  174.4 7.4 %collective-permute-done.24 = bf16[256,128]{1,0:T(8,128)(2,1)S(1)} collective-permute-done((bf16[256,128]{1,0:T(8,128)(2,1)S(1)}, bf16[256,128]{1,0:T(8,128)(2,1)S(1)}, u32[]{:S(2)}, u32[]{:S(2)}) %collective-permute-start.24) | collective-permute-done | bytes 65568 | tf_op jit(solution)/shard_map/ppermute | solution.py:268
  181.9 1.3 collective-permute-start.33
  183.2 0.7 fusion.16
  184.5 1.3 collective-permute-start.30
  185.8 0.7 add_dynamic-update-slice_fusion.1
  186.5 2.4 %collective-permute-done.29 = bf16[256,128]{1,0:T(8,128)(2,1)S(1)} collective-permute-done((bf16[256,128]{1,0:T(8,128)(2,1)S(1)}, bf16[256,128]{1,0:T(8,128)(2,1)S(1)}, u32[]{:S(2)}, u32[]{:S(2)}) %collective-permute-start.29) | collective-permute-done | bytes 65568 | tf_op jit(solution)/shard_map/ppermute | solution.py:268
  188.8 0.6 collective-permute-done.30
  189.4 0.7 fusion.14
  190.1 0.7 add_dynamic-update-slice_fusion
  190.8 13.2 %collective-permute-done.33 = bf16[256,1024]{1,0:T(8,128)(2,1)S(1)} collective-permute-done((bf16[256,1024]{1,0:T(8,128)(2,1)S(1)}, bf16[256,1024]{1,0:T(8,128)(2,1)S(1)}, u32[]{:S(2)}, u32[]{:S(2)}) %collective-permute-start.33) | collective-permute-done | bytes 524320 | tf_op jit(solution)/shard_map/ppermute | solution.py:268
  204.1 1.0 fusion.6
  205.1 1.0 fusion.3
  (92 shorter events, 5.5 us)
Async XLA Ops:
  0.1 1.6 copy-start.6
  1.7 9.9 %copy-start.16 = (s32[512,128]{1,0:T(8,128)S(1)}, s32[512,128]{1,0:T(8,128)}, u32[]{:S(2)}) copy-start(s32[512,128]{1,0:T(8,128)} %mask.1) | copy-start | bytes 786436
  3.0 27.3 %collective-permute-start = (bf16[256,2048]{1,0:T(8,128)(2,1)S(1)}, bf16[256,2048]{1,0:T(8,128)(2,1)S(1)}, u32[]{:S(2)}, u32[]{:S(2)}) collective-permute-start(bf16[256,2048]{1,0:T(8,128)(2,1)S(1)} %get-tuple-element.43.refs_0_), channel_id=1, source_target_pairs={{0,4},{2,6},{12,8},{14,10},{1,5},{3,7},{13,9},{15,11},{16,20},{18,... | collective-permute-start | bytes 3145736 | tf_op jit(solution)/shard_map/ppermute | solution.py:268
  8.0 22.3 %collective-permute-start.1 = (bf16[256,2048]{1,0:T(8,128)(2,1)S(1)}, bf16[256,2048]{1,0:T(8,128)(2,1)S(1)}, u32[]{:S(2)}, u32[]{:S(2)}) collective-permute-start(bf16[256,2048]{1,0:T(8,128)(2,1)S(1)} %get-tuple-element.43.refs_0_), channel_id=1, source_target_pairs={{4,8},{6,10},{8,4},{10,6},{5,9},{7,11},{9,5},{11,7},{20,24},{22,26... | collective-permute-start | bytes 3145736 | tf_op jit(solution)/shard_map/ppermute | solution.py:268
  8.7 24.7 %collective-permute-start.2 = (bf16[256,2048]{1,0:T(8,128)(2,1)S(1)}, bf16[256,2048]{1,0:T(8,128)(2,1)S(1)}, u32[]{:S(2)}, u32[]{:S(2)}) collective-permute-start(bf16[256,2048]{1,0:T(8,128)(2,1)S(1)} %get-tuple-element.44), channel_id=1, source_target_pairs={{0,2},{2,0},{4,6},{6,4},{8,10},{10,8},{12,14},{14,12},{1,3},{3,1},... | collective-permute-start | bytes 3145736 | tf_op jit(solution)/shard_map/ppermute | solution.py:268
  10.3 17.8 %collective-permute-start.3 = (bf16[256,1280]{1,0:T(8,128)(2,1)S(1)}, bf16[256,1280]{1,0:T(8,128)(2,1)S(1)}, u32[]{:S(2)}, u32[]{:S(2)}) collective-permute-start(bf16[256,1280]{1,0:T(8,128)(2,1)S(1)} %get-tuple-element.45), channel_id=1, source_target_pairs={{4,0},{6,2},{8,12},{10,14},{5,1},{7,3},{9,13},{11,15},{20,16},{22,... | collective-permute-start | bytes 1966088 | tf_op jit(solution)/shard_map/ppermute | solution.py:268
  25.1 1.3 copy-start.2
  33.4 39.6 %copy-start.5 = (bf16[256,2048]{1,0:T(8,128)(2,1)}, bf16[256,2048]{1,0:T(8,128)(2,1)S(1)}, u32[]{:S(2)}) copy-start(bf16[256,2048]{1,0:T(8,128)(2,1)S(1)} %get-tuple-element.51.refs_2_.refs_0_) | copy-start | bytes 3145732
  33.4 39.6 %copy-start.11 = (bf16[256,2048]{1,0:T(8,128)(2,1)}, bf16[256,2048]{1,0:T(8,128)(2,1)S(1)}, u32[]{:S(2)}) copy-start(bf16[256,2048]{1,0:T(8,128)(2,1)S(1)} %get-tuple-element.49.refs_0_) | copy-start | bytes 3145732
  33.4 38.5 %collective-permute-start.4 = (bf16[512,1280]{1,0:T(8,128)(2,1)S(1)}, bf16[512,1280]{1,0:T(8,128)(2,1)S(1)}, u32[]{:S(2)}, u32[]{:S(2)}) collective-permute-start(bf16[512,1280]{1,0:T(8,128)(2,1)S(1)} %get-tuple-element.46), channel_id=1, source_target_pairs={{0,2},{2,0},{4,6},{6,4},{8,10},{10,8},{12,14},{14,12},{1,3},{3,1},... | collective-permute-start | bytes 3932168 | tf_op jit(solution)/shard_map/ppermute | solution.py:268
  34.9 37.0 %collective-permute-start.5 = (bf16[256,2048]{1,0:T(8,128)(2,1)S(1)}, bf16[256,2048]{1,0:T(8,128)(2,1)S(1)}, u32[]{:S(2)}, u32[]{:S(2)}) collective-permute-start(bf16[256,2048]{1,0:T(8,128)(2,1)S(1)} %get-tuple-element.49.refs_0_), channel_id=1, source_target_pairs={{4,8},{6,10},{8,4},{10,6},{5,9},{7,11},{9,5},{11,7},{20,24},{22,26... | collective-permute-start | bytes 3145736 | tf_op jit(solution)/shard_map/ppermute | solution.py:268
  35.6 36.3 %collective-permute-start.6 = (bf16[256,2048]{1,0:T(8,128)(2,1)S(1)}, bf16[256,2048]{1,0:T(8,128)(2,1)S(1)}, u32[]{:S(2)}, u32[]{:S(2)}) collective-permute-start(bf16[256,2048]{1,0:T(8,128)(2,1)S(1)} %get-tuple-element.50.refs_3_), channel_id=1, source_target_pairs={{0,4},{2,6},{12,8},{14,10},{1,5},{3,7},{13,9},{15,11},{16,20},{18,... | collective-permute-start | bytes 3145736 | tf_op jit(solution)/shard_map/ppermute | solution.py:268
  41.4 19.6 %collective-permute-start.7 = (bf16[256,1280]{1,0:T(8,128)(2,1)S(1)}, bf16[256,1280]{1,0:T(8,128)(2,1)S(1)}, u32[]{:S(2)}, u32[]{:S(2)}) collective-permute-start(bf16[256,1280]{1,0:T(8,128)(2,1)S(1)} %slice.87), channel_id=1, source_target_pairs={{4,0},{6,2},{8,12},{10,14},{5,1},{7,3},{9,13},{11,15},{20,16},{22,... | collective-permute-start | bytes 1966088 | tf_op jit(solution)/shard_map/ppermute | solution.py:268
  42.8 29.2 %collective-permute-start.8 = (bf16[256,1280]{1,0:T(8,128)(2,1)S(1)}, bf16[256,1280]{1,0:T(8,128)(2,1)S(1)}, u32[]{:S(2)}, u32[]{:S(2)}) collective-permute-start(bf16[256,1280]{1,0:T(8,128)(2,1)S(1)} %slice.88), channel_id=1, source_target_pairs={{4,0},{6,2},{8,12},{10,14},{5,1},{7,3},{9,13},{11,15},{20,16},{22,... | collective-permute-start | bytes 1966088 | tf_op jit(solution)/shard_map/ppermute | solution.py:268
  71.9 1.1 copy-start
  73.0 0.8 copy-start.12
  73.8 31.7 %copy-start.4 = (bf16[256,2048]{1,0:T(8,128)(2,1)}, bf16[256,2048]{1,0:T(8,128)(2,1)S(1)}, u32[]{:S(2)}) copy-start(bf16[256,2048]{1,0:T(8,128)(2,1)S(1)} %get-tuple-element.58.refs_1_) | copy-start | bytes 3145732
  73.8 22.9 %collective-permute-start.10 = (bf16[256,2048]{1,0:T(8,128)(2,1)S(1)}, bf16[256,2048]{1,0:T(8,128)(2,1)S(1)}, u32[]{:S(2)}, u32[]{:S(2)}) collective-permute-start(bf16[256,2048]{1,0:T(8,128)(2,1)S(1)} %get-tuple-element.53.refs_1_), channel_id=1, source_target_pairs={{4,8},{6,10},{8,4},{10,6},{5,9},{7,11},{9,5},{11,7},{20,24},{22,26... | collective-permute-start | bytes 3145736 | tf_op jit(solution)/shard_map/ppermute | solution.py:268
  74.6 25.6 %collective-permute-start.11 = (bf16[256,2048]{1,0:T(8,128)(2,1)S(1)}, bf16[256,2048]{1,0:T(8,128)(2,1)S(1)}, u32[]{:S(2)}, u32[]{:S(2)}) collective-permute-start(bf16[256,2048]{1,0:T(8,128)(2,1)S(1)} %get-tuple-element.54.refs_0_), channel_id=1, source_target_pairs={{4,0},{6,2},{8,12},{10,14},{5,1},{7,3},{9,13},{11,15},{20,16},{22,... | collective-permute-start | bytes 3145736 | tf_op jit(solution)/shard_map/ppermute | solution.py:268
  75.9 16.5 %collective-permute-start.9 = (bf16[512,768]{1,0:T(8,128)(2,1)S(1)}, bf16[512,768]{1,0:T(8,128)(2,1)S(1)}, u32[]{:S(2)}, u32[]{:S(2)}) collective-permute-start(bf16[512,768]{1,0:T(8,128)(2,1)S(1)} %get-tuple-element.52), channel_id=1, source_target_pairs={{0,2},{2,0},{4,6},{6,4},{8,10},{10,8},{12,14},{14,12},{1,3},{3,1},... | collective-permute-start | bytes 2359304 | tf_op jit(solution)/shard_map/ppermute | solution.py:268
  76.4 21.7 %collective-permute-start.12 = (bf16[512,768]{1,0:T(8,128)(2,1)S(1)}, bf16[512,768]{1,0:T(8,128)(2,1)S(1)}, u32[]{:S(2)}, u32[]{:S(2)}) collective-permute-start(bf16[512,768]{1,0:T(8,128)(2,1)S(1)} %get-tuple-element.55), channel_id=1, source_target_pairs={{0,4},{2,6},{12,8},{14,10},{1,5},{3,7},{13,9},{15,11},{16,20},{18,... | collective-permute-start | bytes 2359304 | tf_op jit(solution)/shard_map/ppermute | solution.py:268
  92.4 18.9 %collective-permute-start.16 = (bf16[512,768]{1,0:T(8,128)(2,1)S(1)}, bf16[512,768]{1,0:T(8,128)(2,1)S(1)}, u32[]{:S(2)}, u32[]{:S(2)}) collective-permute-start(bf16[512,768]{1,0:T(8,128)(2,1)S(1)} %collective-permute-done.9.far_lent), channel_id=1, source_target_pairs={{0,4},{2,6},{12,8},{14,10},{1,5},{3,7},{13,9},{15,11},{16,20},{18,... | collective-permute-start | bytes 2359304 | tf_op jit(solution)/shard_map/ppermute | solution.py:268
  96.8 3.4 %copy-start.21 = (bf16[256,2048]{1,0:T(8,128)(2,1)}, bf16[256,2048]{1,0:T(8,128)(2,1)S(1)}, u32[]{:S(2)}) copy-start(bf16[256,2048]{1,0:T(8,128)(2,1)S(1)} %collective-permute-done.10.refs_2_.refs_3_.refs_1_) | copy-start | bytes 3145732
  96.8 15.7 %collective-permute-start.15 = (bf16[256,1280]{1,0:T(8,128)(2,1)S(1)}, bf16[256,1280]{1,0:T(8,128)(2,1)S(1)}, u32[]{:S(2)}, u32[]{:S(2)}) collective-permute-start(bf16[256,1280]{1,0:T(8,128)(2,1)S(1)} %slice.118), channel_id=1, source_target_pairs={{4,0},{6,2},{8,12},{10,14},{5,1},{7,3},{9,13},{11,15},{20,16},{22,... | collective-permute-start | bytes 1966088 | tf_op jit(solution)/shard_map/ppermute | solution.py:268
  100.1 1.0 copy-start.7
  105.5 2.8 %copy-start.9 = (f32[512,512]{1,0:T(8,128)}, f32[512,512]{1,0:T(8,128)S(1)}, u32[]{:S(2)}) copy-start(f32[512,512]{1,0:T(8,128)S(1)} %get-tuple-element.56) | copy-start | bytes 3145732
  105.5 2.6 %collective-permute-start.13 = (bf16[512,512]{1,0:T(8,128)(2,1)S(1)}, bf16[512,512]{1,0:T(8,128)(2,1)S(1)}, u32[]{:S(2)}, u32[]{:S(2)}) collective-permute-start(bf16[512,512]{1,0:T(8,128)(2,1)S(1)} %get-tuple-element.57.refs_4_), channel_id=1, source_target_pairs={{0,1},{1,0},{2,3},{3,2},{4,5},{5,4},{6,7},{7,6},{8,9},{9,8},{10,11... | collective-permute-start | bytes 1572872 | tf_op jit(solution)/shard_map/ppermute | solution.py:274
  106.6 1.7 collective-permute-start.17
  108.2 9.6 %copy-start.19 = (f32[512,512]{1,0:T(8,128)}, f32[512,512]{1,0:T(8,128)S(1)}, u32[]{:S(2)}) copy-start(f32[512,512]{1,0:T(8,128)S(1)} %convert_element_type.72) | copy-start | bytes 3145732
  112.6 5.2 %copy-start.14 = (bf16[256,1280]{1,0:T(8,128)(2,1)}, bf16[256,1280]{1,0:T(8,128)(2,1)S(1)}, u32[]{:S(2)}) copy-start(bf16[256,1280]{1,0:T(8,128)(2,1)S(1)} %collective-permute-done.15.refs_5_.refs_3_) | copy-start | bytes 1966084
  121.0 7.6 %collective-permute-start.19 = (bf16[512,1024]{1,0:T(8,128)(2,1)}, bf16[512,1024]{1,0:T(8,128)(2,1)}, u32[]{:S(2)}, u32[]{:S(2)}) collective-permute-start(bf16[512,1024]{1,0:T(8,128)(2,1)} %get-tuple-element.60.refs_4_), channel_id=1, source_target_pairs={{4,5},{5,4},{6,7},{7,6},{8,9},{9,8},{10,11},{11,10},{20,21},{21,20... | collective-permute-start | bytes 3145736 | tf_op jit(solution)/shard_map/ppermute | solution.py:340
  122.7 2.8 %collective-permute-start.21 = (bf16[128,2048]{1,0:T(8,128)(2,1)}, bf16[128,2048]{1,0:T(8,128)(2,1)}, u32[]{:S(2)}, u32[]{:S(2)}) collective-permute-start(bf16[128,2048]{1,0:T(8,128)(2,1)} %get-tuple-element.77), channel_id=1, source_target_pairs={{4,8},{6,10},{8,4},{10,6},{5,9},{7,11},{9,5},{11,7},{20,24},{22,26... | collective-permute-start | bytes 1572872 | tf_op jit(solution)/shard_map/ppermute | solution.py:268
  124.2 3.2 %collective-permute-start.18 = (bf16[512,512]{1,0:T(8,128)(2,1)}, bf16[512,512]{1,0:T(8,128)(2,1)}, u32[]{:S(2)}, u32[]{:S(2)}) collective-permute-start(bf16[512,512]{1,0:T(8,128)(2,1)} %get-tuple-element.59.refs_4_), channel_id=1, source_target_pairs={{0,1},{1,0},{2,3},{3,2},{4,5},{5,4},{6,7},{7,6},{8,9},{9,8},{10,11... | collective-permute-start | bytes 1572872 | tf_op jit(solution)/shard_map/ppermute | solution.py:274
  124.2 29.7 %collective-permute-start.20 = (bf16[128,2048]{1,0:T(8,128)(2,1)}, bf16[128,2048]{1,0:T(8,128)(2,1)S(1)}, u32[]{:S(2)}, u32[]{:S(2)}) collective-permute-start(bf16[128,2048]{1,0:T(8,128)(2,1)} %collective-permute-done.17.refs_7_.inner), channel_id=1, source_target_pairs={{4,0},{6,2},{8,12},{10,14},{5,1},{7,3},{9,13},{11,15},{20,16},{22,... | collective-permute-start | bytes 1572872 | tf_op jit(solution)/shard_map/ppermute | solution.py:268
  125.5 46.5 %collective-permute-start.28 = (bf16[128,2048]{1,0:T(8,128)(2,1)}, bf16[128,2048]{1,0:T(8,128)(2,1)S(1)}, u32[]{:S(2)}, u32[]{:S(2)}) collective-permute-start(bf16[128,2048]{1,0:T(8,128)(2,1)} %collective-permute-done.21.refs_8_.inner), channel_id=1, source_target_pairs={{4,0},{6,2},{8,12},{10,14},{5,1},{7,3},{9,13},{11,15},{20,16},{22,... | collective-permute-start | bytes 1572872 | tf_op jit(solution)/shard_map/ppermute | solution.py:268
  126.8 35.0 %collective-permute-start.14 = (bf16[256,512]{1,0:T(8,128)(2,1)S(1)}, bf16[256,512]{1,0:T(8,128)(2,1)S(1)}, u32[]{:S(2)}, u32[]{:S(2)}) collective-permute-start(bf16[256,512]{1,0:T(8,128)(2,1)S(1)} %fusion.9.refs_5_), channel_id=1, source_target_pairs={{0,2},{2,0},{4,6},{6,4},{8,10},{10,8},{12,14},{14,12},{1,3},{3,1},... | collective-permute-start | bytes 786440 | tf_op jit(solution)/shard_map/ppermute | solution.py:268
  128.5 1.0 copy-start.17
  128.5 2.5 %copy-start.22 = (f32[512,1024]{1,0:T(8,128)S(1)}, f32[512,1024]{1,0:T(8,128)}, u32[]{:S(2)}) copy-start(f32[512,1024]{1,0:T(8,128)} %get-tuple-element.62) | copy-start | bytes 6291460
  131.0 22.9 %copy-start.13 = (bf16[256,1280]{1,0:T(8,128)(2,1)S(1)}, bf16[256,1280]{1,0:T(8,128)(2,1)}, u32[]{:S(2)}) copy-start(bf16[256,1280]{1,0:T(8,128)(2,1)} %copy-done.12) | copy-start | bytes 1966084
  131.0 22.8 %copy-start.15 = (bf16[256,1280]{1,0:T(8,128)(2,1)S(1)}, bf16[256,1280]{1,0:T(8,128)(2,1)}, u32[]{:S(2)}) copy-start(bf16[256,1280]{1,0:T(8,128)(2,1)} %copy-done.14) | copy-start | bytes 1966084
  131.2 27.1 %copy-start.1 = (bf16[512,1280]{1,0:T(8,128)(2,1)S(1)}, bf16[512,1280]{1,0:T(8,128)(2,1)}, u32[]{:S(2)}) copy-start(bf16[512,1280]{1,0:T(8,128)(2,1)} %copy-done) | copy-start | bytes 3932164
  131.2 27.1 %copy-start.8 = (bf16[256,2048]{1,0:T(8,128)(2,1)S(1)}, bf16[256,2048]{1,0:T(8,128)(2,1)}, u32[]{:S(2)}) copy-start(bf16[256,2048]{1,0:T(8,128)(2,1)} %copy-done.7) | copy-start | bytes 3145732
  131.2 34.7 %collective-permute-start.23 = (bf16[256,1024]{1,0:T(8,128)(2,1)S(1)}, bf16[256,1024]{1,0:T(8,128)(2,1)S(1)}, u32[]{:S(2)}, u32[]{:S(2)}) collective-permute-start(bf16[256,1024]{1,0:T(8,128)(2,1)S(1)} %fusion.2.refs_6_), channel_id=1, source_target_pairs={{4,6},{6,4},{8,10},{10,8},{5,7},{7,5},{9,11},{11,9},{20,22},{22,20... | collective-permute-start | bytes 1572872 | tf_op jit(solution)/shard_map/ppermute | solution.py:268
  158.2 7.0 %collective-permute-start.34 = (bf16[512,512]{1,0:T(8,128)(2,1)S(1)}, bf16[512,512]{1,0:T(8,128)(2,1)S(1)}, u32[]{:S(2)}, u32[]{:S(2)}) collective-permute-start(bf16[512,512]{1,0:T(8,128)(2,1)S(1)} %get-tuple-element.63.refs_2_), channel_id=1, source_target_pairs={{0,1},{1,0},{2,3},{3,2},{4,5},{5,4},{6,7},{7,6},{8,9},{9,8},{10,11... | collective-permute-start | bytes 1572872 | tf_op jit(solution)/shard_map/ppermute | solution.py:274
  161.2 1.2 copy-start.10
  161.2 1.5 copy-start.20
  161.2 2.2 %collective-permute-start.22 = (bf16[512,256]{1,0:T(8,128)(2,1)S(1)}, bf16[512,256]{1,0:T(8,128)(2,1)S(1)}, u32[]{:S(2)}, u32[]{:S(2)}) collective-permute-start(bf16[512,256]{1,0:T(8,128)(2,1)S(1)} %get-tuple-element.65.refs_0_), channel_id=1, source_target_pairs={{0,1},{1,0},{2,3},{3,2},{4,5},{5,4},{6,7},{7,6},{8,9},{9,8},{10,11... | collective-permute-start | bytes 786440 | tf_op jit(solution)/shard_map/ppermute | solution.py:274
  162.9 3.1 %copy-start.23 = (f32[256,2048]{1,0:T(8,128)}, f32[256,2048]{1,0:T(8,128)S(1)}, u32[]{:S(2)}) copy-start(f32[256,2048]{1,0:T(8,128)S(1)} %fusion.11) | copy-start | bytes 6291460
  162.9 41.2 %collective-permute-start.32 = (bf16[256,512]{1,0:T(8,128)(2,1)S(1)}, bf16[256,512]{1,0:T(8,128)(2,1)S(1)}, u32[]{:S(2)}, u32[]{:S(2)}) collective-permute-start(bf16[256,512]{1,0:T(8,128)(2,1)S(1)} %fusion.8.refs_5_), channel_id=1, source_target_pairs={{0,2},{2,0},{4,6},{6,4},{8,10},{10,8},{12,14},{14,12},{1,3},{3,1},... | collective-permute-start | bytes 786440 | tf_op jit(solution)/shard_map/ppermute | solution.py:268
  163.6 20.4 %collective-permute-start.27 = (bf16[256,256]{1,0:T(8,128)(2,1)S(1)}, bf16[256,256]{1,0:T(8,128)(2,1)S(1)}, u32[]{:S(2)}, u32[]{:S(2)}) collective-permute-start(bf16[256,256]{1,0:T(8,128)(2,1)S(1)} %get-tuple-element.75), channel_id=1, source_target_pairs={{0,2},{2,0},{4,6},{6,4},{8,10},{10,8},{12,14},{14,12},{1,3},{3,1},... | collective-permute-start | bytes 393224 | tf_op jit(solution)/shard_map/ppermute | solution.py:268
  165.4 39.7 %collective-permute-start.35 = (bf16[256,512]{1,0:T(8,128)(2,1)S(1)}, bf16[256,512]{1,0:T(8,128)(2,1)S(1)}, u32[]{:S(2)}, u32[]{:S(2)}) collective-permute-start(bf16[256,512]{1,0:T(8,128)(2,1)S(1)} %fusion.4), channel_id=1, source_target_pairs={{0,2},{2,0},{4,6},{6,4},{8,10},{10,8},{12,14},{14,12},{1,3},{3,1},... | collective-permute-start | bytes 786440 | tf_op jit(solution)/shard_map/ppermute | solution.py:268
  168.9 3.2 %copy-start.3 = (bf16[512,2048]{1,0:T(8,128)(2,1)S(1)}, bf16[512,2048]{1,0:T(8,128)(2,1)}, u32[]{:S(2)}) copy-start(bf16[512,2048]{1,0:T(8,128)(2,1)} %copy-done.2) | copy-start | bytes 6291460
  168.9 13.0 %collective-permute-start.24 = (bf16[256,128]{1,0:T(8,128)(2,1)S(1)}, bf16[256,128]{1,0:T(8,128)(2,1)S(1)}, u32[]{:S(2)}, u32[]{:S(2)}) collective-permute-start(bf16[256,128]{1,0:T(8,128)(2,1)S(1)} %get-tuple-element.66), channel_id=1, source_target_pairs={{0,2},{2,0},{4,6},{6,4},{8,10},{10,8},{12,14},{14,12},{1,3},{3,1},... | collective-permute-start | bytes 196616 | tf_op jit(solution)/shard_map/ppermute | solution.py:268
  172.0 11.1 %collective-permute-start.25 = (bf16[256,128]{1,0:T(8,128)(2,1)S(1)}, bf16[256,128]{1,0:T(8,128)(2,1)S(1)}, u32[]{:S(2)}, u32[]{:S(2)}) collective-permute-start(bf16[256,128]{1,0:T(8,128)(2,1)S(1)} %get-tuple-element.67), channel_id=1, source_target_pairs={{0,3},{1,2},{2,1},{3,0},{4,7},{5,6},{6,5},{7,4},{8,11},{9,10},{10,... | collective-permute-start | bytes 196616 | tf_op jit(solution)/shard_map/ppermute | solution.py:277
  174.4 29.7 %copy-start.18 = (f32[512,512]{1,0:T(8,128)S(1)}, f32[512,512]{1,0:T(8,128)}, u32[]{:S(2)}) copy-start(f32[512,512]{1,0:T(8,128)} %copy-done.17) | copy-start | bytes 3145732
  181.9 22.1 %collective-permute-start.33 = (bf16[256,1024]{1,0:T(8,128)(2,1)S(1)}, bf16[256,1024]{1,0:T(8,128)(2,1)S(1)}, u32[]{:S(2)}, u32[]{:S(2)}) collective-permute-start(bf16[256,1024]{1,0:T(8,128)(2,1)S(1)} %fusion.1), channel_id=1, source_target_pairs={{4,0},{6,2},{8,12},{10,14},{5,1},{7,3},{9,13},{11,15},{20,16},{22,... | collective-permute-start | bytes 1572872 | tf_op jit(solution)/shard_map/ppermute | solution.py:268
  183.2 1.3 collective-permute-start.26
  183.9 4.9 %collective-permute-start.29 = (bf16[256,128]{1,0:T(8,128)(2,1)S(1)}, bf16[256,128]{1,0:T(8,128)(2,1)S(1)}, u32[]{:S(2)}, u32[]{:S(2)}) collective-permute-start(bf16[256,128]{1,0:T(8,128)(2,1)S(1)} %get-tuple-element.70), channel_id=1, source_target_pairs={{0,2},{2,0},{4,6},{6,4},{8,10},{10,8},{12,14},{14,12},{1,3},{3,1},... | collective-permute-start | bytes 196616 | tf_op jit(solution)/shard_map/ppermute | solution.py:268
  184.5 4.9 %collective-permute-start.30 = (bf16[256,128]{1,0:T(8,128)(2,1)S(1)}, bf16[256,128]{1,0:T(8,128)(2,1)S(1)}, u32[]{:S(2)}, u32[]{:S(2)}) collective-permute-start(bf16[256,128]{1,0:T(8,128)(2,1)S(1)} %get-tuple-element.71), channel_id=1, source_target_pairs={{0,3},{1,2},{2,1},{3,0},{4,7},{5,6},{6,5},{7,4},{8,11},{9,10},{10,... | collective-permute-start | bytes 196616 | tf_op jit(solution)/shard_map/ppermute | solution.py:277
  188.8 1.3 collective-permute-start.31

commit v9 on v7

--- a/solution.py
+++ b/solution.py
@@ -21,31 +21,36 @@
     return jax.ShapeDtypeStruct(shape, kind)
 
 
-def prepare_body(spot, query_grads, mine, *sending):
+def prepare_body(spot, low, high, *outs):
     rank = LANES // 2
+    for m in range(low.shape[1] // LANES):
+        at = slice(m * LANES, (m + 1) * LANES)
+        even = jnp.concatenate([low[:, at][:, :rank], high[:, at][:, :rank]], 1)
+        odd = jnp.concatenate([low[:, at][:, rank:], high[:, at][:, rank:]], 1)
+        for i, out in enumerate(outs):
+            cut = slice(i * out.shape[0], (i + 1) * out.shape[0])
+            out[:, 2 * m * LANES:(2 * m + 1) * LANES] = even[cut, :]
+            out[:, (2 * m + 1) * LANES:(2 * m + 2) * LANES] = odd[cut, :]
+
+
+def prepare(query_grads, side, parts):
     rows, width = query_grads.shape
-    for outs, side in (((mine,), spot[0]), (sending, 1 - spot[0])):
-        for m in range(width // 4 // LANES):
-            at = pl.multiple_of(side * (width // 4) + m * LANES, LANES)
-            low = query_grads[:, pl.ds(at, LANES)]
-            high = query_grads[:, pl.ds(at + width // 2, LANES)]
-            even = jnp.concatenate([low[:, :rank], high[:, :rank]], 1)
-            odd = jnp.concatenate([low[:, rank:], high[:, rank:]], 1)
-            for i, out in enumerate(outs):
-                cut = slice(i * out.shape[0], (i + 1) * out.shape[0])
-                out[:, 2 * m * LANES:(2 * m + 1) * LANES] = even[cut, :]
-                out[:, (2 * m + 1) * LANES:(2 * m + 2) * LANES] = odd[cut, :]
-
-
-def prepare(query_grads, spot):
-    rows, width = query_grads.shape
+    steps = 2
+    take = width // 4 // steps
     return pl.pallas_call(
         prepare_body,
-        in_specs=[SCALARS, WHOLE],
-        out_specs=[WHOLE] * 3,
-        out_shape=[shaped(bf16, size, width // 2) for size in (rows, rows // 2, rows // 2)],
-        compiler_params=LIMIT,
-    )(spot, query_grads)
+        grid_spec=pltpu.PrefetchScalarGridSpec(
+            num_scalar_prefetch=1,
+            grid=(steps,),
+            in_specs=[
+                pl.BlockSpec((rows, take), lambda g, spot: (0, spot[0] * steps + g)),
+                pl.BlockSpec((rows, take), lambda g, spot: (0, (2 + spot[0]) * steps + g)),
+            ],
+            out_specs=[pl.BlockSpec((rows // parts, 2 * take), lambda g, spot: (0, g))] * parts,
+        ),
+        out_shape=[shaped(bf16, rows // parts, width // 2)] * parts,
+        compiler_params=LIMIT,
+    )(side.astype(jnp.int32).reshape(1), query_grads, query_grads)
 
 
 def form_body(rows, rank, spot, inputs, outgrads, mask, kept, sent, rounds):
@@ -112,19 +117,18 @@
 def score_body(count, spot, own, far, *refs):
     keep, give = refs[-2:]
     part = own.shape[0] // 2
-    rows = refs[0].shape[0]
     for i, block in enumerate(refs[:count]):
         size = block.shape[0]
-        if count == 1:
-            at = slice(None)
-        elif i == 0:
-            at = pl.ds(pl.multiple_of(spot[0] * rows, rows), size)
+        if count == 3:
+            rows = refs[0].shape[0]
+            at = spot[0] * rows if i == 0 else (1 - spot[0]) * rows + (i - 1) * size
+            columns = pl.ds(pl.multiple_of(at, size), size)
         else:
-            at = pl.ds(pl.multiple_of((1 - spot[0]) * rows + (i - 1) * size, size), size)
-        keep[:part, at] = dot(own[:part, :], block[...])
-        keep[part:, at] = dot(far[:part, :], block[...])
-        give[:part, at] = dot(own[part:, :], block[...]).astype(bf16)
-        give[part:, at] = dot(far[part:, :], block[...]).astype(bf16)
+            columns = pl.ds(i * size, size)
+        keep[:part, columns] = dot(own[:part, :], block[...])
+        keep[part:, columns] = dot(far[:part, :], block[...])
+        give[:part, columns] = dot(own[part:, :], block[...]).astype(bf16)
+        give[part:, columns] = dot(far[part:, :], block[...]).astype(bf16)
 
 
 def score(spot, own, far, blocks, *after):
@@ -188,8 +192,9 @@
     def swap_diagonal(x):
         return lax.ppermute(x, ("blk", "proj"), diagonal)
 
-    mine, *sending = prepare(query_grads, spot)
+    (mine,) = prepare(query_grads, side, 1)
     ahead = pass_on(mine)
+    sending = prepare(query_grads, 1 - side, 2)
     other = [swap_across(x) for x in sending]
     own, sent = form(
         doc_inputs.reshape(docs, *doc_inputs.shape[2:]), doc_outgrads.reshape(docs, *doc_outgrads.shape[2:]), token_mask, spot
@@ -214,29 +219,33 @@
         return keep[:part] + got[:part], (keep[part:] + got[part:]).astype(bf16)
 
     besides = []
-    last = ()
-    for step in range(places - 1):
-        if step == places - 2:
-            keep, give = score(spot, own, far, [first[-1]], *last)
-            final_own, final_far = over_cores(keep, give)
-            final_beside = swap_across(final_far)
-            last = (give,) + tuple(besides)
+    last = (first[2], second[1][0]) if places > 2 else ()
+    for step in range(places - 2):
         keep, give = score(spot, own, far, [first[step]] + second[step], *last)
         total, reach = over_cores(keep, give)
         besides.append(swap_across(reach))
         out = put(out, total + besides[-1].astype(f32), step, 0)
         last = (give,)
-    last = (give,)
+
+    keep, give = score(spot, own, far, first[-2:], *last)
+    early, early_reach = over_cores(keep, give)
+    early_beside = swap_across(early_reach)
+    keep, give = score(spot, own, far, second[-2], give, *besides)
+    late, late_reach = over_cores(keep, give)
+    late_beside = swap_across(late_reach)
+    out = put(out, early[:, :queries] + late_beside.astype(f32), places - 2, side * queries)
+    out = put(out, late + early_beside[:, :queries].astype(f32), places - 2, (1 - side) * queries)
 
     size = queries // 2
+    last = (give, early_beside)
     for i, piece in enumerate(pieces):
         near, give, facing, opposite = last_score(own, far, piece, *last)
-        cut = slice(i * size, (i + 1) * size)
-        mine_total = final_own[:, cut] + swap_across(facing).astype(f32) + swap_diagonal(opposite).astype(f32)
-        other_total = near + swap_cores(give).astype(f32) + final_beside[:, cut].astype(f32)
+        cut = slice(queries + i * size, queries + (i + 1) * size)
+        mine_total = early[:, cut] + swap_across(facing).astype(f32) + swap_diagonal(opposite).astype(f32)
+        other_total = near + swap_cores(give).astype(f32) + early_beside[:, cut].astype(f32)
         out = put(out, mine_total, places - 1, side * queries + i * size)
         out = put(out, other_total, places - 1, (1 - side) * queries + i * size)
-        last = (near, final_beside, reach)
+        last = (near, late_reach)
     return out
 
 

time: 161 us -> 168 us (1.043)
  waiting for transfers between devices: 90.1 us -> 96.4 us
    ppermute x9, waiting for transfers between devices: 71.3 us -> 85.8 us  [pass_on(): return lax.ppermute(x, 'blk', onward)]
    ppermute x9, waiting for transfers between devices: 17.4 us -> 10.5 us  [swap_across(): return lax.ppermute(x, 'blk', across)]
    convert_element_type x4, other arithmetic: 2.69 us -> 0.4 us  [over_cores(): got = swap_cores(give).astype(f32)]
    ppermute x6, starting transfers between devices: 1.29 us -> 3.56 us  [swap_cores(): return lax.ppermute(x, 'proj', [(0, 1), (1, 0)])]
    ppermute x9, starting transfers between devices: 9.9 us -> 7.82 us  [swap_across(): return lax.ppermute(x, 'blk', across)]
  transfers between devices with their start and end apart: 26 -> 26, of which waited for: 11 -> 8; matrix products, arithmetic and copies ran while one was open for 3% -> 2% of each run, Pallas kernels for 23% -> 23%
where the time goes in v9:
time: 168 us
  waiting for transfers between devices  96.4 us (57%)
  Pallas kernels  39.3 us (23%)
  starting transfers between devices  19.4 us (12%)
  local copies, waits for them, and re-layouts  7.57 us (5%)
  other arithmetic  4.52 us (3%)
    ppermute x9, waiting for transfers between devices, pass_on(): return lax.ppermute(x, 'blk', onward)  85.8 us
    pallas_call x4, Pallas kernels, score(): pl.pallas_call(functools.partial(score_body, count), in_specs=[SCALARS] +...  20.3 us
    pallas_call x1, Pallas kernels, form(): pl.pallas_call(functools.partial(form_body, rows, rank), grid_spec=pltpu....  13.4 us
    ppermute x9, waiting for transfers between devices, swap_across(): return lax.ppermute(x, 'blk', across)  10.5 us
    ppermute x9, starting transfers between devices, swap_across(): return lax.ppermute(x, 'blk', across)  7.82 us
    ppermute x9, starting transfers between devices, pass_on(): return lax.ppermute(x, 'blk', onward)  7.43 us
    unnamed x38, local copies, waits for them, and re-layouts  7.34 us
    ppermute x6, starting transfers between devices, swap_cores(): return lax.ppermute(x, 'proj', [(0, 1), (1, 0)])  3.56 us
  transfers between devices with their start and end apart: 26, of which 8 were waited for; matrix products, arithmetic and copies ran while one was open for 2% of the time, Pallas kernels for 23%

profile of v9, /device:TPU:0, one launch (start us, length us, event | category | flops | bytes accessed | tf_op | source)
XLA Modules:
  0.0 167.5 jit_solution(304130729482358132)
XLA Ops:
  0.0 1.6 copy-done.4
  1.6 0.7 shard_map.47.refs_0_
  2.3 3.1 %collective-permute-start = (bf16[256,2048]{1,0:T(8,128)(2,1)S(1)}, bf16[256,2048]{1,0:T(8,128)(2,1)}, u32[]{:S(2)}, u32[]{:S(2)}) collective-permute-start(bf16[256,2048]{1,0:T(8,128)(2,1)S(1)} %shard_map.47.refs_0_), channel_id=1, source_target_pairs={{0,4},{2,6},{4,8},{6,10},{8,12},{10,14},{12,0},{14,2},{1,5},{3,7},... | collective-permute-start | bytes 3145736 | tf_op jit(solution)/shard_map/ppermute | solution.py:190
  5.3 1.4 shard_map.48
  6.7 1.5 collective-permute-start.1
  8.2 0.5 collective-permute-start.2
  8.7 0.1 pad_add_fusion.spot
  8.8 13.4 %shard_map.46 = (bf16[512,2048]{1,0:T(8,128)(2,1)S(1)}, bf16[512,2048]{1,0:T(8,128)(2,1)S(1)}) custom-call(s32[2]{0:T(128)S(1)} %pad_add_fusion.spot, bf16[512,64,128]{2,1,0:T(8,128)(2,1)} %bitcast.5, bf16[512,64,128]{2,1,0:T(8,128)(2,1)} %bitcast.6, s32[512,128]{1,0:T(8,128)S(1)} %copy-done.12), custom_call_target="tpu_custom_call" | custom-call | flops 10737418240 | bytes 20971520 | tf_op jit(solution)/shard_map/pallas_call | solution.py:77
  22.2 0.0 copy-start
  22.2 1.3 copy-done
  23.5 0.0 collective-permute-done.1.refs_2_
  23.5 8.0 %collective-permute-done.2.refs_3_ = bf16[128,2048]{1,0:T(8,128)(2,1)S(1)} collective-permute-done((bf16[128,2048]{1,0:T(8,128)(2,1)}, bf16[128,2048]{1,0:T(8,128)(2,1)S(1)}, u32[]{:S(2)}, u32[]{:S(2)}) %collective-permute-start.2) | collective-permute-done | bytes 524320 | tf_op jit(solution)/shard_map/ppermute | solution.py:184
  31.6 0.0 collective-permute-done.refs_1_
  31.6 1.5 collective-permute-start.3
  33.1 1.6 collective-permute-start.4
  34.7 24.0 %collective-permute-done.4.refs_3_.refs_0_ = bf16[256,2048]{1,0:T(8,128)(2,1)S(1)} collective-permute-done((bf16[256,2048]{1,0:T(8,128)(2,1)}, bf16[256,2048]{1,0:T(8,128)(2,1)S(1)}, u32[]{:S(2)}, u32[]{:S(2)}) %collective-permute-start.4) | collective-permute-done | bytes 1048608 | tf_op jit(solution)/shard_map/ppermute | solution.py:190
  58.6 0.0 collective-permute-start.11
  58.6 1.2 collective-permute-start.5
  59.9 1.5 collective-permute-start.8
  61.3 36.4 %collective-permute-done.5.refs_4_.refs_1_ = bf16[128,2048]{1,0:T(8,128)(2,1)S(1)} collective-permute-done((bf16[128,2048]{1,0:T(8,128)(2,1)S(1)}, bf16[128,2048]{1,0:T(8,128)(2,1)S(1)}, u32[]{:S(2)}, u32[]{:S(2)}) %collective-permute-start.5) | collective-permute-done | bytes 524320 | tf_op jit(solution)/shard_map/ppermute | solution.py:190
  97.8 1.3 copy-done.2
  99.1 5.7 %shard_map.50 = (f32[512,512]{1,0:T(8,128)S(1)}, bf16[512,512]{1,0:T(8,128)(2,1)S(1)}) custom-call(s32[2]{0:T(128)S(1)} %pad_add_fusion.spot, bf16[512,2048]{1,0:T(8,128)(2,1)} %copy-done, bf16[512,2048]{1,0:T(8,128)(2,1)} %copy-done.2, bf16[256,2048]{1,0:T(8,128)(2,1)S(1)} %shard_map.47.refs_0_, bf16[128,2048]{1,0:T(8,128)(2,1)S(1)} %get-tuple-element.34.refs_1_, ...), custom_call_target="tpu_custom_call" | custom-call | flops 1024 | bytes 1024 | tf_op jit(solution)/shard_map/pallas_call | solution.py:138
  104.8 4.3 %collective-permute-done.8.refs_2_ = bf16[128,2048]{1,0:T(8,128)(2,1)} collective-permute-done((bf16[128,2048]{1,0:T(8,128)(2,1)S(1)}, bf16[128,2048]{1,0:T(8,128)(2,1)}, u32[]{:S(2)}, u32[]{:S(2)}) %collective-permute-start.8) | collective-permute-done | bytes 524320 | tf_op jit(solution)/shard_map/ppermute | solution.py:190
  109.1 6.1 %shard_map.51 = (f32[512,512]{1,0:T(8,128)S(1)}, bf16[512,512]{1,0:T(8,128)(2,1)S(1)}) custom-call(s32[2]{0:T(128)S(1)} %pad_add_fusion.spot, bf16[512,2048]{1,0:T(8,128)(2,1)} %copy-done, bf16[512,2048]{1,0:T(8,128)(2,1)} %copy-done.2, bf16[256,2048]{1,0:T(8,128)(2,1)} %get-tuple-element.36.refs_0_, ...), custom_call_target="tpu_custom_call" | custom-call | flops 1024 | bytes 1024 | tf_op jit(solution)/shard_map/pallas_call | solution.py:138
  115.2 0.1 collective-permute-start.9
  115.3 0.5 collective-permute-start.6
  115.8 4.6 %shard_map.52 = (f32[512,512]{1,0:T(8,128)S(1)}, bf16[512,512]{1,0:T(8,128)(2,1)S(1)}) custom-call(s32[2]{0:T(128)S(1)} %pad_add_fusion.spot, bf16[512,2048]{1,0:T(8,128)(2,1)} %copy-done, bf16[512,2048]{1,0:T(8,128)(2,1)} %copy-done.2, bf16[256,2048]{1,0:T(8,128)(2,1)S(1)} %collective-permute-done.4.refs_3_.refs_0_, ...), custom_call_target="tpu_custom_call" | custom-call | flops 1024 | bytes 1024 | tf_op jit(solution)/shard_map/pallas_call | solution.py:138
  120.4 0.1 collective-permute-start.12
  120.5 0.1 collective-permute-start.18
  120.6 0.1 convert_element_type.63
  120.7 0.9 fusion.1
  121.6 0.5 collective-permute-start.10
  122.1 0.1 convert_element_type.60
  122.3 0.9 fusion.4
  123.2 1.5 collective-permute-start.7
  124.7 0.1 convert_element_type.66
  124.9 1.1 fusion
  126.0 0.5 collective-permute-start.17
  126.5 10.7 %collective-permute-done.14.refs_1_ = bf16[128,2048]{1,0:T(8,128)(2,1)S(1)} collective-permute-done((bf16[128,2048]{1,0:T(8,128)(2,1)}, bf16[128,2048]{1,0:T(8,128)(2,1)S(1)}, u32[]{:S(2)}, u32[]{:S(2)}) %collective-permute-start.14) | collective-permute-done | bytes 524320 | tf_op jit(solution)/shard_map/ppermute | solution.py:190
  137.2 0.0 collective-permute-start.22
  137.3 1.0 copy-done.11
  138.3 4.0 %shard_map.53 = (f32[512,256]{1,0:T(8,128)S(1)}, bf16[512,256]{1,0:T(8,128)(2,1)S(1)}) custom-call(s32[2]{0:T(128)S(1)} %pad_add_fusion.spot, bf16[512,2048]{1,0:T(8,128)(2,1)S(1)} %copy-done.1, bf16[512,2048]{1,0:T(8,128)(2,1)} %copy-done.2, bf16[128,2048]{1,0:T(8,128)(2,1)} %collective-permute-done.13.refs_0_, ...), custom_call_target="tpu_custom_call" | custom-call | flops 1024 | bytes 1024 | tf_op jit(solution)/shard_map/pallas_call | solution.py:138
  142.3 0.1 collective-permute-start.15
  142.4 6.2 %collective-permute-done.18.block = bf16[128,2048]{1,0:T(8,128)(2,1)} collective-permute-done((bf16[128,2048]{1,0:T(8,128)(2,1)}, bf16[128,2048]{1,0:T(8,128)(2,1)}, u32[]{:S(2)}, u32[]{:S(2)}) %collective-permute-start.18) | collective-permute-done | bytes 524320 | tf_op jit(solution)/shard_map/ppermute | solution.py:190
  148.6 2.3 %shard_map.54 = (f32[256,128]{1,0:T(8,128)S(1)}, bf16[256,128]{1,0:T(8,128)(2,1)S(1)}, bf16[256,128]{1,0:T(8,128)(2,1)S(1)}, bf16[256,128]{1,0:T(8,128)(2,1)S(1)}) custom-call(bf16[512,2048]{1,0:T(8,128)(2,1)S(1)} %copy-done.1, bf16[512,2048]{1,0:T(8,128)(2,1)S(1)} %copy-done.3, bf16[128,2048]{1,0:T(8,128)(2,1)} %collective-permute-done.18.block, ...), custom_call_target="tpu_custom_call" | custom-call | flops 1024 | bytes 1024 | tf_op jit(solution)/shard_map/pallas_call | solution.py:159
  150.9 0.6 collective-permute-start.19
  151.5 0.0 collective-permute-start.20
  151.5 1.6 collective-permute-start.21
  153.1 0.2 broadcast_in_dim.3
  153.4 0.1 fusion.6
  153.6 0.6 collective-permute-start.16
  154.2 0.4 copy-done.7
  154.6 0.3 copy-done.14
  154.9 0.1 fusion.3
  155.0 4.2 %collective-permute-done.22.block = bf16[128,2048]{1,0:T(8,128)(2,1)S(1)} collective-permute-done((bf16[128,2048]{1,0:T(8,128)(2,1)S(1)}, bf16[128,2048]{1,0:T(8,128)(2,1)S(1)}, u32[]{:S(2)}, u32[]{:S(2)}) %collective-permute-start.22) | collective-permute-done | bytes 524320 | tf_op jit(solution)/shard_map/ppermute | solution.py:190
  159.3 1.2 shard_map.55
  160.5 0.6 collective-permute-start.23
  161.1 0.5 collective-permute-start.24
  161.6 0.1 fusion.8
  161.7 1.2 collective-permute-start.25
  163.0 2.5 %collective-permute-done.23 = bf16[256,128]{1,0:T(8,128)(2,1)S(1)} collective-permute-done((bf16[256,128]{1,0:T(8,128)(2,1)S(1)}, bf16[256,128]{1,0:T(8,128)(2,1)S(1)}, u32[]{:S(2)}, u32[]{:S(2)}) %collective-permute-start.23) | collective-permute-done | bytes 65568 | tf_op jit(solution)/shard_map/ppermute | solution.py:184
  165.5 0.0 copy-start.17
  165.5 1.3 copy-done.17
  166.8 0.7 add_dynamic-update-slice_fusion
  (54 shorter events, 0.3 us)
Async XLA Ops:
  0.0 1.6 copy-start.4
  1.6 3.7 %copy-start.5 = (bf16[256,4096]{1,0:T(8,128)(2,1)S(1)}, bf16[256,4096]{1,0:T(8,128)(2,1)}, u32[]{:S(2)}) copy-start(bf16[256,4096]{1,0:T(8,128)(2,1)} %high.3) | copy-start | bytes 6291460
  2.3 29.3 %collective-permute-start = (bf16[256,2048]{1,0:T(8,128)(2,1)S(1)}, bf16[256,2048]{1,0:T(8,128)(2,1)}, u32[]{:S(2)}, u32[]{:S(2)}) collective-permute-start(bf16[256,2048]{1,0:T(8,128)(2,1)S(1)} %shard_map.47.refs_0_), channel_id=1, source_target_pairs={{0,4},{2,6},{4,8},{6,10},{8,12},{10,14},{12,0},{14,2},{1,5},{3,7},... | collective-permute-start | bytes 3145736 | tf_op jit(solution)/shard_map/ppermute | solution.py:190
  5.3 3.5 %copy-start.12 = (s32[512,128]{1,0:T(8,128)S(1)}, s32[512,128]{1,0:T(8,128)}, u32[]{:S(2)}) copy-start(s32[512,128]{1,0:T(8,128)} %mask.1) | copy-start | bytes 786436
  6.7 16.8 %collective-permute-start.1 = (bf16[128,2048]{1,0:T(8,128)(2,1)}, bf16[128,2048]{1,0:T(8,128)(2,1)S(1)}, u32[]{:S(2)}, u32[]{:S(2)}) collective-permute-start(bf16[128,2048]{1,0:T(8,128)(2,1)} %get-tuple-element.31), channel_id=1, source_target_pairs={{0,2},{2,0},{4,6},{6,4},{8,10},{10,8},{12,14},{14,12},{1,3},{3,1},... | collective-permute-start | bytes 1572872 | tf_op jit(solution)/shard_map/ppermute | solution.py:184
  8.2 23.3 %collective-permute-start.2 = (bf16[128,2048]{1,0:T(8,128)(2,1)}, bf16[128,2048]{1,0:T(8,128)(2,1)S(1)}, u32[]{:S(2)}, u32[]{:S(2)}) collective-permute-start(bf16[128,2048]{1,0:T(8,128)(2,1)} %get-tuple-element.32), channel_id=1, source_target_pairs={{0,2},{2,0},{4,6},{6,4},{8,10},{10,8},{12,14},{14,12},{1,3},{3,1},... | collective-permute-start | bytes 1572872 | tf_op jit(solution)/shard_map/ppermute | solution.py:184
  22.2 1.3 copy-start
  31.6 66.2 %collective-permute-start.3 = (bf16[512,2048]{1,0:T(8,128)(2,1)S(1)}, bf16[512,2048]{1,0:T(8,128)(2,1)S(1)}, u32[]{:S(2)}, u32[]{:S(2)}) collective-permute-start(bf16[512,2048]{1,0:T(8,128)(2,1)S(1)} %get-tuple-element.33), channel_id=1, source_target_pairs={{0,2},{2,0},{4,6},{6,4},{8,10},{10,8},{12,14},{14,12},{1,3},{3,1},... | collective-permute-start | bytes 6291464 | tf_op jit(solution)/shard_map/ppermute | solution.py:184
  33.1 25.5 %collective-permute-start.4 = (bf16[256,2048]{1,0:T(8,128)(2,1)}, bf16[256,2048]{1,0:T(8,128)(2,1)S(1)}, u32[]{:S(2)}, u32[]{:S(2)}) collective-permute-start(bf16[256,2048]{1,0:T(8,128)(2,1)} %get-tuple-element.36.refs_0_), channel_id=1, source_target_pairs={{0,4},{2,6},{4,8},{6,10},{8,12},{10,14},{12,0},{14,2},{1,5},{3,7},... | collective-permute-start | bytes 3145736 | tf_op jit(solution)/shard_map/ppermute | solution.py:190
  58.6 57.1 %collective-permute-start.11 = (bf16[256,2048]{1,0:T(8,128)(2,1)S(1)}, bf16[256,2048]{1,0:T(8,128)(2,1)S(1)}, u32[]{:S(2)}, u32[]{:S(2)}) collective-permute-start(bf16[256,2048]{1,0:T(8,128)(2,1)S(1)} %collective-permute-done.4.refs_3_.refs_0_), channel_id=1, source_target_pairs={{0,4},{2,6},{4,8},{6,10},{8,12},{10,14},{12,0},{14,2},{1,5},{3,7},... | collective-permute-start | bytes 3145736 | tf_op jit(solution)/shard_map/ppermute | solution.py:190
  58.6 39.1 %collective-permute-start.5 = (bf16[128,2048]{1,0:T(8,128)(2,1)S(1)}, bf16[128,2048]{1,0:T(8,128)(2,1)S(1)}, u32[]{:S(2)}, u32[]{:S(2)}) collective-permute-start(bf16[128,2048]{1,0:T(8,128)(2,1)S(1)} %get-tuple-element.34.refs_1_), channel_id=1, source_target_pairs={{0,4},{2,6},{4,8},{6,10},{8,12},{10,14},{12,0},{14,2},{1,5},{3,7},... | collective-permute-start | bytes 1572872 | tf_op jit(solution)/shard_map/ppermute | solution.py:190
  59.9 49.2 %collective-permute-start.8 = (bf16[128,2048]{1,0:T(8,128)(2,1)S(1)}, bf16[128,2048]{1,0:T(8,128)(2,1)}, u32[]{:S(2)}, u32[]{:S(2)}) collective-permute-start(bf16[128,2048]{1,0:T(8,128)(2,1)S(1)} %get-tuple-element.35.refs_2_), channel_id=1, source_target_pairs={{0,4},{2,6},{4,8},{6,10},{8,12},{10,14},{12,0},{14,2},{1,5},{3,7},... | collective-permute-start | bytes 1572872 | tf_op jit(solution)/shard_map/ppermute | solution.py:190
  97.7 22.8 %collective-permute-start.13 = (bf16[128,2048]{1,0:T(8,128)(2,1)S(1)}, bf16[128,2048]{1,0:T(8,128)(2,1)}, u32[]{:S(2)}, u32[]{:S(2)}) collective-permute-start(bf16[128,2048]{1,0:T(8,128)(2,1)S(1)} %collective-permute-done.5.refs_4_.refs_1_), channel_id=1, source_target_pairs={{0,4},{2,6},{4,8},{6,10},{8,12},{10,14},{12,0},{14,2},{1,5},{3,7},... | collective-permute-start | bytes 1572872 | tf_op jit(solution)/shard_map/ppermute | solution.py:190
  97.8 1.3 copy-start.2
  104.8 17.5 %copy-start.8 = (f32[512,512]{1,0:T(8,128)}, f32[512,512]{1,0:T(8,128)S(1)}, u32[]{:S(2)}) copy-start(f32[512,512]{1,0:T(8,128)S(1)} %get-tuple-element.37) | copy-start | bytes 3145732
  115.2 5.6 %copy-start.6 = (f32[512,512]{1,0:T(8,128)}, f32[512,512]{1,0:T(8,128)S(1)}, u32[]{:S(2)}) copy-start(f32[512,512]{1,0:T(8,128)S(1)} %get-tuple-element.39) | copy-start | bytes 3145732
  115.2 5.4 %collective-permute-start.9 = (bf16[512,512]{1,0:T(8,128)(2,1)S(1)}, bf16[512,512]{1,0:T(8,128)(2,1)S(1)}, u32[]{:S(2)}, u32[]{:S(2)}) collective-permute-start(bf16[512,512]{1,0:T(8,128)(2,1)S(1)} %get-tuple-element.40.refs_2_), channel_id=1, source_target_pairs={{0,1},{1,0},{2,3},{3,2},{4,5},{5,4},{6,7},{7,6},{8,9},{9,8},{10,11... | collective-permute-start | bytes 1572872 | tf_op jit(solution)/shard_map/ppermute | solution.py:187
  115.3 6.9 %collective-permute-start.6 = (bf16[512,512]{1,0:T(8,128)(2,1)S(1)}, bf16[512,512]{1,0:T(8,128)(2,1)S(1)}, u32[]{:S(2)}, u32[]{:S(2)}) collective-permute-start(bf16[512,512]{1,0:T(8,128)(2,1)S(1)} %get-tuple-element.38.refs_3_), channel_id=1, source_target_pairs={{0,1},{1,0},{2,3},{3,2},{4,5},{5,4},{6,7},{7,6},{8,9},{9,8},{10,11... | collective-permute-start | bytes 1572872 | tf_op jit(solution)/shard_map/ppermute | solution.py:187
  120.4 1.9 %copy-start.10 = (bf16[512,512]{1,0:T(8,128)(2,1)}, bf16[512,512]{1,0:T(8,128)(2,1)S(1)}, u32[]{:S(2)}) copy-start(bf16[512,512]{1,0:T(8,128)(2,1)S(1)} %get-tuple-element.42.refs_2_) | copy-start | bytes 1572868
  120.4 4.4 %collective-permute-start.12 = (bf16[512,512]{1,0:T(8,128)(2,1)S(1)}, bf16[512,512]{1,0:T(8,128)(2,1)S(1)}, u32[]{:S(2)}, u32[]{:S(2)}) collective-permute-start(bf16[512,512]{1,0:T(8,128)(2,1)S(1)} %get-tuple-element.42.refs_2_), channel_id=1, source_target_pairs={{0,1},{1,0},{2,3},{3,2},{4,5},{5,4},{6,7},{7,6},{8,9},{9,8},{10,11... | collective-permute-start | bytes 1572872 | tf_op jit(solution)/shard_map/ppermute | solution.py:187
  120.5 16.7 %collective-permute-start.14 = (bf16[128,2048]{1,0:T(8,128)(2,1)}, bf16[128,2048]{1,0:T(8,128)(2,1)S(1)}, u32[]{:S(2)}, u32[]{:S(2)}) collective-permute-start(bf16[128,2048]{1,0:T(8,128)(2,1)} %collective-permute-done.8.refs_2_), channel_id=1, source_target_pairs={{0,4},{2,6},{4,8},{6,10},{8,12},{10,14},{12,0},{14,2},{1,5},{3,7},... | collective-permute-start | bytes 1572872 | tf_op jit(solution)/shard_map/ppermute | solution.py:190
  120.5 28.1 %collective-permute-start.18 = (bf16[128,2048]{1,0:T(8,128)(2,1)}, bf16[128,2048]{1,0:T(8,128)(2,1)}, u32[]{:S(2)}, u32[]{:S(2)}) collective-permute-start(bf16[128,2048]{1,0:T(8,128)(2,1)} %collective-permute-done.13.refs_0_), channel_id=1, source_target_pairs={{0,4},{2,6},{4,8},{6,10},{8,12},{10,14},{12,0},{14,2},{1,5},{3,7},... | collective-permute-start | bytes 1572872 | tf_op jit(solution)/shard_map/ppermute | solution.py:190
  120.7 2.5 %copy-start.13 = (f32[512,512]{1,0:T(8,128)}, f32[512,512]{1,0:T(8,128)S(1)}, u32[]{:S(2)}) copy-start(f32[512,512]{1,0:T(8,128)S(1)} %convert_element_type.63) | copy-start | bytes 3145732
  121.6 15.6 %collective-permute-start.10 = (bf16[256,512]{1,0:T(8,128)(2,1)}, bf16[256,512]{1,0:T(8,128)(2,1)S(1)}, u32[]{:S(2)}, u32[]{:S(2)}) collective-permute-start(bf16[256,512]{1,0:T(8,128)(2,1)} %fusion.1), channel_id=1, source_target_pairs={{0,2},{2,0},{4,6},{6,4},{8,10},{10,8},{12,14},{14,12},{1,3},{3,1},... | collective-permute-start | bytes 786440 | tf_op jit(solution)/shard_map/ppermute | solution.py:184
  122.3 3.7 %copy-start.15 = (f32[512,512]{1,0:T(8,128)}, f32[512,512]{1,0:T(8,128)S(1)}, u32[]{:S(2)}) copy-start(f32[512,512]{1,0:T(8,128)S(1)} %convert_element_type.60) | copy-start | bytes 3145732
  123.2 14.0 %copy-start.1 = (bf16[512,2048]{1,0:T(8,128)(2,1)S(1)}, bf16[512,2048]{1,0:T(8,128)(2,1)}, u32[]{:S(2)}) copy-start(bf16[512,2048]{1,0:T(8,128)(2,1)} %copy-done) | copy-start | bytes 6291460
  123.2 14.0 %collective-permute-start.7 = (bf16[256,512]{1,0:T(8,128)(2,1)}, bf16[256,512]{1,0:T(8,128)(2,1)S(1)}, u32[]{:S(2)}, u32[]{:S(2)}) collective-permute-start(bf16[256,512]{1,0:T(8,128)(2,1)} %fusion.4), channel_id=1, source_target_pairs={{0,2},{2,0},{4,6},{6,4},{8,10},{10,8},{12,14},{14,12},{1,3},{3,1},... | collective-permute-start | bytes 786440 | tf_op jit(solution)/shard_map/ppermute | solution.py:184
  126.0 22.6 %collective-permute-start.17 = (bf16[256,512]{1,0:T(8,128)(2,1)}, bf16[256,512]{1,0:T(8,128)(2,1)S(1)}, u32[]{:S(2)}, u32[]{:S(2)}) collective-permute-start(bf16[256,512]{1,0:T(8,128)(2,1)} %get-tuple-element.53), channel_id=1, source_target_pairs={{0,2},{2,0},{4,6},{6,4},{8,10},{10,8},{12,14},{14,12},{1,3},{3,1},... | collective-permute-start | bytes 786440 | tf_op jit(solution)/shard_map/ppermute | solution.py:184
  126.5 22.1 %copy-start.3 = (bf16[512,2048]{1,0:T(8,128)(2,1)S(1)}, bf16[512,2048]{1,0:T(8,128)(2,1)}, u32[]{:S(2)}) copy-start(bf16[512,2048]{1,0:T(8,128)(2,1)} %copy-done.2) | copy-start | bytes 6291460
  137.2 22.0 %collective-permute-start.22 = (bf16[128,2048]{1,0:T(8,128)(2,1)S(1)}, bf16[128,2048]{1,0:T(8,128)(2,1)S(1)}, u32[]{:S(2)}, u32[]{:S(2)}) collective-permute-start(bf16[128,2048]{1,0:T(8,128)(2,1)S(1)} %collective-permute-done.14.refs_1_), channel_id=1, source_target_pairs={{0,4},{2,6},{4,8},{6,10},{8,12},{10,14},{12,0},{14,2},{1,5},{3,7},... | collective-permute-start | bytes 1572872 | tf_op jit(solution)/shard_map/ppermute | solution.py:190
  137.3 1.0 copy-start.11
  142.3 11.2 %collective-permute-start.15 = (bf16[512,256]{1,0:T(8,128)(2,1)S(1)}, bf16[512,256]{1,0:T(8,128)(2,1)S(1)}, u32[]{:S(2)}, u32[]{:S(2)}) collective-permute-start(bf16[512,256]{1,0:T(8,128)(2,1)S(1)} %get-tuple-element.44.refs_0_), channel_id=1, source_target_pairs={{0,1},{1,0},{2,3},{3,2},{4,5},{5,4},{6,7},{7,6},{8,9},{9,8},{10,11... | collective-permute-start | bytes 786440 | tf_op jit(solution)/shard_map/ppermute | solution.py:187
  150.9 2.5 %copy-start.9 = (f32[512,512]{1,0:T(8,128)S(1)}, f32[512,512]{1,0:T(8,128)}, u32[]{:S(2)}) copy-start(f32[512,512]{1,0:T(8,128)} %copy-done.8) | copy-start | bytes 3145732
  150.9 2.5 %copy-start.16 = (f32[512,512]{1,0:T(8,128)S(1)}, f32[512,512]{1,0:T(8,128)}, u32[]{:S(2)}) copy-start(f32[512,512]{1,0:T(8,128)} %copy-done.15) | copy-start | bytes 3145732
  150.9 10.8 %collective-permute-start.19 = (bf16[256,128]{1,0:T(8,128)(2,1)S(1)}, bf16[256,128]{1,0:T(8,128)(2,1)S(1)}, u32[]{:S(2)}, u32[]{:S(2)}) collective-permute-start(bf16[256,128]{1,0:T(8,128)(2,1)S(1)} %get-tuple-element.45), channel_id=1, source_target_pairs={{0,2},{2,0},{4,6},{6,4},{8,10},{10,8},{12,14},{14,12},{1,3},{3,1},... | collective-permute-start | bytes 196616 | tf_op jit(solution)/shard_map/ppermute | solution.py:184
  151.5 11.4 %collective-permute-start.20 = (bf16[256,128]{1,0:T(8,128)(2,1)S(1)}, bf16[256,128]{1,0:T(8,128)(2,1)S(1)}, u32[]{:S(2)}, u32[]{:S(2)}) collective-permute-start(bf16[256,128]{1,0:T(8,128)(2,1)S(1)} %get-tuple-element.46), channel_id=1, source_target_pairs={{0,3},{1,2},{2,1},{3,0},{4,7},{5,6},{6,5},{7,4},{8,11},{9,10},{10,... | collective-permute-start | bytes 196616 | tf_op jit(solution)/shard_map/ppermute | solution.py:193
  151.5 11.4 %collective-permute-start.21 = (bf16[256,128]{1,0:T(8,128)(2,1)S(1)}, bf16[256,128]{1,0:T(8,128)(2,1)S(1)}, u32[]{:S(2)}, u32[]{:S(2)}) collective-permute-start(bf16[256,128]{1,0:T(8,128)(2,1)S(1)} %get-tuple-element.48), channel_id=1, source_target_pairs={{0,1},{1,0},{2,3},{3,2},{4,5},{5,4},{6,7},{7,6},{8,9},{9,8},{10,11... | collective-permute-start | bytes 196616 | tf_op jit(solution)/shard_map/ppermute | solution.py:187
  153.4 1.2 copy-start.7
  153.4 1.5 copy-start.14
  153.6 7.5 %collective-permute-start.16 = (bf16[256,256]{1,0:T(8,128)(2,1)S(1)}, bf16[256,256]{1,0:T(8,128)(2,1)S(1)}, u32[]{:S(2)}, u32[]{:S(2)}) collective-permute-start(bf16[256,256]{1,0:T(8,128)(2,1)S(1)} %fusion.9.refs_1_), channel_id=1, source_target_pairs={{0,2},{2,0},{4,6},{6,4},{8,10},{10,8},{12,14},{14,12},{1,3},{3,1},... | collective-permute-start | bytes 393224 | tf_op jit(solution)/shard_map/ppermute | solution.py:184
  159.3 2.3 %copy-start.18 = (f32[256,512]{1,0:T(8,128)S(1)}, f32[256,512]{1,0:T(8,128)}, u32[]{:S(2)}) copy-start(f32[256,512]{1,0:T(8,128)} %get-tuple-element.54) | copy-start | bytes 1572868
  160.5 5.0 %collective-permute-start.23 = (bf16[256,128]{1,0:T(8,128)(2,1)S(1)}, bf16[256,128]{1,0:T(8,128)(2,1)S(1)}, u32[]{:S(2)}, u32[]{:S(2)}) collective-permute-start(bf16[256,128]{1,0:T(8,128)(2,1)S(1)} %get-tuple-element.49), channel_id=1, source_target_pairs={{0,2},{2,0},{4,6},{6,4},{8,10},{10,8},{12,14},{14,12},{1,3},{3,1},... | collective-permute-start | bytes 196616 | tf_op jit(solution)/shard_map/ppermute | solution.py:184
  161.1 4.4 %collective-permute-start.24 = (bf16[256,128]{1,0:T(8,128)(2,1)S(1)}, bf16[256,128]{1,0:T(8,128)(2,1)S(1)}, u32[]{:S(2)}, u32[]{:S(2)}) collective-permute-start(bf16[256,128]{1,0:T(8,128)(2,1)S(1)} %get-tuple-element.50), channel_id=1, source_target_pairs={{0,3},{1,2},{2,1},{3,0},{4,7},{5,6},{6,5},{7,4},{8,11},{9,10},{10,... | collective-permute-start | bytes 196616 | tf_op jit(solution)/shard_map/ppermute | solution.py:193
  161.7 3.8 %collective-permute-start.25 = (bf16[256,128]{1,0:T(8,128)(2,1)S(1)}, bf16[256,128]{1,0:T(8,128)(2,1)S(1)}, u32[]{:S(2)}, u32[]{:S(2)}) collective-permute-start(bf16[256,128]{1,0:T(8,128)(2,1)S(1)} %get-tuple-element.52), channel_id=1, source_target_pairs={{0,1},{1,0},{2,3},{3,2},{4,5},{5,4},{6,7},{7,6},{8,9},{9,8},{10,11... | collective-permute-start | bytes 196616 | tf_op jit(solution)/shard_map/ppermute | solution.py:187
  165.5 1.3 copy-start.17

commit v10 on v7

--- a/solution.py
+++ b/solution.py
@@ -112,19 +112,18 @@
 def score_body(count, spot, own, far, *refs):
     keep, give = refs[-2:]
     part = own.shape[0] // 2
-    rows = refs[0].shape[0]
     for i, block in enumerate(refs[:count]):
         size = block.shape[0]
-        if count == 1:
-            at = slice(None)
-        elif i == 0:
-            at = pl.ds(pl.multiple_of(spot[0] * rows, rows), size)
+        if count == 3:
+            rows = refs[0].shape[0]
+            at = spot[0] * rows if i == 0 else (1 - spot[0]) * rows + (i - 1) * size
+            columns = pl.ds(pl.multiple_of(at, size), size)
         else:
-            at = pl.ds(pl.multiple_of((1 - spot[0]) * rows + (i - 1) * size, size), size)
-        keep[:part, at] = dot(own[:part, :], block[...])
-        keep[part:, at] = dot(far[:part, :], block[...])
-        give[:part, at] = dot(own[part:, :], block[...]).astype(bf16)
-        give[part:, at] = dot(far[part:, :], block[...]).astype(bf16)
+            columns = pl.ds(i * size, size)
+        keep[:part, columns] = dot(own[:part, :], block[...])
+        keep[part:, columns] = dot(far[:part, :], block[...])
+        give[:part, columns] = dot(own[part:, :], block[...]).astype(bf16)
+        give[part:, columns] = dot(far[part:, :], block[...]).astype(bf16)
 
 
 def score(spot, own, far, blocks, *after):
@@ -214,29 +213,33 @@
         return keep[:part] + got[:part], (keep[part:] + got[part:]).astype(bf16)
 
     besides = []
-    last = ()
-    for step in range(places - 1):
-        if step == places - 2:
-            keep, give = score(spot, own, far, [first[-1]], *last)
-            final_own, final_far = over_cores(keep, give)
-            final_beside = swap_across(final_far)
-            last = (give,) + tuple(besides)
+    last = (first[2], second[1][0]) if places > 2 else ()
+    for step in range(places - 2):
         keep, give = score(spot, own, far, [first[step]] + second[step], *last)
         total, reach = over_cores(keep, give)
         besides.append(swap_across(reach))
         out = put(out, total + besides[-1].astype(f32), step, 0)
         last = (give,)
-    last = (give,)
+
+    keep, give = score(spot, own, far, first[-2:], *last)
+    early, early_reach = over_cores(keep, give)
+    early_beside = swap_across(early_reach)
+    keep, give = score(spot, own, far, second[-2], give, besides[0])
+    late, late_reach = over_cores(keep, give)
+    late_beside = swap_across(late_reach)
+    out = put(out, early[:, :queries] + late_beside.astype(f32), places - 2, side * queries)
+    out = put(out, late + early_beside[:, :queries].astype(f32), places - 2, (1 - side) * queries)
 
     size = queries // 2
+    last = (give, early_reach)
     for i, piece in enumerate(pieces):
         near, give, facing, opposite = last_score(own, far, piece, *last)
-        cut = slice(i * size, (i + 1) * size)
-        mine_total = final_own[:, cut] + swap_across(facing).astype(f32) + swap_diagonal(opposite).astype(f32)
-        other_total = near + swap_cores(give).astype(f32) + final_beside[:, cut].astype(f32)
+        cut = slice(queries + i * size, queries + (i + 1) * size)
+        mine_total = early[:, cut] + swap_across(facing).astype(f32) + swap_diagonal(opposite).astype(f32)
+        other_total = near + swap_cores(give).astype(f32) + early_beside[:, cut].astype(f32)
         out = put(out, mine_total, places - 1, side * queries + i * size)
         out = put(out, other_total, places - 1, (1 - side) * queries + i * size)
-        last = (near, final_beside, reach)
+        last = (near, early_beside, late_reach)
     return out
 
 

time: 161 us -> 167 us (1.037)
  waiting for transfers between devices: 90.1 us -> 99 us
  starting transfers between devices: 18.6 us -> 16.7 us
    ppermute x9, waiting for transfers between devices: 71.3 us -> 80.6 us  [pass_on(): return lax.ppermute(x, 'blk', onward)]
    unnamed x38 -> x24, local copies, waits for them, and re-layouts: 7.67 us -> 7.52 us
  transfers between devices with their start and end apart: 26 -> 26, of which waited for: 11 -> 11; matrix products, arithmetic and copies ran while one was open for 3% -> 2% of each run, Pallas kernels for 23% -> 23%
where the time goes in v10:
time: 167 us
  waiting for transfers between devices  99 us (59%)
  Pallas kernels  38.9 us (23%)
  starting transfers between devices  16.7 us (10%)
  local copies, waits for them, and re-layouts  7.74 us (5%)
  other arithmetic  4.11 us (2%)
    ppermute x9, waiting for transfers between devices, pass_on(): return lax.ppermute(x, 'blk', onward)  80.6 us
    pallas_call x4, Pallas kernels, score(): pl.pallas_call(functools.partial(score_body, count), in_specs=[SCALARS] +...  21.8 us
    ppermute x9, waiting for transfers between devices, swap_across(): return lax.ppermute(x, 'blk', across)  17.8 us
    pallas_call x1, Pallas kernels, form(): pl.pallas_call(functools.partial(form_body, rows, rank), grid_spec=pltpu....  13.4 us
    ppermute x9, starting transfers between devices, swap_across(): return lax.ppermute(x, 'blk', across)  8.87 us
    unnamed x24, local copies, waits for them, and re-layouts  7.52 us
    ppermute x9, starting transfers between devices, pass_on(): return lax.ppermute(x, 'blk', onward)  5.66 us
  transfers between devices with their start and end apart: 26, of which 11 were waited for; matrix products, arithmetic and copies ran while one was open for 2% of the time, Pallas kernels for 23%

profile of v10, /device:TPU:0, one launch (start us, length us, event | category | flops | bytes accessed | tf_op | source)
XLA Modules:
  0.0 166.8 jit_solution(9850234362771864434)
XLA Ops:
  0.0 0.1 pad_add_fusion.spot
  0.1 1.6 copy-done.4
  1.7 1.3 shard_map.47
  2.9 3.1 %collective-permute-start = (bf16[256,2048]{1,0:T(8,128)(2,1)S(1)}, bf16[256,2048]{1,0:T(8,128)(2,1)S(1)}, u32[]{:S(2)}, u32[]{:S(2)}) collective-permute-start(bf16[256,2048]{1,0:T(8,128)(2,1)S(1)} %get-tuple-element.32.refs_0_), channel_id=1, source_target_pairs={{0,4},{2,6},{4,8},{6,10},{8,12},{10,14},{12,0},{14,2},{1,5},{3,7},... | collective-permute-start | bytes 3145736 | tf_op jit(solution)/shard_map/ppermute | solution.py:185
  6.0 1.5 collective-permute-start.1
  7.5 0.5 collective-permute-start.2
  8.0 13.4 %shard_map.46 = (bf16[512,2048]{1,0:T(8,128)(2,1)S(1)}, bf16[512,2048]{1,0:T(8,128)(2,1)S(1)}) custom-call(s32[2]{0:T(128)S(1)} %pad_add_fusion.spot, bf16[512,64,128]{2,1,0:T(8,128)(2,1)} %bitcast.4, bf16[512,64,128]{2,1,0:T(8,128)(2,1)} %bitcast.5, s32[512,128]{1,0:T(8,128)S(1)} %copy-done.10), custom_call_target="tpu_custom_call" | custom-call | flops 10737418240 | bytes 20971520 | tf_op jit(solution)/shard_map/pallas_call | solution.py:72
  21.4 0.0 copy-start
  21.4 1.3 copy-done
  22.8 7.9 %collective-permute-done.2.refs_3_ = bf16[128,2048]{1,0:T(8,128)(2,1)S(1)} collective-permute-done((bf16[128,2048]{1,0:T(8,128)(2,1)S(1)}, bf16[128,2048]{1,0:T(8,128)(2,1)S(1)}, u32[]{:S(2)}, u32[]{:S(2)}) %collective-permute-start.2) | collective-permute-done | bytes 524320 | tf_op jit(solution)/shard_map/ppermute | solution.py:179
  30.6 0.6 collective-permute-done.refs_1_
  31.2 1.5 collective-permute-start.3
  32.7 1.0 collective-permute-start.4
  33.7 24.6 %collective-permute-done.4.refs_3_.refs_0_ = bf16[256,2048]{1,0:T(8,128)(2,1)S(1)} collective-permute-done((bf16[256,2048]{1,0:T(8,128)(2,1)S(1)}, bf16[256,2048]{1,0:T(8,128)(2,1)S(1)}, u32[]{:S(2)}, u32[]{:S(2)}) %collective-permute-start.4) | collective-permute-done | bytes 1048608 | tf_op jit(solution)/shard_map/ppermute | solution.py:185
  58.3 0.0 collective-permute-start.11
  58.3 0.4 collective-permute-start.5
  58.7 0.6 collective-permute-start.8
  59.3 38.1 %collective-permute-done.5.refs_4_.refs_1_ = bf16[128,2048]{1,0:T(8,128)(2,1)S(1)} collective-permute-done((bf16[128,2048]{1,0:T(8,128)(2,1)S(1)}, bf16[128,2048]{1,0:T(8,128)(2,1)S(1)}, u32[]{:S(2)}, u32[]{:S(2)}) %collective-permute-start.5) | collective-permute-done | bytes 524320 | tf_op jit(solution)/shard_map/ppermute | solution.py:185
  97.5 11.3 %collective-permute-done.8.refs_2_ = bf16[128,2048]{1,0:T(8,128)(2,1)} collective-permute-done((bf16[128,2048]{1,0:T(8,128)(2,1)S(1)}, bf16[128,2048]{1,0:T(8,128)(2,1)}, u32[]{:S(2)}, u32[]{:S(2)}) %collective-permute-start.8) | collective-permute-done | bytes 524320 | tf_op jit(solution)/shard_map/ppermute | solution.py:185
  108.8 0.0 collective-permute-start.14
  108.8 0.0 collective-permute-done.3.far
  108.8 1.3 copy-done.2
  110.2 6.5 %shard_map.49 = (f32[512,512]{1,0:T(8,128)S(1)}, bf16[512,512]{1,0:T(8,128)(2,1)}) custom-call(s32[2]{0:T(128)S(1)} %pad_add_fusion.spot, bf16[512,2048]{1,0:T(8,128)(2,1)} %copy-done, bf16[512,2048]{1,0:T(8,128)(2,1)} %copy-done.2, bf16[256,2048]{1,0:T(8,128)(2,1)S(1)} %get-tuple-element.32.refs_0_, bf16[128,2048]{1,0:T(8,128)(2,1)S(1)} %get-tuple-element.36.refs_1_, ...), custom_call_target="tpu_custom_call" | custom-call | flops 1024 | bytes 1024 | tf_op jit(solution)/shard_map/pallas_call | solution.py:133
  116.6 1.0 copy-done.5
  117.6 0.0 collective-permute-start.6
  117.6 5.8 %shard_map.50 = (f32[512,512]{1,0:T(8,128)S(1)}, bf16[512,512]{1,0:T(8,128)(2,1)S(1)}) custom-call(s32[2]{0:T(128)S(1)} %pad_add_fusion.spot, bf16[512,2048]{1,0:T(8,128)(2,1)} %copy-done, bf16[512,2048]{1,0:T(8,128)(2,1)} %copy-done.2, bf16[256,2048]{1,0:T(8,128)(2,1)S(1)} %get-tuple-element.38.refs_0_, ...), custom_call_target="tpu_custom_call" | custom-call | flops 1024 | bytes 1024 | tf_op jit(solution)/shard_map/pallas_call | solution.py:133
  123.4 5.6 %shard_map.51 = (f32[512,512]{1,0:T(8,128)S(1)}, bf16[512,512]{1,0:T(8,128)(2,1)}) custom-call(s32[2]{0:T(128)S(1)} %pad_add_fusion.spot, bf16[512,2048]{1,0:T(8,128)(2,1)} %copy-done, bf16[512,2048]{1,0:T(8,128)(2,1)} %copy-done.2, bf16[256,2048]{1,0:T(8,128)(2,1)S(1)} %collective-permute-done.4.refs_3_.refs_0_, ...), custom_call_target="tpu_custom_call" | custom-call | flops 1024 | bytes 1024 | tf_op jit(solution)/shard_map/pallas_call | solution.py:133
  129.0 1.0 copy-done.7
  130.0 0.5 collective-permute-start.12
  130.5 0.0 collective-permute-done.13.refs_0_
  130.5 0.0 collective-permute-start.18
  130.5 0.6 collective-permute-start.22
  131.1 1.2 convert_element_type.60
  132.2 0.1 fusion.4
  132.3 0.8 collective-permute-start.7
  133.2 1.2 convert_element_type.66
  134.3 0.2 fusion
  134.6 0.0 copy-start.1
  134.6 1.3 collective-permute-start.17
  135.9 0.1 convert_element_type.63
  136.1 0.1 fusion.1
  136.2 0.8 collective-permute-start.10
  137.0 4.5 %collective-permute-done.7.refs_3_ = bf16[256,512]{1,0:T(8,128)(2,1)S(1)} collective-permute-done((bf16[256,512]{1,0:T(8,128)(2,1)S(1)}, bf16[256,512]{1,0:T(8,128)(2,1)S(1)}, u32[]{:S(2)}, u32[]{:S(2)}) %collective-permute-start.7) | collective-permute-done | bytes 262176 | tf_op jit(solution)/shard_map/ppermute | solution.py:179
  141.5 4.0 %shard_map.52 = (f32[512,256]{1,0:T(8,128)S(1)}, bf16[512,256]{1,0:T(8,128)(2,1)S(1)}) custom-call(s32[2]{0:T(128)S(1)} %pad_add_fusion.spot, bf16[512,2048]{1,0:T(8,128)(2,1)S(1)} %copy-done.1, bf16[512,2048]{1,0:T(8,128)(2,1)} %copy-done.2, bf16[128,2048]{1,0:T(8,128)(2,1)} %collective-permute-done.13.refs_0_, ...), custom_call_target="tpu_custom_call" | custom-call | flops 1024 | bytes 1024 | tf_op jit(solution)/shard_map/pallas_call | solution.py:133
  145.5 0.1 collective-permute-start.15
  145.6 1.6 collective-permute-done.18.block
  147.2 1.2 shard_map.53
  148.5 0.8 collective-permute-start.19
  149.3 0.2 broadcast_in_dim.3
  149.5 0.1 fusion.6
  149.7 0.1 collective-permute-start.20
  149.8 2.9 %collective-permute-done.10 = bf16[256,512]{1,0:T(8,128)(2,1)S(1)} collective-permute-done((bf16[256,512]{1,0:T(8,128)(2,1)S(1)}, bf16[256,512]{1,0:T(8,128)(2,1)S(1)}, u32[]{:S(2)}, u32[]{:S(2)}) %collective-permute-start.10) | collective-permute-done | bytes 262176 | tf_op jit(solution)/shard_map/ppermute | solution.py:179
  152.7 0.7 collective-permute-start.16
  153.5 0.1 fusion.3
  153.6 4.3 %collective-permute-done.22.block = bf16[128,2048]{1,0:T(8,128)(2,1)S(1)} collective-permute-done((bf16[128,2048]{1,0:T(8,128)(2,1)S(1)}, bf16[128,2048]{1,0:T(8,128)(2,1)S(1)}, u32[]{:S(2)}, u32[]{:S(2)}) %collective-permute-start.22) | collective-permute-done | bytes 524320 | tf_op jit(solution)/shard_map/ppermute | solution.py:185
  157.9 1.2 shard_map.54
  159.2 0.8 collective-permute-start.23
  160.0 1.1 collective-permute-start.24
  161.2 0.4 collective-permute-start.25
  161.6 2.5 %collective-permute-done.23 = bf16[256,128]{1,0:T(8,128)(2,1)S(1)} collective-permute-done((bf16[256,128]{1,0:T(8,128)(2,1)S(1)}, bf16[256,128]{1,0:T(8,128)(2,1)S(1)}, u32[]{:S(2)}, u32[]{:S(2)}) %collective-permute-start.23) | collective-permute-done | bytes 65568 | tf_op jit(solution)/shard_map/ppermute | solution.py:179
  164.1 0.6 collective-permute-done.24
  164.8 0.0 copy-start.11
  164.8 1.3 copy-done.11
  166.1 0.7 add_dynamic-update-slice_fusion
  (39 shorter events, 0.3 us)
Async XLA Ops:
  0.1 1.6 copy-start.4
  1.7 6.4 %copy-start.10 = (s32[512,128]{1,0:T(8,128)S(1)}, s32[512,128]{1,0:T(8,128)}, u32[]{:S(2)}) copy-start(s32[512,128]{1,0:T(8,128)} %mask.1) | copy-start | bytes 786436
  2.9 28.3 %collective-permute-start = (bf16[256,2048]{1,0:T(8,128)(2,1)S(1)}, bf16[256,2048]{1,0:T(8,128)(2,1)S(1)}, u32[]{:S(2)}, u32[]{:S(2)}) collective-permute-start(bf16[256,2048]{1,0:T(8,128)(2,1)S(1)} %get-tuple-element.32.refs_0_), channel_id=1, source_target_pairs={{0,4},{2,6},{4,8},{6,10},{8,12},{10,14},{12,0},{14,2},{1,5},{3,7},... | collective-permute-start | bytes 3145736 | tf_op jit(solution)/shard_map/ppermute | solution.py:185
  6.0 16.7 %collective-permute-start.1 = (bf16[128,2048]{1,0:T(8,128)(2,1)S(1)}, bf16[128,2048]{1,0:T(8,128)(2,1)S(1)}, u32[]{:S(2)}, u32[]{:S(2)}) collective-permute-start(bf16[128,2048]{1,0:T(8,128)(2,1)S(1)} %get-tuple-element.33), channel_id=1, source_target_pairs={{0,2},{2,0},{4,6},{6,4},{8,10},{10,8},{12,14},{14,12},{1,3},{3,1},... | collective-permute-start | bytes 1572872 | tf_op jit(solution)/shard_map/ppermute | solution.py:179
  7.5 23.1 %collective-permute-start.2 = (bf16[128,2048]{1,0:T(8,128)(2,1)S(1)}, bf16[128,2048]{1,0:T(8,128)(2,1)S(1)}, u32[]{:S(2)}, u32[]{:S(2)}) collective-permute-start(bf16[128,2048]{1,0:T(8,128)(2,1)S(1)} %get-tuple-element.34), channel_id=1, source_target_pairs={{0,2},{2,0},{4,6},{6,4},{8,10},{10,8},{12,14},{14,12},{1,3},{3,1},... | collective-permute-start | bytes 1572872 | tf_op jit(solution)/shard_map/ppermute | solution.py:179
  21.4 1.3 copy-start
  31.2 77.6 %collective-permute-start.3 = (bf16[512,2048]{1,0:T(8,128)(2,1)S(1)}, bf16[512,2048]{1,0:T(8,128)(2,1)S(1)}, u32[]{:S(2)}, u32[]{:S(2)}) collective-permute-start(bf16[512,2048]{1,0:T(8,128)(2,1)S(1)} %get-tuple-element.35), channel_id=1, source_target_pairs={{0,2},{2,0},{4,6},{6,4},{8,10},{10,8},{12,14},{14,12},{1,3},{3,1},... | collective-permute-start | bytes 6291464 | tf_op jit(solution)/shard_map/ppermute | solution.py:179
  32.7 25.6 %collective-permute-start.4 = (bf16[256,2048]{1,0:T(8,128)(2,1)S(1)}, bf16[256,2048]{1,0:T(8,128)(2,1)S(1)}, u32[]{:S(2)}, u32[]{:S(2)}) collective-permute-start(bf16[256,2048]{1,0:T(8,128)(2,1)S(1)} %get-tuple-element.38.refs_0_), channel_id=1, source_target_pairs={{0,4},{2,6},{4,8},{6,10},{8,12},{10,14},{12,0},{14,2},{1,5},{3,7},... | collective-permute-start | bytes 3145736 | tf_op jit(solution)/shard_map/ppermute | solution.py:185
  58.3 65.0 %collective-permute-start.11 = (bf16[256,2048]{1,0:T(8,128)(2,1)S(1)}, bf16[256,2048]{1,0:T(8,128)(2,1)S(1)}, u32[]{:S(2)}, u32[]{:S(2)}) collective-permute-start(bf16[256,2048]{1,0:T(8,128)(2,1)S(1)} %collective-permute-done.4.refs_3_.refs_0_), channel_id=1, source_target_pairs={{0,4},{2,6},{4,8},{6,10},{8,12},{10,14},{12,0},{14,2},{1,5},{3,7},... | collective-permute-start | bytes 3145736 | tf_op jit(solution)/shard_map/ppermute | solution.py:185
  58.3 39.1 %collective-permute-start.5 = (bf16[128,2048]{1,0:T(8,128)(2,1)S(1)}, bf16[128,2048]{1,0:T(8,128)(2,1)S(1)}, u32[]{:S(2)}, u32[]{:S(2)}) collective-permute-start(bf16[128,2048]{1,0:T(8,128)(2,1)S(1)} %get-tuple-element.36.refs_1_), channel_id=1, source_target_pairs={{0,4},{2,6},{4,8},{6,10},{8,12},{10,14},{12,0},{14,2},{1,5},{3,7},... | collective-permute-start | bytes 1572872 | tf_op jit(solution)/shard_map/ppermute | solution.py:185
  58.7 50.1 %collective-permute-start.8 = (bf16[128,2048]{1,0:T(8,128)(2,1)S(1)}, bf16[128,2048]{1,0:T(8,128)(2,1)}, u32[]{:S(2)}, u32[]{:S(2)}) collective-permute-start(bf16[128,2048]{1,0:T(8,128)(2,1)S(1)} %get-tuple-element.37.refs_2_), channel_id=1, source_target_pairs={{0,4},{2,6},{4,8},{6,10},{8,12},{10,14},{12,0},{14,2},{1,5},{3,7},... | collective-permute-start | bytes 1572872 | tf_op jit(solution)/shard_map/ppermute | solution.py:185
  97.5 33.0 %collective-permute-start.13 = (bf16[128,2048]{1,0:T(8,128)(2,1)S(1)}, bf16[128,2048]{1,0:T(8,128)(2,1)}, u32[]{:S(2)}, u32[]{:S(2)}) collective-permute-start(bf16[128,2048]{1,0:T(8,128)(2,1)S(1)} %collective-permute-done.5.refs_4_.refs_1_), channel_id=1, source_target_pairs={{0,4},{2,6},{4,8},{6,10},{8,12},{10,14},{12,0},{14,2},{1,5},{3,7},... | collective-permute-start | bytes 1572872 | tf_op jit(solution)/shard_map/ppermute | solution.py:185
  108.8 21.7 %collective-permute-start.14 = (bf16[128,2048]{1,0:T(8,128)(2,1)}, bf16[128,2048]{1,0:T(8,128)(2,1)S(1)}, u32[]{:S(2)}, u32[]{:S(2)}) collective-permute-start(bf16[128,2048]{1,0:T(8,128)(2,1)} %collective-permute-done.8.refs_2_), channel_id=1, source_target_pairs={{0,4},{2,6},{4,8},{6,10},{8,12},{10,14},{12,0},{14,2},{1,5},{3,7},... | collective-permute-start | bytes 1572872 | tf_op jit(solution)/shard_map/ppermute | solution.py:185
  108.8 1.3 copy-start.2
  116.6 1.0 copy-start.5
  117.6 13.5 %collective-permute-start.6 = (bf16[512,512]{1,0:T(8,128)(2,1)}, bf16[512,512]{1,0:T(8,128)(2,1)}, u32[]{:S(2)}, u32[]{:S(2)}) collective-permute-start(bf16[512,512]{1,0:T(8,128)(2,1)} %get-tuple-element.40.refs_3_), channel_id=1, source_target_pairs={{0,1},{1,0},{2,3},{3,2},{4,5},{5,4},{6,7},{7,6},{8,9},{9,8},{10,11... | collective-permute-start | bytes 1572872 | tf_op jit(solution)/shard_map/ppermute | solution.py:182
  123.4 5.6 %copy-start.9 = (bf16[512,512]{1,0:T(8,128)(2,1)}, bf16[512,512]{1,0:T(8,128)(2,1)S(1)}, u32[]{:S(2)}) copy-start(bf16[512,512]{1,0:T(8,128)(2,1)S(1)} %get-tuple-element.42.refs_2_) | copy-start | bytes 1572868
  129.0 1.0 copy-start.7
  130.0 2.3 %copy-start.6 = (f32[512,512]{1,0:T(8,128)S(1)}, f32[512,512]{1,0:T(8,128)}, u32[]{:S(2)}) copy-start(f32[512,512]{1,0:T(8,128)} %copy-done.5) | copy-start | bytes 3145732
  130.0 3.2 %collective-permute-start.12 = (bf16[512,512]{1,0:T(8,128)(2,1)}, bf16[512,512]{1,0:T(8,128)(2,1)}, u32[]{:S(2)}, u32[]{:S(2)}) collective-permute-start(bf16[512,512]{1,0:T(8,128)(2,1)} %get-tuple-element.44.refs_2_), channel_id=1, source_target_pairs={{0,1},{1,0},{2,3},{3,2},{4,5},{5,4},{6,7},{7,6},{8,9},{9,8},{10,11... | collective-permute-start | bytes 1572872 | tf_op jit(solution)/shard_map/ppermute | solution.py:182
  130.5 3.9 %copy-start.8 = (f32[512,512]{1,0:T(8,128)S(1)}, f32[512,512]{1,0:T(8,128)}, u32[]{:S(2)}) copy-start(f32[512,512]{1,0:T(8,128)} %copy-done.7) | copy-start | bytes 3145732
  130.5 16.8 %collective-permute-start.18 = (bf16[128,2048]{1,0:T(8,128)(2,1)}, bf16[128,2048]{1,0:T(8,128)(2,1)S(1)}, u32[]{:S(2)}, u32[]{:S(2)}) collective-permute-start(bf16[128,2048]{1,0:T(8,128)(2,1)} %collective-permute-done.13.refs_0_), channel_id=1, source_target_pairs={{0,4},{2,6},{4,8},{6,10},{8,12},{10,14},{12,0},{14,2},{1,5},{3,7},... | collective-permute-start | bytes 1572872 | tf_op jit(solution)/shard_map/ppermute | solution.py:185
  130.5 27.4 %collective-permute-start.22 = (bf16[128,2048]{1,0:T(8,128)(2,1)S(1)}, bf16[128,2048]{1,0:T(8,128)(2,1)S(1)}, u32[]{:S(2)}, u32[]{:S(2)}) collective-permute-start(bf16[128,2048]{1,0:T(8,128)(2,1)S(1)} %collective-permute-done.14.refs_1_), channel_id=1, source_target_pairs={{0,4},{2,6},{4,8},{6,10},{8,12},{10,14},{12,0},{14,2},{1,5},{3,7},... | collective-permute-start | bytes 1572872 | tf_op jit(solution)/shard_map/ppermute | solution.py:185
  131.1 4.9 %collective-permute-start.9 = (bf16[512,512]{1,0:T(8,128)(2,1)}, bf16[512,512]{1,0:T(8,128)(2,1)S(1)}, u32[]{:S(2)}, u32[]{:S(2)}) collective-permute-start(bf16[512,512]{1,0:T(8,128)(2,1)} %copy-done.9), channel_id=1, source_target_pairs={{0,1},{1,0},{2,3},{3,2},{4,5},{5,4},{6,7},{7,6},{8,9},{9,8},{10,11... | collective-permute-start | bytes 1572872 | tf_op jit(solution)/shard_map/ppermute | solution.py:182
  132.3 9.2 %collective-permute-start.7 = (bf16[256,512]{1,0:T(8,128)(2,1)S(1)}, bf16[256,512]{1,0:T(8,128)(2,1)S(1)}, u32[]{:S(2)}, u32[]{:S(2)}) collective-permute-start(bf16[256,512]{1,0:T(8,128)(2,1)S(1)} %fusion.4), channel_id=1, source_target_pairs={{0,2},{2,0},{4,6},{6,4},{8,10},{10,8},{12,14},{14,12},{1,3},{3,1},... | collective-permute-start | bytes 786440 | tf_op jit(solution)/shard_map/ppermute | solution.py:179
  134.6 6.9 %copy-start.1 = (bf16[512,2048]{1,0:T(8,128)(2,1)S(1)}, bf16[512,2048]{1,0:T(8,128)(2,1)}, u32[]{:S(2)}) copy-start(bf16[512,2048]{1,0:T(8,128)(2,1)} %copy-done) | copy-start | bytes 6291460
  134.6 23.3 %collective-permute-start.17 = (bf16[256,512]{1,0:T(8,128)(2,1)S(1)}, bf16[256,512]{1,0:T(8,128)(2,1)S(1)}, u32[]{:S(2)}, u32[]{:S(2)}) collective-permute-start(bf16[256,512]{1,0:T(8,128)(2,1)S(1)} %get-tuple-element.55.refs_1_), channel_id=1, source_target_pairs={{0,2},{2,0},{4,6},{6,4},{8,10},{10,8},{12,14},{14,12},{1,3},{3,1},... | collective-permute-start | bytes 786440 | tf_op jit(solution)/shard_map/ppermute | solution.py:179
  136.2 11.1 %copy-start.3 = (bf16[512,2048]{1,0:T(8,128)(2,1)S(1)}, bf16[512,2048]{1,0:T(8,128)(2,1)}, u32[]{:S(2)}) copy-start(bf16[512,2048]{1,0:T(8,128)(2,1)} %copy-done.2) | copy-start | bytes 6291460
  136.2 16.6 %collective-permute-start.10 = (bf16[256,512]{1,0:T(8,128)(2,1)S(1)}, bf16[256,512]{1,0:T(8,128)(2,1)S(1)}, u32[]{:S(2)}, u32[]{:S(2)}) collective-permute-start(bf16[256,512]{1,0:T(8,128)(2,1)S(1)} %fusion.1), channel_id=1, source_target_pairs={{0,2},{2,0},{4,6},{6,4},{8,10},{10,8},{12,14},{14,12},{1,3},{3,1},... | collective-permute-start | bytes 786440 | tf_op jit(solution)/shard_map/ppermute | solution.py:179
  145.5 4.2 %collective-permute-start.15 = (bf16[512,256]{1,0:T(8,128)(2,1)S(1)}, bf16[512,256]{1,0:T(8,128)(2,1)S(1)}, u32[]{:S(2)}, u32[]{:S(2)}) collective-permute-start(bf16[512,256]{1,0:T(8,128)(2,1)S(1)} %get-tuple-element.46.refs_0_), channel_id=1, source_target_pairs={{0,1},{1,0},{2,3},{3,2},{4,5},{5,4},{6,7},{7,6},{8,9},{9,8},{10,11... | collective-permute-start | bytes 786440 | tf_op jit(solution)/shard_map/ppermute | solution.py:182
  148.5 12.7 %collective-permute-start.19 = (bf16[256,128]{1,0:T(8,128)(2,1)S(1)}, bf16[256,128]{1,0:T(8,128)(2,1)S(1)}, u32[]{:S(2)}, u32[]{:S(2)}) collective-permute-start(bf16[256,128]{1,0:T(8,128)(2,1)S(1)} %get-tuple-element.47), channel_id=1, source_target_pairs={{0,2},{2,0},{4,6},{6,4},{8,10},{10,8},{12,14},{14,12},{1,3},{3,1},... | collective-permute-start | bytes 196616 | tf_op jit(solution)/shard_map/ppermute | solution.py:179
  149.7 11.9 %collective-permute-start.20 = (bf16[256,128]{1,0:T(8,128)(2,1)S(1)}, bf16[256,128]{1,0:T(8,128)(2,1)S(1)}, u32[]{:S(2)}, u32[]{:S(2)}) collective-permute-start(bf16[256,128]{1,0:T(8,128)(2,1)S(1)} %get-tuple-element.48), channel_id=1, source_target_pairs={{0,3},{1,2},{2,1},{3,0},{4,7},{5,6},{6,5},{7,4},{8,11},{9,10},{10,... | collective-permute-start | bytes 196616 | tf_op jit(solution)/shard_map/ppermute | solution.py:188
  152.7 7.2 %collective-permute-start.16 = (bf16[256,256]{1,0:T(8,128)(2,1)S(1)}, bf16[256,256]{1,0:T(8,128)(2,1)S(1)}, u32[]{:S(2)}, u32[]{:S(2)}) collective-permute-start(bf16[256,256]{1,0:T(8,128)(2,1)S(1)} %fusion.9.refs_2_), channel_id=1, source_target_pairs={{0,2},{2,0},{4,6},{6,4},{8,10},{10,8},{12,14},{14,12},{1,3},{3,1},... | collective-permute-start | bytes 393224 | tf_op jit(solution)/shard_map/ppermute | solution.py:179
  157.9 3.7 %collective-permute-start.21 = (bf16[256,128]{1,0:T(8,128)(2,1)S(1)}, bf16[256,128]{1,0:T(8,128)(2,1)S(1)}, u32[]{:S(2)}, u32[]{:S(2)}) collective-permute-start(bf16[256,128]{1,0:T(8,128)(2,1)S(1)} %get-tuple-element.50), channel_id=1, source_target_pairs={{0,1},{1,0},{2,3},{3,2},{4,5},{5,4},{6,7},{7,6},{8,9},{9,8},{10,11... | collective-permute-start | bytes 196616 | tf_op jit(solution)/shard_map/ppermute | solution.py:182
  159.2 5.0 %collective-permute-start.23 = (bf16[256,128]{1,0:T(8,128)(2,1)S(1)}, bf16[256,128]{1,0:T(8,128)(2,1)S(1)}, u32[]{:S(2)}, u32[]{:S(2)}) collective-permute-start(bf16[256,128]{1,0:T(8,128)(2,1)S(1)} %get-tuple-element.51), channel_id=1, source_target_pairs={{0,2},{2,0},{4,6},{6,4},{8,10},{10,8},{12,14},{14,12},{1,3},{3,1},... | collective-permute-start | bytes 196616 | tf_op jit(solution)/shard_map/ppermute | solution.py:179
  160.0 4.8 %collective-permute-start.24 = (bf16[256,128]{1,0:T(8,128)(2,1)S(1)}, bf16[256,128]{1,0:T(8,128)(2,1)S(1)}, u32[]{:S(2)}, u32[]{:S(2)}) collective-permute-start(bf16[256,128]{1,0:T(8,128)(2,1)S(1)} %get-tuple-element.52), channel_id=1, source_target_pairs={{0,3},{1,2},{2,1},{3,0},{4,7},{5,6},{6,5},{7,4},{8,11},{9,10},{10,... | collective-permute-start | bytes 196616 | tf_op jit(solution)/shard_map/ppermute | solution.py:188
  161.2 3.6 %collective-permute-start.25 = (bf16[256,128]{1,0:T(8,128)(2,1)S(1)}, bf16[256,128]{1,0:T(8,128)(2,1)S(1)}, u32[]{:S(2)}, u32[]{:S(2)}) collective-permute-start(bf16[256,128]{1,0:T(8,128)(2,1)S(1)} %get-tuple-element.54), channel_id=1, source_target_pairs={{0,1},{1,0},{2,3},{3,2},{4,5},{5,4},{6,7},{7,6},{8,9},{9,8},{10,11... | collective-permute-start | bytes 196616 | tf_op jit(solution)/shard_map/ppermute | solution.py:182
  164.8 1.3 copy-start.11

commit v11 on v10

--- a/solution.py
+++ b/solution.py
@@ -213,7 +213,7 @@
         return keep[:part] + got[:part], (keep[part:] + got[part:]).astype(bf16)
 
     besides = []
-    last = (first[2], second[1][0]) if places > 2 else ()
+    last = ()
     for step in range(places - 2):
         keep, give = score(spot, own, far, [first[step]] + second[step], *last)
         total, reach = over_cores(keep, give)
@@ -221,17 +221,17 @@
         out = put(out, total + besides[-1].astype(f32), step, 0)
         last = (give,)
 
-    keep, give = score(spot, own, far, first[-2:], *last)
+    keep, give = score(spot, own, far, first[-2:], *last, besides[0])
     early, early_reach = over_cores(keep, give)
     early_beside = swap_across(early_reach)
-    keep, give = score(spot, own, far, second[-2], give, besides[0])
+    keep, give = score(spot, own, far, second[-2], give, *besides)
     late, late_reach = over_cores(keep, give)
     late_beside = swap_across(late_reach)
     out = put(out, early[:, :queries] + late_beside.astype(f32), places - 2, side * queries)
     out = put(out, late + early_beside[:, :queries].astype(f32), places - 2, (1 - side) * queries)
 
     size = queries // 2
-    last = (give, early_reach)
+    last = (give,)
     for i, piece in enumerate(pieces):
         near, give, facing, opposite = last_score(own, far, piece, *last)
         cut = slice(queries + i * size, queries + (i + 1) * size)
@@ -239,7 +239,7 @@
         other_total = near + swap_cores(give).astype(f32) + early_beside[:, cut].astype(f32)
         out = put(out, mine_total, places - 1, side * queries + i * size)
         out = put(out, other_total, places - 1, (1 - side) * queries + i * size)
-        last = (near, early_beside, late_reach)
+        last = (near, late_reach)
     return out
 
 

time: 167 us -> 163 us (0.976)
  waiting for transfers between devices: 99 us -> 96.5 us
    ppermute x9, waiting for transfers between devices: 80.6 us -> 71.5 us  [pass_on(): return lax.ppermute(x, 'blk', onward)]
    ppermute x9, waiting for transfers between devices: 17.8 us -> 21.9 us  [swap_across(): return lax.ppermute(x, 'blk', across)]
    ppermute x2, waiting for transfers between devices: 0.62 us -> 3.06 us  [swap_diagonal(): return lax.ppermute(x, ('blk', 'proj'), diagonal)]
    ppermute x9, starting transfers between devices: 5.66 us -> 8.05 us  [pass_on(): return lax.ppermute(x, 'blk', onward)]
    unnamed x24 -> x34, local copies, waits for them, and re-layouts: 7.52 us -> 5.98 us
  transfers between devices with their start and end apart: 26 -> 26, of which waited for: 11 -> 13; matrix products, arithmetic and copies ran while one was open for 2% -> 2% of each run, Pallas kernels for 23% -> 23%
where the time goes in v11:
time: 163 us; the launch traced here: 162 us
  waiting for transfers between devices  96.5 us (59%)
  Pallas kernels  38.4 us (24%)
  starting transfers between devices  17.8 us (11%)
  local copies, waits for them, and re-layouts  6.21 us (4%)
  other arithmetic  3.08 us (2%)
    ppermute x9, waiting for transfers between devices, pass_on(): return lax.ppermute(x, 'blk', onward)  71.5 us
    ppermute x9, waiting for transfers between devices, swap_across(): return lax.ppermute(x, 'blk', across)  21.9 us
    pallas_call x4, Pallas kernels, score(): pl.pallas_call(functools.partial(score_body, count), in_specs=[SCALARS] +...  20.2 us
    pallas_call x1, Pallas kernels, form(): pl.pallas_call(functools.partial(form_body, rows, rank), grid_spec=pltpu....  13.4 us
    ppermute x9, starting transfers between devices, swap_across(): return lax.ppermute(x, 'blk', across)  8.78 us
    ppermute x9, starting transfers between devices, pass_on(): return lax.ppermute(x, 'blk', onward)  8.05 us
    unnamed x34, local copies, waits for them, and re-layouts  5.98 us
    pallas_call x2, Pallas kernels, last_score(): pl.pallas_call(last_body, in_specs=[WHOLE] * 3 + [ANYWHERE] * len(after),...  3.51 us
  transfers between devices with their start and end apart: 26, of which 13 were waited for; matrix products, arithmetic and copies ran while one was open for 2% of the time, Pallas kernels for 23%

profile of v11, /device:TPU:0, one launch (start us, length us, event | category | flops | bytes accessed | tf_op | source)
XLA Modules:
  0.0 162.3 jit_solution(2459521231833734194)
XLA Ops:
  0.0 0.1 pad_add_fusion.spot
  0.1 1.6 copy-done.4
  1.7 1.3 shard_map.47
  2.9 3.1 %collective-permute-start = (bf16[256,2048]{1,0:T(8,128)(2,1)S(1)}, bf16[256,2048]{1,0:T(8,128)(2,1)S(1)}, u32[]{:S(2)}, u32[]{:S(2)}) collective-permute-start(bf16[256,2048]{1,0:T(8,128)(2,1)S(1)} %get-tuple-element.32.refs_0_), channel_id=1, source_target_pairs={{0,4},{2,6},{4,8},{6,10},{8,12},{10,14},{12,0},{14,2},{1,5},{3,7},... | collective-permute-start | bytes 3145736 | tf_op jit(solution)/shard_map/ppermute | solution.py:185
  6.0 1.5 collective-permute-start.1
  7.5 0.5 collective-permute-start.2
  8.0 13.4 %shard_map.46 = (bf16[512,2048]{1,0:T(8,128)(2,1)S(1)}, bf16[512,2048]{1,0:T(8,128)(2,1)S(1)}) custom-call(s32[2]{0:T(128)S(1)} %pad_add_fusion.spot, bf16[512,64,128]{2,1,0:T(8,128)(2,1)} %bitcast.4, bf16[512,64,128]{2,1,0:T(8,128)(2,1)} %bitcast.5, s32[512,128]{1,0:T(8,128)S(1)} %copy-done.11), custom_call_target="tpu_custom_call" | custom-call | flops 10737418240 | bytes 20971520 | tf_op jit(solution)/shard_map/pallas_call | solution.py:72
  21.5 0.0 collective-permute-done.1.refs_2_
  21.5 9.2 %collective-permute-done.2.refs_3_ = bf16[128,2048]{1,0:T(8,128)(2,1)S(1)} collective-permute-done((bf16[128,2048]{1,0:T(8,128)(2,1)S(1)}, bf16[128,2048]{1,0:T(8,128)(2,1)S(1)}, u32[]{:S(2)}, u32[]{:S(2)}) %collective-permute-start.2) | collective-permute-done | bytes 524320 | tf_op jit(solution)/shard_map/ppermute | solution.py:179
  30.6 0.6 collective-permute-done.refs_1_
  31.2 1.5 collective-permute-start.3
  32.7 1.0 collective-permute-start.10
  33.7 1.6 collective-permute-start.6
  35.3 0.4 collective-permute-start.7
  35.7 36.2 %collective-permute-done.6.refs_1_ = bf16[128,2048]{1,0:T(8,128)(2,1)S(1)} collective-permute-done((bf16[128,2048]{1,0:T(8,128)(2,1)S(1)}, bf16[128,2048]{1,0:T(8,128)(2,1)S(1)}, u32[]{:S(2)}, u32[]{:S(2)}) %collective-permute-start.6) | collective-permute-done | bytes 524320 | tf_op jit(solution)/shard_map/ppermute | solution.py:185
  71.8 6.2 %collective-permute-done.3.far = bf16[512,2048]{1,0:T(8,128)(2,1)S(1)} collective-permute-done((bf16[512,2048]{1,0:T(8,128)(2,1)S(1)}, bf16[512,2048]{1,0:T(8,128)(2,1)S(1)}, u32[]{:S(2)}, u32[]{:S(2)}) %collective-permute-start.3) | collective-permute-done | bytes 2097184 | tf_op jit(solution)/shard_map/ppermute | solution.py:179
  78.0 1.3 copy-done.2
  79.3 5.0 %shard_map.49 = (f32[512,512]{1,0:T(8,128)S(1)}, bf16[512,512]{1,0:T(8,128)(2,1)S(1)}) custom-call(s32[2]{0:T(128)S(1)} %pad_add_fusion.spot, bf16[512,2048]{1,0:T(8,128)(2,1)S(1)} %get-tuple-element.30.own, bf16[512,2048]{1,0:T(8,128)(2,1)} %copy-done.2, bf16[256,2048]{1,0:T(8,128)(2,1)S(1)} %get-tuple-element.32.refs_0_, ...), custom_call_target="tpu_custom_call" | custom-call | flops 1024 | bytes 1024 | tf_op jit(solution)/shard_map/pallas_call | solution.py:133
  84.4 0.1 collective-permute-start.4
  84.5 0.4 collective-permute-start.11
  84.9 0.0 collective-permute-done.7.refs_2_
  84.9 5.8 %shard_map.50 = (f32[512,512]{1,0:T(8,128)S(1)}, bf16[512,512]{1,0:T(8,128)(2,1)S(1)}) custom-call(s32[2]{0:T(128)S(1)} %pad_add_fusion.spot, bf16[512,2048]{1,0:T(8,128)(2,1)} %copy-done, bf16[512,2048]{1,0:T(8,128)(2,1)} %copy-done.2, bf16[256,2048]{1,0:T(8,128)(2,1)S(1)} %get-tuple-element.40.refs_0_, ...), custom_call_target="tpu_custom_call" | custom-call | flops 1024 | bytes 1024 | tf_op jit(solution)/shard_map/pallas_call | solution.py:133
  90.7 0.2 collective-permute-start.8
  90.9 1.6 collective-permute-start.14
  92.5 1.9 %collective-permute-done.13.refs_0_ = bf16[128,2048]{1,0:T(8,128)(2,1)} collective-permute-done((bf16[128,2048]{1,0:T(8,128)(2,1)S(1)}, bf16[128,2048]{1,0:T(8,128)(2,1)}, u32[]{:S(2)}, u32[]{:S(2)}) %collective-permute-start.13) | collective-permute-done | bytes 524320 | tf_op jit(solution)/shard_map/ppermute | solution.py:185
  94.4 0.0 collective-permute-start.18
  94.4 0.1 convert_element_type.60
  94.6 0.1 fusion.4
  94.7 0.6 collective-permute-start.5
  95.3 0.1 convert_element_type.63
  95.4 0.1 fusion.1
  95.5 0.0 copy-done.14
  95.6 1.6 collective-permute-start.9
  97.1 19.7 %collective-permute-done.11.refs_1_ = bf16[256,2048]{1,0:T(8,128)(2,1)S(1)} collective-permute-done((bf16[256,2048]{1,0:T(8,128)(2,1)S(1)}, bf16[256,2048]{1,0:T(8,128)(2,1)S(1)}, u32[]{:S(2)}, u32[]{:S(2)}) %collective-permute-start.11) | collective-permute-done | bytes 1048608 | tf_op jit(solution)/shard_map/ppermute | solution.py:185
  116.8 5.4 %shard_map.51 = (f32[512,512]{1,0:T(8,128)S(1)}, bf16[512,512]{1,0:T(8,128)(2,1)}) custom-call(s32[2]{0:T(128)S(1)} %pad_add_fusion.spot, bf16[512,2048]{1,0:T(8,128)(2,1)} %copy-done, bf16[512,2048]{1,0:T(8,128)(2,1)} %copy-done.2, bf16[256,2048]{1,0:T(8,128)(2,1)S(1)} %collective-permute-done.10.refs_0_, ...), custom_call_target="tpu_custom_call" | custom-call | flops 1024 | bytes 1024 | tf_op jit(solution)/shard_map/pallas_call | solution.py:133
  122.2 1.0 copy-done.9
  123.2 4.8 %collective-permute-done.14.refs_1_ = bf16[128,2048]{1,0:T(8,128)(2,1)S(1)} collective-permute-done((bf16[128,2048]{1,0:T(8,128)(2,1)}, bf16[128,2048]{1,0:T(8,128)(2,1)S(1)}, u32[]{:S(2)}, u32[]{:S(2)}) %collective-permute-start.14) | collective-permute-done | bytes 524320 | tf_op jit(solution)/shard_map/ppermute | solution.py:185
  128.0 0.0 collective-permute-start.22
  128.0 4.0 %shard_map.52 = (f32[512,256]{1,0:T(8,128)S(1)}, bf16[512,256]{1,0:T(8,128)(2,1)S(1)}) custom-call(s32[2]{0:T(128)S(1)} %pad_add_fusion.spot, bf16[512,2048]{1,0:T(8,128)(2,1)S(1)} %copy-done.1, bf16[512,2048]{1,0:T(8,128)(2,1)} %copy-done.2, bf16[128,2048]{1,0:T(8,128)(2,1)} %collective-permute-done.13.refs_0_, ...), custom_call_target="tpu_custom_call" | custom-call | flops 1024 | bytes 1024 | tf_op jit(solution)/shard_map/pallas_call | solution.py:133
  132.0 0.1 collective-permute-start.15
  132.1 7.2 %collective-permute-done.18.block = bf16[128,2048]{1,0:T(8,128)(2,1)} collective-permute-done((bf16[128,2048]{1,0:T(8,128)(2,1)}, bf16[128,2048]{1,0:T(8,128)(2,1)}, u32[]{:S(2)}, u32[]{:S(2)}) %collective-permute-start.18) | collective-permute-done | bytes 524320 | tf_op jit(solution)/shard_map/ppermute | solution.py:185
  139.4 2.3 %shard_map.53 = (f32[256,128]{1,0:T(8,128)S(1)}, bf16[256,128]{1,0:T(8,128)(2,1)S(1)}, bf16[256,128]{1,0:T(8,128)(2,1)S(1)}, bf16[256,128]{1,0:T(8,128)(2,1)S(1)}) custom-call(bf16[512,2048]{1,0:T(8,128)(2,1)S(1)} %copy-done.1, bf16[512,2048]{1,0:T(8,128)(2,1)S(1)} %copy-done.3, bf16[128,2048]{1,0:T(8,128)(2,1)} %collective-permute-done.18.block, ...), custom_call_target="tpu_custom_call" | custom-call | flops 1024 | bytes 1024 | tf_op jit(solution)/shard_map/pallas_call | solution.py:154
  141.7 0.6 collective-permute-start.19
  142.2 0.2 broadcast_in_dim.3
  142.5 0.4 copy-done.8
  142.9 0.3 copy-done.15
  143.2 0.1 fusion.6
  143.4 0.9 collective-permute-start.16
  144.4 1.2 convert_element_type.66
  145.5 0.2 fusion
  145.8 1.3 collective-permute-start.17
  147.0 0.1 fusion.3
  147.2 1.1 collective-permute-done.22.block
  148.2 1.2 shard_map.54
  149.5 0.9 collective-permute-done.16
  150.4 0.4 collective-permute-start.23
  150.8 5.2 %collective-permute-done.17 = bf16[256,512]{1,0:T(8,128)(2,1)S(1)} collective-permute-done((bf16[256,512]{1,0:T(8,128)(2,1)S(1)}, bf16[256,512]{1,0:T(8,128)(2,1)S(1)}, u32[]{:S(2)}, u32[]{:S(2)}) %collective-permute-start.17) | collective-permute-done | bytes 262176 | tf_op jit(solution)/shard_map/ppermute | solution.py:179
  156.0 0.1 collective-permute-start.24
  156.1 0.5 collective-permute-start.25
  156.7 0.5 collective-permute-done.23
  157.2 3.1 %collective-permute-done.24 = bf16[256,128]{1,0:T(8,128)(2,1)S(1)} collective-permute-done((bf16[256,128]{1,0:T(8,128)(2,1)S(1)}, bf16[256,128]{1,0:T(8,128)(2,1)S(1)}, u32[]{:S(2)}, u32[]{:S(2)}) %collective-permute-start.24) | collective-permute-done | bytes 65568 | tf_op jit(solution)/shard_map/ppermute | solution.py:188
  160.3 0.0 copy-start.16
  160.3 1.3 copy-done.16
  161.6 0.7 add_dynamic-update-slice_fusion
  (49 shorter events, 0.3 us)
Async XLA Ops:
  0.1 1.6 copy-start.4
  1.7 6.4 %copy-start.11 = (s32[512,128]{1,0:T(8,128)S(1)}, s32[512,128]{1,0:T(8,128)}, u32[]{:S(2)}) copy-start(s32[512,128]{1,0:T(8,128)} %mask.1) | copy-start | bytes 786436
  2.9 28.3 %collective-permute-start = (bf16[256,2048]{1,0:T(8,128)(2,1)S(1)}, bf16[256,2048]{1,0:T(8,128)(2,1)S(1)}, u32[]{:S(2)}, u32[]{:S(2)}) collective-permute-start(bf16[256,2048]{1,0:T(8,128)(2,1)S(1)} %get-tuple-element.32.refs_0_), channel_id=1, source_target_pairs={{0,4},{2,6},{4,8},{6,10},{8,12},{10,14},{12,0},{14,2},{1,5},{3,7},... | collective-permute-start | bytes 3145736 | tf_op jit(solution)/shard_map/ppermute | solution.py:185
  6.0 15.4 %collective-permute-start.1 = (bf16[128,2048]{1,0:T(8,128)(2,1)S(1)}, bf16[128,2048]{1,0:T(8,128)(2,1)S(1)}, u32[]{:S(2)}, u32[]{:S(2)}) collective-permute-start(bf16[128,2048]{1,0:T(8,128)(2,1)S(1)} %get-tuple-element.33), channel_id=1, source_target_pairs={{0,2},{2,0},{4,6},{6,4},{8,10},{10,8},{12,14},{14,12},{1,3},{3,1},... | collective-permute-start | bytes 1572872 | tf_op jit(solution)/shard_map/ppermute | solution.py:179
  7.5 23.1 %collective-permute-start.2 = (bf16[128,2048]{1,0:T(8,128)(2,1)S(1)}, bf16[128,2048]{1,0:T(8,128)(2,1)S(1)}, u32[]{:S(2)}, u32[]{:S(2)}) collective-permute-start(bf16[128,2048]{1,0:T(8,128)(2,1)S(1)} %get-tuple-element.34), channel_id=1, source_target_pairs={{0,2},{2,0},{4,6},{6,4},{8,10},{10,8},{12,14},{14,12},{1,3},{3,1},... | collective-permute-start | bytes 1572872 | tf_op jit(solution)/shard_map/ppermute | solution.py:179
  21.4 56.6 %copy-start = (bf16[512,2048]{1,0:T(8,128)(2,1)}, bf16[512,2048]{1,0:T(8,128)(2,1)S(1)}, u32[]{:S(2)}) copy-start(bf16[512,2048]{1,0:T(8,128)(2,1)S(1)} %get-tuple-element.30.own) | copy-start | bytes 6291460
  31.2 46.8 %collective-permute-start.3 = (bf16[512,2048]{1,0:T(8,128)(2,1)S(1)}, bf16[512,2048]{1,0:T(8,128)(2,1)S(1)}, u32[]{:S(2)}, u32[]{:S(2)}) collective-permute-start(bf16[512,2048]{1,0:T(8,128)(2,1)S(1)} %get-tuple-element.35), channel_id=1, source_target_pairs={{0,2},{2,0},{4,6},{6,4},{8,10},{10,8},{12,14},{14,12},{1,3},{3,1},... | collective-permute-start | bytes 6291464 | tf_op jit(solution)/shard_map/ppermute | solution.py:179
  32.7 51.8 %collective-permute-start.10 = (bf16[256,2048]{1,0:T(8,128)(2,1)S(1)}, bf16[256,2048]{1,0:T(8,128)(2,1)S(1)}, u32[]{:S(2)}, u32[]{:S(2)}) collective-permute-start(bf16[256,2048]{1,0:T(8,128)(2,1)S(1)} %get-tuple-element.40.refs_0_), channel_id=1, source_target_pairs={{0,4},{2,6},{4,8},{6,10},{8,12},{10,14},{12,0},{14,2},{1,5},{3,7},... | collective-permute-start | bytes 3145736 | tf_op jit(solution)/shard_map/ppermute | solution.py:185
  33.7 38.1 %collective-permute-start.6 = (bf16[128,2048]{1,0:T(8,128)(2,1)S(1)}, bf16[128,2048]{1,0:T(8,128)(2,1)S(1)}, u32[]{:S(2)}, u32[]{:S(2)}) collective-permute-start(bf16[128,2048]{1,0:T(8,128)(2,1)S(1)} %get-tuple-element.36.refs_1_), channel_id=1, source_target_pairs={{0,4},{2,6},{4,8},{6,10},{8,12},{10,14},{12,0},{14,2},{1,5},{3,7},... | collective-permute-start | bytes 1572872 | tf_op jit(solution)/shard_map/ppermute | solution.py:185
  35.3 49.6 %collective-permute-start.7 = (bf16[128,2048]{1,0:T(8,128)(2,1)S(1)}, bf16[128,2048]{1,0:T(8,128)(2,1)}, u32[]{:S(2)}, u32[]{:S(2)}) collective-permute-start(bf16[128,2048]{1,0:T(8,128)(2,1)S(1)} %get-tuple-element.37.refs_2_), channel_id=1, source_target_pairs={{0,4},{2,6},{4,8},{6,10},{8,12},{10,14},{12,0},{14,2},{1,5},{3,7},... | collective-permute-start | bytes 1572872 | tf_op jit(solution)/shard_map/ppermute | solution.py:185
  71.8 22.6 %collective-permute-start.13 = (bf16[128,2048]{1,0:T(8,128)(2,1)S(1)}, bf16[128,2048]{1,0:T(8,128)(2,1)}, u32[]{:S(2)}, u32[]{:S(2)}) collective-permute-start(bf16[128,2048]{1,0:T(8,128)(2,1)S(1)} %collective-permute-done.6.refs_1_), channel_id=1, source_target_pairs={{0,4},{2,6},{4,8},{6,10},{8,12},{10,14},{12,0},{14,2},{1,5},{3,7},... | collective-permute-start | bytes 1572872 | tf_op jit(solution)/shard_map/ppermute | solution.py:185
  78.0 1.3 copy-start.2
  84.4 10.2 %copy-start.7 = (f32[512,512]{1,0:T(8,128)}, f32[512,512]{1,0:T(8,128)S(1)}, u32[]{:S(2)}) copy-start(f32[512,512]{1,0:T(8,128)S(1)} %get-tuple-element.38) | copy-start | bytes 3145732
  84.4 10.0 %collective-permute-start.4 = (bf16[512,512]{1,0:T(8,128)(2,1)S(1)}, bf16[512,512]{1,0:T(8,128)(2,1)S(1)}, u32[]{:S(2)}, u32[]{:S(2)}) collective-permute-start(bf16[512,512]{1,0:T(8,128)(2,1)S(1)} %get-tuple-element.39.refs_3_), channel_id=1, source_target_pairs={{0,1},{1,0},{2,3},{3,2},{4,5},{5,4},{6,7},{7,6},{8,9},{9,8},{10,11... | collective-permute-start | bytes 1572872 | tf_op jit(solution)/shard_map/ppermute | solution.py:182
  84.5 32.3 %collective-permute-start.11 = (bf16[256,2048]{1,0:T(8,128)(2,1)S(1)}, bf16[256,2048]{1,0:T(8,128)(2,1)S(1)}, u32[]{:S(2)}, u32[]{:S(2)}) collective-permute-start(bf16[256,2048]{1,0:T(8,128)(2,1)S(1)} %collective-permute-done.10.refs_0_), channel_id=1, source_target_pairs={{0,4},{2,6},{4,8},{6,10},{8,12},{10,14},{12,0},{14,2},{1,5},{3,7},... | collective-permute-start | bytes 3145736 | tf_op jit(solution)/shard_map/ppermute | solution.py:185
  90.7 4.7 %copy-start.5 = (f32[512,512]{1,0:T(8,128)}, f32[512,512]{1,0:T(8,128)S(1)}, u32[]{:S(2)}) copy-start(f32[512,512]{1,0:T(8,128)S(1)} %get-tuple-element.41) | copy-start | bytes 3145732
  90.7 4.6 %collective-permute-start.8 = (bf16[512,512]{1,0:T(8,128)(2,1)S(1)}, bf16[512,512]{1,0:T(8,128)(2,1)S(1)}, u32[]{:S(2)}, u32[]{:S(2)}) collective-permute-start(bf16[512,512]{1,0:T(8,128)(2,1)S(1)} %get-tuple-element.42.refs_2_), channel_id=1, source_target_pairs={{0,1},{1,0},{2,3},{3,2},{4,5},{5,4},{6,7},{7,6},{8,9},{9,8},{10,11... | collective-permute-start | bytes 1572872 | tf_op jit(solution)/shard_map/ppermute | solution.py:182
  90.9 37.1 %collective-permute-start.14 = (bf16[128,2048]{1,0:T(8,128)(2,1)}, bf16[128,2048]{1,0:T(8,128)(2,1)S(1)}, u32[]{:S(2)}, u32[]{:S(2)}) collective-permute-start(bf16[128,2048]{1,0:T(8,128)(2,1)} %collective-permute-done.7.refs_2_), channel_id=1, source_target_pairs={{0,4},{2,6},{4,8},{6,10},{8,12},{10,14},{12,0},{14,2},{1,5},{3,7},... | collective-permute-start | bytes 1572872 | tf_op jit(solution)/shard_map/ppermute | solution.py:185
  94.4 44.9 %collective-permute-start.18 = (bf16[128,2048]{1,0:T(8,128)(2,1)}, bf16[128,2048]{1,0:T(8,128)(2,1)}, u32[]{:S(2)}, u32[]{:S(2)}) collective-permute-start(bf16[128,2048]{1,0:T(8,128)(2,1)} %collective-permute-done.13.refs_0_), channel_id=1, source_target_pairs={{0,4},{2,6},{4,8},{6,10},{8,12},{10,14},{12,0},{14,2},{1,5},{3,7},... | collective-permute-start | bytes 1572872 | tf_op jit(solution)/shard_map/ppermute | solution.py:185
  94.6 1.0 copy-start.14
  94.7 22.1 %collective-permute-start.5 = (bf16[256,512]{1,0:T(8,128)(2,1)S(1)}, bf16[256,512]{1,0:T(8,128)(2,1)S(1)}, u32[]{:S(2)}, u32[]{:S(2)}) collective-permute-start(bf16[256,512]{1,0:T(8,128)(2,1)S(1)} %fusion.4), channel_id=1, source_target_pairs={{0,2},{2,0},{4,6},{6,4},{8,10},{10,8},{12,14},{14,12},{1,3},{3,1},... | collective-permute-start | bytes 786440 | tf_op jit(solution)/shard_map/ppermute | solution.py:179
  95.4 21.4 %copy-start.12 = (f32[512,512]{1,0:T(8,128)}, f32[512,512]{1,0:T(8,128)S(1)}, u32[]{:S(2)}) copy-start(f32[512,512]{1,0:T(8,128)S(1)} %convert_element_type.63) | copy-start | bytes 3145732
  95.5 32.5 %copy-start.1 = (bf16[512,2048]{1,0:T(8,128)(2,1)S(1)}, bf16[512,2048]{1,0:T(8,128)(2,1)}, u32[]{:S(2)}) copy-start(bf16[512,2048]{1,0:T(8,128)(2,1)} %copy-done) | copy-start | bytes 6291460
  95.6 32.5 %collective-permute-start.9 = (bf16[256,512]{1,0:T(8,128)(2,1)S(1)}, bf16[256,512]{1,0:T(8,128)(2,1)S(1)}, u32[]{:S(2)}, u32[]{:S(2)}) collective-permute-start(bf16[256,512]{1,0:T(8,128)(2,1)S(1)} %fusion.1), channel_id=1, source_target_pairs={{0,2},{2,0},{4,6},{6,4},{8,10},{10,8},{12,14},{14,12},{1,3},{3,1},... | collective-permute-start | bytes 786440 | tf_op jit(solution)/shard_map/ppermute | solution.py:179
  122.2 1.0 copy-start.9
  123.2 21.2 %collective-permute-start.12 = (bf16[512,512]{1,0:T(8,128)(2,1)}, bf16[512,512]{1,0:T(8,128)(2,1)}, u32[]{:S(2)}, u32[]{:S(2)}) collective-permute-start(bf16[512,512]{1,0:T(8,128)(2,1)} %get-tuple-element.44.refs_2_), channel_id=1, source_target_pairs={{0,1},{1,0},{2,3},{3,2},{4,5},{5,4},{6,7},{7,6},{8,9},{9,8},{10,11... | collective-permute-start | bytes 1572872 | tf_op jit(solution)/shard_map/ppermute | solution.py:182
  123.2 16.2 %copy-start.3 = (bf16[512,2048]{1,0:T(8,128)(2,1)S(1)}, bf16[512,2048]{1,0:T(8,128)(2,1)}, u32[]{:S(2)}) copy-start(bf16[512,2048]{1,0:T(8,128)(2,1)} %copy-done.2) | copy-start | bytes 6291460
  128.0 20.2 %collective-permute-start.22 = (bf16[128,2048]{1,0:T(8,128)(2,1)S(1)}, bf16[128,2048]{1,0:T(8,128)(2,1)S(1)}, u32[]{:S(2)}, u32[]{:S(2)}) collective-permute-start(bf16[128,2048]{1,0:T(8,128)(2,1)S(1)} %collective-permute-done.14.refs_1_), channel_id=1, source_target_pairs={{0,4},{2,6},{4,8},{6,10},{8,12},{10,14},{12,0},{14,2},{1,5},{3,7},... | collective-permute-start | bytes 1572872 | tf_op jit(solution)/shard_map/ppermute | solution.py:185
  132.0 11.3 %collective-permute-start.15 = (bf16[512,256]{1,0:T(8,128)(2,1)S(1)}, bf16[512,256]{1,0:T(8,128)(2,1)S(1)}, u32[]{:S(2)}, u32[]{:S(2)}) collective-permute-start(bf16[512,256]{1,0:T(8,128)(2,1)S(1)} %get-tuple-element.46.refs_0_), channel_id=1, source_target_pairs={{0,1},{1,0},{2,3},{3,2},{4,5},{5,4},{6,7},{7,6},{8,9},{9,8},{10,11... | collective-permute-start | bytes 786440 | tf_op jit(solution)/shard_map/ppermute | solution.py:182
  141.6 1.2 copy-start.8
  141.7 1.5 copy-start.15
  141.7 14.4 %collective-permute-start.19 = (bf16[256,128]{1,0:T(8,128)(2,1)S(1)}, bf16[256,128]{1,0:T(8,128)(2,1)S(1)}, u32[]{:S(2)}, u32[]{:S(2)}) collective-permute-start(bf16[256,128]{1,0:T(8,128)(2,1)S(1)} %get-tuple-element.47), channel_id=1, source_target_pairs={{0,2},{2,0},{4,6},{6,4},{8,10},{10,8},{12,14},{14,12},{1,3},{3,1},... | collective-permute-start | bytes 196616 | tf_op jit(solution)/shard_map/ppermute | solution.py:179
  142.2 14.4 %collective-permute-start.20 = (bf16[256,128]{1,0:T(8,128)(2,1)S(1)}, bf16[256,128]{1,0:T(8,128)(2,1)S(1)}, u32[]{:S(2)}, u32[]{:S(2)}) collective-permute-start(bf16[256,128]{1,0:T(8,128)(2,1)S(1)} %get-tuple-element.48), channel_id=1, source_target_pairs={{0,3},{1,2},{2,1},{3,0},{4,7},{5,6},{6,5},{7,4},{8,11},{9,10},{10,... | collective-permute-start | bytes 196616 | tf_op jit(solution)/shard_map/ppermute | solution.py:188
  143.2 2.3 %copy-start.10 = (f32[512,512]{1,0:T(8,128)S(1)}, f32[512,512]{1,0:T(8,128)}, u32[]{:S(2)}) copy-start(f32[512,512]{1,0:T(8,128)} %copy-done.9) | copy-start | bytes 3145732
  143.4 3.6 %copy-start.6 = (f32[512,512]{1,0:T(8,128)S(1)}, f32[512,512]{1,0:T(8,128)}, u32[]{:S(2)}) copy-start(f32[512,512]{1,0:T(8,128)} %copy-done.5) | copy-start | bytes 3145732
  143.4 3.6 %copy-start.13 = (f32[512,512]{1,0:T(8,128)S(1)}, f32[512,512]{1,0:T(8,128)}, u32[]{:S(2)}) copy-start(f32[512,512]{1,0:T(8,128)} %copy-done.12) | copy-start | bytes 3145732
  143.4 6.9 %collective-permute-start.16 = (bf16[256,256]{1,0:T(8,128)(2,1)S(1)}, bf16[256,256]{1,0:T(8,128)(2,1)S(1)}, u32[]{:S(2)}, u32[]{:S(2)}) collective-permute-start(bf16[256,256]{1,0:T(8,128)(2,1)S(1)} %fusion.9.refs_1_), channel_id=1, source_target_pairs={{0,2},{2,0},{4,6},{6,4},{8,10},{10,8},{12,14},{14,12},{1,3},{3,1},... | collective-permute-start | bytes 393224 | tf_op jit(solution)/shard_map/ppermute | solution.py:179
  145.8 10.2 %collective-permute-start.17 = (bf16[256,512]{1,0:T(8,128)(2,1)S(1)}, bf16[256,512]{1,0:T(8,128)(2,1)S(1)}, u32[]{:S(2)}, u32[]{:S(2)}) collective-permute-start(bf16[256,512]{1,0:T(8,128)(2,1)S(1)} %get-tuple-element.55), channel_id=1, source_target_pairs={{0,2},{2,0},{4,6},{6,4},{8,10},{10,8},{12,14},{14,12},{1,3},{3,1},... | collective-permute-start | bytes 786440 | tf_op jit(solution)/shard_map/ppermute | solution.py:179
  148.2 8.4 %collective-permute-start.21 = (bf16[256,128]{1,0:T(8,128)(2,1)S(1)}, bf16[256,128]{1,0:T(8,128)(2,1)S(1)}, u32[]{:S(2)}, u32[]{:S(2)}) collective-permute-start(bf16[256,128]{1,0:T(8,128)(2,1)S(1)} %get-tuple-element.50), channel_id=1, source_target_pairs={{0,1},{1,0},{2,3},{3,2},{4,5},{5,4},{6,7},{7,6},{8,9},{9,8},{10,11... | collective-permute-start | bytes 196616 | tf_op jit(solution)/shard_map/ppermute | solution.py:182
  150.4 6.8 %collective-permute-start.23 = (bf16[256,128]{1,0:T(8,128)(2,1)S(1)}, bf16[256,128]{1,0:T(8,128)(2,1)S(1)}, u32[]{:S(2)}, u32[]{:S(2)}) collective-permute-start(bf16[256,128]{1,0:T(8,128)(2,1)S(1)} %get-tuple-element.51), channel_id=1, source_target_pairs={{0,2},{2,0},{4,6},{6,4},{8,10},{10,8},{12,14},{14,12},{1,3},{3,1},... | collective-permute-start | bytes 196616 | tf_op jit(solution)/shard_map/ppermute | solution.py:179
  156.0 4.2 %collective-permute-start.24 = (bf16[256,128]{1,0:T(8,128)(2,1)S(1)}, bf16[256,128]{1,0:T(8,128)(2,1)S(1)}, u32[]{:S(2)}, u32[]{:S(2)}) collective-permute-start(bf16[256,128]{1,0:T(8,128)(2,1)S(1)} %get-tuple-element.52), channel_id=1, source_target_pairs={{0,3},{1,2},{2,1},{3,0},{4,7},{5,6},{6,5},{7,4},{8,11},{9,10},{10,... | collective-permute-start | bytes 196616 | tf_op jit(solution)/shard_map/ppermute | solution.py:188
  156.1 4.2 %collective-permute-start.25 = (bf16[256,128]{1,0:T(8,128)(2,1)S(1)}, bf16[256,128]{1,0:T(8,128)(2,1)S(1)}, u32[]{:S(2)}, u32[]{:S(2)}) collective-permute-start(bf16[256,128]{1,0:T(8,128)(2,1)S(1)} %get-tuple-element.54), channel_id=1, source_target_pairs={{0,1},{1,0},{2,3},{3,2},{4,5},{5,4},{6,7},{7,6},{8,9},{9,8},{10,11... | collective-permute-start | bytes 196616 | tf_op jit(solution)/shard_map/ppermute | solution.py:182
  160.3 1.3 copy-start.16

commit v12 on v11

--- a/solution.py
+++ b/solution.py
@@ -221,25 +221,26 @@
         out = put(out, total + besides[-1].astype(f32), step, 0)
         last = (give,)
 
-    keep, give = score(spot, own, far, first[-2:], *last, besides[0])
+    keep, give = score(spot, own, far, first[-2:], *last, besides[0], reach)
     early, early_reach = over_cores(keep, give)
     early_beside = swap_across(early_reach)
-    keep, give = score(spot, own, far, second[-2], give, *besides)
+    keep, give = score(spot, own, far, second[-2], give)
     late, late_reach = over_cores(keep, give)
     late_beside = swap_across(late_reach)
     out = put(out, early[:, :queries] + late_beside.astype(f32), places - 2, side * queries)
     out = put(out, late + early_beside[:, :queries].astype(f32), places - 2, (1 - side) * queries)
 
     size = queries // 2
-    last = (give,)
+    last = (give, early_reach)
     for i, piece in enumerate(pieces):
         near, give, facing, opposite = last_score(own, far, piece, *last)
         cut = slice(queries + i * size, queries + (i + 1) * size)
-        mine_total = early[:, cut] + swap_across(facing).astype(f32) + swap_diagonal(opposite).astype(f32)
+        faced, opposed = swap_across(facing), swap_diagonal(opposite)
+        mine_total = early[:, cut] + faced.astype(f32) + opposed.astype(f32)
         other_total = near + swap_cores(give).astype(f32) + early_beside[:, cut].astype(f32)
         out = put(out, mine_total, places - 1, side * queries + i * size)
         out = put(out, other_total, places - 1, (1 - side) * queries + i * size)
-        last = (near, late_reach)
+        last = (near, faced, opposed)
     return out
 
 

time: 163 us -> 158 us (0.969)
  waiting for transfers between devices: 96.5 us -> 89.8 us
  starting transfers between devices: 17.8 us -> 20 us
    ppermute x9, waiting for transfers between devices: 71.5 us -> 58.7 us  [pass_on(): return lax.ppermute(x, 'blk', onward)]
    ppermute x9, waiting for transfers between devices: 21.9 us -> 28.5 us  [swap_across(): return lax.ppermute(x, 'blk', across)]
where the time goes in v12:
time: 158 us
  waiting for transfers between devices  89.8 us (57%)
  Pallas kernels  38.1 us (24%)
  starting transfers between devices  20 us (13%)
  local copies, waits for them, and re-layouts  6.41 us (4%)
  other arithmetic  3.09 us (2%)
    ppermute x9, waiting for transfers between devices, pass_on(): return lax.ppermute(x, 'blk', onward)  58.7 us
    ppermute x9, waiting for transfers between devices, swap_across(): return lax.ppermute(x, 'blk', across)  28.5 us
    pallas_call x4, Pallas kernels, score(): pl.pallas_call(functools.partial(score_body, count), in_specs=[SCALARS] +...  21 us
    pallas_call x1, Pallas kernels, form(): pl.pallas_call(functools.partial(form_body, rows, rank), grid_spec=pltpu....  13.4 us
    ppermute x9, starting transfers between devices, swap_across(): return lax.ppermute(x, 'blk', across)  10.3 us
    ppermute x9, starting transfers between devices, pass_on(): return lax.ppermute(x, 'blk', onward)  7.99 us
    unnamed x34, local copies, waits for them, and re-layouts  6.18 us
  transfers between devices with their start and end apart: 26, of which 13 were waited for; matrix products, arithmetic and copies ran while one was open for 2% of the time, Pallas kernels for 23%

profile of v12, /device:TPU:0, one launch (start us, length us, event | category | flops | bytes accessed | tf_op | source)
XLA Modules:
  0.0 157.8 jit_solution(12858176162933427830)
XLA Ops:
  0.0 0.1 pad_add_fusion.spot
  0.1 1.6 %copy-done.4 = bf16[256,4096]{1,0:T(8,128)(2,1)S(1)} copy-done((bf16[256,4096]{1,0:T(8,128)(2,1)S(1)}, bf16[256,4096]{1,0:T(8,128)(2,1)}, u32[]{:S(2)}) %copy-start.4) | copy-done | bytes 2097176
  1.7 1.3 shard_map.47
  2.9 3.1 %collective-permute-start = (bf16[256,2048]{1,0:T(8,128)(2,1)S(1)}, bf16[256,2048]{1,0:T(8,128)(2,1)S(1)}, u32[]{:S(2)}, u32[]{:S(2)}) collective-permute-start(bf16[256,2048]{1,0:T(8,128)(2,1)S(1)} %get-tuple-element.32.refs_0_), channel_id=1, source_target_pairs={{0,4},{2,6},{4,8},{6,10},{8,12},{10,14},{12,0},{14,2},{1,5},{3,7},... | collective-permute-start | bytes 3145736 | tf_op jit(solution)/shard_map/ppermute | solution.py:185
  6.0 1.5 collective-permute-start.1
  7.5 0.5 collective-permute-start.2
  8.0 13.4 %shard_map.46 = (bf16[512,2048]{1,0:T(8,128)(2,1)S(1)}, bf16[512,2048]{1,0:T(8,128)(2,1)S(1)}) custom-call(s32[2]{0:T(128)S(1)} %pad_add_fusion.spot, bf16[512,64,128]{2,1,0:T(8,128)(2,1)} %bitcast.4, bf16[512,64,128]{2,1,0:T(8,128)(2,1)} %bitcast.5, s32[512,128]{1,0:T(8,128)S(1)} %copy-done.11), custom_call_target="tpu_custom_call" | custom-call | flops 10737418240 | bytes 20971520 | tf_op jit(solution)/shard_map/pallas_call | solution.py:72
  21.5 0.0 collective-permute-done.1.refs_2_
  21.5 9.2 %collective-permute-done.2.refs_3_ = bf16[128,2048]{1,0:T(8,128)(2,1)S(1)} collective-permute-done((bf16[128,2048]{1,0:T(8,128)(2,1)S(1)}, bf16[128,2048]{1,0:T(8,128)(2,1)S(1)}, u32[]{:S(2)}, u32[]{:S(2)}) %collective-permute-start.2) | collective-permute-done | bytes 524320 | tf_op jit(solution)/shard_map/ppermute | solution.py:179
  30.6 0.6 collective-permute-done.refs_1_
  31.2 1.5 collective-permute-start.3
  32.7 1.0 collective-permute-start.10
  33.7 1.6 collective-permute-start.6
  35.3 0.4 collective-permute-start.7
  35.7 24.9 %collective-permute-done.10.refs_0_ = bf16[256,2048]{1,0:T(8,128)(2,1)S(1)} collective-permute-done((bf16[256,2048]{1,0:T(8,128)(2,1)S(1)}, bf16[256,2048]{1,0:T(8,128)(2,1)S(1)}, u32[]{:S(2)}, u32[]{:S(2)}) %collective-permute-start.10) | collective-permute-done | bytes 1048608 | tf_op jit(solution)/shard_map/ppermute | solution.py:185
  60.6 17.4 %collective-permute-done.3.far = bf16[512,2048]{1,0:T(8,128)(2,1)S(1)} collective-permute-done((bf16[512,2048]{1,0:T(8,128)(2,1)S(1)}, bf16[512,2048]{1,0:T(8,128)(2,1)S(1)}, u32[]{:S(2)}, u32[]{:S(2)}) %collective-permute-start.3) | collective-permute-done | bytes 2097184 | tf_op jit(solution)/shard_map/ppermute | solution.py:179
  78.0 1.3 copy-done.2
  79.3 5.0 %shard_map.49 = (f32[512,512]{1,0:T(8,128)S(1)}, bf16[512,512]{1,0:T(8,128)(2,1)S(1)}) custom-call(s32[2]{0:T(128)S(1)} %pad_add_fusion.spot, bf16[512,2048]{1,0:T(8,128)(2,1)S(1)} %get-tuple-element.30.own, bf16[512,2048]{1,0:T(8,128)(2,1)} %copy-done.2, bf16[256,2048]{1,0:T(8,128)(2,1)S(1)} %get-tuple-element.32.refs_0_, ...), custom_call_target="tpu_custom_call" | custom-call | flops 1024 | bytes 1024 | tf_op jit(solution)/shard_map/pallas_call | solution.py:133
  84.4 0.1 collective-permute-start.4
  84.5 6.2 %shard_map.50 = (f32[512,512]{1,0:T(8,128)S(1)}, bf16[512,512]{1,0:T(8,128)(2,1)S(1)}) custom-call(s32[2]{0:T(128)S(1)} %pad_add_fusion.spot, bf16[512,2048]{1,0:T(8,128)(2,1)} %copy-done, bf16[512,2048]{1,0:T(8,128)(2,1)} %copy-done.2, bf16[256,2048]{1,0:T(8,128)(2,1)S(1)} %get-tuple-element.40.refs_0_, bf16[128,2048]{1,0:T(8,128)(2,1)} %collective-permute-done.6.refs_1_, ...), custom_call_target="tpu_custom_call" | custom-call | flops 1024 | bytes 1024 | tf_op jit(solution)/shard_map/pallas_call | solution.py:133
  90.7 0.3 collective-permute-start.8
  91.0 0.4 collective-permute-start.13
  91.4 1.6 collective-permute-start.14
  92.9 0.1 convert_element_type.60
  93.1 0.1 fusion.4
  93.2 1.6 collective-permute-start.5
  94.7 0.1 convert_element_type.63
  94.9 0.1 fusion.1.refs_4_
  95.0 10.5 %collective-permute-done.11.refs_1_ = bf16[256,2048]{1,0:T(8,128)(2,1)S(1)} collective-permute-done((bf16[256,2048]{1,0:T(8,128)(2,1)S(1)}, bf16[256,2048]{1,0:T(8,128)(2,1)S(1)}, u32[]{:S(2)}, u32[]{:S(2)}) %collective-permute-start.11) | collective-permute-done | bytes 1048608 | tf_op jit(solution)/shard_map/ppermute | solution.py:185
  105.5 5.5 %shard_map.51 = (f32[512,512]{1,0:T(8,128)S(1)}, bf16[512,512]{1,0:T(8,128)(2,1)}) custom-call(s32[2]{0:T(128)S(1)} %pad_add_fusion.spot, bf16[512,2048]{1,0:T(8,128)(2,1)} %copy-done, bf16[512,2048]{1,0:T(8,128)(2,1)} %copy-done.2, bf16[256,2048]{1,0:T(8,128)(2,1)S(1)} %collective-permute-done.10.refs_0_, ...), custom_call_target="tpu_custom_call" | custom-call | flops 1024 | bytes 1024 | tf_op jit(solution)/shard_map/pallas_call | solution.py:133
  111.1 1.0 copy-done.7
  112.1 4.8 %collective-permute-done.13.refs_0_ = bf16[128,2048]{1,0:T(8,128)(2,1)} collective-permute-done((bf16[128,2048]{1,0:T(8,128)(2,1)}, bf16[128,2048]{1,0:T(8,128)(2,1)}, u32[]{:S(2)}, u32[]{:S(2)}) %collective-permute-start.13) | collective-permute-done | bytes 524320 | tf_op jit(solution)/shard_map/ppermute | solution.py:185
  116.9 11.2 %collective-permute-done.14.refs_1_ = bf16[128,2048]{1,0:T(8,128)(2,1)} collective-permute-done((bf16[128,2048]{1,0:T(8,128)(2,1)}, bf16[128,2048]{1,0:T(8,128)(2,1)}, u32[]{:S(2)}, u32[]{:S(2)}) %collective-permute-start.14) | collective-permute-done | bytes 524320 | tf_op jit(solution)/shard_map/ppermute | solution.py:185
  128.1 0.0 collective-permute-start.22
  128.1 0.5 collective-permute-start.9
  128.6 4.2 %shard_map.52 = (f32[512,256]{1,0:T(8,128)S(1)}, bf16[512,256]{1,0:T(8,128)(2,1)S(1)}) custom-call(s32[2]{0:T(128)S(1)} %pad_add_fusion.spot, bf16[512,2048]{1,0:T(8,128)(2,1)S(1)} %copy-done.1, bf16[512,2048]{1,0:T(8,128)(2,1)} %copy-done.2, bf16[128,2048]{1,0:T(8,128)(2,1)} %collective-permute-done.13.refs_0_, ...), custom_call_target="tpu_custom_call" | custom-call | flops 1024 | bytes 1024 | tf_op jit(solution)/shard_map/pallas_call | solution.py:133
  132.9 0.1 collective-permute-start.15
  133.0 0.2 broadcast_in_dim.3
  133.2 0.9 copy-done.6
  134.1 0.0 copy-done.10
  134.2 0.1 fusion.6
  134.3 0.2 collective-permute-done.15
  134.6 1.6 collective-permute-start.16
  136.2 1.2 convert_element_type.66
  137.4 0.0 copy-start.3
  137.4 0.2 fusion
  137.6 0.6 collective-permute-start.17
  138.2 0.1 fusion.3
  138.3 0.9 collective-permute-done.18.block
  139.2 1.2 shard_map.53
  140.5 0.1 collective-permute-start.20
  140.6 1.2 collective-permute-start.19
  141.8 0.7 collective-permute-start.21
  142.5 5.7 %collective-permute-done.22.block = bf16[128,2048]{1,0:T(8,128)(2,1)S(1)} collective-permute-done((bf16[128,2048]{1,0:T(8,128)(2,1)}, bf16[128,2048]{1,0:T(8,128)(2,1)S(1)}, u32[]{:S(2)}, u32[]{:S(2)}) %collective-permute-start.22) | collective-permute-done | bytes 524320 | tf_op jit(solution)/shard_map/ppermute | solution.py:185
  148.2 0.4 collective-permute-done.19.refs_1_
  148.6 1.2 shard_map.54
  149.9 0.3 collective-permute-start.24
  150.2 1.3 collective-permute-start.23
  151.5 0.3 collective-permute-start.25
  151.9 2.3 %collective-permute-done.24 = bf16[256,128]{1,0:T(8,128)(2,1)S(1)} collective-permute-done((bf16[256,128]{1,0:T(8,128)(2,1)S(1)}, bf16[256,128]{1,0:T(8,128)(2,1)S(1)}, u32[]{:S(2)}, u32[]{:S(2)}) %collective-permute-start.24) | collective-permute-done | bytes 65568 | tf_op jit(solution)/shard_map/ppermute | solution.py:188
  154.3 1.5 collective-permute-done.23
  155.8 0.0 copy-start.16
  155.8 1.3 copy-done.16
  157.1 0.7 add_dynamic-update-slice_fusion
  (49 shorter events, 0.3 us)
Async XLA Ops:
  0.1 1.6 %copy-start.4 = (bf16[256,4096]{1,0:T(8,128)(2,1)S(1)}, bf16[256,4096]{1,0:T(8,128)(2,1)}, u32[]{:S(2)}) copy-start(bf16[256,4096]{1,0:T(8,128)(2,1)} %query_grads.1) | copy-start | bytes 6291460
  1.7 6.4 %copy-start.11 = (s32[512,128]{1,0:T(8,128)S(1)}, s32[512,128]{1,0:T(8,128)}, u32[]{:S(2)}) copy-start(s32[512,128]{1,0:T(8,128)} %mask.1) | copy-start | bytes 786436
  2.9 28.3 %collective-permute-start = (bf16[256,2048]{1,0:T(8,128)(2,1)S(1)}, bf16[256,2048]{1,0:T(8,128)(2,1)S(1)}, u32[]{:S(2)}, u32[]{:S(2)}) collective-permute-start(bf16[256,2048]{1,0:T(8,128)(2,1)S(1)} %get-tuple-element.32.refs_0_), channel_id=1, source_target_pairs={{0,4},{2,6},{4,8},{6,10},{8,12},{10,14},{12,0},{14,2},{1,5},{3,7},... | collective-permute-start | bytes 3145736 | tf_op jit(solution)/shard_map/ppermute | solution.py:185
  6.0 15.4 %collective-permute-start.1 = (bf16[128,2048]{1,0:T(8,128)(2,1)S(1)}, bf16[128,2048]{1,0:T(8,128)(2,1)S(1)}, u32[]{:S(2)}, u32[]{:S(2)}) collective-permute-start(bf16[128,2048]{1,0:T(8,128)(2,1)S(1)} %get-tuple-element.33), channel_id=1, source_target_pairs={{0,2},{2,0},{4,6},{6,4},{8,10},{10,8},{12,14},{14,12},{1,3},{3,1},... | collective-permute-start | bytes 1572872 | tf_op jit(solution)/shard_map/ppermute | solution.py:179
  7.5 23.1 %collective-permute-start.2 = (bf16[128,2048]{1,0:T(8,128)(2,1)S(1)}, bf16[128,2048]{1,0:T(8,128)(2,1)S(1)}, u32[]{:S(2)}, u32[]{:S(2)}) collective-permute-start(bf16[128,2048]{1,0:T(8,128)(2,1)S(1)} %get-tuple-element.34), channel_id=1, source_target_pairs={{0,2},{2,0},{4,6},{6,4},{8,10},{10,8},{12,14},{14,12},{1,3},{3,1},... | collective-permute-start | bytes 1572872 | tf_op jit(solution)/shard_map/ppermute | solution.py:179
  21.4 56.6 %copy-start = (bf16[512,2048]{1,0:T(8,128)(2,1)}, bf16[512,2048]{1,0:T(8,128)(2,1)S(1)}, u32[]{:S(2)}) copy-start(bf16[512,2048]{1,0:T(8,128)(2,1)S(1)} %get-tuple-element.30.own) | copy-start | bytes 6291460
  31.2 46.8 %collective-permute-start.3 = (bf16[512,2048]{1,0:T(8,128)(2,1)S(1)}, bf16[512,2048]{1,0:T(8,128)(2,1)S(1)}, u32[]{:S(2)}, u32[]{:S(2)}) collective-permute-start(bf16[512,2048]{1,0:T(8,128)(2,1)S(1)} %get-tuple-element.35), channel_id=1, source_target_pairs={{0,2},{2,0},{4,6},{6,4},{8,10},{10,8},{12,14},{14,12},{1,3},{3,1},... | collective-permute-start | bytes 6291464 | tf_op jit(solution)/shard_map/ppermute | solution.py:179
  32.7 27.9 %collective-permute-start.10 = (bf16[256,2048]{1,0:T(8,128)(2,1)S(1)}, bf16[256,2048]{1,0:T(8,128)(2,1)S(1)}, u32[]{:S(2)}, u32[]{:S(2)}) collective-permute-start(bf16[256,2048]{1,0:T(8,128)(2,1)S(1)} %get-tuple-element.40.refs_0_), channel_id=1, source_target_pairs={{0,4},{2,6},{4,8},{6,10},{8,12},{10,14},{12,0},{14,2},{1,5},{3,7},... | collective-permute-start | bytes 3145736 | tf_op jit(solution)/shard_map/ppermute | solution.py:185
  33.7 50.8 %collective-permute-start.6 = (bf16[128,2048]{1,0:T(8,128)(2,1)S(1)}, bf16[128,2048]{1,0:T(8,128)(2,1)}, u32[]{:S(2)}, u32[]{:S(2)}) collective-permute-start(bf16[128,2048]{1,0:T(8,128)(2,1)S(1)} %get-tuple-element.36.refs_1_), channel_id=1, source_target_pairs={{0,4},{2,6},{4,8},{6,10},{8,12},{10,14},{12,0},{14,2},{1,5},{3,7},... | collective-permute-start | bytes 1572872 | tf_op jit(solution)/shard_map/ppermute | solution.py:185
  35.3 49.2 %collective-permute-start.7 = (bf16[128,2048]{1,0:T(8,128)(2,1)S(1)}, bf16[128,2048]{1,0:T(8,128)(2,1)}, u32[]{:S(2)}, u32[]{:S(2)}) collective-permute-start(bf16[128,2048]{1,0:T(8,128)(2,1)S(1)} %get-tuple-element.37.refs_2_), channel_id=1, source_target_pairs={{0,4},{2,6},{4,8},{6,10},{8,12},{10,14},{12,0},{14,2},{1,5},{3,7},... | collective-permute-start | bytes 1572872 | tf_op jit(solution)/shard_map/ppermute | solution.py:185
  60.6 44.9 %collective-permute-start.11 = (bf16[256,2048]{1,0:T(8,128)(2,1)S(1)}, bf16[256,2048]{1,0:T(8,128)(2,1)S(1)}, u32[]{:S(2)}, u32[]{:S(2)}) collective-permute-start(bf16[256,2048]{1,0:T(8,128)(2,1)S(1)} %collective-permute-done.10.refs_0_), channel_id=1, source_target_pairs={{0,4},{2,6},{4,8},{6,10},{8,12},{10,14},{12,0},{14,2},{1,5},{3,7},... | collective-permute-start | bytes 3145736 | tf_op jit(solution)/shard_map/ppermute | solution.py:185
  78.0 1.3 copy-start.2
  84.4 8.7 %copy-start.5 = (f32[512,512]{1,0:T(8,128)}, f32[512,512]{1,0:T(8,128)S(1)}, u32[]{:S(2)}) copy-start(f32[512,512]{1,0:T(8,128)S(1)} %get-tuple-element.38) | copy-start | bytes 3145732
  84.4 8.5 %collective-permute-start.4 = (bf16[512,512]{1,0:T(8,128)(2,1)S(1)}, bf16[512,512]{1,0:T(8,128)(2,1)S(1)}, u32[]{:S(2)}, u32[]{:S(2)}) collective-permute-start(bf16[512,512]{1,0:T(8,128)(2,1)S(1)} %get-tuple-element.39.refs_3_), channel_id=1, source_target_pairs={{0,1},{1,0},{2,3},{3,2},{4,5},{5,4},{6,7},{7,6},{8,9},{9,8},{10,11... | collective-permute-start | bytes 1572872 | tf_op jit(solution)/shard_map/ppermute | solution.py:182
  90.7 4.0 %collective-permute-start.8 = (bf16[512,512]{1,0:T(8,128)(2,1)S(1)}, bf16[512,512]{1,0:T(8,128)(2,1)S(1)}, u32[]{:S(2)}, u32[]{:S(2)}) collective-permute-start(bf16[512,512]{1,0:T(8,128)(2,1)S(1)} %get-tuple-element.42.refs_2_), channel_id=1, source_target_pairs={{0,1},{1,0},{2,3},{3,2},{4,5},{5,4},{6,7},{7,6},{8,9},{9,8},{10,11... | collective-permute-start | bytes 1572872 | tf_op jit(solution)/shard_map/ppermute | solution.py:182
  91.0 25.9 %collective-permute-start.13 = (bf16[128,2048]{1,0:T(8,128)(2,1)}, bf16[128,2048]{1,0:T(8,128)(2,1)}, u32[]{:S(2)}, u32[]{:S(2)}) collective-permute-start(bf16[128,2048]{1,0:T(8,128)(2,1)} %collective-permute-done.6.refs_1_), channel_id=1, source_target_pairs={{0,4},{2,6},{4,8},{6,10},{8,12},{10,14},{12,0},{14,2},{1,5},{3,7},... | collective-permute-start | bytes 1572872 | tf_op jit(solution)/shard_map/ppermute | solution.py:185
  91.4 36.8 %collective-permute-start.14 = (bf16[128,2048]{1,0:T(8,128)(2,1)}, bf16[128,2048]{1,0:T(8,128)(2,1)}, u32[]{:S(2)}, u32[]{:S(2)}) collective-permute-start(bf16[128,2048]{1,0:T(8,128)(2,1)} %collective-permute-done.7.refs_2_), channel_id=1, source_target_pairs={{0,4},{2,6},{4,8},{6,10},{8,12},{10,14},{12,0},{14,2},{1,5},{3,7},... | collective-permute-start | bytes 1572872 | tf_op jit(solution)/shard_map/ppermute | solution.py:185
  93.1 1.7 %copy-start.14 = (f32[512,512]{1,0:T(8,128)}, f32[512,512]{1,0:T(8,128)S(1)}, u32[]{:S(2)}) copy-start(f32[512,512]{1,0:T(8,128)S(1)} %convert_element_type.60) | copy-start | bytes 3145732
  93.2 12.4 %collective-permute-start.5 = (bf16[256,512]{1,0:T(8,128)(2,1)S(1)}, bf16[256,512]{1,0:T(8,128)(2,1)S(1)}, u32[]{:S(2)}, u32[]{:S(2)}) collective-permute-start(bf16[256,512]{1,0:T(8,128)(2,1)S(1)} %fusion.4), channel_id=1, source_target_pairs={{0,2},{2,0},{4,6},{6,4},{8,10},{10,8},{12,14},{14,12},{1,3},{3,1},... | collective-permute-start | bytes 786440 | tf_op jit(solution)/shard_map/ppermute | solution.py:179
  94.9 16.2 %copy-start.12 = (f32[512,512]{1,0:T(8,128)}, f32[512,512]{1,0:T(8,128)S(1)}, u32[]{:S(2)}) copy-start(f32[512,512]{1,0:T(8,128)S(1)} %convert_element_type.63) | copy-start | bytes 3145732
  95.0 33.6 %copy-start.1 = (bf16[512,2048]{1,0:T(8,128)(2,1)S(1)}, bf16[512,2048]{1,0:T(8,128)(2,1)}, u32[]{:S(2)}) copy-start(bf16[512,2048]{1,0:T(8,128)(2,1)} %copy-done) | copy-start | bytes 6291460
  105.5 5.5 %copy-start.9 = (bf16[256,512]{1,0:T(8,128)(2,1)}, bf16[256,512]{1,0:T(8,128)(2,1)S(1)}, u32[]{:S(2)}) copy-start(bf16[256,512]{1,0:T(8,128)(2,1)S(1)} %collective-permute-done.5.refs_3_) | copy-start | bytes 786436
  111.1 1.0 copy-start.7
  112.1 24.1 %collective-permute-start.12 = (bf16[512,512]{1,0:T(8,128)(2,1)}, bf16[512,512]{1,0:T(8,128)(2,1)}, u32[]{:S(2)}, u32[]{:S(2)}) collective-permute-start(bf16[512,512]{1,0:T(8,128)(2,1)} %get-tuple-element.44.refs_2_), channel_id=1, source_target_pairs={{0,1},{1,0},{2,3},{3,2},{4,5},{5,4},{6,7},{7,6},{8,9},{9,8},{10,11... | collective-permute-start | bytes 1572872 | tf_op jit(solution)/shard_map/ppermute | solution.py:182
  116.9 22.4 %collective-permute-start.18 = (bf16[128,2048]{1,0:T(8,128)(2,1)}, bf16[128,2048]{1,0:T(8,128)(2,1)S(1)}, u32[]{:S(2)}, u32[]{:S(2)}) collective-permute-start(bf16[128,2048]{1,0:T(8,128)(2,1)} %collective-permute-done.13.refs_0_), channel_id=1, source_target_pairs={{0,4},{2,6},{4,8},{6,10},{8,12},{10,14},{12,0},{14,2},{1,5},{3,7},... | collective-permute-start | bytes 1572872 | tf_op jit(solution)/shard_map/ppermute | solution.py:185
  128.1 20.1 %collective-permute-start.22 = (bf16[128,2048]{1,0:T(8,128)(2,1)}, bf16[128,2048]{1,0:T(8,128)(2,1)S(1)}, u32[]{:S(2)}, u32[]{:S(2)}) collective-permute-start(bf16[128,2048]{1,0:T(8,128)(2,1)} %collective-permute-done.14.refs_1_), channel_id=1, source_target_pairs={{0,4},{2,6},{4,8},{6,10},{8,12},{10,14},{12,0},{14,2},{1,5},{3,7},... | collective-permute-start | bytes 1572872 | tf_op jit(solution)/shard_map/ppermute | solution.py:185
  128.1 10.1 %collective-permute-start.9 = (bf16[256,512]{1,0:T(8,128)(2,1)S(1)}, bf16[256,512]{1,0:T(8,128)(2,1)S(1)}, u32[]{:S(2)}, u32[]{:S(2)}) collective-permute-start(bf16[256,512]{1,0:T(8,128)(2,1)S(1)} %fusion.1.refs_4_), channel_id=1, source_target_pairs={{0,2},{2,0},{4,6},{6,4},{8,10},{10,8},{12,14},{14,12},{1,3},{3,1},... | collective-permute-start | bytes 786440 | tf_op jit(solution)/shard_map/ppermute | solution.py:179
  128.6 4.6 %copy-start.15 = (f32[512,512]{1,0:T(8,128)S(1)}, f32[512,512]{1,0:T(8,128)}, u32[]{:S(2)}) copy-start(f32[512,512]{1,0:T(8,128)} %copy-done.14) | copy-start | bytes 3145732
  132.9 1.2 copy-start.6
  132.9 1.3 copy-start.10
  132.9 1.6 %collective-permute-start.15 = (bf16[512,256]{1,0:T(8,128)(2,1)S(1)}, bf16[512,256]{1,0:T(8,128)(2,1)S(1)}, u32[]{:S(2)}, u32[]{:S(2)}) collective-permute-start(bf16[512,256]{1,0:T(8,128)(2,1)S(1)} %get-tuple-element.46.refs_0_), channel_id=1, source_target_pairs={{0,1},{1,0},{2,3},{3,2},{4,5},{5,4},{6,7},{7,6},{8,9},{9,8},{10,11... | collective-permute-start | bytes 786440 | tf_op jit(solution)/shard_map/ppermute | solution.py:182
  134.2 3.2 %copy-start.8 = (f32[512,512]{1,0:T(8,128)S(1)}, f32[512,512]{1,0:T(8,128)}, u32[]{:S(2)}) copy-start(f32[512,512]{1,0:T(8,128)} %copy-done.7) | copy-start | bytes 3145732
  134.6 3.6 %copy-start.13 = (f32[512,512]{1,0:T(8,128)S(1)}, f32[512,512]{1,0:T(8,128)}, u32[]{:S(2)}) copy-start(f32[512,512]{1,0:T(8,128)} %copy-done.12) | copy-start | bytes 3145732
  134.6 7.1 %collective-permute-start.16 = (bf16[256,256]{1,0:T(8,128)(2,1)S(1)}, bf16[256,256]{1,0:T(8,128)(2,1)S(1)}, u32[]{:S(2)}, u32[]{:S(2)}) collective-permute-start(bf16[256,256]{1,0:T(8,128)(2,1)S(1)} %fusion.9), channel_id=1, source_target_pairs={{0,2},{2,0},{4,6},{6,4},{8,10},{10,8},{12,14},{14,12},{1,3},{3,1},... | collective-permute-start | bytes 393224 | tf_op jit(solution)/shard_map/ppermute | solution.py:179
  137.4 1.9 %copy-start.3 = (bf16[512,2048]{1,0:T(8,128)(2,1)S(1)}, bf16[512,2048]{1,0:T(8,128)(2,1)}, u32[]{:S(2)}) copy-start(bf16[512,2048]{1,0:T(8,128)(2,1)} %copy-done.2) | copy-start | bytes 6291460
  137.6 14.2 %collective-permute-start.17 = (bf16[256,512]{1,0:T(8,128)(2,1)S(1)}, bf16[256,512]{1,0:T(8,128)(2,1)S(1)}, u32[]{:S(2)}, u32[]{:S(2)}) collective-permute-start(bf16[256,512]{1,0:T(8,128)(2,1)S(1)} %get-tuple-element.55.refs_1_), channel_id=1, source_target_pairs={{0,2},{2,0},{4,6},{6,4},{8,10},{10,8},{12,14},{14,12},{1,3},{3,1},... | collective-permute-start | bytes 786440 | tf_op jit(solution)/shard_map/ppermute | solution.py:179
  140.5 7.7 %collective-permute-start.20 = (bf16[256,128]{1,0:T(8,128)(2,1)S(1)}, bf16[256,128]{1,0:T(8,128)(2,1)S(1)}, u32[]{:S(2)}, u32[]{:S(2)}) collective-permute-start(bf16[256,128]{1,0:T(8,128)(2,1)S(1)} %get-tuple-element.48), channel_id=1, source_target_pairs={{0,3},{1,2},{2,1},{3,0},{4,7},{5,6},{6,5},{7,4},{8,11},{9,10},{10,... | collective-permute-start | bytes 196616 | tf_op jit(solution)/shard_map/ppermute | solution.py:188
  140.6 8.1 %collective-permute-start.19 = (bf16[256,128]{1,0:T(8,128)(2,1)S(1)}, bf16[256,128]{1,0:T(8,128)(2,1)S(1)}, u32[]{:S(2)}, u32[]{:S(2)}) collective-permute-start(bf16[256,128]{1,0:T(8,128)(2,1)S(1)} %get-tuple-element.47), channel_id=1, source_target_pairs={{0,2},{2,0},{4,6},{6,4},{8,10},{10,8},{12,14},{14,12},{1,3},{3,1},... | collective-permute-start | bytes 196616 | tf_op jit(solution)/shard_map/ppermute | solution.py:179
  141.8 10.1 %collective-permute-start.21 = (bf16[256,128]{1,0:T(8,128)(2,1)S(1)}, bf16[256,128]{1,0:T(8,128)(2,1)S(1)}, u32[]{:S(2)}, u32[]{:S(2)}) collective-permute-start(bf16[256,128]{1,0:T(8,128)(2,1)S(1)} %get-tuple-element.50), channel_id=1, source_target_pairs={{0,1},{1,0},{2,3},{3,2},{4,5},{5,4},{6,7},{7,6},{8,9},{9,8},{10,11... | collective-permute-start | bytes 196616 | tf_op jit(solution)/shard_map/ppermute | solution.py:182
  149.9 4.4 %collective-permute-start.24 = (bf16[256,128]{1,0:T(8,128)(2,1)S(1)}, bf16[256,128]{1,0:T(8,128)(2,1)S(1)}, u32[]{:S(2)}, u32[]{:S(2)}) collective-permute-start(bf16[256,128]{1,0:T(8,128)(2,1)S(1)} %get-tuple-element.52), channel_id=1, source_target_pairs={{0,3},{1,2},{2,1},{3,0},{4,7},{5,6},{6,5},{7,4},{8,11},{9,10},{10,... | collective-permute-start | bytes 196616 | tf_op jit(solution)/shard_map/ppermute | solution.py:188
  150.2 5.6 %collective-permute-start.23 = (bf16[256,128]{1,0:T(8,128)(2,1)S(1)}, bf16[256,128]{1,0:T(8,128)(2,1)S(1)}, u32[]{:S(2)}, u32[]{:S(2)}) collective-permute-start(bf16[256,128]{1,0:T(8,128)(2,1)S(1)} %get-tuple-element.51), channel_id=1, source_target_pairs={{0,2},{2,0},{4,6},{6,4},{8,10},{10,8},{12,14},{14,12},{1,3},{3,1},... | collective-permute-start | bytes 196616 | tf_op jit(solution)/shard_map/ppermute | solution.py:179
  151.5 4.3 %collective-permute-start.25 = (bf16[256,128]{1,0:T(8,128)(2,1)S(1)}, bf16[256,128]{1,0:T(8,128)(2,1)S(1)}, u32[]{:S(2)}, u32[]{:S(2)}) collective-permute-start(bf16[256,128]{1,0:T(8,128)(2,1)S(1)} %get-tuple-element.54), channel_id=1, source_target_pairs={{0,1},{1,0},{2,3},{3,2},{4,5},{5,4},{6,7},{7,6},{8,9},{9,8},{10,11... | collective-permute-start | bytes 196616 | tf_op jit(solution)/shard_map/ppermute | solution.py:182
  155.8 1.3 copy-start.16

commit v13 on v12

--- a/solution.py
+++ b/solution.py
@@ -44,7 +44,7 @@
         in_specs=[SCALARS, WHOLE],
         out_specs=[WHOLE] * 3,
         out_shape=[shaped(bf16, size, width // 2) for size in (rows, rows // 2, rows // 2)],
-        compiler_params=LIMIT,
+        compiler_params=pltpu.CompilerParams(vmem_limit_bytes=60 * 1024 * 1024),
     )(spot, query_grads)
 
 
@@ -238,8 +238,8 @@
         faced, opposed = swap_across(facing), swap_diagonal(opposite)
         mine_total = early[:, cut] + faced.astype(f32) + opposed.astype(f32)
         other_total = near + swap_cores(give).astype(f32) + early_beside[:, cut].astype(f32)
+        out = put(out, other_total, places - 1, (1 - side) * queries + i * size)
         out = put(out, mine_total, places - 1, side * queries + i * size)
-        out = put(out, other_total, places - 1, (1 - side) * queries + i * size)
         last = (near, faced, opposed)
     return out
 

time: 158 us -> 158 us (level)
  local copies, waits for them, and re-layouts: 6.41 us -> 3.52 us
  Pallas kernels: 38.1 us -> 40.4 us
    unnamed x34 -> x36, local copies, waits for them, and re-layouts: 6.18 us -> 3.3 us
    pallas_call x1, Pallas kernels: 1.26 us -> 3.54 us  [prepare(): pl.pallas_call(prepare_body, in_specs=[SCALARS, WHOLE], out_specs=[WHOLE]...]
    ppermute x2, starting transfers between devices: 0.37 us -> 2.38 us  [swap_diagonal(): return lax.ppermute(x, ('blk', 'proj'), diagonal)]
where the time goes in v13:
time: 158 us
  waiting for transfers between devices  89.5 us (57%)
  Pallas kernels  40.4 us (26%)
  starting transfers between devices  20.5 us (13%)
  other arithmetic  3.6 us (2%)
  local copies, waits for them, and re-layouts  3.52 us (2%)
    ppermute x9, waiting for transfers between devices, pass_on(): return lax.ppermute(x, 'blk', onward)  58.5 us
    ppermute x9, waiting for transfers between devices, swap_across(): return lax.ppermute(x, 'blk', across)  29.1 us
    pallas_call x4, Pallas kernels, score(): pl.pallas_call(functools.partial(score_body, count), in_specs=[SCALARS] +...  21 us
    pallas_call x1, Pallas kernels, form(): pl.pallas_call(functools.partial(form_body, rows, rank), grid_spec=pltpu....  13.4 us
    ppermute x9, starting transfers between devices, swap_across(): return lax.ppermute(x, 'blk', across)  9.71 us
    ppermute x9, starting transfers between devices, pass_on(): return lax.ppermute(x, 'blk', onward)  7.86 us
    pallas_call x1, Pallas kernels, prepare(): pl.pallas_call(prepare_body, in_specs=[SCALARS, WHOLE], out_specs=[WHOLE]...  3.54 us
    unnamed x36, local copies, waits for them, and re-layouts  3.3 us
  transfers between devices with their start and end apart: 26, of which 13 were waited for; matrix products, arithmetic and copies ran while one was open for 2% of the time, Pallas kernels for 23%

profile of v13, /device:TPU:0, one launch (start us, length us, event | category | flops | bytes accessed | tf_op | source)
XLA Modules:
  0.0 157.9 jit_solution(10692333760618882721)
XLA Ops:
  0.0 0.6 pad_add_fusion.spot
  0.6 3.5 %shard_map.47 = (bf16[256,2048]{1,0:T(8,128)(2,1)}, bf16[128,2048]{1,0:T(8,128)(2,1)}, bf16[128,2048]{1,0:T(8,128)(2,1)}) custom-call(s32[2]{0:T(128)} %pad_add_fusion.spot, bf16[256,4096]{1,0:T(8,128)(2,1)} %query_grads.1), custom_call_target="tpu_custom_call" | custom-call | tf_op jit(solution)/shard_map/pallas_call | solution.py:42
  4.1 3.0 %collective-permute-start = (bf16[256,2048]{1,0:T(8,128)(2,1)}, bf16[256,2048]{1,0:T(8,128)(2,1)S(1)}, u32[]{:S(2)}, u32[]{:S(2)}) collective-permute-start(bf16[256,2048]{1,0:T(8,128)(2,1)} %get-tuple-element.32.refs_0_), channel_id=1, source_target_pairs={{0,4},{2,6},{4,8},{6,10},{8,12},{10,14},{12,0},{14,2},{1,5},{3,7},... | collective-permute-start | bytes 3145736 | tf_op jit(solution)/shard_map/ppermute | solution.py:185
  7.1 1.5 collective-permute-start.1
  8.7 0.5 collective-permute-start.2
  9.2 13.4 %shard_map.46 = (bf16[512,2048]{1,0:T(8,128)(2,1)S(1)}, bf16[512,2048]{1,0:T(8,128)(2,1)S(1)}) custom-call(s32[2]{0:T(128)S(1)} %copy-done.11, bf16[512,64,128]{2,1,0:T(8,128)(2,1)} %bitcast.4, bf16[512,64,128]{2,1,0:T(8,128)(2,1)} %bitcast.5, s32[512,128]{1,0:T(8,128)S(1)} %copy-done.12), custom_call_target="tpu_custom_call" | custom-call | flops 10737418240 | bytes 20971520 | tf_op jit(solution)/shard_map/pallas_call | solution.py:72
  22.6 9.4 %collective-permute-done.2.refs_3_ = bf16[128,2048]{1,0:T(8,128)(2,1)S(1)} collective-permute-done((bf16[128,2048]{1,0:T(8,128)(2,1)}, bf16[128,2048]{1,0:T(8,128)(2,1)S(1)}, u32[]{:S(2)}, u32[]{:S(2)}) %collective-permute-start.2) | collective-permute-done | bytes 524320 | tf_op jit(solution)/shard_map/ppermute | solution.py:179
  32.0 0.6 collective-permute-done.refs_1_
  32.5 1.5 collective-permute-start.3
  34.1 1.0 collective-permute-start.10
  35.1 1.6 collective-permute-start.6
  36.7 0.3 collective-permute-start.7
  36.9 25.0 %collective-permute-done.10.refs_0_ = bf16[256,2048]{1,0:T(8,128)(2,1)S(1)} collective-permute-done((bf16[256,2048]{1,0:T(8,128)(2,1)S(1)}, bf16[256,2048]{1,0:T(8,128)(2,1)S(1)}, u32[]{:S(2)}, u32[]{:S(2)}) %collective-permute-start.10) | collective-permute-done | bytes 1048608 | tf_op jit(solution)/shard_map/ppermute | solution.py:185
  62.0 17.4 %collective-permute-done.3.far = bf16[512,2048]{1,0:T(8,128)(2,1)S(1)} collective-permute-done((bf16[512,2048]{1,0:T(8,128)(2,1)S(1)}, bf16[512,2048]{1,0:T(8,128)(2,1)S(1)}, u32[]{:S(2)}, u32[]{:S(2)}) %collective-permute-start.3) | collective-permute-done | bytes 2097184 | tf_op jit(solution)/shard_map/ppermute | solution.py:179
  79.4 1.3 copy-done.2
  80.7 5.1 %shard_map.49 = (f32[512,512]{1,0:T(8,128)S(1)}, bf16[512,512]{1,0:T(8,128)(2,1)S(1)}) custom-call(s32[2]{0:T(128)S(1)} %copy-done.11, bf16[512,2048]{1,0:T(8,128)(2,1)S(1)} %get-tuple-element.30.own, bf16[512,2048]{1,0:T(8,128)(2,1)} %copy-done.2, bf16[256,2048]{1,0:T(8,128)(2,1)S(1)} %copy-done.4, bf16[128,2048]{1,0:T(8,128)(2,1)S(1)} %get-tuple-element.36.refs_1_, ...), custom_call_target="tpu_custom_call" | custom-call | flops 1024 | bytes 1024 | tf_op jit(solution)/shard_map/pallas_call | solution.py:133
  85.8 0.1 collective-permute-start.4
  85.8 0.0 collective-permute-done.6.refs_1_
  85.9 6.2 %shard_map.50 = (f32[512,512]{1,0:T(8,128)S(1)}, bf16[512,512]{1,0:T(8,128)(2,1)S(1)}) custom-call(s32[2]{0:T(128)S(1)} %copy-done.11, bf16[512,2048]{1,0:T(8,128)(2,1)} %copy-done, bf16[512,2048]{1,0:T(8,128)(2,1)} %copy-done.2, bf16[256,2048]{1,0:T(8,128)(2,1)S(1)} %get-tuple-element.40.refs_0_, bf16[128,2048]{1,0:T(8,128)(2,1)} %collective-permute-done.6.refs_1_, ...), custom_call_target="tpu_custom_call" | custom-call | flops 1024 | bytes 1024 | tf_op jit(solution)/shard_map/pallas_call | solution.py:133
  92.1 0.3 collective-permute-start.8
  92.3 0.4 collective-permute-start.13
  92.7 1.6 collective-permute-start.14
  94.3 0.1 convert_element_type.60
  94.4 0.1 fusion.4
  94.5 1.6 %collective-permute-start.5 = (bf16[256,512]{1,0:T(8,128)(2,1)S(1)}, bf16[256,512]{1,0:T(8,128)(2,1)S(1)}, u32[]{:S(2)}, u32[]{:S(2)}) collective-permute-start(bf16[256,512]{1,0:T(8,128)(2,1)S(1)} %fusion.4), channel_id=1, source_target_pairs={{0,2},{2,0},{4,6},{6,4},{8,10},{10,8},{12,14},{14,12},{1,3},{3,1},... | collective-permute-start | bytes 786440 | tf_op jit(solution)/shard_map/ppermute | solution.py:179
  96.1 0.0 collective-permute-done.8
  96.1 0.1 convert_element_type.63
  96.3 0.1 fusion.1.refs_4_
  96.4 10.5 %collective-permute-done.11.refs_1_ = bf16[256,2048]{1,0:T(8,128)(2,1)S(1)} collective-permute-done((bf16[256,2048]{1,0:T(8,128)(2,1)S(1)}, bf16[256,2048]{1,0:T(8,128)(2,1)S(1)}, u32[]{:S(2)}, u32[]{:S(2)}) %collective-permute-start.11) | collective-permute-done | bytes 1048608 | tf_op jit(solution)/shard_map/ppermute | solution.py:185
  106.9 5.5 %shard_map.51 = (f32[512,512]{1,0:T(8,128)S(1)}, bf16[512,512]{1,0:T(8,128)(2,1)}) custom-call(s32[2]{0:T(128)S(1)} %copy-done.11, bf16[512,2048]{1,0:T(8,128)(2,1)} %copy-done, bf16[512,2048]{1,0:T(8,128)(2,1)} %copy-done.2, bf16[256,2048]{1,0:T(8,128)(2,1)S(1)} %collective-permute-done.10.refs_0_, bf16[256,2048]{1,0:T(8,128)(2,1)S(1)} %collective-permute-done.11.refs_1_, ...), custom_call_target="tpu_custom_call" | custom-call | flops 1024 | bytes 1024 | tf_op jit(solution)/shard_map/pallas_call | solution.py:133
  112.4 1.0 copy-done.7
  113.4 4.8 %collective-permute-done.13.refs_0_ = bf16[128,2048]{1,0:T(8,128)(2,1)} collective-permute-done((bf16[128,2048]{1,0:T(8,128)(2,1)}, bf16[128,2048]{1,0:T(8,128)(2,1)}, u32[]{:S(2)}, u32[]{:S(2)}) %collective-permute-start.13) | collective-permute-done | bytes 524320 | tf_op jit(solution)/shard_map/ppermute | solution.py:185
  118.2 0.0 collective-permute-start.18
  118.2 11.2 %collective-permute-done.14.refs_1_ = bf16[128,2048]{1,0:T(8,128)(2,1)} collective-permute-done((bf16[128,2048]{1,0:T(8,128)(2,1)}, bf16[128,2048]{1,0:T(8,128)(2,1)}, u32[]{:S(2)}, u32[]{:S(2)}) %collective-permute-start.14) | collective-permute-done | bytes 524320 | tf_op jit(solution)/shard_map/ppermute | solution.py:185
  129.5 0.0 collective-permute-start.22
  129.5 0.5 collective-permute-start.9
  130.0 4.2 %shard_map.52 = (f32[512,256]{1,0:T(8,128)S(1)}, bf16[512,256]{1,0:T(8,128)(2,1)S(1)}) custom-call(s32[2]{0:T(128)S(1)} %copy-done.11, bf16[512,2048]{1,0:T(8,128)(2,1)S(1)} %copy-done.1, bf16[512,2048]{1,0:T(8,128)(2,1)} %copy-done.2, bf16[128,2048]{1,0:T(8,128)(2,1)} %collective-permute-done.13.refs_0_, bf16[128,2048]{1,0:T(8,128)(2,1)} %collective-permute-done.14.refs_1_, ...), custom_call_target="tpu_custom_call" | custom-call | flops 1024 | bytes 1024 | tf_op jit(solution)/shard_map/pallas_call | solution.py:133
  134.3 0.1 collective-permute-start.15
  134.3 0.2 broadcast_in_dim.3
  134.6 0.9 copy-done.6
  135.5 0.0 copy-done.10
  135.5 0.1 fusion.6
  135.7 0.2 collective-permute-done.15
  136.0 1.6 %collective-permute-start.16 = (bf16[256,256]{1,0:T(8,128)(2,1)S(1)}, bf16[256,256]{1,0:T(8,128)(2,1)S(1)}, u32[]{:S(2)}, u32[]{:S(2)}) collective-permute-start(bf16[256,256]{1,0:T(8,128)(2,1)S(1)} %fusion.9), channel_id=1, source_target_pairs={{0,2},{2,0},{4,6},{6,4},{8,10},{10,8},{12,14},{14,12},{1,3},{3,1},... | collective-permute-start | bytes 393224 | tf_op jit(solution)/shard_map/ppermute | solution.py:179
  137.5 1.2 convert_element_type.66
  138.7 0.0 copy-start.3
  138.7 0.2 fusion
  139.0 0.6 collective-permute-start.17
  139.6 0.1 fusion.3
  139.7 0.9 collective-permute-done.18.block
  140.6 1.2 shard_map.53
  141.8 0.1 collective-permute-start.19
  141.9 0.7 collective-permute-start.21
  142.7 1.4 collective-permute-start.20
  144.1 5.4 %collective-permute-done.22.block = bf16[128,2048]{1,0:T(8,128)(2,1)S(1)} collective-permute-done((bf16[128,2048]{1,0:T(8,128)(2,1)}, bf16[128,2048]{1,0:T(8,128)(2,1)S(1)}, u32[]{:S(2)}, u32[]{:S(2)}) %collective-permute-start.22) | collective-permute-done | bytes 524320 | tf_op jit(solution)/shard_map/ppermute | solution.py:185
  149.6 0.4 collective-permute-done.20.refs_1_
  150.0 1.2 shard_map.54
  151.2 0.1 collective-permute-start.23
  151.3 1.6 %collective-permute-start.25 = (bf16[256,128]{1,0:T(8,128)(2,1)S(1)}, bf16[256,128]{1,0:T(8,128)(2,1)S(1)}, u32[]{:S(2)}, u32[]{:S(2)}) collective-permute-start(bf16[256,128]{1,0:T(8,128)(2,1)S(1)} %get-tuple-element.54), channel_id=1, source_target_pairs={{0,3},{1,2},{2,1},{3,0},{4,7},{5,6},{6,5},{7,4},{8,11},{9,10},{10,... | collective-permute-start | bytes 196616 | tf_op jit(solution)/shard_map/ppermute | solution.py:188
  152.9 0.5 collective-permute-start.24
  153.6 0.0 copy-start.17
  153.6 1.7 %collective-permute-done.25 = bf16[256,128]{1,0:T(8,128)(2,1)S(1)} collective-permute-done((bf16[256,128]{1,0:T(8,128)(2,1)S(1)}, bf16[256,128]{1,0:T(8,128)(2,1)S(1)}, u32[]{:S(2)}, u32[]{:S(2)}) %collective-permute-start.25) | collective-permute-done | bytes 65568 | tf_op jit(solution)/shard_map/ppermute | solution.py:188
  155.4 1.8 %collective-permute-done.24 = bf16[256,128]{1,0:T(8,128)(2,1)S(1)} collective-permute-done((bf16[256,128]{1,0:T(8,128)(2,1)S(1)}, bf16[256,128]{1,0:T(8,128)(2,1)S(1)}, u32[]{:S(2)}, u32[]{:S(2)}) %collective-permute-start.24) | collective-permute-done | bytes 65568 | tf_op jit(solution)/shard_map/ppermute | solution.py:179
  157.2 0.7 fusion.12
  (51 shorter events, 0.3 us)
Async XLA Ops:
  0.0 9.2 %copy-start.12 = (s32[512,128]{1,0:T(8,128)S(1)}, s32[512,128]{1,0:T(8,128)}, u32[]{:S(2)}) copy-start(s32[512,128]{1,0:T(8,128)} %mask.1) | copy-start | bytes 786436
  0.6 8.6 %copy-start.11 = (s32[2]{0:T(128)S(1)}, s32[2]{0:T(128)}, u32[]{:S(2)}) copy-start(s32[2]{0:T(128)} %pad_add_fusion.spot) | copy-start | bytes 28
  4.1 28.4 %collective-permute-start = (bf16[256,2048]{1,0:T(8,128)(2,1)}, bf16[256,2048]{1,0:T(8,128)(2,1)S(1)}, u32[]{:S(2)}, u32[]{:S(2)}) collective-permute-start(bf16[256,2048]{1,0:T(8,128)(2,1)} %get-tuple-element.32.refs_0_), channel_id=1, source_target_pairs={{0,4},{2,6},{4,8},{6,10},{8,12},{10,14},{12,0},{14,2},{1,5},{3,7},... | collective-permute-start | bytes 3145736 | tf_op jit(solution)/shard_map/ppermute | solution.py:185
  7.1 15.4 %collective-permute-start.1 = (bf16[128,2048]{1,0:T(8,128)(2,1)}, bf16[128,2048]{1,0:T(8,128)(2,1)S(1)}, u32[]{:S(2)}, u32[]{:S(2)}) collective-permute-start(bf16[128,2048]{1,0:T(8,128)(2,1)} %get-tuple-element.33), channel_id=1, source_target_pairs={{0,2},{2,0},{4,6},{6,4},{8,10},{10,8},{12,14},{14,12},{1,3},{3,1},... | collective-permute-start | bytes 1572872 | tf_op jit(solution)/shard_map/ppermute | solution.py:179
  8.7 23.3 %collective-permute-start.2 = (bf16[128,2048]{1,0:T(8,128)(2,1)}, bf16[128,2048]{1,0:T(8,128)(2,1)S(1)}, u32[]{:S(2)}, u32[]{:S(2)}) collective-permute-start(bf16[128,2048]{1,0:T(8,128)(2,1)} %get-tuple-element.34), channel_id=1, source_target_pairs={{0,2},{2,0},{4,6},{6,4},{8,10},{10,8},{12,14},{14,12},{1,3},{3,1},... | collective-permute-start | bytes 1572872 | tf_op jit(solution)/shard_map/ppermute | solution.py:179
  22.6 56.8 %copy-start = (bf16[512,2048]{1,0:T(8,128)(2,1)}, bf16[512,2048]{1,0:T(8,128)(2,1)S(1)}, u32[]{:S(2)}) copy-start(bf16[512,2048]{1,0:T(8,128)(2,1)S(1)} %get-tuple-element.30.own) | copy-start | bytes 6291460
  32.5 48.1 %copy-start.4 = (bf16[256,2048]{1,0:T(8,128)(2,1)S(1)}, bf16[256,2048]{1,0:T(8,128)(2,1)}, u32[]{:S(2)}) copy-start(bf16[256,2048]{1,0:T(8,128)(2,1)} %get-tuple-element.32.refs_0_) | copy-start | bytes 3145732
  32.5 46.8 %collective-permute-start.3 = (bf16[512,2048]{1,0:T(8,128)(2,1)S(1)}, bf16[512,2048]{1,0:T(8,128)(2,1)S(1)}, u32[]{:S(2)}, u32[]{:S(2)}) collective-permute-start(bf16[512,2048]{1,0:T(8,128)(2,1)S(1)} %get-tuple-element.35), channel_id=1, source_target_pairs={{0,2},{2,0},{4,6},{6,4},{8,10},{10,8},{12,14},{14,12},{1,3},{3,1},... | collective-permute-start | bytes 6291464 | tf_op jit(solution)/shard_map/ppermute | solution.py:179
  34.1 27.9 %collective-permute-start.10 = (bf16[256,2048]{1,0:T(8,128)(2,1)S(1)}, bf16[256,2048]{1,0:T(8,128)(2,1)S(1)}, u32[]{:S(2)}, u32[]{:S(2)}) collective-permute-start(bf16[256,2048]{1,0:T(8,128)(2,1)S(1)} %get-tuple-element.40.refs_0_), channel_id=1, source_target_pairs={{0,4},{2,6},{4,8},{6,10},{8,12},{10,14},{12,0},{14,2},{1,5},{3,7},... | collective-permute-start | bytes 3145736 | tf_op jit(solution)/shard_map/ppermute | solution.py:185
  35.1 50.8 %collective-permute-start.6 = (bf16[128,2048]{1,0:T(8,128)(2,1)S(1)}, bf16[128,2048]{1,0:T(8,128)(2,1)}, u32[]{:S(2)}, u32[]{:S(2)}) collective-permute-start(bf16[128,2048]{1,0:T(8,128)(2,1)S(1)} %get-tuple-element.36.refs_1_), channel_id=1, source_target_pairs={{0,4},{2,6},{4,8},{6,10},{8,12},{10,14},{12,0},{14,2},{1,5},{3,7},... | collective-permute-start | bytes 1572872 | tf_op jit(solution)/shard_map/ppermute | solution.py:185
  36.7 49.2 %collective-permute-start.7 = (bf16[128,2048]{1,0:T(8,128)(2,1)S(1)}, bf16[128,2048]{1,0:T(8,128)(2,1)}, u32[]{:S(2)}, u32[]{:S(2)}) collective-permute-start(bf16[128,2048]{1,0:T(8,128)(2,1)S(1)} %get-tuple-element.37.refs_2_), channel_id=1, source_target_pairs={{0,4},{2,6},{4,8},{6,10},{8,12},{10,14},{12,0},{14,2},{1,5},{3,7},... | collective-permute-start | bytes 1572872 | tf_op jit(solution)/shard_map/ppermute | solution.py:185
  62.0 44.9 %collective-permute-start.11 = (bf16[256,2048]{1,0:T(8,128)(2,1)S(1)}, bf16[256,2048]{1,0:T(8,128)(2,1)S(1)}, u32[]{:S(2)}, u32[]{:S(2)}) collective-permute-start(bf16[256,2048]{1,0:T(8,128)(2,1)S(1)} %collective-permute-done.10.refs_0_), channel_id=1, source_target_pairs={{0,4},{2,6},{4,8},{6,10},{8,12},{10,14},{12,0},{14,2},{1,5},{3,7},... | collective-permute-start | bytes 3145736 | tf_op jit(solution)/shard_map/ppermute | solution.py:185
  79.4 1.3 copy-start.2
  85.7 8.7 %copy-start.5 = (f32[512,512]{1,0:T(8,128)}, f32[512,512]{1,0:T(8,128)S(1)}, u32[]{:S(2)}) copy-start(f32[512,512]{1,0:T(8,128)S(1)} %get-tuple-element.38) | copy-start | bytes 3145732
  85.8 8.5 %collective-permute-start.4 = (bf16[512,512]{1,0:T(8,128)(2,1)S(1)}, bf16[512,512]{1,0:T(8,128)(2,1)S(1)}, u32[]{:S(2)}, u32[]{:S(2)}) collective-permute-start(bf16[512,512]{1,0:T(8,128)(2,1)S(1)} %get-tuple-element.39.refs_3_), channel_id=1, source_target_pairs={{0,1},{1,0},{2,3},{3,2},{4,5},{5,4},{6,7},{7,6},{8,9},{9,8},{10,11... | collective-permute-start | bytes 1572872 | tf_op jit(solution)/shard_map/ppermute | solution.py:182
  92.1 4.1 %collective-permute-start.8 = (bf16[512,512]{1,0:T(8,128)(2,1)S(1)}, bf16[512,512]{1,0:T(8,128)(2,1)S(1)}, u32[]{:S(2)}, u32[]{:S(2)}) collective-permute-start(bf16[512,512]{1,0:T(8,128)(2,1)S(1)} %get-tuple-element.42.refs_2_), channel_id=1, source_target_pairs={{0,1},{1,0},{2,3},{3,2},{4,5},{5,4},{6,7},{7,6},{8,9},{9,8},{10,11... | collective-permute-start | bytes 1572872 | tf_op jit(solution)/shard_map/ppermute | solution.py:182
  92.3 25.9 %collective-permute-start.13 = (bf16[128,2048]{1,0:T(8,128)(2,1)}, bf16[128,2048]{1,0:T(8,128)(2,1)}, u32[]{:S(2)}, u32[]{:S(2)}) collective-permute-start(bf16[128,2048]{1,0:T(8,128)(2,1)} %collective-permute-done.6.refs_1_), channel_id=1, source_target_pairs={{0,4},{2,6},{4,8},{6,10},{8,12},{10,14},{12,0},{14,2},{1,5},{3,7},... | collective-permute-start | bytes 1572872 | tf_op jit(solution)/shard_map/ppermute | solution.py:185
  92.7 36.8 %collective-permute-start.14 = (bf16[128,2048]{1,0:T(8,128)(2,1)}, bf16[128,2048]{1,0:T(8,128)(2,1)}, u32[]{:S(2)}, u32[]{:S(2)}) collective-permute-start(bf16[128,2048]{1,0:T(8,128)(2,1)} %collective-permute-done.7.refs_2_), channel_id=1, source_target_pairs={{0,4},{2,6},{4,8},{6,10},{8,12},{10,14},{12,0},{14,2},{1,5},{3,7},... | collective-permute-start | bytes 1572872 | tf_op jit(solution)/shard_map/ppermute | solution.py:185
  94.4 1.7 %copy-start.15 = (f32[512,512]{1,0:T(8,128)}, f32[512,512]{1,0:T(8,128)S(1)}, u32[]{:S(2)}) copy-start(f32[512,512]{1,0:T(8,128)S(1)} %convert_element_type.60) | copy-start | bytes 3145732
  94.5 12.4 %collective-permute-start.5 = (bf16[256,512]{1,0:T(8,128)(2,1)S(1)}, bf16[256,512]{1,0:T(8,128)(2,1)S(1)}, u32[]{:S(2)}, u32[]{:S(2)}) collective-permute-start(bf16[256,512]{1,0:T(8,128)(2,1)S(1)} %fusion.4), channel_id=1, source_target_pairs={{0,2},{2,0},{4,6},{6,4},{8,10},{10,8},{12,14},{14,12},{1,3},{3,1},... | collective-permute-start | bytes 786440 | tf_op jit(solution)/shard_map/ppermute | solution.py:179
  96.3 16.2 %copy-start.13 = (f32[512,512]{1,0:T(8,128)}, f32[512,512]{1,0:T(8,128)S(1)}, u32[]{:S(2)}) copy-start(f32[512,512]{1,0:T(8,128)S(1)} %convert_element_type.63) | copy-start | bytes 3145732
  96.4 33.6 %copy-start.1 = (bf16[512,2048]{1,0:T(8,128)(2,1)S(1)}, bf16[512,2048]{1,0:T(8,128)(2,1)}, u32[]{:S(2)}) copy-start(bf16[512,2048]{1,0:T(8,128)(2,1)} %copy-done) | copy-start | bytes 6291460
  106.9 5.5 %copy-start.9 = (bf16[256,512]{1,0:T(8,128)(2,1)}, bf16[256,512]{1,0:T(8,128)(2,1)S(1)}, u32[]{:S(2)}) copy-start(bf16[256,512]{1,0:T(8,128)(2,1)S(1)} %collective-permute-done.5.refs_3_) | copy-start | bytes 786436
  112.4 1.0 copy-start.7
  113.4 24.1 %collective-permute-start.12 = (bf16[512,512]{1,0:T(8,128)(2,1)}, bf16[512,512]{1,0:T(8,128)(2,1)}, u32[]{:S(2)}, u32[]{:S(2)}) collective-permute-start(bf16[512,512]{1,0:T(8,128)(2,1)} %get-tuple-element.44.refs_2_), channel_id=1, source_target_pairs={{0,1},{1,0},{2,3},{3,2},{4,5},{5,4},{6,7},{7,6},{8,9},{9,8},{10,11... | collective-permute-start | bytes 1572872 | tf_op jit(solution)/shard_map/ppermute | solution.py:182
  118.2 22.4 %collective-permute-start.18 = (bf16[128,2048]{1,0:T(8,128)(2,1)}, bf16[128,2048]{1,0:T(8,128)(2,1)S(1)}, u32[]{:S(2)}, u32[]{:S(2)}) collective-permute-start(bf16[128,2048]{1,0:T(8,128)(2,1)} %collective-permute-done.13.refs_0_), channel_id=1, source_target_pairs={{0,4},{2,6},{4,8},{6,10},{8,12},{10,14},{12,0},{14,2},{1,5},{3,7},... | collective-permute-start | bytes 1572872 | tf_op jit(solution)/shard_map/ppermute | solution.py:185
  129.5 20.1 %collective-permute-start.22 = (bf16[128,2048]{1,0:T(8,128)(2,1)}, bf16[128,2048]{1,0:T(8,128)(2,1)S(1)}, u32[]{:S(2)}, u32[]{:S(2)}) collective-permute-start(bf16[128,2048]{1,0:T(8,128)(2,1)} %collective-permute-done.14.refs_1_), channel_id=1, source_target_pairs={{0,4},{2,6},{4,8},{6,10},{8,12},{10,14},{12,0},{14,2},{1,5},{3,7},... | collective-permute-start | bytes 1572872 | tf_op jit(solution)/shard_map/ppermute | solution.py:185
  129.5 10.1 %collective-permute-start.9 = (bf16[256,512]{1,0:T(8,128)(2,1)S(1)}, bf16[256,512]{1,0:T(8,128)(2,1)S(1)}, u32[]{:S(2)}, u32[]{:S(2)}) collective-permute-start(bf16[256,512]{1,0:T(8,128)(2,1)S(1)} %fusion.1.refs_4_), channel_id=1, source_target_pairs={{0,2},{2,0},{4,6},{6,4},{8,10},{10,8},{12,14},{14,12},{1,3},{3,1},... | collective-permute-start | bytes 786440 | tf_op jit(solution)/shard_map/ppermute | solution.py:179
  130.0 4.6 %copy-start.16 = (f32[512,512]{1,0:T(8,128)S(1)}, f32[512,512]{1,0:T(8,128)}, u32[]{:S(2)}) copy-start(f32[512,512]{1,0:T(8,128)} %copy-done.15) | copy-start | bytes 3145732
  134.2 1.2 copy-start.6
  134.3 1.3 copy-start.10
  134.3 1.6 %collective-permute-start.15 = (bf16[512,256]{1,0:T(8,128)(2,1)S(1)}, bf16[512,256]{1,0:T(8,128)(2,1)S(1)}, u32[]{:S(2)}, u32[]{:S(2)}) collective-permute-start(bf16[512,256]{1,0:T(8,128)(2,1)S(1)} %get-tuple-element.46.refs_0_), channel_id=1, source_target_pairs={{0,1},{1,0},{2,3},{3,2},{4,5},{5,4},{6,7},{7,6},{8,9},{9,8},{10,11... | collective-permute-start | bytes 786440 | tf_op jit(solution)/shard_map/ppermute | solution.py:182
  135.5 3.2 %copy-start.8 = (f32[512,512]{1,0:T(8,128)S(1)}, f32[512,512]{1,0:T(8,128)}, u32[]{:S(2)}) copy-start(f32[512,512]{1,0:T(8,128)} %copy-done.7) | copy-start | bytes 3145732
  135.9 3.6 %copy-start.14 = (f32[512,512]{1,0:T(8,128)S(1)}, f32[512,512]{1,0:T(8,128)}, u32[]{:S(2)}) copy-start(f32[512,512]{1,0:T(8,128)} %copy-done.13) | copy-start | bytes 3145732
  136.0 6.7 %collective-permute-start.16 = (bf16[256,256]{1,0:T(8,128)(2,1)S(1)}, bf16[256,256]{1,0:T(8,128)(2,1)S(1)}, u32[]{:S(2)}, u32[]{:S(2)}) collective-permute-start(bf16[256,256]{1,0:T(8,128)(2,1)S(1)} %fusion.9), channel_id=1, source_target_pairs={{0,2},{2,0},{4,6},{6,4},{8,10},{10,8},{12,14},{14,12},{1,3},{3,1},... | collective-permute-start | bytes 393224 | tf_op jit(solution)/shard_map/ppermute | solution.py:179
  138.7 1.9 %copy-start.3 = (bf16[512,2048]{1,0:T(8,128)(2,1)S(1)}, bf16[512,2048]{1,0:T(8,128)(2,1)}, u32[]{:S(2)}) copy-start(bf16[512,2048]{1,0:T(8,128)(2,1)} %copy-done.2) | copy-start | bytes 6291460
  139.0 14.5 %collective-permute-start.17 = (bf16[256,512]{1,0:T(8,128)(2,1)S(1)}, bf16[256,512]{1,0:T(8,128)(2,1)S(1)}, u32[]{:S(2)}, u32[]{:S(2)}) collective-permute-start(bf16[256,512]{1,0:T(8,128)(2,1)S(1)} %get-tuple-element.55.refs_1_), channel_id=1, source_target_pairs={{0,2},{2,0},{4,6},{6,4},{8,10},{10,8},{12,14},{14,12},{1,3},{3,1},... | collective-permute-start | bytes 786440 | tf_op jit(solution)/shard_map/ppermute | solution.py:179
  141.8 11.7 %collective-permute-start.19 = (bf16[256,128]{1,0:T(8,128)(2,1)S(1)}, bf16[256,128]{1,0:T(8,128)(2,1)S(1)}, u32[]{:S(2)}, u32[]{:S(2)}) collective-permute-start(bf16[256,128]{1,0:T(8,128)(2,1)S(1)} %get-tuple-element.48), channel_id=1, source_target_pairs={{0,1},{1,0},{2,3},{3,2},{4,5},{5,4},{6,7},{7,6},{8,9},{9,8},{10,11... | collective-permute-start | bytes 196616 | tf_op jit(solution)/shard_map/ppermute | solution.py:182
  141.9 7.6 %collective-permute-start.21 = (bf16[256,128]{1,0:T(8,128)(2,1)S(1)}, bf16[256,128]{1,0:T(8,128)(2,1)S(1)}, u32[]{:S(2)}, u32[]{:S(2)}) collective-permute-start(bf16[256,128]{1,0:T(8,128)(2,1)S(1)} %get-tuple-element.50), channel_id=1, source_target_pairs={{0,3},{1,2},{2,1},{3,0},{4,7},{5,6},{6,5},{7,4},{8,11},{9,10},{10,... | collective-permute-start | bytes 196616 | tf_op jit(solution)/shard_map/ppermute | solution.py:188
  142.7 7.3 %collective-permute-start.20 = (bf16[256,128]{1,0:T(8,128)(2,1)S(1)}, bf16[256,128]{1,0:T(8,128)(2,1)S(1)}, u32[]{:S(2)}, u32[]{:S(2)}) collective-permute-start(bf16[256,128]{1,0:T(8,128)(2,1)S(1)} %get-tuple-element.49), channel_id=1, source_target_pairs={{0,2},{2,0},{4,6},{6,4},{8,10},{10,8},{12,14},{14,12},{1,3},{3,1},... | collective-permute-start | bytes 196616 | tf_op jit(solution)/shard_map/ppermute | solution.py:179
  151.2 2.4 %collective-permute-start.23 = (bf16[256,128]{1,0:T(8,128)(2,1)S(1)}, bf16[256,128]{1,0:T(8,128)(2,1)S(1)}, u32[]{:S(2)}, u32[]{:S(2)}) collective-permute-start(bf16[256,128]{1,0:T(8,128)(2,1)S(1)} %get-tuple-element.52), channel_id=1, source_target_pairs={{0,1},{1,0},{2,3},{3,2},{4,5},{5,4},{6,7},{7,6},{8,9},{9,8},{10,11... | collective-permute-start | bytes 196616 | tf_op jit(solution)/shard_map/ppermute | solution.py:182
  151.3 4.1 %collective-permute-start.25 = (bf16[256,128]{1,0:T(8,128)(2,1)S(1)}, bf16[256,128]{1,0:T(8,128)(2,1)S(1)}, u32[]{:S(2)}, u32[]{:S(2)}) collective-permute-start(bf16[256,128]{1,0:T(8,128)(2,1)S(1)} %get-tuple-element.54), channel_id=1, source_target_pairs={{0,3},{1,2},{2,1},{3,0},{4,7},{5,6},{6,5},{7,4},{8,11},{9,10},{10,... | collective-permute-start | bytes 196616 | tf_op jit(solution)/shard_map/ppermute | solution.py:188
  152.9 4.3 %collective-permute-start.24 = (bf16[256,128]{1,0:T(8,128)(2,1)S(1)}, bf16[256,128]{1,0:T(8,128)(2,1)S(1)}, u32[]{:S(2)}, u32[]{:S(2)}) collective-permute-start(bf16[256,128]{1,0:T(8,128)(2,1)S(1)} %get-tuple-element.53), channel_id=1, source_target_pairs={{0,2},{2,0},{4,6},{6,4},{8,10},{10,8},{12,14},{14,12},{1,3},{3,1},... | collective-permute-start | bytes 196616 | tf_op jit(solution)/shard_map/ppermute | solution.py:179
  153.6 3.6 %copy-start.17 = (f32[256,2048]{1,0:T(8,128)}, f32[256,2048]{1,0:T(8,128)S(1)}, u32[]{:S(2)}) copy-start(f32[256,2048]{1,0:T(8,128)S(1)} %add_dynamic-update-slice_fusion) | copy-start | bytes 6291460

commit v14 on v13

--- a/solution.py
+++ b/solution.py
@@ -44,7 +44,7 @@
         in_specs=[SCALARS, WHOLE],
         out_specs=[WHOLE] * 3,
         out_shape=[shaped(bf16, size, width // 2) for size in (rows, rows // 2, rows // 2)],
-        compiler_params=pltpu.CompilerParams(vmem_limit_bytes=60 * 1024 * 1024),
+        compiler_params=LIMIT,
     )(spot, query_grads)
 
 

time: 158 us -> 157 us (level)
  Pallas kernels: 40.4 us -> 38.1 us
  local copies, waits for them, and re-layouts: 3.52 us -> 5.11 us
    pallas_call x1, Pallas kernels: 3.54 us -> 1.26 us  [prepare(): pl.pallas_call(prepare_body, in_specs=[SCALARS, WHOLE], out_specs=[WHOLE]...]
    unnamed x36 -> x34, local copies, waits for them, and re-layouts: 3.3 us -> 4.89 us
  transfers between devices with their start and end apart: 26 -> 26, of which waited for: 13 -> 13; matrix products, arithmetic and copies ran while one was open for 2% -> 2% of each run, Pallas kernels for 23% -> 24%
where the time goes in v14:
time: 157 us
  waiting for transfers between devices  89.2 us (57%)
  Pallas kernels  38.1 us (24%)
  starting transfers between devices  20.6 us (13%)
  local copies, waits for them, and re-layouts  5.11 us (3%)
  other arithmetic  3.09 us (2%)
    ppermute x9, waiting for transfers between devices, pass_on(): return lax.ppermute(x, 'blk', onward)  58.4 us
    ppermute x9, waiting for transfers between devices, swap_across(): return lax.ppermute(x, 'blk', across)  28.9 us
    pallas_call x4, Pallas kernels, score(): pl.pallas_call(functools.partial(score_body, count), in_specs=[SCALARS] +...  21 us
    pallas_call x1, Pallas kernels, form(): pl.pallas_call(functools.partial(form_body, rows, rank), grid_spec=pltpu....  13.4 us
    ppermute x9, starting transfers between devices, swap_across(): return lax.ppermute(x, 'blk', across)  9.69 us
    ppermute x9, starting transfers between devices, pass_on(): return lax.ppermute(x, 'blk', onward)  7.99 us
    unnamed x34, local copies, waits for them, and re-layouts  4.89 us
  transfers between devices with their start and end apart: 26, of which 13 were waited for; matrix products, arithmetic and copies ran while one was open for 2% of the time, Pallas kernels for 24%

profile of v14, /device:TPU:0, one launch (start us, length us, event | category | flops | bytes accessed | tf_op | source)
XLA Modules:
  0.0 156.5 jit_solution(10518692617882309441)
XLA Ops:
  0.0 0.1 pad_add_fusion.spot
  0.1 1.6 %copy-done.4 = bf16[256,4096]{1,0:T(8,128)(2,1)S(1)} copy-done((bf16[256,4096]{1,0:T(8,128)(2,1)S(1)}, bf16[256,4096]{1,0:T(8,128)(2,1)}, u32[]{:S(2)}) %copy-start.4) | copy-done | bytes 2097176
  1.7 1.3 shard_map.47
  2.9 3.1 %collective-permute-start = (bf16[256,2048]{1,0:T(8,128)(2,1)S(1)}, bf16[256,2048]{1,0:T(8,128)(2,1)S(1)}, u32[]{:S(2)}, u32[]{:S(2)}) collective-permute-start(bf16[256,2048]{1,0:T(8,128)(2,1)S(1)} %get-tuple-element.32.refs_0_), channel_id=1, source_target_pairs={{0,4},{2,6},{4,8},{6,10},{8,12},{10,14},{12,0},{14,2},{1,5},{3,7},... | collective-permute-start | bytes 3145736 | tf_op jit(solution)/shard_map/ppermute | solution.py:185
  6.0 1.5 collective-permute-start.1
  7.5 0.5 collective-permute-start.2
  8.0 13.4 %shard_map.46 = (bf16[512,2048]{1,0:T(8,128)(2,1)S(1)}, bf16[512,2048]{1,0:T(8,128)(2,1)S(1)}) custom-call(s32[2]{0:T(128)S(1)} %pad_add_fusion.spot, bf16[512,64,128]{2,1,0:T(8,128)(2,1)} %bitcast.4, bf16[512,64,128]{2,1,0:T(8,128)(2,1)} %bitcast.5, s32[512,128]{1,0:T(8,128)S(1)} %copy-done.11), custom_call_target="tpu_custom_call" | custom-call | flops 10737418240 | bytes 20971520 | tf_op jit(solution)/shard_map/pallas_call | solution.py:72
  21.5 9.2 %collective-permute-done.2.refs_3_ = bf16[128,2048]{1,0:T(8,128)(2,1)S(1)} collective-permute-done((bf16[128,2048]{1,0:T(8,128)(2,1)S(1)}, bf16[128,2048]{1,0:T(8,128)(2,1)S(1)}, u32[]{:S(2)}, u32[]{:S(2)}) %collective-permute-start.2) | collective-permute-done | bytes 524320 | tf_op jit(solution)/shard_map/ppermute | solution.py:179
  30.6 0.6 collective-permute-done.refs_1_
  31.2 1.5 collective-permute-start.3
  32.7 1.0 collective-permute-start.10
  33.7 1.6 %collective-permute-start.6 = (bf16[128,2048]{1,0:T(8,128)(2,1)S(1)}, bf16[128,2048]{1,0:T(8,128)(2,1)}, u32[]{:S(2)}, u32[]{:S(2)}) collective-permute-start(bf16[128,2048]{1,0:T(8,128)(2,1)S(1)} %get-tuple-element.36.refs_1_), channel_id=1, source_target_pairs={{0,4},{2,6},{4,8},{6,10},{8,12},{10,14},{12,0},{14,2},{1,5},{3,7},... | collective-permute-start | bytes 1572872 | tf_op jit(solution)/shard_map/ppermute | solution.py:185
  35.3 0.4 collective-permute-start.7
  35.7 24.9 %collective-permute-done.10.refs_0_ = bf16[256,2048]{1,0:T(8,128)(2,1)S(1)} collective-permute-done((bf16[256,2048]{1,0:T(8,128)(2,1)S(1)}, bf16[256,2048]{1,0:T(8,128)(2,1)S(1)}, u32[]{:S(2)}, u32[]{:S(2)}) %collective-permute-start.10) | collective-permute-done | bytes 1048608 | tf_op jit(solution)/shard_map/ppermute | solution.py:185
  60.6 0.0 collective-permute-start.11
  60.6 17.4 %collective-permute-done.3.far = bf16[512,2048]{1,0:T(8,128)(2,1)S(1)} collective-permute-done((bf16[512,2048]{1,0:T(8,128)(2,1)S(1)}, bf16[512,2048]{1,0:T(8,128)(2,1)S(1)}, u32[]{:S(2)}, u32[]{:S(2)}) %collective-permute-start.3) | collective-permute-done | bytes 2097184 | tf_op jit(solution)/shard_map/ppermute | solution.py:179
  78.0 1.3 copy-done.2
  79.3 5.0 %shard_map.49 = (f32[512,512]{1,0:T(8,128)S(1)}, bf16[512,512]{1,0:T(8,128)(2,1)S(1)}) custom-call(s32[2]{0:T(128)S(1)} %pad_add_fusion.spot, bf16[512,2048]{1,0:T(8,128)(2,1)S(1)} %get-tuple-element.30.own, bf16[512,2048]{1,0:T(8,128)(2,1)} %copy-done.2, bf16[256,2048]{1,0:T(8,128)(2,1)S(1)} %get-tuple-element.32.refs_0_, ...), custom_call_target="tpu_custom_call" | custom-call | flops 1024 | bytes 1024 | tf_op jit(solution)/shard_map/pallas_call | solution.py:133
  84.4 0.1 collective-permute-start.4
  84.5 0.0 collective-permute-done.6.refs_1_
  84.5 6.2 %shard_map.50 = (f32[512,512]{1,0:T(8,128)S(1)}, bf16[512,512]{1,0:T(8,128)(2,1)S(1)}) custom-call(s32[2]{0:T(128)S(1)} %pad_add_fusion.spot, bf16[512,2048]{1,0:T(8,128)(2,1)} %copy-done, bf16[512,2048]{1,0:T(8,128)(2,1)} %copy-done.2, bf16[256,2048]{1,0:T(8,128)(2,1)S(1)} %get-tuple-element.40.refs_0_, bf16[128,2048]{1,0:T(8,128)(2,1)} %collective-permute-done.6.refs_1_, ...), custom_call_target="tpu_custom_call" | custom-call | flops 1024 | bytes 1024 | tf_op jit(solution)/shard_map/pallas_call | solution.py:133
  90.7 0.3 collective-permute-start.8
  91.0 0.4 collective-permute-start.13
  91.4 1.6 %collective-permute-start.14 = (bf16[128,2048]{1,0:T(8,128)(2,1)}, bf16[128,2048]{1,0:T(8,128)(2,1)}, u32[]{:S(2)}, u32[]{:S(2)}) collective-permute-start(bf16[128,2048]{1,0:T(8,128)(2,1)} %collective-permute-done.7.refs_2_), channel_id=1, source_target_pairs={{0,4},{2,6},{4,8},{6,10},{8,12},{10,14},{12,0},{14,2},{1,5},{3,7},... | collective-permute-start | bytes 1572872 | tf_op jit(solution)/shard_map/ppermute | solution.py:185
  92.9 0.1 convert_element_type.60
  93.1 0.1 fusion.4
  93.2 1.6 collective-permute-start.5
  94.7 0.1 convert_element_type.63
  94.9 0.1 fusion.1.refs_4_
  95.0 10.5 %collective-permute-done.11.refs_1_ = bf16[256,2048]{1,0:T(8,128)(2,1)S(1)} collective-permute-done((bf16[256,2048]{1,0:T(8,128)(2,1)S(1)}, bf16[256,2048]{1,0:T(8,128)(2,1)S(1)}, u32[]{:S(2)}, u32[]{:S(2)}) %collective-permute-start.11) | collective-permute-done | bytes 1048608 | tf_op jit(solution)/shard_map/ppermute | solution.py:185
  105.5 5.5 %shard_map.51 = (f32[512,512]{1,0:T(8,128)S(1)}, bf16[512,512]{1,0:T(8,128)(2,1)}) custom-call(s32[2]{0:T(128)S(1)} %pad_add_fusion.spot, bf16[512,2048]{1,0:T(8,128)(2,1)} %copy-done, bf16[512,2048]{1,0:T(8,128)(2,1)} %copy-done.2, bf16[256,2048]{1,0:T(8,128)(2,1)S(1)} %collective-permute-done.10.refs_0_, ...), custom_call_target="tpu_custom_call" | custom-call | flops 1024 | bytes 1024 | tf_op jit(solution)/shard_map/pallas_call | solution.py:133
  111.1 1.0 copy-done.7
  112.1 4.8 %collective-permute-done.13.refs_0_ = bf16[128,2048]{1,0:T(8,128)(2,1)} collective-permute-done((bf16[128,2048]{1,0:T(8,128)(2,1)}, bf16[128,2048]{1,0:T(8,128)(2,1)}, u32[]{:S(2)}, u32[]{:S(2)}) %collective-permute-start.13) | collective-permute-done | bytes 524320 | tf_op jit(solution)/shard_map/ppermute | solution.py:185
  116.9 11.2 %collective-permute-done.14.refs_1_ = bf16[128,2048]{1,0:T(8,128)(2,1)} collective-permute-done((bf16[128,2048]{1,0:T(8,128)(2,1)}, bf16[128,2048]{1,0:T(8,128)(2,1)}, u32[]{:S(2)}, u32[]{:S(2)}) %collective-permute-start.14) | collective-permute-done | bytes 524320 | tf_op jit(solution)/shard_map/ppermute | solution.py:185
  128.1 0.0 collective-permute-start.22
  128.1 0.5 collective-permute-start.9
  128.6 4.2 %shard_map.52 = (f32[512,256]{1,0:T(8,128)S(1)}, bf16[512,256]{1,0:T(8,128)(2,1)S(1)}) custom-call(s32[2]{0:T(128)S(1)} %pad_add_fusion.spot, bf16[512,2048]{1,0:T(8,128)(2,1)S(1)} %copy-done.1, bf16[512,2048]{1,0:T(8,128)(2,1)} %copy-done.2, bf16[128,2048]{1,0:T(8,128)(2,1)} %collective-permute-done.13.refs_0_, ...), custom_call_target="tpu_custom_call" | custom-call | flops 1024 | bytes 1024 | tf_op jit(solution)/shard_map/pallas_call | solution.py:133
  132.9 0.1 collective-permute-start.15
  133.0 0.2 broadcast_in_dim.3
  133.2 0.9 copy-done.6
  134.1 0.0 copy-done.10
  134.2 0.1 fusion.6
  134.3 0.2 collective-permute-done.15
  134.6 1.6 %collective-permute-start.16 = (bf16[256,256]{1,0:T(8,128)(2,1)S(1)}, bf16[256,256]{1,0:T(8,128)(2,1)S(1)}, u32[]{:S(2)}, u32[]{:S(2)}) collective-permute-start(bf16[256,256]{1,0:T(8,128)(2,1)S(1)} %fusion.9), channel_id=1, source_target_pairs={{0,2},{2,0},{4,6},{6,4},{8,10},{10,8},{12,14},{14,12},{1,3},{3,1},... | collective-permute-start | bytes 393224 | tf_op jit(solution)/shard_map/ppermute | solution.py:179
  136.2 1.2 convert_element_type.66
  137.4 0.0 copy-start.3
  137.4 0.2 fusion
  137.6 0.6 collective-permute-start.17
  138.2 0.1 fusion.3
  138.3 0.9 collective-permute-done.18.block
  139.2 1.2 shard_map.53
  140.5 0.1 collective-permute-start.19
  140.6 0.7 collective-permute-start.21
  141.3 1.4 collective-permute-start.20
  142.8 5.4 %collective-permute-done.22.block = bf16[128,2048]{1,0:T(8,128)(2,1)S(1)} collective-permute-done((bf16[128,2048]{1,0:T(8,128)(2,1)}, bf16[128,2048]{1,0:T(8,128)(2,1)S(1)}, u32[]{:S(2)}, u32[]{:S(2)}) %collective-permute-start.22) | collective-permute-done | bytes 524320 | tf_op jit(solution)/shard_map/ppermute | solution.py:185
  148.2 0.4 collective-permute-done.20.refs_1_
  148.6 1.2 shard_map.54
  149.9 0.1 collective-permute-start.23
  150.0 1.6 %collective-permute-start.25 = (bf16[256,128]{1,0:T(8,128)(2,1)S(1)}, bf16[256,128]{1,0:T(8,128)(2,1)S(1)}, u32[]{:S(2)}, u32[]{:S(2)}) collective-permute-start(bf16[256,128]{1,0:T(8,128)(2,1)S(1)} %get-tuple-element.54), channel_id=1, source_target_pairs={{0,3},{1,2},{2,1},{3,0},{4,7},{5,6},{6,5},{7,4},{8,11},{9,10},{10,... | collective-permute-start | bytes 196616 | tf_op jit(solution)/shard_map/ppermute | solution.py:188
  151.6 0.5 collective-permute-start.24
  152.3 0.0 copy-start.16
  152.3 1.7 %collective-permute-done.25 = bf16[256,128]{1,0:T(8,128)(2,1)S(1)} collective-permute-done((bf16[256,128]{1,0:T(8,128)(2,1)S(1)}, bf16[256,128]{1,0:T(8,128)(2,1)S(1)}, u32[]{:S(2)}, u32[]{:S(2)}) %collective-permute-start.25) | collective-permute-done | bytes 65568 | tf_op jit(solution)/shard_map/ppermute | solution.py:188
  154.0 1.8 %collective-permute-done.24 = bf16[256,128]{1,0:T(8,128)(2,1)S(1)} collective-permute-done((bf16[256,128]{1,0:T(8,128)(2,1)S(1)}, bf16[256,128]{1,0:T(8,128)(2,1)S(1)}, u32[]{:S(2)}, u32[]{:S(2)}) %collective-permute-start.24) | collective-permute-done | bytes 65568 | tf_op jit(solution)/shard_map/ppermute | solution.py:179
  155.8 0.7 fusion.12
  (49 shorter events, 0.3 us)
Async XLA Ops:
  0.1 1.6 %copy-start.4 = (bf16[256,4096]{1,0:T(8,128)(2,1)S(1)}, bf16[256,4096]{1,0:T(8,128)(2,1)}, u32[]{:S(2)}) copy-start(bf16[256,4096]{1,0:T(8,128)(2,1)} %query_grads.1) | copy-start | bytes 6291460
  1.7 6.4 %copy-start.11 = (s32[512,128]{1,0:T(8,128)S(1)}, s32[512,128]{1,0:T(8,128)}, u32[]{:S(2)}) copy-start(s32[512,128]{1,0:T(8,128)} %mask.1) | copy-start | bytes 786436
  2.9 28.3 %collective-permute-start = (bf16[256,2048]{1,0:T(8,128)(2,1)S(1)}, bf16[256,2048]{1,0:T(8,128)(2,1)S(1)}, u32[]{:S(2)}, u32[]{:S(2)}) collective-permute-start(bf16[256,2048]{1,0:T(8,128)(2,1)S(1)} %get-tuple-element.32.refs_0_), channel_id=1, source_target_pairs={{0,4},{2,6},{4,8},{6,10},{8,12},{10,14},{12,0},{14,2},{1,5},{3,7},... | collective-permute-start | bytes 3145736 | tf_op jit(solution)/shard_map/ppermute | solution.py:185
  6.0 15.4 %collective-permute-start.1 = (bf16[128,2048]{1,0:T(8,128)(2,1)S(1)}, bf16[128,2048]{1,0:T(8,128)(2,1)S(1)}, u32[]{:S(2)}, u32[]{:S(2)}) collective-permute-start(bf16[128,2048]{1,0:T(8,128)(2,1)S(1)} %get-tuple-element.33), channel_id=1, source_target_pairs={{0,2},{2,0},{4,6},{6,4},{8,10},{10,8},{12,14},{14,12},{1,3},{3,1},... | collective-permute-start | bytes 1572872 | tf_op jit(solution)/shard_map/ppermute | solution.py:179
  7.5 23.1 %collective-permute-start.2 = (bf16[128,2048]{1,0:T(8,128)(2,1)S(1)}, bf16[128,2048]{1,0:T(8,128)(2,1)S(1)}, u32[]{:S(2)}, u32[]{:S(2)}) collective-permute-start(bf16[128,2048]{1,0:T(8,128)(2,1)S(1)} %get-tuple-element.34), channel_id=1, source_target_pairs={{0,2},{2,0},{4,6},{6,4},{8,10},{10,8},{12,14},{14,12},{1,3},{3,1},... | collective-permute-start | bytes 1572872 | tf_op jit(solution)/shard_map/ppermute | solution.py:179
  21.4 56.6 %copy-start = (bf16[512,2048]{1,0:T(8,128)(2,1)}, bf16[512,2048]{1,0:T(8,128)(2,1)S(1)}, u32[]{:S(2)}) copy-start(bf16[512,2048]{1,0:T(8,128)(2,1)S(1)} %get-tuple-element.30.own) | copy-start | bytes 6291460
  31.2 46.8 %collective-permute-start.3 = (bf16[512,2048]{1,0:T(8,128)(2,1)S(1)}, bf16[512,2048]{1,0:T(8,128)(2,1)S(1)}, u32[]{:S(2)}, u32[]{:S(2)}) collective-permute-start(bf16[512,2048]{1,0:T(8,128)(2,1)S(1)} %get-tuple-element.35), channel_id=1, source_target_pairs={{0,2},{2,0},{4,6},{6,4},{8,10},{10,8},{12,14},{14,12},{1,3},{3,1},... | collective-permute-start | bytes 6291464 | tf_op jit(solution)/shard_map/ppermute | solution.py:179
  32.7 27.9 %collective-permute-start.10 = (bf16[256,2048]{1,0:T(8,128)(2,1)S(1)}, bf16[256,2048]{1,0:T(8,128)(2,1)S(1)}, u32[]{:S(2)}, u32[]{:S(2)}) collective-permute-start(bf16[256,2048]{1,0:T(8,128)(2,1)S(1)} %get-tuple-element.40.refs_0_), channel_id=1, source_target_pairs={{0,4},{2,6},{4,8},{6,10},{8,12},{10,14},{12,0},{14,2},{1,5},{3,7},... | collective-permute-start | bytes 3145736 | tf_op jit(solution)/shard_map/ppermute | solution.py:185
  33.7 50.8 %collective-permute-start.6 = (bf16[128,2048]{1,0:T(8,128)(2,1)S(1)}, bf16[128,2048]{1,0:T(8,128)(2,1)}, u32[]{:S(2)}, u32[]{:S(2)}) collective-permute-start(bf16[128,2048]{1,0:T(8,128)(2,1)S(1)} %get-tuple-element.36.refs_1_), channel_id=1, source_target_pairs={{0,4},{2,6},{4,8},{6,10},{8,12},{10,14},{12,0},{14,2},{1,5},{3,7},... | collective-permute-start | bytes 1572872 | tf_op jit(solution)/shard_map/ppermute | solution.py:185
  35.3 49.2 %collective-permute-start.7 = (bf16[128,2048]{1,0:T(8,128)(2,1)S(1)}, bf16[128,2048]{1,0:T(8,128)(2,1)}, u32[]{:S(2)}, u32[]{:S(2)}) collective-permute-start(bf16[128,2048]{1,0:T(8,128)(2,1)S(1)} %get-tuple-element.37.refs_2_), channel_id=1, source_target_pairs={{0,4},{2,6},{4,8},{6,10},{8,12},{10,14},{12,0},{14,2},{1,5},{3,7},... | collective-permute-start | bytes 1572872 | tf_op jit(solution)/shard_map/ppermute | solution.py:185
  60.6 44.9 %collective-permute-start.11 = (bf16[256,2048]{1,0:T(8,128)(2,1)S(1)}, bf16[256,2048]{1,0:T(8,128)(2,1)S(1)}, u32[]{:S(2)}, u32[]{:S(2)}) collective-permute-start(bf16[256,2048]{1,0:T(8,128)(2,1)S(1)} %collective-permute-done.10.refs_0_), channel_id=1, source_target_pairs={{0,4},{2,6},{4,8},{6,10},{8,12},{10,14},{12,0},{14,2},{1,5},{3,7},... | collective-permute-start | bytes 3145736 | tf_op jit(solution)/shard_map/ppermute | solution.py:185
  78.0 1.3 copy-start.2
  84.4 8.7 %copy-start.5 = (f32[512,512]{1,0:T(8,128)}, f32[512,512]{1,0:T(8,128)S(1)}, u32[]{:S(2)}) copy-start(f32[512,512]{1,0:T(8,128)S(1)} %get-tuple-element.38) | copy-start | bytes 3145732
  84.4 8.5 %collective-permute-start.4 = (bf16[512,512]{1,0:T(8,128)(2,1)S(1)}, bf16[512,512]{1,0:T(8,128)(2,1)S(1)}, u32[]{:S(2)}, u32[]{:S(2)}) collective-permute-start(bf16[512,512]{1,0:T(8,128)(2,1)S(1)} %get-tuple-element.39.refs_3_), channel_id=1, source_target_pairs={{0,1},{1,0},{2,3},{3,2},{4,5},{5,4},{6,7},{7,6},{8,9},{9,8},{10,11... | collective-permute-start | bytes 1572872 | tf_op jit(solution)/shard_map/ppermute | solution.py:182
  90.7 4.0 %collective-permute-start.8 = (bf16[512,512]{1,0:T(8,128)(2,1)S(1)}, bf16[512,512]{1,0:T(8,128)(2,1)S(1)}, u32[]{:S(2)}, u32[]{:S(2)}) collective-permute-start(bf16[512,512]{1,0:T(8,128)(2,1)S(1)} %get-tuple-element.42.refs_2_), channel_id=1, source_target_pairs={{0,1},{1,0},{2,3},{3,2},{4,5},{5,4},{6,7},{7,6},{8,9},{9,8},{10,11... | collective-permute-start | bytes 1572872 | tf_op jit(solution)/shard_map/ppermute | solution.py:182
  91.0 25.9 %collective-permute-start.13 = (bf16[128,2048]{1,0:T(8,128)(2,1)}, bf16[128,2048]{1,0:T(8,128)(2,1)}, u32[]{:S(2)}, u32[]{:S(2)}) collective-permute-start(bf16[128,2048]{1,0:T(8,128)(2,1)} %collective-permute-done.6.refs_1_), channel_id=1, source_target_pairs={{0,4},{2,6},{4,8},{6,10},{8,12},{10,14},{12,0},{14,2},{1,5},{3,7},... | collective-permute-start | bytes 1572872 | tf_op jit(solution)/shard_map/ppermute | solution.py:185
  91.4 36.8 %collective-permute-start.14 = (bf16[128,2048]{1,0:T(8,128)(2,1)}, bf16[128,2048]{1,0:T(8,128)(2,1)}, u32[]{:S(2)}, u32[]{:S(2)}) collective-permute-start(bf16[128,2048]{1,0:T(8,128)(2,1)} %collective-permute-done.7.refs_2_), channel_id=1, source_target_pairs={{0,4},{2,6},{4,8},{6,10},{8,12},{10,14},{12,0},{14,2},{1,5},{3,7},... | collective-permute-start | bytes 1572872 | tf_op jit(solution)/shard_map/ppermute | solution.py:185
  93.1 1.7 %copy-start.14 = (f32[512,512]{1,0:T(8,128)}, f32[512,512]{1,0:T(8,128)S(1)}, u32[]{:S(2)}) copy-start(f32[512,512]{1,0:T(8,128)S(1)} %convert_element_type.60) | copy-start | bytes 3145732
  93.2 12.4 %collective-permute-start.5 = (bf16[256,512]{1,0:T(8,128)(2,1)S(1)}, bf16[256,512]{1,0:T(8,128)(2,1)S(1)}, u32[]{:S(2)}, u32[]{:S(2)}) collective-permute-start(bf16[256,512]{1,0:T(8,128)(2,1)S(1)} %fusion.4), channel_id=1, source_target_pairs={{0,2},{2,0},{4,6},{6,4},{8,10},{10,8},{12,14},{14,12},{1,3},{3,1},... | collective-permute-start | bytes 786440 | tf_op jit(solution)/shard_map/ppermute | solution.py:179
  94.9 16.2 %copy-start.12 = (f32[512,512]{1,0:T(8,128)}, f32[512,512]{1,0:T(8,128)S(1)}, u32[]{:S(2)}) copy-start(f32[512,512]{1,0:T(8,128)S(1)} %convert_element_type.63) | copy-start | bytes 3145732
  95.0 33.6 %copy-start.1 = (bf16[512,2048]{1,0:T(8,128)(2,1)S(1)}, bf16[512,2048]{1,0:T(8,128)(2,1)}, u32[]{:S(2)}) copy-start(bf16[512,2048]{1,0:T(8,128)(2,1)} %copy-done) | copy-start | bytes 6291460
  105.5 5.5 %copy-start.9 = (bf16[256,512]{1,0:T(8,128)(2,1)}, bf16[256,512]{1,0:T(8,128)(2,1)S(1)}, u32[]{:S(2)}) copy-start(bf16[256,512]{1,0:T(8,128)(2,1)S(1)} %collective-permute-done.5.refs_3_) | copy-start | bytes 786436
  111.1 1.0 copy-start.7
  112.1 24.1 %collective-permute-start.12 = (bf16[512,512]{1,0:T(8,128)(2,1)}, bf16[512,512]{1,0:T(8,128)(2,1)}, u32[]{:S(2)}, u32[]{:S(2)}) collective-permute-start(bf16[512,512]{1,0:T(8,128)(2,1)} %get-tuple-element.44.refs_2_), channel_id=1, source_target_pairs={{0,1},{1,0},{2,3},{3,2},{4,5},{5,4},{6,7},{7,6},{8,9},{9,8},{10,11... | collective-permute-start | bytes 1572872 | tf_op jit(solution)/shard_map/ppermute | solution.py:182
  116.9 22.4 %collective-permute-start.18 = (bf16[128,2048]{1,0:T(8,128)(2,1)}, bf16[128,2048]{1,0:T(8,128)(2,1)S(1)}, u32[]{:S(2)}, u32[]{:S(2)}) collective-permute-start(bf16[128,2048]{1,0:T(8,128)(2,1)} %collective-permute-done.13.refs_0_), channel_id=1, source_target_pairs={{0,4},{2,6},{4,8},{6,10},{8,12},{10,14},{12,0},{14,2},{1,5},{3,7},... | collective-permute-start | bytes 1572872 | tf_op jit(solution)/shard_map/ppermute | solution.py:185
  128.1 20.1 %collective-permute-start.22 = (bf16[128,2048]{1,0:T(8,128)(2,1)}, bf16[128,2048]{1,0:T(8,128)(2,1)S(1)}, u32[]{:S(2)}, u32[]{:S(2)}) collective-permute-start(bf16[128,2048]{1,0:T(8,128)(2,1)} %collective-permute-done.14.refs_1_), channel_id=1, source_target_pairs={{0,4},{2,6},{4,8},{6,10},{8,12},{10,14},{12,0},{14,2},{1,5},{3,7},... | collective-permute-start | bytes 1572872 | tf_op jit(solution)/shard_map/ppermute | solution.py:185
  128.1 10.1 %collective-permute-start.9 = (bf16[256,512]{1,0:T(8,128)(2,1)S(1)}, bf16[256,512]{1,0:T(8,128)(2,1)S(1)}, u32[]{:S(2)}, u32[]{:S(2)}) collective-permute-start(bf16[256,512]{1,0:T(8,128)(2,1)S(1)} %fusion.1.refs_4_), channel_id=1, source_target_pairs={{0,2},{2,0},{4,6},{6,4},{8,10},{10,8},{12,14},{14,12},{1,3},{3,1},... | collective-permute-start | bytes 786440 | tf_op jit(solution)/shard_map/ppermute | solution.py:179
  128.6 4.6 %copy-start.15 = (f32[512,512]{1,0:T(8,128)S(1)}, f32[512,512]{1,0:T(8,128)}, u32[]{:S(2)}) copy-start(f32[512,512]{1,0:T(8,128)} %copy-done.14) | copy-start | bytes 3145732
  132.9 1.2 copy-start.6
  132.9 1.3 copy-start.10
  132.9 1.6 %collective-permute-start.15 = (bf16[512,256]{1,0:T(8,128)(2,1)S(1)}, bf16[512,256]{1,0:T(8,128)(2,1)S(1)}, u32[]{:S(2)}, u32[]{:S(2)}) collective-permute-start(bf16[512,256]{1,0:T(8,128)(2,1)S(1)} %get-tuple-element.46.refs_0_), channel_id=1, source_target_pairs={{0,1},{1,0},{2,3},{3,2},{4,5},{5,4},{6,7},{7,6},{8,9},{9,8},{10,11... | collective-permute-start | bytes 786440 | tf_op jit(solution)/shard_map/ppermute | solution.py:182
  134.2 3.2 %copy-start.8 = (f32[512,512]{1,0:T(8,128)S(1)}, f32[512,512]{1,0:T(8,128)}, u32[]{:S(2)}) copy-start(f32[512,512]{1,0:T(8,128)} %copy-done.7) | copy-start | bytes 3145732
  134.6 3.6 %copy-start.13 = (f32[512,512]{1,0:T(8,128)S(1)}, f32[512,512]{1,0:T(8,128)}, u32[]{:S(2)}) copy-start(f32[512,512]{1,0:T(8,128)} %copy-done.12) | copy-start | bytes 3145732
  134.6 6.7 %collective-permute-start.16 = (bf16[256,256]{1,0:T(8,128)(2,1)S(1)}, bf16[256,256]{1,0:T(8,128)(2,1)S(1)}, u32[]{:S(2)}, u32[]{:S(2)}) collective-permute-start(bf16[256,256]{1,0:T(8,128)(2,1)S(1)} %fusion.9), channel_id=1, source_target_pairs={{0,2},{2,0},{4,6},{6,4},{8,10},{10,8},{12,14},{14,12},{1,3},{3,1},... | collective-permute-start | bytes 393224 | tf_op jit(solution)/shard_map/ppermute | solution.py:179
  137.4 1.9 %copy-start.3 = (bf16[512,2048]{1,0:T(8,128)(2,1)S(1)}, bf16[512,2048]{1,0:T(8,128)(2,1)}, u32[]{:S(2)}) copy-start(bf16[512,2048]{1,0:T(8,128)(2,1)} %copy-done.2) | copy-start | bytes 6291460
  137.6 14.5 %collective-permute-start.17 = (bf16[256,512]{1,0:T(8,128)(2,1)S(1)}, bf16[256,512]{1,0:T(8,128)(2,1)S(1)}, u32[]{:S(2)}, u32[]{:S(2)}) collective-permute-start(bf16[256,512]{1,0:T(8,128)(2,1)S(1)} %get-tuple-element.55.refs_1_), channel_id=1, source_target_pairs={{0,2},{2,0},{4,6},{6,4},{8,10},{10,8},{12,14},{14,12},{1,3},{3,1},... | collective-permute-start | bytes 786440 | tf_op jit(solution)/shard_map/ppermute | solution.py:179
  140.5 11.7 %collective-permute-start.19 = (bf16[256,128]{1,0:T(8,128)(2,1)S(1)}, bf16[256,128]{1,0:T(8,128)(2,1)S(1)}, u32[]{:S(2)}, u32[]{:S(2)}) collective-permute-start(bf16[256,128]{1,0:T(8,128)(2,1)S(1)} %get-tuple-element.48), channel_id=1, source_target_pairs={{0,1},{1,0},{2,3},{3,2},{4,5},{5,4},{6,7},{7,6},{8,9},{9,8},{10,11... | collective-permute-start | bytes 196616 | tf_op jit(solution)/shard_map/ppermute | solution.py:182
  140.6 7.6 %collective-permute-start.21 = (bf16[256,128]{1,0:T(8,128)(2,1)S(1)}, bf16[256,128]{1,0:T(8,128)(2,1)S(1)}, u32[]{:S(2)}, u32[]{:S(2)}) collective-permute-start(bf16[256,128]{1,0:T(8,128)(2,1)S(1)} %get-tuple-element.50), channel_id=1, source_target_pairs={{0,3},{1,2},{2,1},{3,0},{4,7},{5,6},{6,5},{7,4},{8,11},{9,10},{10,... | collective-permute-start | bytes 196616 | tf_op jit(solution)/shard_map/ppermute | solution.py:188
  141.3 7.3 %collective-permute-start.20 = (bf16[256,128]{1,0:T(8,128)(2,1)S(1)}, bf16[256,128]{1,0:T(8,128)(2,1)S(1)}, u32[]{:S(2)}, u32[]{:S(2)}) collective-permute-start(bf16[256,128]{1,0:T(8,128)(2,1)S(1)} %get-tuple-element.49), channel_id=1, source_target_pairs={{0,2},{2,0},{4,6},{6,4},{8,10},{10,8},{12,14},{14,12},{1,3},{3,1},... | collective-permute-start | bytes 196616 | tf_op jit(solution)/shard_map/ppermute | solution.py:179
  149.9 2.4 %collective-permute-start.23 = (bf16[256,128]{1,0:T(8,128)(2,1)S(1)}, bf16[256,128]{1,0:T(8,128)(2,1)S(1)}, u32[]{:S(2)}, u32[]{:S(2)}) collective-permute-start(bf16[256,128]{1,0:T(8,128)(2,1)S(1)} %get-tuple-element.52), channel_id=1, source_target_pairs={{0,1},{1,0},{2,3},{3,2},{4,5},{5,4},{6,7},{7,6},{8,9},{9,8},{10,11... | collective-permute-start | bytes 196616 | tf_op jit(solution)/shard_map/ppermute | solution.py:182
  150.0 4.0 %collective-permute-start.25 = (bf16[256,128]{1,0:T(8,128)(2,1)S(1)}, bf16[256,128]{1,0:T(8,128)(2,1)S(1)}, u32[]{:S(2)}, u32[]{:S(2)}) collective-permute-start(bf16[256,128]{1,0:T(8,128)(2,1)S(1)} %get-tuple-element.54), channel_id=1, source_target_pairs={{0,3},{1,2},{2,1},{3,0},{4,7},{5,6},{6,5},{7,4},{8,11},{9,10},{10,... | collective-permute-start | bytes 196616 | tf_op jit(solution)/shard_map/ppermute | solution.py:188
  151.6 4.3 %collective-permute-start.24 = (bf16[256,128]{1,0:T(8,128)(2,1)S(1)}, bf16[256,128]{1,0:T(8,128)(2,1)S(1)}, u32[]{:S(2)}, u32[]{:S(2)}) collective-permute-start(bf16[256,128]{1,0:T(8,128)(2,1)S(1)} %get-tuple-element.53), channel_id=1, source_target_pairs={{0,2},{2,0},{4,6},{6,4},{8,10},{10,8},{12,14},{14,12},{1,3},{3,1},... | collective-permute-start | bytes 196616 | tf_op jit(solution)/shard_map/ppermute | solution.py:179
  152.3 3.6 %copy-start.16 = (f32[256,2048]{1,0:T(8,128)}, f32[256,2048]{1,0:T(8,128)S(1)}, u32[]{:S(2)}) copy-start(f32[256,2048]{1,0:T(8,128)S(1)} %add_dynamic-update-slice_fusion) | copy-start | bytes 6291460

commit v15 on v14

--- a/solution.py
+++ b/solution.py
@@ -48,16 +48,17 @@
     )(spot, query_grads)
 
 
-def form_body(rows, rank, spot, inputs, outgrads, mask, kept, sent, rounds):
+def form_body(rows, rank, spot, inputs, outgrads, mask, kept, sent, sent_rest, rounds):
     for d in range(rows):
         masked = outgrads[d] * mask[d:d + 1, :].astype(bf16)
         product = lax.dot_general(inputs[d], masked, NT, preferred_element_type=f32)
         pairs = jnp.concatenate([product[:rank // 2], product[rank // 2:]], 1)
         rounds[pl.ds(d, rank // 2, stride=rows), :] = pairs
-    for out, side in ((kept, spot[0]), (sent, 1 - spot[0])):
+    for side, outs in ((spot[0], (kept,)), (1 - spot[0], (sent, sent_rest))):
         for k in range(rank // 4):
             at = pl.multiple_of((side * (rank // 4) + k) * rows, rows)
-            out[:, k * LANES:(k + 1) * LANES] = rounds[pl.ds(at, rows), :].astype(bf16)
+            out, place = outs[k * len(outs) // (rank // 4)], k % (rank // 4 // len(outs))
+            out[:, place * LANES:(place + 1) * LANES] = rounds[pl.ds(at, rows), :].astype(bf16)
 
 
 def form(doc_inputs, doc_outgrads, token_mask, spot):
@@ -65,6 +66,7 @@
     rows = 64
     steps = docs // rows
     half = rank * rank // 2
+    widths = (half, half // 2, half // 2)
 
     def at(g, spot):
         return lax.rem(g + spot[1] * (steps // 2), steps)
@@ -79,10 +81,10 @@
                 pl.BlockSpec((rows, rank, length), lambda g, spot: (at(g, spot), 0, 0)),
                 pl.BlockSpec((rows, length), lambda g, spot: (at(g, spot), 0)),
             ],
-            out_specs=[pl.BlockSpec((rows, half), lambda g, spot: (g, 0))] * 2,
+            out_specs=[pl.BlockSpec((rows, width), lambda g, spot: (g, 0)) for width in widths],
             scratch_shapes=[pltpu.VMEM((rank // 2 * rows, LANES), f32)],
         ),
-        out_shape=[shaped(bf16, docs, half)] * 2,
+        out_shape=[shaped(bf16, docs, width) for width in widths],
         compiler_params=LIMIT,
         cost_estimate=pl.CostEstimate(
             flops=40 * docs * rank * rank * length, bytes_accessed=4 * docs * rank * length + 2 * docs * rank * rank, transcendentals=0
@@ -109,7 +111,12 @@
 FREE = pl.CostEstimate(flops=1024, bytes_accessed=1024, transcendentals=0)
 
 
-def score_body(count, spot, own, far, *refs):
+def reach(far, rest, rows, block):
+    half = far.shape[1]
+    return dot(far[rows, :], block[:, :half]) + dot(rest[rows, :], block[:, half:])
+
+
+def score_body(count, spot, own, far, rest, *refs):
     keep, give = refs[-2:]
     part = own.shape[0] // 2
     for i, block in enumerate(refs[:count]):
@@ -121,9 +128,9 @@
         else:
             columns = pl.ds(i * size, size)
         keep[:part, columns] = dot(own[:part, :], block[...])
-        keep[part:, columns] = dot(far[:part, :], block[...])
+        keep[part:, columns] = reach(far, rest, slice(part), block)
         give[:part, columns] = dot(own[part:, :], block[...]).astype(bf16)
-        give[part:, columns] = dot(far[part:, :], block[...]).astype(bf16)
+        give[part:, columns] = reach(far, rest, slice(part, None), block).astype(bf16)
 
 
 def score(spot, own, far, blocks, *after):
@@ -132,20 +139,20 @@
     queries = sum(block.shape[0] for block in blocks)
     return pl.pallas_call(
         functools.partial(score_body, count),
-        in_specs=[SCALARS] + [WHOLE] * (2 + count) + [ANYWHERE] * len(after),
+        in_specs=[SCALARS] + [WHOLE] * (3 + count) + [ANYWHERE] * len(after),
         out_specs=[WHOLE] * 2,
         out_shape=[shaped(f32, docs, queries), shaped(bf16, docs, queries)],
         compiler_params=LIMIT,
         cost_estimate=FREE,
-    )(spot, own, far, *blocks, *after)
-
-
-def last_body(own, far, block, *refs):
+    )(spot, own, *far, *blocks, *after)
+
+
+def last_body(own, far, rest, block, *refs):
     near, mate, across, diagonal = refs[-4:]
     part = near.shape[0]
     mate[...] = dot(own[part:, :], block[...]).astype(bf16)
-    across[...] = dot(far[:part, :], block[...]).astype(bf16)
-    diagonal[...] = dot(far[part:, :], block[...]).astype(bf16)
+    across[...] = reach(far, rest, slice(part), block).astype(bf16)
+    diagonal[...] = reach(far, rest, slice(part, None), block).astype(bf16)
     near[...] = dot(own[:part, :], block[...])
 
 
@@ -153,12 +160,12 @@
     shape = (own.shape[0] // 2, block.shape[0])
     return pl.pallas_call(
         last_body,
-        in_specs=[WHOLE] * 3 + [ANYWHERE] * len(after),
+        in_specs=[WHOLE] * 4 + [ANYWHERE] * len(after),
         out_specs=[WHOLE] * 4,
         out_shape=[shaped(f32, *shape)] + [shaped(bf16, *shape)] * 3,
         compiler_params=LIMIT,
         cost_estimate=FREE,
-    )(own, far, block, *after)
+    )(own, *far, block, *after)
 
 
 def on_device(doc_inputs, doc_outgrads, token_mask, query_grads):
@@ -190,11 +197,12 @@
     mine, *sending = prepare(query_grads, spot)
     ahead = pass_on(mine)
     other = [swap_across(x) for x in sending]
-    own, sent = form(
+    own, *sent = form(
         doc_inputs.reshape(docs, *doc_inputs.shape[2:]), doc_outgrads.reshape(docs, *doc_outgrads.shape[2:]), token_mask, spot
     )
-    sent, ahead, *other = tie((sent, ahead, *other))
-    far = swap_across(sent)
+    *sent, ahead, second_half, first_half = tie((*sent, ahead, *other[::-1]))
+    other = [first_half, second_half]
+    far = [swap_across(x) for x in sent]
     first, second = [mine, ahead], [other]
     for step in range(2, places):
         first.append(pass_on(first[-1]))

time: 157 us -> 156 us (level)
  waiting for transfers between devices: 89.2 us -> 86.8 us
  starting transfers between devices: 20.6 us -> 22.4 us
    ppermute x9, waiting for transfers between devices: 58.4 us -> 49 us  [pass_on(): return lax.ppermute(x, 'blk', onward)]
    ppermute x9 -> x10, waiting for transfers between devices: 28.9 us -> 36 us  [swap_across(): return lax.ppermute(x, 'blk', across)]
    ppermute x9 -> x10, starting transfers between devices: 9.69 us -> 11.4 us  [swap_across(): return lax.ppermute(x, 'blk', across)]
  transfers between devices with their start and end apart: 26 -> 27, of which waited for: 13 -> 13; matrix products, arithmetic and copies ran while one was open for 2% -> 2% of each run, Pallas kernels for 24% -> 23%
where the time goes in v15:
time: 156 us
  waiting for transfers between devices  86.8 us (56%)
  Pallas kernels  37.3 us (24%)
  starting transfers between devices  22.4 us (14%)
  local copies, waits for them, and re-layouts  6.08 us (4%)
  other arithmetic  3.09 us (2%)
    ppermute x9, waiting for transfers between devices, pass_on(): return lax.ppermute(x, 'blk', onward)  49 us
    ppermute x10, waiting for transfers between devices, swap_across(): return lax.ppermute(x, 'blk', across)  36 us
    pallas_call x4, Pallas kernels, score(): pl.pallas_call(functools.partial(score_body, count), in_specs=[SCALARS] +...  20.2 us
    pallas_call x1, Pallas kernels, form(): pl.pallas_call(functools.partial(form_body, rows, rank), grid_spec=pltpu....  13.4 us
    ppermute x10, starting transfers between devices, swap_across(): return lax.ppermute(x, 'blk', across)  11.4 us
    ppermute x9, starting transfers between devices, pass_on(): return lax.ppermute(x, 'blk', onward)  8.29 us
    unnamed x34, local copies, waits for them, and re-layouts  5.85 us
  transfers between devices with their start and end apart: 27, of which 13 were waited for; matrix products, arithmetic and copies ran while one was open for 2% of the time, Pallas kernels for 23%

profile of v15, /device:TPU:0, one launch (start us, length us, event | category | flops | bytes accessed | tf_op | source)
XLA Modules:
  0.0 156.0 jit_solution(18003012641094815418)
XLA Ops:
  0.0 0.1 pad_add_fusion.spot
  0.1 1.6 %copy-done.3 = bf16[256,4096]{1,0:T(8,128)(2,1)S(1)} copy-done((bf16[256,4096]{1,0:T(8,128)(2,1)S(1)}, bf16[256,4096]{1,0:T(8,128)(2,1)}, u32[]{:S(2)}) %copy-start.3) | copy-done | bytes 2097176
  1.7 1.3 shard_map.47
  2.9 3.1 %collective-permute-start = (bf16[256,2048]{1,0:T(8,128)(2,1)S(1)}, bf16[256,2048]{1,0:T(8,128)(2,1)S(1)}, u32[]{:S(2)}, u32[]{:S(2)}) collective-permute-start(bf16[256,2048]{1,0:T(8,128)(2,1)S(1)} %get-tuple-element.35.refs_0_), channel_id=1, source_target_pairs={{0,4},{2,6},{4,8},{6,10},{8,12},{10,14},{12,0},{14,2},{1,5},{3,7},... | collective-permute-start | bytes 3145736 | tf_op jit(solution)/shard_map/ppermute | solution.py:192
  6.0 1.5 collective-permute-start.1
  7.5 0.5 collective-permute-start.2
  8.0 13.4 %shard_map.46 = (bf16[512,2048]{1,0:T(8,128)(2,1)S(1)}, bf16[512,1024]{1,0:T(8,128)(2,1)S(1)}, bf16[512,1024]{1,0:T(8,128)(2,1)S(1)}) custom-call(s32[2]{0:T(128)S(1)} %pad_add_fusion.spot, bf16[512,64,128]{2,1,0:T(8,128)(2,1)} %bitcast.4, bf16[512,64,128]{2,1,0:T(8,128)(2,1)} %bitcast.5, s32[512,128]{1,0:T(8,128)S(1)} %copy-done.10), custom_call_target="tpu_custom_call" | custom-call | flops 10737418240 | bytes 20971520 | tf_op jit(solution)/shard_map/pallas_call | solution.py:74
  21.4 0.0 copy-start
  21.5 1.3 copy-done
  22.8 7.9 %collective-permute-done.2.refs_4_ = bf16[128,2048]{1,0:T(8,128)(2,1)S(1)} collective-permute-done((bf16[128,2048]{1,0:T(8,128)(2,1)S(1)}, bf16[128,2048]{1,0:T(8,128)(2,1)S(1)}, u32[]{:S(2)}, u32[]{:S(2)}) %collective-permute-start.2) | collective-permute-done | bytes 524320 | tf_op jit(solution)/shard_map/ppermute | solution.py:186
  30.6 0.6 collective-permute-done.refs_2_
  31.2 1.0 collective-permute-start.11
  32.2 1.5 collective-permute-start.3
  33.7 0.5 collective-permute-start.4
  34.2 1.6 %collective-permute-start.7 = (bf16[128,2048]{1,0:T(8,128)(2,1)S(1)}, bf16[128,2048]{1,0:T(8,128)(2,1)}, u32[]{:S(2)}, u32[]{:S(2)}) collective-permute-start(bf16[128,2048]{1,0:T(8,128)(2,1)S(1)} %get-tuple-element.40.refs_1_), channel_id=1, source_target_pairs={{0,4},{2,6},{4,8},{6,10},{8,12},{10,14},{12,0},{14,2},{1,5},{3,7},... | collective-permute-start | bytes 1572872 | tf_op jit(solution)/shard_map/ppermute | solution.py:192
  35.8 0.4 collective-permute-start.8
  36.2 22.9 %collective-permute-done.11.refs_0_ = bf16[256,2048]{1,0:T(8,128)(2,1)S(1)} collective-permute-done((bf16[256,2048]{1,0:T(8,128)(2,1)S(1)}, bf16[256,2048]{1,0:T(8,128)(2,1)S(1)}, u32[]{:S(2)}, u32[]{:S(2)}) %collective-permute-start.11) | collective-permute-done | bytes 1048608 | tf_op jit(solution)/shard_map/ppermute | solution.py:192
  59.1 19.0 %collective-permute-done.4.rest = bf16[512,1024]{1,0:T(8,128)(2,1)S(1)} collective-permute-done((bf16[512,1024]{1,0:T(8,128)(2,1)S(1)}, bf16[512,1024]{1,0:T(8,128)(2,1)S(1)}, u32[]{:S(2)}, u32[]{:S(2)}) %collective-permute-start.4) | collective-permute-done | bytes 1048608 | tf_op jit(solution)/shard_map/ppermute | solution.py:186
  78.1 5.0 %shard_map.49 = (f32[512,512]{1,0:T(8,128)S(1)}, bf16[512,512]{1,0:T(8,128)(2,1)S(1)}) custom-call(s32[2]{0:T(128)S(1)} %pad_add_fusion.spot, bf16[512,2048]{1,0:T(8,128)(2,1)} %copy-done, bf16[512,1024]{1,0:T(8,128)(2,1)S(1)} %collective-permute-done.3.far, bf16[512,1024]{1,0:T(8,128)(2,1)S(1)} %collective-permute-done.4.rest, ...), custom_call_target="tpu_custom_call" | custom-call | flops 1024 | bytes 1024 | tf_op jit(solution)/shard_map/pallas_call | solution.py:140
  83.2 0.1 collective-permute-start.5
  83.3 5.9 %shard_map.50 = (f32[512,512]{1,0:T(8,128)S(1)}, bf16[512,512]{1,0:T(8,128)(2,1)S(1)}) custom-call(s32[2]{0:T(128)S(1)} %pad_add_fusion.spot, bf16[512,2048]{1,0:T(8,128)(2,1)} %copy-done, bf16[512,1024]{1,0:T(8,128)(2,1)S(1)} %collective-permute-done.3.far, bf16[512,1024]{1,0:T(8,128)(2,1)S(1)} %collective-permute-done.4.rest, bf16[256,2048]{1,0:T(8,128)(2,1)} %copy-done.2, ...), custom_call_target="tpu_custom_call" | custom-call | flops 1024 | bytes 1024 | tf_op jit(solution)/shard_map/pallas_call | solution.py:140
  89.2 0.3 collective-permute-start.9
  89.4 1.6 %collective-permute-start.14 = (bf16[128,2048]{1,0:T(8,128)(2,1)}, bf16[128,2048]{1,0:T(8,128)(2,1)}, u32[]{:S(2)}, u32[]{:S(2)}) collective-permute-start(bf16[128,2048]{1,0:T(8,128)(2,1)} %collective-permute-done.7.refs_1_), channel_id=1, source_target_pairs={{0,4},{2,6},{4,8},{6,10},{8,12},{10,14},{12,0},{14,2},{1,5},{3,7},... | collective-permute-start | bytes 1572872 | tf_op jit(solution)/shard_map/ppermute | solution.py:192
  91.0 0.7 collective-permute-start.15
  91.7 0.1 convert_element_type.60
  91.8 0.1 fusion.4
  91.9 1.5 collective-permute-start.6
  93.4 0.1 convert_element_type.63
  93.6 0.1 fusion.1.refs_4_
  93.7 6.3 %collective-permute-done.6.refs_3_ = bf16[256,512]{1,0:T(8,128)(2,1)S(1)} collective-permute-done((bf16[256,512]{1,0:T(8,128)(2,1)S(1)}, bf16[256,512]{1,0:T(8,128)(2,1)S(1)}, u32[]{:S(2)}, u32[]{:S(2)}) %collective-permute-start.6) | collective-permute-done | bytes 262176 | tf_op jit(solution)/shard_map/ppermute | solution.py:186
  100.0 4.1 %collective-permute-done.12.refs_1_ = bf16[256,2048]{1,0:T(8,128)(2,1)S(1)} collective-permute-done((bf16[256,2048]{1,0:T(8,128)(2,1)S(1)}, bf16[256,2048]{1,0:T(8,128)(2,1)S(1)}, u32[]{:S(2)}, u32[]{:S(2)}) %collective-permute-start.12) | collective-permute-done | bytes 1048608 | tf_op jit(solution)/shard_map/ppermute | solution.py:192
  104.0 1.0 copy-done.16
  105.0 5.0 %shard_map.51 = (f32[512,512]{1,0:T(8,128)S(1)}, bf16[512,512]{1,0:T(8,128)(2,1)}) custom-call(s32[2]{0:T(128)S(1)} %pad_add_fusion.spot, bf16[512,2048]{1,0:T(8,128)(2,1)} %copy-done, bf16[512,1024]{1,0:T(8,128)(2,1)S(1)} %collective-permute-done.3.far, bf16[512,1024]{1,0:T(8,128)(2,1)S(1)} %collective-permute-done.4.rest, ...), custom_call_target="tpu_custom_call" | custom-call | flops 1024 | bytes 1024 | tf_op jit(solution)/shard_map/pallas_call | solution.py:140
  110.1 1.0 copy-done.6
  111.0 4.3 %collective-permute-done.14.refs_0_ = bf16[128,2048]{1,0:T(8,128)(2,1)} collective-permute-done((bf16[128,2048]{1,0:T(8,128)(2,1)}, bf16[128,2048]{1,0:T(8,128)(2,1)}, u32[]{:S(2)}, u32[]{:S(2)}) %collective-permute-start.14) | collective-permute-done | bytes 524320 | tf_op jit(solution)/shard_map/ppermute | solution.py:192
  115.4 11.2 %collective-permute-done.15.refs_1_ = bf16[128,2048]{1,0:T(8,128)(2,1)} collective-permute-done((bf16[128,2048]{1,0:T(8,128)(2,1)}, bf16[128,2048]{1,0:T(8,128)(2,1)}, u32[]{:S(2)}, u32[]{:S(2)}) %collective-permute-start.15) | collective-permute-done | bytes 524320 | tf_op jit(solution)/shard_map/ppermute | solution.py:192
  126.6 1.5 collective-permute-start.10
  128.1 4.2 %shard_map.52 = (f32[512,256]{1,0:T(8,128)S(1)}, bf16[512,256]{1,0:T(8,128)(2,1)S(1)}) custom-call(s32[2]{0:T(128)S(1)} %pad_add_fusion.spot, bf16[512,2048]{1,0:T(8,128)(2,1)} %copy-done, bf16[512,1024]{1,0:T(8,128)(2,1)S(1)} %collective-permute-done.3.far, bf16[512,1024]{1,0:T(8,128)(2,1)S(1)} %collective-permute-done.4.rest, ...), custom_call_target="tpu_custom_call" | custom-call | flops 1024 | bytes 1024 | tf_op jit(solution)/shard_map/pallas_call | solution.py:140
  132.4 0.1 collective-permute-start.16
  132.5 0.2 broadcast_in_dim.3
  132.7 0.9 copy-done.5
  133.6 0.0 copy-done.9
  133.7 0.1 fusion.6
  133.8 0.2 collective-permute-done.16
  134.1 0.6 collective-permute-start.17
  134.7 1.2 convert_element_type.66
  135.9 0.0 copy-start.1
  135.9 0.2 fusion
  136.1 1.6 %collective-permute-start.18 = (bf16[256,512]{1,0:T(8,128)(2,1)S(1)}, bf16[256,512]{1,0:T(8,128)(2,1)S(1)}, u32[]{:S(2)}, u32[]{:S(2)}) collective-permute-start(bf16[256,512]{1,0:T(8,128)(2,1)S(1)} %get-tuple-element.59.refs_1_), channel_id=1, source_target_pairs={{0,2},{2,0},{4,6},{6,4},{8,10},{10,8},{12,14},{14,12},{1,3},{3,1},... | collective-permute-start | bytes 786440 | tf_op jit(solution)/shard_map/ppermute | solution.py:186
  137.7 0.1 fusion.3
  137.9 1.2 shard_map.53
  139.1 0.1 collective-permute-start.20
  139.2 1.5 collective-permute-start.22
  140.7 0.6 collective-permute-start.21
  141.4 5.9 %collective-permute-done.23.block = bf16[128,2048]{1,0:T(8,128)(2,1)S(1)} collective-permute-done((bf16[128,2048]{1,0:T(8,128)(2,1)}, bf16[128,2048]{1,0:T(8,128)(2,1)S(1)}, u32[]{:S(2)}, u32[]{:S(2)}) %collective-permute-start.23) | collective-permute-done | bytes 524320 | tf_op jit(solution)/shard_map/ppermute | solution.py:192
  147.2 0.9 collective-permute-done.21.refs_1_
  148.1 1.2 shard_map.54
  149.4 0.1 collective-permute-start.24
  149.5 0.6 collective-permute-start.26
  150.1 1.5 collective-permute-start.25
  151.8 0.0 copy-start.15
  151.8 1.6 collective-permute-done.26
  153.3 2.0 %collective-permute-done.25 = bf16[256,128]{1,0:T(8,128)(2,1)S(1)} collective-permute-done((bf16[256,128]{1,0:T(8,128)(2,1)S(1)}, bf16[256,128]{1,0:T(8,128)(2,1)S(1)}, u32[]{:S(2)}, u32[]{:S(2)}) %collective-permute-start.25) | collective-permute-done | bytes 65568 | tf_op jit(solution)/shard_map/ppermute | solution.py:186
  155.3 0.7 fusion.12
  (51 shorter events, 0.3 us)
Async XLA Ops:
  0.1 1.6 %copy-start.3 = (bf16[256,4096]{1,0:T(8,128)(2,1)S(1)}, bf16[256,4096]{1,0:T(8,128)(2,1)}, u32[]{:S(2)}) copy-start(bf16[256,4096]{1,0:T(8,128)(2,1)} %query_grads.1) | copy-start | bytes 6291460
  1.7 6.4 %copy-start.10 = (s32[512,128]{1,0:T(8,128)S(1)}, s32[512,128]{1,0:T(8,128)}, u32[]{:S(2)}) copy-start(s32[512,128]{1,0:T(8,128)} %mask.1) | copy-start | bytes 786436
  2.9 28.3 %collective-permute-start = (bf16[256,2048]{1,0:T(8,128)(2,1)S(1)}, bf16[256,2048]{1,0:T(8,128)(2,1)S(1)}, u32[]{:S(2)}, u32[]{:S(2)}) collective-permute-start(bf16[256,2048]{1,0:T(8,128)(2,1)S(1)} %get-tuple-element.35.refs_0_), channel_id=1, source_target_pairs={{0,4},{2,6},{4,8},{6,10},{8,12},{10,14},{12,0},{14,2},{1,5},{3,7},... | collective-permute-start | bytes 3145736 | tf_op jit(solution)/shard_map/ppermute | solution.py:192
  6.0 16.8 %collective-permute-start.1 = (bf16[128,2048]{1,0:T(8,128)(2,1)S(1)}, bf16[128,2048]{1,0:T(8,128)(2,1)S(1)}, u32[]{:S(2)}, u32[]{:S(2)}) collective-permute-start(bf16[128,2048]{1,0:T(8,128)(2,1)S(1)} %get-tuple-element.36), channel_id=1, source_target_pairs={{0,2},{2,0},{4,6},{6,4},{8,10},{10,8},{12,14},{14,12},{1,3},{3,1},... | collective-permute-start | bytes 1572872 | tf_op jit(solution)/shard_map/ppermute | solution.py:186
  7.5 23.1 %collective-permute-start.2 = (bf16[128,2048]{1,0:T(8,128)(2,1)S(1)}, bf16[128,2048]{1,0:T(8,128)(2,1)S(1)}, u32[]{:S(2)}, u32[]{:S(2)}) collective-permute-start(bf16[128,2048]{1,0:T(8,128)(2,1)S(1)} %get-tuple-element.37), channel_id=1, source_target_pairs={{0,2},{2,0},{4,6},{6,4},{8,10},{10,8},{12,14},{14,12},{1,3},{3,1},... | collective-permute-start | bytes 1572872 | tf_op jit(solution)/shard_map/ppermute | solution.py:186
  21.4 1.3 copy-start
  31.2 52.0 %copy-start.2 = (bf16[256,2048]{1,0:T(8,128)(2,1)}, bf16[256,2048]{1,0:T(8,128)(2,1)S(1)}, u32[]{:S(2)}) copy-start(bf16[256,2048]{1,0:T(8,128)(2,1)S(1)} %get-tuple-element.44.refs_0_) | copy-start | bytes 3145732
  31.2 27.9 %collective-permute-start.11 = (bf16[256,2048]{1,0:T(8,128)(2,1)S(1)}, bf16[256,2048]{1,0:T(8,128)(2,1)S(1)}, u32[]{:S(2)}, u32[]{:S(2)}) collective-permute-start(bf16[256,2048]{1,0:T(8,128)(2,1)S(1)} %get-tuple-element.44.refs_0_), channel_id=1, source_target_pairs={{0,4},{2,6},{4,8},{6,10},{8,12},{10,14},{12,0},{14,2},{1,5},{3,7},... | collective-permute-start | bytes 3145736 | tf_op jit(solution)/shard_map/ppermute | solution.py:192
  32.2 26.9 %collective-permute-start.3 = (bf16[512,1024]{1,0:T(8,128)(2,1)S(1)}, bf16[512,1024]{1,0:T(8,128)(2,1)S(1)}, u32[]{:S(2)}, u32[]{:S(2)}) collective-permute-start(bf16[512,1024]{1,0:T(8,128)(2,1)S(1)} %get-tuple-element.38), channel_id=1, source_target_pairs={{0,2},{2,0},{4,6},{6,4},{8,10},{10,8},{12,14},{14,12},{1,3},{3,1},... | collective-permute-start | bytes 3145736 | tf_op jit(solution)/shard_map/ppermute | solution.py:186
  33.7 44.4 %collective-permute-start.4 = (bf16[512,1024]{1,0:T(8,128)(2,1)S(1)}, bf16[512,1024]{1,0:T(8,128)(2,1)S(1)}, u32[]{:S(2)}, u32[]{:S(2)}) collective-permute-start(bf16[512,1024]{1,0:T(8,128)(2,1)S(1)} %get-tuple-element.39), channel_id=1, source_target_pairs={{0,2},{2,0},{4,6},{6,4},{8,10},{10,8},{12,14},{14,12},{1,3},{3,1},... | collective-permute-start | bytes 3145736 | tf_op jit(solution)/shard_map/ppermute | solution.py:186
  34.2 49.0 %collective-permute-start.7 = (bf16[128,2048]{1,0:T(8,128)(2,1)S(1)}, bf16[128,2048]{1,0:T(8,128)(2,1)}, u32[]{:S(2)}, u32[]{:S(2)}) collective-permute-start(bf16[128,2048]{1,0:T(8,128)(2,1)S(1)} %get-tuple-element.40.refs_1_), channel_id=1, source_target_pairs={{0,4},{2,6},{4,8},{6,10},{8,12},{10,14},{12,0},{14,2},{1,5},{3,7},... | collective-permute-start | bytes 1572872 | tf_op jit(solution)/shard_map/ppermute | solution.py:192
  35.8 47.5 %collective-permute-start.8 = (bf16[128,2048]{1,0:T(8,128)(2,1)S(1)}, bf16[128,2048]{1,0:T(8,128)(2,1)}, u32[]{:S(2)}, u32[]{:S(2)}) collective-permute-start(bf16[128,2048]{1,0:T(8,128)(2,1)S(1)} %get-tuple-element.41.refs_2_), channel_id=1, source_target_pairs={{0,4},{2,6},{4,8},{6,10},{8,12},{10,14},{12,0},{14,2},{1,5},{3,7},... | collective-permute-start | bytes 1572872 | tf_op jit(solution)/shard_map/ppermute | solution.py:192
  59.1 44.9 %collective-permute-start.12 = (bf16[256,2048]{1,0:T(8,128)(2,1)S(1)}, bf16[256,2048]{1,0:T(8,128)(2,1)S(1)}, u32[]{:S(2)}, u32[]{:S(2)}) collective-permute-start(bf16[256,2048]{1,0:T(8,128)(2,1)S(1)} %collective-permute-done.11.refs_0_), channel_id=1, source_target_pairs={{0,4},{2,6},{4,8},{6,10},{8,12},{10,14},{12,0},{14,2},{1,5},{3,7},... | collective-permute-start | bytes 3145736 | tf_op jit(solution)/shard_map/ppermute | solution.py:192
  83.2 8.7 %copy-start.4 = (f32[512,512]{1,0:T(8,128)}, f32[512,512]{1,0:T(8,128)S(1)}, u32[]{:S(2)}) copy-start(f32[512,512]{1,0:T(8,128)S(1)} %get-tuple-element.42) | copy-start | bytes 3145732
  83.2 8.5 %collective-permute-start.5 = (bf16[512,512]{1,0:T(8,128)(2,1)S(1)}, bf16[512,512]{1,0:T(8,128)(2,1)S(1)}, u32[]{:S(2)}, u32[]{:S(2)}) collective-permute-start(bf16[512,512]{1,0:T(8,128)(2,1)S(1)} %get-tuple-element.43.refs_3_), channel_id=1, source_target_pairs={{0,1},{1,0},{2,3},{3,2},{4,5},{5,4},{6,7},{7,6},{8,9},{9,8},{10,11... | collective-permute-start | bytes 1572872 | tf_op jit(solution)/shard_map/ppermute | solution.py:189
  89.2 4.3 %collective-permute-start.9 = (bf16[512,512]{1,0:T(8,128)(2,1)S(1)}, bf16[512,512]{1,0:T(8,128)(2,1)S(1)}, u32[]{:S(2)}, u32[]{:S(2)}) collective-permute-start(bf16[512,512]{1,0:T(8,128)(2,1)S(1)} %get-tuple-element.46.refs_2_), channel_id=1, source_target_pairs={{0,1},{1,0},{2,3},{3,2},{4,5},{5,4},{6,7},{7,6},{8,9},{9,8},{10,11... | collective-permute-start | bytes 1572872 | tf_op jit(solution)/shard_map/ppermute | solution.py:189
  89.4 25.9 %collective-permute-start.14 = (bf16[128,2048]{1,0:T(8,128)(2,1)}, bf16[128,2048]{1,0:T(8,128)(2,1)}, u32[]{:S(2)}, u32[]{:S(2)}) collective-permute-start(bf16[128,2048]{1,0:T(8,128)(2,1)} %collective-permute-done.7.refs_1_), channel_id=1, source_target_pairs={{0,4},{2,6},{4,8},{6,10},{8,12},{10,14},{12,0},{14,2},{1,5},{3,7},... | collective-permute-start | bytes 1572872 | tf_op jit(solution)/shard_map/ppermute | solution.py:192
  91.0 35.6 %collective-permute-start.15 = (bf16[128,2048]{1,0:T(8,128)(2,1)}, bf16[128,2048]{1,0:T(8,128)(2,1)}, u32[]{:S(2)}, u32[]{:S(2)}) collective-permute-start(bf16[128,2048]{1,0:T(8,128)(2,1)} %collective-permute-done.8.refs_2_), channel_id=1, source_target_pairs={{0,4},{2,6},{4,8},{6,10},{8,12},{10,14},{12,0},{14,2},{1,5},{3,7},... | collective-permute-start | bytes 1572872 | tf_op jit(solution)/shard_map/ppermute | solution.py:192
  91.8 1.6 %copy-start.13 = (f32[512,512]{1,0:T(8,128)}, f32[512,512]{1,0:T(8,128)S(1)}, u32[]{:S(2)}) copy-start(f32[512,512]{1,0:T(8,128)S(1)} %convert_element_type.60) | copy-start | bytes 3145732
  91.9 8.0 %collective-permute-start.6 = (bf16[256,512]{1,0:T(8,128)(2,1)S(1)}, bf16[256,512]{1,0:T(8,128)(2,1)S(1)}, u32[]{:S(2)}, u32[]{:S(2)}) collective-permute-start(bf16[256,512]{1,0:T(8,128)(2,1)S(1)} %fusion.4), channel_id=1, source_target_pairs={{0,2},{2,0},{4,6},{6,4},{8,10},{10,8},{12,14},{14,12},{1,3},{3,1},... | collective-permute-start | bytes 786440 | tf_op jit(solution)/shard_map/ppermute | solution.py:186
  93.6 16.5 %copy-start.11 = (f32[512,512]{1,0:T(8,128)}, f32[512,512]{1,0:T(8,128)S(1)}, u32[]{:S(2)}) copy-start(f32[512,512]{1,0:T(8,128)S(1)} %convert_element_type.63) | copy-start | bytes 3145732
  100.0 10.1 %copy-start.8 = (bf16[256,512]{1,0:T(8,128)(2,1)}, bf16[256,512]{1,0:T(8,128)(2,1)S(1)}, u32[]{:S(2)}) copy-start(bf16[256,512]{1,0:T(8,128)(2,1)S(1)} %collective-permute-done.6.refs_3_) | copy-start | bytes 786436
  104.0 1.0 copy-start.16
  110.1 1.0 copy-start.6
  111.0 23.6 %collective-permute-start.13 = (bf16[512,512]{1,0:T(8,128)(2,1)}, bf16[512,512]{1,0:T(8,128)(2,1)}, u32[]{:S(2)}, u32[]{:S(2)}) collective-permute-start(bf16[512,512]{1,0:T(8,128)(2,1)} %get-tuple-element.48.refs_2_), channel_id=1, source_target_pairs={{0,1},{1,0},{2,3},{3,2},{4,5},{5,4},{6,7},{7,6},{8,9},{9,8},{10,11... | collective-permute-start | bytes 1572872 | tf_op jit(solution)/shard_map/ppermute | solution.py:189
  115.4 22.5 %collective-permute-start.19 = (bf16[128,2048]{1,0:T(8,128)(2,1)}, bf16[128,2048]{1,0:T(8,128)(2,1)S(1)}, u32[]{:S(2)}, u32[]{:S(2)}) collective-permute-start(bf16[128,2048]{1,0:T(8,128)(2,1)} %collective-permute-done.14.refs_0_), channel_id=1, source_target_pairs={{0,4},{2,6},{4,8},{6,10},{8,12},{10,14},{12,0},{14,2},{1,5},{3,7},... | collective-permute-start | bytes 1572872 | tf_op jit(solution)/shard_map/ppermute | solution.py:192
  126.6 20.6 %collective-permute-start.23 = (bf16[128,2048]{1,0:T(8,128)(2,1)}, bf16[128,2048]{1,0:T(8,128)(2,1)S(1)}, u32[]{:S(2)}, u32[]{:S(2)}) collective-permute-start(bf16[128,2048]{1,0:T(8,128)(2,1)} %collective-permute-done.15.refs_1_), channel_id=1, source_target_pairs={{0,4},{2,6},{4,8},{6,10},{8,12},{10,14},{12,0},{14,2},{1,5},{3,7},... | collective-permute-start | bytes 1572872 | tf_op jit(solution)/shard_map/ppermute | solution.py:192
  126.6 11.1 %collective-permute-start.10 = (bf16[256,512]{1,0:T(8,128)(2,1)S(1)}, bf16[256,512]{1,0:T(8,128)(2,1)S(1)}, u32[]{:S(2)}, u32[]{:S(2)}) collective-permute-start(bf16[256,512]{1,0:T(8,128)(2,1)S(1)} %fusion.1.refs_4_), channel_id=1, source_target_pairs={{0,2},{2,0},{4,6},{6,4},{8,10},{10,8},{12,14},{14,12},{1,3},{3,1},... | collective-permute-start | bytes 786440 | tf_op jit(solution)/shard_map/ppermute | solution.py:186
  128.1 4.6 %copy-start.14 = (f32[512,512]{1,0:T(8,128)S(1)}, f32[512,512]{1,0:T(8,128)}, u32[]{:S(2)}) copy-start(f32[512,512]{1,0:T(8,128)} %copy-done.13) | copy-start | bytes 3145732
  132.4 1.2 copy-start.5
  132.4 1.3 copy-start.9
  132.4 1.6 %collective-permute-start.16 = (bf16[512,256]{1,0:T(8,128)(2,1)S(1)}, bf16[512,256]{1,0:T(8,128)(2,1)S(1)}, u32[]{:S(2)}, u32[]{:S(2)}) collective-permute-start(bf16[512,256]{1,0:T(8,128)(2,1)S(1)} %get-tuple-element.50.refs_0_), channel_id=1, source_target_pairs={{0,1},{1,0},{2,3},{3,2},{4,5},{5,4},{6,7},{7,6},{8,9},{9,8},{10,11... | collective-permute-start | bytes 786440 | tf_op jit(solution)/shard_map/ppermute | solution.py:189
  133.7 2.2 %copy-start.7 = (f32[512,512]{1,0:T(8,128)S(1)}, f32[512,512]{1,0:T(8,128)}, u32[]{:S(2)}) copy-start(f32[512,512]{1,0:T(8,128)} %copy-done.6) | copy-start | bytes 3145732
  134.1 3.6 %copy-start.12 = (f32[512,512]{1,0:T(8,128)S(1)}, f32[512,512]{1,0:T(8,128)}, u32[]{:S(2)}) copy-start(f32[512,512]{1,0:T(8,128)} %copy-done.11) | copy-start | bytes 3145732
  134.1 6.6 %collective-permute-start.17 = (bf16[256,256]{1,0:T(8,128)(2,1)S(1)}, bf16[256,256]{1,0:T(8,128)(2,1)S(1)}, u32[]{:S(2)}, u32[]{:S(2)}) collective-permute-start(bf16[256,256]{1,0:T(8,128)(2,1)S(1)} %fusion.9), channel_id=1, source_target_pairs={{0,2},{2,0},{4,6},{6,4},{8,10},{10,8},{12,14},{14,12},{1,3},{3,1},... | collective-permute-start | bytes 393224 | tf_op jit(solution)/shard_map/ppermute | solution.py:186
  135.9 2.0 %copy-start.1 = (bf16[512,2048]{1,0:T(8,128)(2,1)S(1)}, bf16[512,2048]{1,0:T(8,128)(2,1)}, u32[]{:S(2)}) copy-start(bf16[512,2048]{1,0:T(8,128)(2,1)} %copy-done) | copy-start | bytes 6291460
  136.1 15.5 %collective-permute-start.18 = (bf16[256,512]{1,0:T(8,128)(2,1)S(1)}, bf16[256,512]{1,0:T(8,128)(2,1)S(1)}, u32[]{:S(2)}, u32[]{:S(2)}) collective-permute-start(bf16[256,512]{1,0:T(8,128)(2,1)S(1)} %get-tuple-element.59.refs_1_), channel_id=1, source_target_pairs={{0,2},{2,0},{4,6},{6,4},{8,10},{10,8},{12,14},{14,12},{1,3},{3,1},... | collective-permute-start | bytes 786440 | tf_op jit(solution)/shard_map/ppermute | solution.py:186
  139.1 12.6 %collective-permute-start.20 = (bf16[256,128]{1,0:T(8,128)(2,1)S(1)}, bf16[256,128]{1,0:T(8,128)(2,1)S(1)}, u32[]{:S(2)}, u32[]{:S(2)}) collective-permute-start(bf16[256,128]{1,0:T(8,128)(2,1)S(1)} %get-tuple-element.52), channel_id=1, source_target_pairs={{0,1},{1,0},{2,3},{3,2},{4,5},{5,4},{6,7},{7,6},{8,9},{9,8},{10,11... | collective-permute-start | bytes 196616 | tf_op jit(solution)/shard_map/ppermute | solution.py:189
  139.2 8.0 %collective-permute-start.22 = (bf16[256,128]{1,0:T(8,128)(2,1)S(1)}, bf16[256,128]{1,0:T(8,128)(2,1)S(1)}, u32[]{:S(2)}, u32[]{:S(2)}) collective-permute-start(bf16[256,128]{1,0:T(8,128)(2,1)S(1)} %get-tuple-element.54), channel_id=1, source_target_pairs={{0,3},{1,2},{2,1},{3,0},{4,7},{5,6},{6,5},{7,4},{8,11},{9,10},{10,... | collective-permute-start | bytes 196616 | tf_op jit(solution)/shard_map/ppermute | solution.py:195
  140.7 7.4 %collective-permute-start.21 = (bf16[256,128]{1,0:T(8,128)(2,1)S(1)}, bf16[256,128]{1,0:T(8,128)(2,1)S(1)}, u32[]{:S(2)}, u32[]{:S(2)}) collective-permute-start(bf16[256,128]{1,0:T(8,128)(2,1)S(1)} %get-tuple-element.53), channel_id=1, source_target_pairs={{0,2},{2,0},{4,6},{6,4},{8,10},{10,8},{12,14},{14,12},{1,3},{3,1},... | collective-permute-start | bytes 196616 | tf_op jit(solution)/shard_map/ppermute | solution.py:186
  149.4 2.4 %collective-permute-start.24 = (bf16[256,128]{1,0:T(8,128)(2,1)S(1)}, bf16[256,128]{1,0:T(8,128)(2,1)S(1)}, u32[]{:S(2)}, u32[]{:S(2)}) collective-permute-start(bf16[256,128]{1,0:T(8,128)(2,1)S(1)} %get-tuple-element.56), channel_id=1, source_target_pairs={{0,1},{1,0},{2,3},{3,2},{4,5},{5,4},{6,7},{7,6},{8,9},{9,8},{10,11... | collective-permute-start | bytes 196616 | tf_op jit(solution)/shard_map/ppermute | solution.py:189
  149.5 3.9 %collective-permute-start.26 = (bf16[256,128]{1,0:T(8,128)(2,1)S(1)}, bf16[256,128]{1,0:T(8,128)(2,1)S(1)}, u32[]{:S(2)}, u32[]{:S(2)}) collective-permute-start(bf16[256,128]{1,0:T(8,128)(2,1)S(1)} %get-tuple-element.58), channel_id=1, source_target_pairs={{0,3},{1,2},{2,1},{3,0},{4,7},{5,6},{6,5},{7,4},{8,11},{9,10},{10,... | collective-permute-start | bytes 196616 | tf_op jit(solution)/shard_map/ppermute | solution.py:195
  150.1 5.2 %collective-permute-start.25 = (bf16[256,128]{1,0:T(8,128)(2,1)S(1)}, bf16[256,128]{1,0:T(8,128)(2,1)S(1)}, u32[]{:S(2)}, u32[]{:S(2)}) collective-permute-start(bf16[256,128]{1,0:T(8,128)(2,1)S(1)} %get-tuple-element.57), channel_id=1, source_target_pairs={{0,2},{2,0},{4,6},{6,4},{8,10},{10,8},{12,14},{14,12},{1,3},{3,1},... | collective-permute-start | bytes 196616 | tf_op jit(solution)/shard_map/ppermute | solution.py:186
  151.8 3.5 %copy-start.15 = (f32[256,2048]{1,0:T(8,128)}, f32[256,2048]{1,0:T(8,128)S(1)}, u32[]{:S(2)}) copy-start(f32[256,2048]{1,0:T(8,128)S(1)} %add_dynamic-update-slice_fusion) | copy-start | bytes 6291460

commit v16 on v15

--- a/solution.py
+++ b/solution.py
@@ -21,18 +21,27 @@
     return jax.ShapeDtypeStruct(shape, kind)
 
 
-def prepare_body(spot, query_grads, mine, *sending):
+def prepare_body(spot, query_grads, mine, first, second, low, high, sems):
     rank = LANES // 2
     rows, width = query_grads.shape
-    for outs, side in (((mine,), spot[0]), (sending, 1 - spot[0])):
-        for m in range(width // 4 // LANES):
-            at = pl.multiple_of(side * (width // 4) + m * LANES, LANES)
-            low = query_grads[:, pl.ds(at, LANES)]
-            high = query_grads[:, pl.ds(at + width // 2, LANES)]
-            even = jnp.concatenate([low[:, :rank], high[:, :rank]], 1)
-            odd = jnp.concatenate([low[:, rank:], high[:, rank:]], 1)
-            for i, out in enumerate(outs):
-                cut = slice(i * out.shape[0], (i + 1) * out.shape[0])
+    quarter = width // 4
+    copies = []
+    for i in range(2):
+        side = spot[0] if i == 0 else 1 - spot[0]
+        for j, buffer in enumerate((low, high)):
+            at = pl.ds(pl.multiple_of(side * quarter + j * (width // 2), LANES), quarter)
+            copies.append(pltpu.make_async_copy(query_grads.at[:, at], buffer.at[i], sems.at[i, j]))
+            copies[-1].start()
+    for i, outs in enumerate(((mine,), (first, second))):
+        copies[2 * i].wait()
+        copies[2 * i + 1].wait()
+        for m in range(quarter // LANES):
+            at = slice(m * LANES, (m + 1) * LANES)
+            lower, upper = low[i, :, at], high[i, :, at]
+            even = jnp.concatenate([lower[:, :rank], upper[:, :rank]], 1)
+            odd = jnp.concatenate([lower[:, rank:], upper[:, rank:]], 1)
+            for n, out in enumerate(outs):
+                cut = slice(n * out.shape[0], (n + 1) * out.shape[0])
                 out[:, 2 * m * LANES:(2 * m + 1) * LANES] = even[cut, :]
                 out[:, (2 * m + 1) * LANES:(2 * m + 2) * LANES] = odd[cut, :]
 
@@ -41,10 +50,11 @@
     rows, width = query_grads.shape
     return pl.pallas_call(
         prepare_body,
-        in_specs=[SCALARS, WHOLE],
+        in_specs=[SCALARS, ANYWHERE],
         out_specs=[WHOLE] * 3,
         out_shape=[shaped(bf16, size, width // 2) for size in (rows, rows // 2, rows // 2)],
-        compiler_params=LIMIT,
+        scratch_shapes=[pltpu.VMEM((2, rows, width // 4), bf16)] * 2 + [pltpu.SemaphoreType.DMA((2, 2))],
+        compiler_params=pltpu.CompilerParams(vmem_limit_bytes=60 * 1024 * 1024),
     )(spot, query_grads)
 
 

time: 156 us -> 158 us (1.013)
  Pallas kernels: 37.3 us -> 39.8 us
  local copies, waits for them, and re-layouts: 6.08 us -> 4.47 us
    pallas_call x1, Pallas kernels: 1.26 us -> 3.75 us  [prepare(): pl.pallas_call(prepare_body, in_specs=[SCALARS, ANYWHERE], out_specs=[WHO...]
    unnamed x34 -> x36, local copies, waits for them, and re-layouts: 5.85 us -> 4.24 us
where the time goes in v16:
time: 158 us
  waiting for transfers between devices  87 us (55%)
  Pallas kernels  39.8 us (25%)
  starting transfers between devices  22.4 us (14%)
  local copies, waits for them, and re-layouts  4.47 us (3%)
  other arithmetic  3.61 us (2%)
    ppermute x9, waiting for transfers between devices, pass_on(): return lax.ppermute(x, 'blk', onward)  48.9 us
    ppermute x10, waiting for transfers between devices, swap_across(): return lax.ppermute(x, 'blk', across)  36.3 us
    pallas_call x4, Pallas kernels, score(): pl.pallas_call(functools.partial(score_body, count), in_specs=[SCALARS] +...  20.2 us
    pallas_call x1, Pallas kernels, form(): pl.pallas_call(functools.partial(form_body, rows, rank), grid_spec=pltpu....  13.4 us
    ppermute x10, starting transfers between devices, swap_across(): return lax.ppermute(x, 'blk', across)  11.3 us
    ppermute x9, starting transfers between devices, pass_on(): return lax.ppermute(x, 'blk', onward)  8.34 us
    unnamed x36, local copies, waits for them, and re-layouts  4.24 us
    pallas_call x1, Pallas kernels, prepare(): pl.pallas_call(prepare_body, in_specs=[SCALARS, ANYWHERE], out_specs=[WHO...  3.75 us
  transfers between devices with their start and end apart: 27, of which 13 were waited for; matrix products, arithmetic and copies ran while one was open for 2% of the time, Pallas kernels for 23%

profile of v16, /device:TPU:0, one launch (start us, length us, event | category | flops | bytes accessed | tf_op | source)
XLA Modules:
  0.0 157.6 jit_solution(9613391659679765597)
XLA Ops:
  0.0 0.6 pad_add_fusion.spot
  0.6 3.7 %shard_map.47 = (bf16[256,2048]{1,0:T(8,128)(2,1)}, bf16[128,2048]{1,0:T(8,128)(2,1)}, bf16[128,2048]{1,0:T(8,128)(2,1)}) custom-call(s32[2]{0:T(128)} %pad_add_fusion.spot, bf16[256,4096]{1,0:T(8,128)(2,1)} %query_grads.1), custom_call_target="tpu_custom_call" | custom-call | tf_op jit(solution)/shard_map/pallas_call | solution.py:51
  4.4 3.1 %collective-permute-start = (bf16[256,2048]{1,0:T(8,128)(2,1)}, bf16[256,2048]{1,0:T(8,128)(2,1)S(1)}, u32[]{:S(2)}, u32[]{:S(2)}) collective-permute-start(bf16[256,2048]{1,0:T(8,128)(2,1)} %get-tuple-element.35.refs_0_), channel_id=1, source_target_pairs={{0,4},{2,6},{4,8},{6,10},{8,12},{10,14},{12,0},{14,2},{1,5},{3,7},... | collective-permute-start | bytes 3145736 | tf_op jit(solution)/shard_map/ppermute | solution.py:202
  7.4 1.5 collective-permute-start.1
  9.0 0.5 collective-permute-start.2
  9.5 13.4 %shard_map.46 = (bf16[512,2048]{1,0:T(8,128)(2,1)S(1)}, bf16[512,1024]{1,0:T(8,128)(2,1)S(1)}, bf16[512,1024]{1,0:T(8,128)(2,1)S(1)}) custom-call(s32[2]{0:T(128)S(1)} %copy-done.10, bf16[512,64,128]{2,1,0:T(8,128)(2,1)} %bitcast.4, bf16[512,64,128]{2,1,0:T(8,128)(2,1)} %bitcast.5, s32[512,128]{1,0:T(8,128)S(1)} %copy-done.11), custom_call_target="tpu_custom_call" | custom-call | flops 10737418240 | bytes 20971520 | tf_op jit(solution)/shard_map/pallas_call | solution.py:84
  22.9 0.0 copy-start
  22.9 1.3 copy-done
  24.2 8.1 %collective-permute-done.2.refs_4_ = bf16[128,2048]{1,0:T(8,128)(2,1)S(1)} collective-permute-done((bf16[128,2048]{1,0:T(8,128)(2,1)}, bf16[128,2048]{1,0:T(8,128)(2,1)S(1)}, u32[]{:S(2)}, u32[]{:S(2)}) %collective-permute-start.2) | collective-permute-done | bytes 524320 | tf_op jit(solution)/shard_map/ppermute | solution.py:196
  32.3 0.6 collective-permute-done.refs_2_
  32.8 1.1 collective-permute-start.11
  33.9 1.5 collective-permute-start.3
  35.4 0.5 collective-permute-start.4
  35.9 1.6 collective-permute-start.7
  37.5 0.4 collective-permute-start.8
  37.9 22.9 %collective-permute-done.11.refs_0_ = bf16[256,2048]{1,0:T(8,128)(2,1)S(1)} collective-permute-done((bf16[256,2048]{1,0:T(8,128)(2,1)S(1)}, bf16[256,2048]{1,0:T(8,128)(2,1)S(1)}, u32[]{:S(2)}, u32[]{:S(2)}) %collective-permute-start.11) | collective-permute-done | bytes 1048608 | tf_op jit(solution)/shard_map/ppermute | solution.py:202
  60.7 19.1 %collective-permute-done.4.rest = bf16[512,1024]{1,0:T(8,128)(2,1)S(1)} collective-permute-done((bf16[512,1024]{1,0:T(8,128)(2,1)S(1)}, bf16[512,1024]{1,0:T(8,128)(2,1)S(1)}, u32[]{:S(2)}, u32[]{:S(2)}) %collective-permute-start.4) | collective-permute-done | bytes 1048608 | tf_op jit(solution)/shard_map/ppermute | solution.py:196
  79.8 5.0 %shard_map.49 = (f32[512,512]{1,0:T(8,128)S(1)}, bf16[512,512]{1,0:T(8,128)(2,1)S(1)}) custom-call(s32[2]{0:T(128)S(1)} %copy-done.10, bf16[512,2048]{1,0:T(8,128)(2,1)} %copy-done, bf16[512,1024]{1,0:T(8,128)(2,1)S(1)} %collective-permute-done.3.far, bf16[512,1024]{1,0:T(8,128)(2,1)S(1)} %collective-permute-done.4.rest, bf16[256,2048]{1,0:T(8,128)(2,1)S(1)} %copy-done.3, ...), custom_call_target="tpu_custom_call" | custom-call | flops 1024 | bytes 1024 | tf_op jit(solution)/shard_map/pallas_call | solution.py:150
  84.9 0.1 collective-permute-start.5
  85.0 5.9 %shard_map.50 = (f32[512,512]{1,0:T(8,128)S(1)}, bf16[512,512]{1,0:T(8,128)(2,1)S(1)}) custom-call(s32[2]{0:T(128)S(1)} %copy-done.10, bf16[512,2048]{1,0:T(8,128)(2,1)} %copy-done, bf16[512,1024]{1,0:T(8,128)(2,1)S(1)} %collective-permute-done.3.far, bf16[512,1024]{1,0:T(8,128)(2,1)S(1)} %collective-permute-done.4.rest, bf16[256,2048]{1,0:T(8,128)(2,1)} %copy-done.2, ...), custom_call_target="tpu_custom_call" | custom-call | flops 1024 | bytes 1024 | tf_op jit(solution)/shard_map/pallas_call | solution.py:150
  90.8 0.3 collective-permute-start.9
  91.1 1.6 %collective-permute-start.14 = (bf16[128,2048]{1,0:T(8,128)(2,1)}, bf16[128,2048]{1,0:T(8,128)(2,1)}, u32[]{:S(2)}, u32[]{:S(2)}) collective-permute-start(bf16[128,2048]{1,0:T(8,128)(2,1)} %collective-permute-done.7.refs_1_), channel_id=1, source_target_pairs={{0,4},{2,6},{4,8},{6,10},{8,12},{10,14},{12,0},{14,2},{1,5},{3,7},... | collective-permute-start | bytes 1572872 | tf_op jit(solution)/shard_map/ppermute | solution.py:202
  92.7 0.7 collective-permute-start.15
  93.4 0.1 convert_element_type.60
  93.5 0.1 fusion.4
  93.6 1.4 collective-permute-start.6
  95.1 0.1 convert_element_type.63
  95.2 0.1 fusion.1.refs_4_
  95.3 6.3 %collective-permute-done.6.refs_3_ = bf16[256,512]{1,0:T(8,128)(2,1)S(1)} collective-permute-done((bf16[256,512]{1,0:T(8,128)(2,1)S(1)}, bf16[256,512]{1,0:T(8,128)(2,1)S(1)}, u32[]{:S(2)}, u32[]{:S(2)}) %collective-permute-start.6) | collective-permute-done | bytes 262176 | tf_op jit(solution)/shard_map/ppermute | solution.py:196
  101.7 4.0 %collective-permute-done.12.refs_1_ = bf16[256,2048]{1,0:T(8,128)(2,1)S(1)} collective-permute-done((bf16[256,2048]{1,0:T(8,128)(2,1)S(1)}, bf16[256,2048]{1,0:T(8,128)(2,1)S(1)}, u32[]{:S(2)}, u32[]{:S(2)}) %collective-permute-start.12) | collective-permute-done | bytes 1048608 | tf_op jit(solution)/shard_map/ppermute | solution.py:202
  105.7 1.0 copy-done.17
  106.6 5.0 %shard_map.51 = (f32[512,512]{1,0:T(8,128)S(1)}, bf16[512,512]{1,0:T(8,128)(2,1)}) custom-call(s32[2]{0:T(128)S(1)} %copy-done.10, bf16[512,2048]{1,0:T(8,128)(2,1)} %copy-done, bf16[512,1024]{1,0:T(8,128)(2,1)S(1)} %collective-permute-done.3.far, bf16[512,1024]{1,0:T(8,128)(2,1)S(1)} %collective-permute-done.4.rest, ...), custom_call_target="tpu_custom_call" | custom-call | flops 1024 | bytes 1024 | tf_op jit(solution)/shard_map/pallas_call | solution.py:150
  111.7 1.0 copy-done.6
  112.6 4.4 %collective-permute-done.14.refs_0_ = bf16[128,2048]{1,0:T(8,128)(2,1)} collective-permute-done((bf16[128,2048]{1,0:T(8,128)(2,1)}, bf16[128,2048]{1,0:T(8,128)(2,1)}, u32[]{:S(2)}, u32[]{:S(2)}) %collective-permute-start.14) | collective-permute-done | bytes 524320 | tf_op jit(solution)/shard_map/ppermute | solution.py:202
  117.0 11.2 %collective-permute-done.15.refs_1_ = bf16[128,2048]{1,0:T(8,128)(2,1)} collective-permute-done((bf16[128,2048]{1,0:T(8,128)(2,1)}, bf16[128,2048]{1,0:T(8,128)(2,1)}, u32[]{:S(2)}, u32[]{:S(2)}) %collective-permute-start.15) | collective-permute-done | bytes 524320 | tf_op jit(solution)/shard_map/ppermute | solution.py:202
  128.2 0.0 collective-permute-start.23
  128.2 1.5 collective-permute-start.10
  129.8 4.2 %shard_map.52 = (f32[512,256]{1,0:T(8,128)S(1)}, bf16[512,256]{1,0:T(8,128)(2,1)S(1)}) custom-call(s32[2]{0:T(128)S(1)} %copy-done.10, bf16[512,2048]{1,0:T(8,128)(2,1)} %copy-done, bf16[512,1024]{1,0:T(8,128)(2,1)S(1)} %collective-permute-done.3.far, bf16[512,1024]{1,0:T(8,128)(2,1)S(1)} %collective-permute-done.4.rest, ...), custom_call_target="tpu_custom_call" | custom-call | flops 1024 | bytes 1024 | tf_op jit(solution)/shard_map/pallas_call | solution.py:150
  134.0 0.1 collective-permute-start.16
  134.1 0.2 broadcast_in_dim.3
  134.4 0.9 copy-done.5
  135.3 0.0 copy-done.9
  135.3 0.1 fusion.6
  135.4 0.2 collective-permute-done.16
  135.7 0.6 collective-permute-start.17
  136.3 1.2 convert_element_type.66
  137.5 0.0 copy-start.1
  137.5 0.2 fusion
  137.7 1.6 %collective-permute-start.18 = (bf16[256,512]{1,0:T(8,128)(2,1)S(1)}, bf16[256,512]{1,0:T(8,128)(2,1)S(1)}, u32[]{:S(2)}, u32[]{:S(2)}) collective-permute-start(bf16[256,512]{1,0:T(8,128)(2,1)S(1)} %get-tuple-element.59.refs_1_), channel_id=1, source_target_pairs={{0,2},{2,0},{4,6},{6,4},{8,10},{10,8},{12,14},{14,12},{1,3},{3,1},... | collective-permute-start | bytes 786440 | tf_op jit(solution)/shard_map/ppermute | solution.py:196
  139.3 0.1 fusion.3
  139.5 1.2 shard_map.53
  140.7 0.1 collective-permute-start.20
  140.8 1.5 collective-permute-start.22
  142.3 0.6 collective-permute-start.21
  143.0 5.9 %collective-permute-done.23.block = bf16[128,2048]{1,0:T(8,128)(2,1)S(1)} collective-permute-done((bf16[128,2048]{1,0:T(8,128)(2,1)}, bf16[128,2048]{1,0:T(8,128)(2,1)S(1)}, u32[]{:S(2)}, u32[]{:S(2)}) %collective-permute-start.23) | collective-permute-done | bytes 524320 | tf_op jit(solution)/shard_map/ppermute | solution.py:202
  148.9 0.9 collective-permute-done.21.refs_1_
  149.8 1.2 shard_map.54
  151.0 0.1 collective-permute-start.24
  151.1 0.6 collective-permute-start.26
  151.7 1.5 collective-permute-start.25
  153.4 0.0 copy-start.16
  153.4 1.6 collective-permute-done.26
  155.0 2.0 %collective-permute-done.25 = bf16[256,128]{1,0:T(8,128)(2,1)S(1)} collective-permute-done((bf16[256,128]{1,0:T(8,128)(2,1)S(1)}, bf16[256,128]{1,0:T(8,128)(2,1)S(1)}, u32[]{:S(2)}, u32[]{:S(2)}) %collective-permute-start.25) | collective-permute-done | bytes 65568 | tf_op jit(solution)/shard_map/ppermute | solution.py:196
  157.0 0.7 fusion.12
  (53 shorter events, 0.3 us)
Async XLA Ops:
  0.0 9.5 %copy-start.11 = (s32[512,128]{1,0:T(8,128)S(1)}, s32[512,128]{1,0:T(8,128)}, u32[]{:S(2)}) copy-start(s32[512,128]{1,0:T(8,128)} %mask.1) | copy-start | bytes 786436
  0.6 8.9 %copy-start.10 = (s32[2]{0:T(128)S(1)}, s32[2]{0:T(128)}, u32[]{:S(2)}) copy-start(s32[2]{0:T(128)} %pad_add_fusion.spot) | copy-start | bytes 28
  4.4 28.5 %collective-permute-start = (bf16[256,2048]{1,0:T(8,128)(2,1)}, bf16[256,2048]{1,0:T(8,128)(2,1)S(1)}, u32[]{:S(2)}, u32[]{:S(2)}) collective-permute-start(bf16[256,2048]{1,0:T(8,128)(2,1)} %get-tuple-element.35.refs_0_), channel_id=1, source_target_pairs={{0,4},{2,6},{4,8},{6,10},{8,12},{10,14},{12,0},{14,2},{1,5},{3,7},... | collective-permute-start | bytes 3145736 | tf_op jit(solution)/shard_map/ppermute | solution.py:202
  7.4 16.8 %collective-permute-start.1 = (bf16[128,2048]{1,0:T(8,128)(2,1)}, bf16[128,2048]{1,0:T(8,128)(2,1)S(1)}, u32[]{:S(2)}, u32[]{:S(2)}) collective-permute-start(bf16[128,2048]{1,0:T(8,128)(2,1)} %get-tuple-element.36), channel_id=1, source_target_pairs={{0,2},{2,0},{4,6},{6,4},{8,10},{10,8},{12,14},{14,12},{1,3},{3,1},... | collective-permute-start | bytes 1572872 | tf_op jit(solution)/shard_map/ppermute | solution.py:196
  9.0 23.3 %collective-permute-start.2 = (bf16[128,2048]{1,0:T(8,128)(2,1)}, bf16[128,2048]{1,0:T(8,128)(2,1)S(1)}, u32[]{:S(2)}, u32[]{:S(2)}) collective-permute-start(bf16[128,2048]{1,0:T(8,128)(2,1)} %get-tuple-element.37), channel_id=1, source_target_pairs={{0,2},{2,0},{4,6},{6,4},{8,10},{10,8},{12,14},{14,12},{1,3},{3,1},... | collective-permute-start | bytes 1572872 | tf_op jit(solution)/shard_map/ppermute | solution.py:196
  22.9 1.3 copy-start
  32.8 47.0 %copy-start.3 = (bf16[256,2048]{1,0:T(8,128)(2,1)S(1)}, bf16[256,2048]{1,0:T(8,128)(2,1)}, u32[]{:S(2)}) copy-start(bf16[256,2048]{1,0:T(8,128)(2,1)} %get-tuple-element.35.refs_0_) | copy-start | bytes 3145732
  32.8 52.0 %copy-start.2 = (bf16[256,2048]{1,0:T(8,128)(2,1)}, bf16[256,2048]{1,0:T(8,128)(2,1)S(1)}, u32[]{:S(2)}) copy-start(bf16[256,2048]{1,0:T(8,128)(2,1)S(1)} %get-tuple-element.44.refs_0_) | copy-start | bytes 3145732
  32.8 27.9 %collective-permute-start.11 = (bf16[256,2048]{1,0:T(8,128)(2,1)S(1)}, bf16[256,2048]{1,0:T(8,128)(2,1)S(1)}, u32[]{:S(2)}, u32[]{:S(2)}) collective-permute-start(bf16[256,2048]{1,0:T(8,128)(2,1)S(1)} %get-tuple-element.44.refs_0_), channel_id=1, source_target_pairs={{0,4},{2,6},{4,8},{6,10},{8,12},{10,14},{12,0},{14,2},{1,5},{3,7},... | collective-permute-start | bytes 3145736 | tf_op jit(solution)/shard_map/ppermute | solution.py:202
  33.9 26.8 %collective-permute-start.3 = (bf16[512,1024]{1,0:T(8,128)(2,1)S(1)}, bf16[512,1024]{1,0:T(8,128)(2,1)S(1)}, u32[]{:S(2)}, u32[]{:S(2)}) collective-permute-start(bf16[512,1024]{1,0:T(8,128)(2,1)S(1)} %get-tuple-element.38), channel_id=1, source_target_pairs={{0,2},{2,0},{4,6},{6,4},{8,10},{10,8},{12,14},{14,12},{1,3},{3,1},... | collective-permute-start | bytes 3145736 | tf_op jit(solution)/shard_map/ppermute | solution.py:196
  35.4 44.4 %collective-permute-start.4 = (bf16[512,1024]{1,0:T(8,128)(2,1)S(1)}, bf16[512,1024]{1,0:T(8,128)(2,1)S(1)}, u32[]{:S(2)}, u32[]{:S(2)}) collective-permute-start(bf16[512,1024]{1,0:T(8,128)(2,1)S(1)} %get-tuple-element.39), channel_id=1, source_target_pairs={{0,2},{2,0},{4,6},{6,4},{8,10},{10,8},{12,14},{14,12},{1,3},{3,1},... | collective-permute-start | bytes 3145736 | tf_op jit(solution)/shard_map/ppermute | solution.py:196
  35.9 49.0 %collective-permute-start.7 = (bf16[128,2048]{1,0:T(8,128)(2,1)S(1)}, bf16[128,2048]{1,0:T(8,128)(2,1)}, u32[]{:S(2)}, u32[]{:S(2)}) collective-permute-start(bf16[128,2048]{1,0:T(8,128)(2,1)S(1)} %get-tuple-element.40.refs_1_), channel_id=1, source_target_pairs={{0,4},{2,6},{4,8},{6,10},{8,12},{10,14},{12,0},{14,2},{1,5},{3,7},... | collective-permute-start | bytes 1572872 | tf_op jit(solution)/shard_map/ppermute | solution.py:202
  37.5 47.5 %collective-permute-start.8 = (bf16[128,2048]{1,0:T(8,128)(2,1)S(1)}, bf16[128,2048]{1,0:T(8,128)(2,1)}, u32[]{:S(2)}, u32[]{:S(2)}) collective-permute-start(bf16[128,2048]{1,0:T(8,128)(2,1)S(1)} %get-tuple-element.41.refs_2_), channel_id=1, source_target_pairs={{0,4},{2,6},{4,8},{6,10},{8,12},{10,14},{12,0},{14,2},{1,5},{3,7},... | collective-permute-start | bytes 1572872 | tf_op jit(solution)/shard_map/ppermute | solution.py:202
  60.7 44.9 %collective-permute-start.12 = (bf16[256,2048]{1,0:T(8,128)(2,1)S(1)}, bf16[256,2048]{1,0:T(8,128)(2,1)S(1)}, u32[]{:S(2)}, u32[]{:S(2)}) collective-permute-start(bf16[256,2048]{1,0:T(8,128)(2,1)S(1)} %collective-permute-done.11.refs_0_), channel_id=1, source_target_pairs={{0,4},{2,6},{4,8},{6,10},{8,12},{10,14},{12,0},{14,2},{1,5},{3,7},... | collective-permute-start | bytes 3145736 | tf_op jit(solution)/shard_map/ppermute | solution.py:202
  84.9 8.7 %copy-start.4 = (f32[512,512]{1,0:T(8,128)}, f32[512,512]{1,0:T(8,128)S(1)}, u32[]{:S(2)}) copy-start(f32[512,512]{1,0:T(8,128)S(1)} %get-tuple-element.42) | copy-start | bytes 3145732
  84.9 8.5 %collective-permute-start.5 = (bf16[512,512]{1,0:T(8,128)(2,1)S(1)}, bf16[512,512]{1,0:T(8,128)(2,1)S(1)}, u32[]{:S(2)}, u32[]{:S(2)}) collective-permute-start(bf16[512,512]{1,0:T(8,128)(2,1)S(1)} %get-tuple-element.43.refs_3_), channel_id=1, source_target_pairs={{0,1},{1,0},{2,3},{3,2},{4,5},{5,4},{6,7},{7,6},{8,9},{9,8},{10,11... | collective-permute-start | bytes 1572872 | tf_op jit(solution)/shard_map/ppermute | solution.py:199
  90.8 4.2 %collective-permute-start.9 = (bf16[512,512]{1,0:T(8,128)(2,1)S(1)}, bf16[512,512]{1,0:T(8,128)(2,1)S(1)}, u32[]{:S(2)}, u32[]{:S(2)}) collective-permute-start(bf16[512,512]{1,0:T(8,128)(2,1)S(1)} %get-tuple-element.46.refs_2_), channel_id=1, source_target_pairs={{0,1},{1,0},{2,3},{3,2},{4,5},{5,4},{6,7},{7,6},{8,9},{9,8},{10,11... | collective-permute-start | bytes 1572872 | tf_op jit(solution)/shard_map/ppermute | solution.py:199
  91.1 25.9 %collective-permute-start.14 = (bf16[128,2048]{1,0:T(8,128)(2,1)}, bf16[128,2048]{1,0:T(8,128)(2,1)}, u32[]{:S(2)}, u32[]{:S(2)}) collective-permute-start(bf16[128,2048]{1,0:T(8,128)(2,1)} %collective-permute-done.7.refs_1_), channel_id=1, source_target_pairs={{0,4},{2,6},{4,8},{6,10},{8,12},{10,14},{12,0},{14,2},{1,5},{3,7},... | collective-permute-start | bytes 1572872 | tf_op jit(solution)/shard_map/ppermute | solution.py:202
  92.7 35.5 %collective-permute-start.15 = (bf16[128,2048]{1,0:T(8,128)(2,1)}, bf16[128,2048]{1,0:T(8,128)(2,1)}, u32[]{:S(2)}, u32[]{:S(2)}) collective-permute-start(bf16[128,2048]{1,0:T(8,128)(2,1)} %collective-permute-done.8.refs_2_), channel_id=1, source_target_pairs={{0,4},{2,6},{4,8},{6,10},{8,12},{10,14},{12,0},{14,2},{1,5},{3,7},... | collective-permute-start | bytes 1572872 | tf_op jit(solution)/shard_map/ppermute | solution.py:202
  93.5 1.6 copy-start.14
  93.6 8.0 %collective-permute-start.6 = (bf16[256,512]{1,0:T(8,128)(2,1)S(1)}, bf16[256,512]{1,0:T(8,128)(2,1)S(1)}, u32[]{:S(2)}, u32[]{:S(2)}) collective-permute-start(bf16[256,512]{1,0:T(8,128)(2,1)S(1)} %fusion.4), channel_id=1, source_target_pairs={{0,2},{2,0},{4,6},{6,4},{8,10},{10,8},{12,14},{14,12},{1,3},{3,1},... | collective-permute-start | bytes 786440 | tf_op jit(solution)/shard_map/ppermute | solution.py:196
  95.2 16.5 %copy-start.12 = (f32[512,512]{1,0:T(8,128)}, f32[512,512]{1,0:T(8,128)S(1)}, u32[]{:S(2)}) copy-start(f32[512,512]{1,0:T(8,128)S(1)} %convert_element_type.63) | copy-start | bytes 3145732
  101.7 10.0 %copy-start.8 = (bf16[256,512]{1,0:T(8,128)(2,1)}, bf16[256,512]{1,0:T(8,128)(2,1)S(1)}, u32[]{:S(2)}) copy-start(bf16[256,512]{1,0:T(8,128)(2,1)S(1)} %collective-permute-done.6.refs_3_) | copy-start | bytes 786436
  105.7 1.0 copy-start.17
  111.7 1.0 copy-start.6
  112.6 23.7 %collective-permute-start.13 = (bf16[512,512]{1,0:T(8,128)(2,1)}, bf16[512,512]{1,0:T(8,128)(2,1)}, u32[]{:S(2)}, u32[]{:S(2)}) collective-permute-start(bf16[512,512]{1,0:T(8,128)(2,1)} %get-tuple-element.48.refs_2_), channel_id=1, source_target_pairs={{0,1},{1,0},{2,3},{3,2},{4,5},{5,4},{6,7},{7,6},{8,9},{9,8},{10,11... | collective-permute-start | bytes 1572872 | tf_op jit(solution)/shard_map/ppermute | solution.py:199
  117.0 22.5 %collective-permute-start.19 = (bf16[128,2048]{1,0:T(8,128)(2,1)}, bf16[128,2048]{1,0:T(8,128)(2,1)S(1)}, u32[]{:S(2)}, u32[]{:S(2)}) collective-permute-start(bf16[128,2048]{1,0:T(8,128)(2,1)} %collective-permute-done.14.refs_0_), channel_id=1, source_target_pairs={{0,4},{2,6},{4,8},{6,10},{8,12},{10,14},{12,0},{14,2},{1,5},{3,7},... | collective-permute-start | bytes 1572872 | tf_op jit(solution)/shard_map/ppermute | solution.py:202
  128.2 20.6 %collective-permute-start.23 = (bf16[128,2048]{1,0:T(8,128)(2,1)}, bf16[128,2048]{1,0:T(8,128)(2,1)S(1)}, u32[]{:S(2)}, u32[]{:S(2)}) collective-permute-start(bf16[128,2048]{1,0:T(8,128)(2,1)} %collective-permute-done.15.refs_1_), channel_id=1, source_target_pairs={{0,4},{2,6},{4,8},{6,10},{8,12},{10,14},{12,0},{14,2},{1,5},{3,7},... | collective-permute-start | bytes 1572872 | tf_op jit(solution)/shard_map/ppermute | solution.py:202
  128.2 11.1 %collective-permute-start.10 = (bf16[256,512]{1,0:T(8,128)(2,1)S(1)}, bf16[256,512]{1,0:T(8,128)(2,1)S(1)}, u32[]{:S(2)}, u32[]{:S(2)}) collective-permute-start(bf16[256,512]{1,0:T(8,128)(2,1)S(1)} %fusion.1.refs_4_), channel_id=1, source_target_pairs={{0,2},{2,0},{4,6},{6,4},{8,10},{10,8},{12,14},{14,12},{1,3},{3,1},... | collective-permute-start | bytes 786440 | tf_op jit(solution)/shard_map/ppermute | solution.py:196
  129.8 4.6 %copy-start.15 = (f32[512,512]{1,0:T(8,128)S(1)}, f32[512,512]{1,0:T(8,128)}, u32[]{:S(2)}) copy-start(f32[512,512]{1,0:T(8,128)} %copy-done.14) | copy-start | bytes 3145732
  134.0 1.2 copy-start.5
  134.0 1.3 copy-start.9
  134.0 1.6 %collective-permute-start.16 = (bf16[512,256]{1,0:T(8,128)(2,1)S(1)}, bf16[512,256]{1,0:T(8,128)(2,1)S(1)}, u32[]{:S(2)}, u32[]{:S(2)}) collective-permute-start(bf16[512,256]{1,0:T(8,128)(2,1)S(1)} %get-tuple-element.50.refs_0_), channel_id=1, source_target_pairs={{0,1},{1,0},{2,3},{3,2},{4,5},{5,4},{6,7},{7,6},{8,9},{9,8},{10,11... | collective-permute-start | bytes 786440 | tf_op jit(solution)/shard_map/ppermute | solution.py:199
  135.3 2.2 %copy-start.7 = (f32[512,512]{1,0:T(8,128)S(1)}, f32[512,512]{1,0:T(8,128)}, u32[]{:S(2)}) copy-start(f32[512,512]{1,0:T(8,128)} %copy-done.6) | copy-start | bytes 3145732
  135.7 3.6 %copy-start.13 = (f32[512,512]{1,0:T(8,128)S(1)}, f32[512,512]{1,0:T(8,128)}, u32[]{:S(2)}) copy-start(f32[512,512]{1,0:T(8,128)} %copy-done.12) | copy-start | bytes 3145732
  135.7 6.6 %collective-permute-start.17 = (bf16[256,256]{1,0:T(8,128)(2,1)S(1)}, bf16[256,256]{1,0:T(8,128)(2,1)S(1)}, u32[]{:S(2)}, u32[]{:S(2)}) collective-permute-start(bf16[256,256]{1,0:T(8,128)(2,1)S(1)} %fusion.9), channel_id=1, source_target_pairs={{0,2},{2,0},{4,6},{6,4},{8,10},{10,8},{12,14},{14,12},{1,3},{3,1},... | collective-permute-start | bytes 393224 | tf_op jit(solution)/shard_map/ppermute | solution.py:196
  137.5 2.0 %copy-start.1 = (bf16[512,2048]{1,0:T(8,128)(2,1)S(1)}, bf16[512,2048]{1,0:T(8,128)(2,1)}, u32[]{:S(2)}) copy-start(bf16[512,2048]{1,0:T(8,128)(2,1)} %copy-done) | copy-start | bytes 6291460
  137.7 15.5 %collective-permute-start.18 = (bf16[256,512]{1,0:T(8,128)(2,1)S(1)}, bf16[256,512]{1,0:T(8,128)(2,1)S(1)}, u32[]{:S(2)}, u32[]{:S(2)}) collective-permute-start(bf16[256,512]{1,0:T(8,128)(2,1)S(1)} %get-tuple-element.59.refs_1_), channel_id=1, source_target_pairs={{0,2},{2,0},{4,6},{6,4},{8,10},{10,8},{12,14},{14,12},{1,3},{3,1},... | collective-permute-start | bytes 786440 | tf_op jit(solution)/shard_map/ppermute | solution.py:196
  140.7 12.6 %collective-permute-start.20 = (bf16[256,128]{1,0:T(8,128)(2,1)S(1)}, bf16[256,128]{1,0:T(8,128)(2,1)S(1)}, u32[]{:S(2)}, u32[]{:S(2)}) collective-permute-start(bf16[256,128]{1,0:T(8,128)(2,1)S(1)} %get-tuple-element.52), channel_id=1, source_target_pairs={{0,1},{1,0},{2,3},{3,2},{4,5},{5,4},{6,7},{7,6},{8,9},{9,8},{10,11... | collective-permute-start | bytes 196616 | tf_op jit(solution)/shard_map/ppermute | solution.py:199
  140.8 8.0 %collective-permute-start.22 = (bf16[256,128]{1,0:T(8,128)(2,1)S(1)}, bf16[256,128]{1,0:T(8,128)(2,1)S(1)}, u32[]{:S(2)}, u32[]{:S(2)}) collective-permute-start(bf16[256,128]{1,0:T(8,128)(2,1)S(1)} %get-tuple-element.54), channel_id=1, source_target_pairs={{0,3},{1,2},{2,1},{3,0},{4,7},{5,6},{6,5},{7,4},{8,11},{9,10},{10,... | collective-permute-start | bytes 196616 | tf_op jit(solution)/shard_map/ppermute | solution.py:205
  142.3 7.4 %collective-permute-start.21 = (bf16[256,128]{1,0:T(8,128)(2,1)S(1)}, bf16[256,128]{1,0:T(8,128)(2,1)S(1)}, u32[]{:S(2)}, u32[]{:S(2)}) collective-permute-start(bf16[256,128]{1,0:T(8,128)(2,1)S(1)} %get-tuple-element.53), channel_id=1, source_target_pairs={{0,2},{2,0},{4,6},{6,4},{8,10},{10,8},{12,14},{14,12},{1,3},{3,1},... | collective-permute-start | bytes 196616 | tf_op jit(solution)/shard_map/ppermute | solution.py:196
  151.0 2.4 %collective-permute-start.24 = (bf16[256,128]{1,0:T(8,128)(2,1)S(1)}, bf16[256,128]{1,0:T(8,128)(2,1)S(1)}, u32[]{:S(2)}, u32[]{:S(2)}) collective-permute-start(bf16[256,128]{1,0:T(8,128)(2,1)S(1)} %get-tuple-element.56), channel_id=1, source_target_pairs={{0,1},{1,0},{2,3},{3,2},{4,5},{5,4},{6,7},{7,6},{8,9},{9,8},{10,11... | collective-permute-start | bytes 196616 | tf_op jit(solution)/shard_map/ppermute | solution.py:199
  151.1 3.9 %collective-permute-start.26 = (bf16[256,128]{1,0:T(8,128)(2,1)S(1)}, bf16[256,128]{1,0:T(8,128)(2,1)S(1)}, u32[]{:S(2)}, u32[]{:S(2)}) collective-permute-start(bf16[256,128]{1,0:T(8,128)(2,1)S(1)} %get-tuple-element.58), channel_id=1, source_target_pairs={{0,3},{1,2},{2,1},{3,0},{4,7},{5,6},{6,5},{7,4},{8,11},{9,10},{10,... | collective-permute-start | bytes 196616 | tf_op jit(solution)/shard_map/ppermute | solution.py:205
  151.7 5.2 %collective-permute-start.25 = (bf16[256,128]{1,0:T(8,128)(2,1)S(1)}, bf16[256,128]{1,0:T(8,128)(2,1)S(1)}, u32[]{:S(2)}, u32[]{:S(2)}) collective-permute-start(bf16[256,128]{1,0:T(8,128)(2,1)S(1)} %get-tuple-element.57), channel_id=1, source_target_pairs={{0,2},{2,0},{4,6},{6,4},{8,10},{10,8},{12,14},{14,12},{1,3},{3,1},... | collective-permute-start | bytes 196616 | tf_op jit(solution)/shard_map/ppermute | solution.py:196
  153.4 3.5 %copy-start.16 = (f32[256,2048]{1,0:T(8,128)}, f32[256,2048]{1,0:T(8,128)S(1)}, u32[]{:S(2)}) copy-start(f32[256,2048]{1,0:T(8,128)S(1)} %add_dynamic-update-slice_fusion) | copy-start | bytes 6291460
